TPU v7x, 32 devices: a whole 2x2x4 slice. The times are simulated.
32 devices in a mesh: seq: 8 (over z, y), rep: 4 (over x, core).
Axes of the slice: x: 2, y: 2, z: 4, core: 2. Of those that a mesh axis runs over, the one named last changes fastest.
Arguments:
- tokens: bfloat16 [1024, 2048], P('seq'), may hold values from -6 to 6
- norm_gain: float32 [2048], replicated, may hold values from 0.25 to 1.75
- refusal_dir: float32 [2048], replicated, may hold values from -6 to 6
- expert_ids: int32 [1024, 8], P('seq'), may hold values from 0 to 127, as said below
- gate_probs: float32 [1024, 8], P('seq'), may hold values from 0.05 to 0.5
- w_gate: bfloat16 [128, 768, 2048], P('seq', 'rep'), may hold values from -0.125 to 0.125
- w_up: bfloat16 [128, 768, 2048], P('seq', 'rep'), may hold values from -0.125 to 0.125
- w_down: bfloat16 [128, 768, 2048], P('seq', 'rep'), may hold values from -0.21875 to 0.21875
Outputs:
- ablated: bfloat16 [1024, 2048], P('seq', 'rep')
Inputs may be any that keep to these rules, and one draw needn't show every extreme that they name: `expert_ids`: each row names 8 different experts. Among the 128 rows of one device no expert is named more than 12 times, and some expert is named exactly 12 times in the rows of every device.
All inputs are finite; a program needn't handle non-finite values.
Results may differ from a plain program's by a relative error of at most 0.0095.
Values may be sent and summed in bfloat16 or wider, within the bound.
No kernel may reach another device: no remote copies, remote signals or barrier semaphores. Data moves between devices by JAX's collectives and lax.ppermute only.
A program may use at most 128 MiB of HBM per device.

v0:
```python
import functools

import jax
import jax.numpy as jnp
from jax import lax
from jax.experimental import pallas as pl
from jax.experimental.pallas import tpu as pltpu
from jax.sharding import PartitionSpec as P

CAP = 12
SLOTS = 16
RING = 6


def contract(lhs, rhs, lhs_dim, rhs_dim):
    return lax.dot_general(
        lhs, rhs, (((lhs_dim,), (rhs_dim,)), ((), ())), preferred_element_type=jnp.float32
    )


def group_offset(rep, color, dx, dc, width):
    return pl.multiple_of((rep ^ (2 * dx + dc)) * 2 * width + color * width, width)


def token_pieces(n_z, width):
    others = range(1, n_z)
    pieces = [[(2 * d, [(0, 0), (1, 0)])] for d in others]
    pieces.append([(1, [(0, 0), (1, 0), (1, 1)])])
    pieces.append([(2 * d, [(1, 1)]) for d in others])
    pieces.append([(2 * d, [(0, 1)]) for d in others] + [(1, [(0, 1)])])
    pieces.append([(2 * d + 1, [(0, 0)]) for d in others])
    pieces.append([(2 * d + 1, [(0, 1)]) for d in others])
    pieces.append([(2 * d + 1, [(1, 0), (1, 1)]) for d in others])
    return pieces


def norm_kernel(
    tokens_ref, gain_ref, refusal_ref, ids_ref, probs_ref,
    normed_ref, to_z_ref, to_y_ref, unit_ref, base_ref, meta_ref,
):
    width = tokens_ref.shape[1] // 8
    top_k = ids_ref.shape[0]
    rep = lax.axis_index("rep")
    meta_ref[:top_k] = ids_ref[...].astype(jnp.float32)
    meta_ref[top_k:] = probs_ref[...]
    toks = tokens_ref[...].astype(jnp.float32)
    refusal = refusal_ref[...]
    unit = refusal / jnp.sqrt(jnp.sum(refusal * refusal, axis=1, keepdims=True) + 1e-06)
    unit_ref[...] = unit
    inv_rms = lax.rsqrt(jnp.mean(toks * toks, axis=1, keepdims=True) + 1e-06)
    normed_ref[...] = (toks * inv_rms * gain_ref[...]).astype(jnp.bfloat16)
    own = pl.ds(group_offset(rep, 0, 0, 0, width), 2 * width)
    to_z_ref[...] = normed_ref[:, own]
    to_y_ref[:, : 2 * width] = normed_ref[:, own]
    to_y_ref[:, 2 * width :] = normed_ref[:, pl.ds(group_offset(rep, 1, 1, 0, width), width)]
    along = jnp.sum(toks * unit, axis=1, keepdims=True)
    base_ref[...] = tokens_ref[:, own].astype(jnp.float32) - along * unit_ref[:, own]


def norm_and_base(tokens, norm_gain, refusal_dir, expert_ids, gate_probs):
    tok_rows, model_width = tokens.shape
    width = model_width // 8
    vmem = pl.BlockSpec(memory_space=pltpu.VMEM)
    return pl.pallas_call(
        norm_kernel,
        out_shape=[
            jax.ShapeDtypeStruct((tok_rows, model_width), jnp.bfloat16),
            jax.ShapeDtypeStruct((tok_rows, 2 * width), jnp.bfloat16),
            jax.ShapeDtypeStruct((tok_rows, 3 * width), jnp.bfloat16),
            jax.ShapeDtypeStruct((1, model_width), jnp.float32),
            jax.ShapeDtypeStruct((tok_rows, 2 * width), jnp.float32),
            jax.ShapeDtypeStruct((2 * expert_ids.shape[1], tok_rows), jnp.float32),
        ],
        in_specs=[vmem] * 5,
        out_specs=[vmem] * 6,
    )(tokens, norm_gain[None, :], refusal_dir[None, :], expert_ids.T, gate_probs.T)


def route_kernel(exp_dev, n_z, *refs):
    near_refs, far_ref, picks_ref, weights_ref, meta_ref = (
        refs[:n_z], refs[n_z], refs[n_z + 1], refs[n_z + 2], refs[n_z + 3]
    )
    n_seq, twice_k, tok_rows = meta_ref.shape
    top_k = twice_k // 2
    for d in range(n_z):
        meta_ref[2 * d] = near_refs[d][...]
        meta_ref[2 * d + 1] = far_ref[d]
    first = (lax.axis_index("seq") * exp_dev).astype(jnp.float32)
    exp_iota = lax.broadcasted_iota(jnp.int32, (exp_dev, tok_rows), 0).astype(jnp.float32) + first
    earlier = (
        lax.broadcasted_iota(jnp.int32, (tok_rows, tok_rows), 0)
        < lax.broadcasted_iota(jnp.int32, (tok_rows, tok_rows), 1)
    ).astype(jnp.float32).astype(jnp.bfloat16)
    slot_iota = lax.broadcasted_iota(jnp.int32, (exp_dev, SLOTS, tok_rows), 1).astype(jnp.float32)

    def place_block(j, carry):
        meta = meta_ref[j]
        hit = jnp.zeros((exp_dev, tok_rows), jnp.float32)
        prob = jnp.zeros((exp_dev, tok_rows), jnp.float32)
        for k in range(top_k):
            same = meta[k : k + 1, :] == exp_iota
            hit = jnp.where(same, 1.0, hit)
            prob = jnp.where(same, meta[top_k + k : top_k + k + 1, :], prob)
        rank = contract(hit.astype(jnp.bfloat16), earlier, 1, 0)
        slot = jnp.where(hit > 0.0, rank, -1.0)
        here = slot[:, None, :] == slot_iota
        onehot = jnp.where(here, 1.0, 0.0).reshape(exp_dev * SLOTS, tok_rows)
        weight = jnp.where(here, prob[:, None, :], 0.0).reshape(exp_dev * SLOTS, tok_rows)
        picks_ref[j] = onehot.astype(jnp.bfloat16)
        weights_ref[j] = weight.T.astype(jnp.bfloat16)
        return carry

    lax.fori_loop(0, n_seq, place_block, 0)


def route(near, far, exp_dev):
    n_z, twice_k, tok_rows = far.shape
    n_seq = 2 * n_z
    vmem = pl.BlockSpec(memory_space=pltpu.VMEM)
    return pl.pallas_call(
        functools.partial(route_kernel, exp_dev, n_z),
        out_shape=[
            jax.ShapeDtypeStruct((n_seq, exp_dev * SLOTS, tok_rows), jnp.bfloat16),
            jax.ShapeDtypeStruct((n_seq, tok_rows, exp_dev * SLOTS), jnp.bfloat16),
        ],
        in_specs=[vmem] * (n_z + 1),
        out_specs=[vmem] * 2,
        scratch_shapes=[pltpu.VMEM((n_seq, twice_k, tok_rows), jnp.float32)],
        cost_estimate=pl.CostEstimate(
            flops=4_000_000_000, bytes_accessed=8 * n_seq * exp_dev * SLOTS * tok_rows,
            transcendentals=0,
        ),
    )(*near, far)


def moe_kernel(n_pieces, *refs):
    picks, weights, unit_ref, own_hbm = refs[:4]
    pieces_hbm = refs[4 : 4 + n_pieces]
    w_gate_hbm, w_up_hbm, w_down_hbm = refs[4 + n_pieces : 7 + n_pieces]
    out_refs = refs[7 + n_pieces : 15 + n_pieces]
    (w_in, w_down, toks, rows, mixed, tok_sems, sems) = refs[15 + n_pieces :]
    n_seq, tok_rows, model_width = toks.shape
    n_z = n_seq // 2
    exp_dev, hid_dev, _ = w_gate_hbm.shape
    width = model_width // 8
    slots_src = exp_dev * SLOTS
    rep = lax.axis_index("rep")

    pltpu.make_async_copy(own_hbm, toks.at[0], tok_sems.at[0]).start()
    kinds = token_pieces(n_z, width)
    for i, piece in enumerate(pieces_hbm):
        dc = i // len(kinds)
        for at, (j, runs) in enumerate(kinds[i % len(kinds)]):
            block = piece if len(piece.shape) == 2 else piece.at[at]
            for n, (color, dx) in enumerate(runs):
                cols = pl.ds(group_offset(rep, color, dx, dc, width), width)
                pltpu.make_async_copy(
                    block.at[:, pl.ds(n * width, width)], toks.at[j, :, cols], tok_sems.at[j]
                ).start()

    def weight_copies(e):
        at = lax.rem(e, RING)
        gate_at, up_at = pl.ds(0, hid_dev), pl.ds(hid_dev, hid_dev)
        return [
            pltpu.make_async_copy(w_gate_hbm.at[e], w_in.at[at, gate_at], sems.at[0, at]),
            pltpu.make_async_copy(w_up_hbm.at[e], w_in.at[at, up_at], sems.at[1, at]),
            pltpu.make_async_copy(w_down_hbm.at[e], w_down.at[at], sems.at[2, at]),
        ]

    def fetch(e, carry):
        for copy in weight_copies(e):
            copy.start()
        return carry

    lax.fori_loop(0, min(RING, exp_dev), fetch, 0)
    quarters = [slice(2 * q * width, 2 * (q + 1) * width) for q in range(4)]

    def pick(j, carry):
        pltpu.make_async_copy(toks.at[j], toks.at[j], tok_sems.at[j]).wait()
        onehot = picks[j]
        for cols in quarters:
            got = contract(onehot, toks[j, :, cols], 1, 0).astype(jnp.bfloat16)
            rows[j, :, :, cols] = got.reshape(exp_dev, SLOTS, 2 * width)
        return carry

    lax.fori_loop(0, n_seq, pick, 0)

    def expert(e, carry):
        at = lax.rem(e, RING)
        for copy in weight_copies(e):
            copy.wait()
        taken = rows[:, e].reshape(n_seq * SLOTS, model_width)
        both = contract(w_in[at], taken, 1, 1)
        gate_val, up_val = both[:hid_dev], both[hid_dev:]
        hidden = gate_val / (1.0 + jnp.exp(-gate_val)) * up_val
        hidden = hidden.T.astype(jnp.bfloat16)
        for cols in quarters:
            piece = contract(hidden, w_down[at, :, cols], 1, 0).astype(jnp.bfloat16)
            rows[:, e, :, cols] = piece.reshape(n_seq, SLOTS, 2 * width)

        @pl.when(e + RING < exp_dev)
        def _():
            fetch(e + RING, 0)

        return carry

    lax.fori_loop(0, exp_dev, expert, 0)

    def combine(dz, carry):
        for dy in range(2):
            j = 2 * dz + dy
            weight = weights[j]
            along = jnp.zeros((tok_rows, 1), jnp.float32)
            for cols in quarters:
                got = contract(weight, rows[j, :, :, cols].reshape(slots_src, 2 * width), 1, 0)
                mixed[:, cols] = got
                along += jnp.sum(got * unit_ref[:, cols], axis=1, keepdims=True)
            for dc in range(2):
                first_far, second_far, first_near, second_near = out_refs[4 * dc : 4 * dc + 4]
                second = second_far if dy else second_near
                for dst, at, start, color, dx in (
                    (first_far, j, 0, 0, 1),
                    (first_near, j, 0, 0, 0),
                    (second, dz, 0, 1, 0),
                    (second, dz, width, 1, 1),
                ):
                    cols = pl.ds(group_offset(rep, color, dx, dc, width), width)
                    value = mixed[:, cols] - along * unit_ref[:, cols]
                    dst[at, :, start : start + width] = value.astype(jnp.bfloat16)
        return carry

    lax.fori_loop(0, n_z, combine, 0)


def moe_partial(picks, weights, unit_dir, own, pieces, w_gate, w_up, w_down):
    n_seq, _, tok_rows = picks.shape
    exp_dev, hid_dev, model_width = w_gate.shape
    width = model_width // 8
    vmem = pl.BlockSpec(memory_space=pltpu.VMEM)
    hbm = pl.BlockSpec(memory_space=pl.ANY)
    n_pieces = len(pieces)
    outs = [
        jax.ShapeDtypeStruct((blocks, tok_rows, runs * width), jnp.bfloat16)
        for _ in range(2)
        for blocks, runs in ((n_seq, 1), (n_seq // 2, 2), (n_seq, 1), (n_seq // 2, 2))
    ]
    return pl.pallas_call(
        functools.partial(moe_kernel, n_pieces),
        out_shape=outs,
        in_specs=[vmem] * 3 + [hbm] * (n_pieces + 4),
        out_specs=[vmem] * len(outs),
        scratch_shapes=[
            pltpu.VMEM((RING, 2 * hid_dev, model_width), jnp.bfloat16),
            pltpu.VMEM((RING, hid_dev, model_width), jnp.bfloat16),
            pltpu.VMEM((n_seq, tok_rows, model_width), jnp.bfloat16),
            pltpu.VMEM((n_seq, exp_dev, SLOTS, model_width), jnp.bfloat16),
            pltpu.VMEM((tok_rows, model_width), jnp.float32),
            pltpu.SemaphoreType.DMA((n_seq,)),
            pltpu.SemaphoreType.DMA((3, RING)),
        ],
        compiler_params=pltpu.CompilerParams(vmem_limit_bytes=42 * 1024 * 1024),
        cost_estimate=pl.CostEstimate(
            flops=6 * n_seq * SLOTS * exp_dev * hid_dev * model_width,
            bytes_accessed=6 * exp_dev * hid_dev * model_width + 4 * n_seq * own.size,
            transcendentals=0,
        ),
    )(picks, weights, unit_dir, own, *pieces, w_gate, w_up, w_down)


def swap(value, axis, distance):
    size = lax.axis_size(axis)
    return lax.ppermute(value, axis, [(i, i ^ distance) for i in range(size)])


def added(*terms):
    return sum(term.astype(jnp.float32) for term in terms).astype(jnp.bfloat16)


def gathered(tokens, norm_gain, refusal_dir, expert_ids, gate_probs, w_gate, w_up, w_down):
    tok_rows, model_width = tokens.shape
    n_z = lax.axis_size("seq") // 2
    others = range(1, n_z)
    exp_dev = w_gate.shape[0]
    width = model_width // 8

    normed, to_z, to_y, unit_dir, base, meta = norm_and_base(
        tokens, norm_gain, refusal_dir, expert_ids, gate_probs
    )
    from_z = [swap(to_z, "seq", 2 * d) for d in others]
    from_y = swap(to_y, "seq", 1)
    near = [meta] + [swap(meta, "seq", 2 * d) for d in others]
    picks, weights = route(near, swap(jnp.stack(near), "seq", 1), exp_dev)

    first = jnp.stack([piece[:, :width] for piece in from_z])
    second = jnp.stack([piece[:, width:] for piece in from_z])
    second, picks, weights = lax.optimization_barrier((second, picks, weights))
    x_two = swap(second, "rep", 2)
    y_two = swap(first, "seq", 1)
    x_one = swap(jnp.concatenate([first, from_y[None, :, :width]]), "rep", 2)
    sibling = [swap(piece, "rep", 1) for piece in (*from_z, from_y)]
    to_y, y_two, *sibling = lax.optimization_barrier(
        (jnp.concatenate([second, x_two], axis=2), y_two, *sibling)
    )
    y_three = swap(to_y, "seq", 1)
    x_three = swap(y_two, "rep", 2)
    last = [x_two, x_one, y_two, x_three, y_three]
    pieces = [*from_z, from_y, *last, *sibling, *[swap(piece, "rep", 1) for piece in last]]

    sums = moe_partial(picks, weights, unit_dir, normed, pieces, w_gate, w_up, w_down)
    kept, sent = sums[:4], sums[4:]
    first_far, second_far, first_near, second_near = [
        added(mine, swap(theirs, "rep", 1)) for mine, theirs in zip(kept, sent)
    ]
    first_sum = added(first_near, swap(first_far, "rep", 2))
    second_sum = added(second_near, swap(second_far, "seq", 1))
    by_y = first_sum.reshape(n_z, 2, tok_rows, width)
    first_sum = added(by_y[:, 0], swap(by_y[:, 1], "seq", 1))
    second_sum = added(second_sum[:, :, :width], swap(second_sum[:, :, width:], "rep", 2))
    blocks = jnp.concatenate([first_sum, second_sum], axis=2)
    arrived = [swap(blocks[d], "seq", 2 * d) for d in others]
    summed = sum(term.astype(jnp.float32) for term in [blocks[0], *arrived])

    return (base + summed).astype(jnp.bfloat16)


def exchanged(tokens, norm_gain, refusal_dir, expert_ids, gate_probs, w_gate, w_up, w_down):
    tok_rows, model_width = tokens.shape
    top_k = expert_ids.shape[1]
    n_seq = lax.axis_size("seq")
    n_rep = lax.axis_size("rep")
    exp_dev = w_gate.shape[0]
    experts = exp_dev * n_seq
    slot_count = tok_rows * top_k
    part_width = model_width // n_rep
    tokens_f32 = tokens.astype(jnp.float32)
    inv_rms = lax.rsqrt(jnp.mean(tokens_f32 * tokens_f32, axis=1, keepdims=True) + 1e-06)
    normed = (tokens_f32 * inv_rms * norm_gain).astype(jnp.bfloat16)
    flat_ids = expert_ids.reshape(slot_count)
    onehot = (flat_ids[:, None] == jnp.arange(experts, dtype=jnp.int32)[None, :]).astype(jnp.int32)
    slot_rank = jnp.sum(jnp.cumsum(onehot, axis=0) * onehot, axis=1) - 1
    target = flat_ids * CAP + slot_rank
    repeated = jnp.broadcast_to(normed[:, None, :], (tok_rows, top_k, model_width)).reshape(
        slot_count, model_width
    )
    sendbuf = jnp.zeros((experts * CAP, model_width), jnp.bfloat16).at[target].set(repeated)
    sendbuf = sendbuf.reshape(n_seq, exp_dev, CAP, model_width)
    arrived = lax.all_to_all(sendbuf, "seq", split_axis=0, concat_axis=0, tiled=True)
    gate_val = jnp.einsum("secd,efd->secf", arrived, w_gate, preferred_element_type=jnp.float32)
    up_val = jnp.einsum("secd,efd->secf", arrived, w_up, preferred_element_type=jnp.float32)
    hidden = (jax.nn.silu(gate_val) * up_val).astype(jnp.bfloat16)
    pieces = jnp.einsum(
        "secf,efd->secd", hidden, w_down, preferred_element_type=jnp.float32
    ).astype(jnp.bfloat16)
    probs_flat = gate_probs.reshape(slot_count)[:, None]
    returned = lax.all_to_all(pieces, "seq", split_axis=0, concat_axis=0, tiled=True)
    returned = returned.reshape(experts * CAP, model_width)
    weighted = returned[target].astype(jnp.float32) * probs_flat
    moe_part = jnp.sum(weighted.reshape(tok_rows, top_k, model_width), axis=1)
    summed = lax.psum_scatter(
        moe_part.astype(jnp.bfloat16), "rep", scatter_dimension=1, tiled=True
    ).astype(jnp.float32)
    unit_dir = refusal_dir / jnp.sqrt(jnp.sum(refusal_dir * refusal_dir) + 1e-06)
    rep_offset = lax.axis_index("rep") * part_width
    unit_slice = lax.dynamic_slice_in_dim(unit_dir, rep_offset, part_width, 0)
    own_tokens = lax.dynamic_slice_in_dim(tokens_f32, rep_offset, part_width, 1)
    residual = own_tokens + summed
    along_dir = lax.psum(jnp.sum(residual * unit_slice, axis=1), "rep")
    return (residual - along_dir[:, None] * unit_slice).astype(jnp.bfloat16)


def local(tokens, norm_gain, refusal_dir, expert_ids, gate_probs, w_gate, w_up, w_down):
    plan = gathered if w_gate.shape[0] * CAP >= tokens.shape[0] else exchanged
    return plan(tokens, norm_gain, refusal_dir, expert_ids, gate_probs, w_gate, w_up, w_down)


def solution(mesh):
    placed = (
        P("seq", None),
        P(),
        P(),
        P("seq", None),
        P("seq", None),
        P("seq", "rep", None),
        P("seq", "rep", None),
        P("seq", "rep", None),
    )
    return jax.shard_map(
        local, mesh=mesh, in_specs=placed, out_specs=P("seq", "rep"), check_vma=False
    )
```

profile of v0, /device:TPU:0, one launch (start us, length us, event | category | flops | bytes accessed | tf_op | source)
XLA Modules:
  0.0 117.7 jit_solution(15814368409996706779)
XLA Ops:
  0.0 2.4 %shard_map.82 = (bf16[128,2048]{1,0:T(8,128)(2,1)}, bf16[128,512]{1,0:T(8,128)(2,1)}, bf16[128,768]{1,0:T(8,128)(2,1)}, f32[1,2048]{1,0:T(1,128)}, f32[128,512]{1,0:T(8,128)}, /*index=5*/f32[16,128]{1,0:T(8,128)}) custom-call(bf16[128,2048]{1,0:T(8,128)(2,1)} %tokens_ref.1, f32[1,2048]{1,0:T(1,128)} %bitcast.47, f32[1,2048]{1,0:T(1,128)} %bitcast.48, ...), custom_call_target="tpu_custom_call" | custom-call | tf_op jit(solution)/shard_map/pallas_call | solution.py:64
  2.4 5.1 %collective-permute-start.5 = (f32[16,128]{1,0:T(8,128)}, f32[16,128]{1,0:T(8,128)S(1)}, u32[]{:S(2)}, u32[]{:S(2)}) collective-permute-start(f32[16,128]{1,0:T(8,128)} %get-tuple-element.32.refs_0_), channel_id=1, source_target_pairs={{0,24},{4,28},{8,16},{12,20},{16,8},{20,12},{24,0},{28,4},{1,25},{... | collective-permute-start | bytes 24584 | tf_op jit(solution)/shard_map/ppermute | solution.py:272
  8.2 1.2 %collective-permute-done.5.refs_3_ = f32[16,128]{1,0:T(8,128)S(1)} collective-permute-done((f32[16,128]{1,0:T(8,128)}, f32[16,128]{1,0:T(8,128)S(1)}, u32[]{:S(2)}, u32[]{:S(2)}) %collective-permute-start.5) | collective-permute-done | bytes 8224 | tf_op jit(solution)/shard_map/ppermute | solution.py:272
  9.4 2.9 %collective-permute-done.4.refs_2_ = f32[16,128]{1,0:T(8,128)S(1)} collective-permute-done((f32[16,128]{1,0:T(8,128)}, f32[16,128]{1,0:T(8,128)S(1)}, u32[]{:S(2)}, u32[]{:S(2)}) %collective-permute-start.4) | collective-permute-done | bytes 8224 | tf_op jit(solution)/shard_map/ppermute | solution.py:272
  13.0 1.5 %collective-permute-start.6 = (f32[4,16,128]{2,1,0:T(8,128)S(1)}, f32[4,16,128]{2,1,0:T(8,128)S(1)}, u32[]{:S(2)}, u32[]{:S(2)}) collective-permute-start(f32[4,16,128]{2,1,0:T(8,128)S(1)} %pad_maximum_fusion.5), channel_id=1, source_target_pairs={{0,4},{4,0},{8,12},{12,8},{16,20},{20,16},{24,28},{28,24},{1,5},{5... | collective-permute-start | bytes 98312 | tf_op jit(solution)/shard_map/ppermute | solution.py:272
  14.5 1.5 %collective-permute-start.2 = (bf16[128,512]{1,0:T(8,128)(2,1)}, bf16[128,512]{1,0:T(8,128)(2,1)S(1)}, u32[]{:S(2)}, u32[]{:S(2)}) collective-permute-start(bf16[128,512]{1,0:T(8,128)(2,1)} %get-tuple-element.31), channel_id=1, source_target_pairs={{0,24},{4,28},{8,16},{12,20},{16,8},{20,12},{24,0},{28,4},{1,25},{... | collective-permute-start | bytes 393224 | tf_op jit(solution)/shard_map/ppermute | solution.py:272
  16.5 2.4 %collective-permute-start = (bf16[128,512]{1,0:T(8,128)(2,1)}, bf16[128,512]{1,0:T(8,128)(2,1)S(1)}, u32[]{:S(2)}, u32[]{:S(2)}) collective-permute-start(bf16[128,512]{1,0:T(8,128)(2,1)} %get-tuple-element.31), channel_id=1, source_target_pairs={{0,8},{4,12},{8,0},{12,4},{16,24},{20,28},{24,16},{28,20},{1,9},{5... | collective-permute-start | bytes 393224 | tf_op jit(solution)/shard_map/ppermute | solution.py:272
  20.0 3.7 %shard_map.83 = (bf16[8,256,128]{2,1,0:T(8,128)(2,1)}, bf16[8,128,256]{2,1,0:T(8,128)(2,1)}) custom-call(f32[16,128]{1,0:T(8,128)} %get-tuple-element.32.refs_0_, f32[16,128]{1,0:T(8,128)} %copy-done.7, f32[16,128]{1,0:T(8,128)} %copy-done.6, f32[16,128]{1,0:T(8,128)} %copy-done.5, f32[4,16,128]{2,1,0:T(8,128)} %copy-done.8), custom_call_target="tpu_custom_call" | custom-call | flops 4000000000 | bytes 2097152 | tf_op jit(solution)/shard_map/pallas_call | solution.py:120
  23.7 3.3 %collective-permute-done.1.refs_5_ = bf16[128,512]{1,0:T(8,128)(2,1)S(1)} collective-permute-done((bf16[128,512]{1,0:T(8,128)(2,1)}, bf16[128,512]{1,0:T(8,128)(2,1)S(1)}, u32[]{:S(2)}, u32[]{:S(2)}) %collective-permute-start.1) | collective-permute-done | bytes 131104 | tf_op jit(solution)/shard_map/ppermute | solution.py:272
  27.1 1.6 %collective-permute-start.8 = (bf16[3,128,256]{2,1,0:T(8,128)(2,1)S(1)}, bf16[3,128,256]{2,1,0:T(8,128)(2,1)S(1)}, u32[]{:S(2)}, u32[]{:S(2)}) collective-permute-start(bf16[3,128,256]{2,1,0:T(8,128)(2,1)S(1)} %pad_maximum_fusion.2), channel_id=1, source_target_pairs={{0,2},{1,3},{2,0},{3,1},{4,6},{5,7},{6,4},{7,5},{8,10},{9,11},{10,... | collective-permute-start | bytes 589832 | tf_op jit(solution)/shard_map/ppermute | solution.py:272
  29.8 3.1 %collective-permute-done.8.refs_8_ = bf16[3,128,256]{2,1,0:T(8,128)(2,1)S(1)} collective-permute-done((bf16[3,128,256]{2,1,0:T(8,128)(2,1)S(1)}, bf16[3,128,256]{2,1,0:T(8,128)(2,1)S(1)}, u32[]{:S(2)}, u32[]{:S(2)}) %collective-permute-start.8) | collective-permute-done | bytes 196640 | tf_op jit(solution)/shard_map/ppermute | solution.py:272
  32.9 1.3 %collective-permute-done.11.refs_13_ = bf16[128,512]{1,0:T(8,128)(2,1)S(1)} collective-permute-done((bf16[128,512]{1,0:T(8,128)(2,1)S(1)}, bf16[128,512]{1,0:T(8,128)(2,1)S(1)}, u32[]{:S(2)}, u32[]{:S(2)}) %collective-permute-start.11) | collective-permute-done | bytes 131104 | tf_op jit(solution)/shard_map/ppermute | solution.py:272
  35.0 1.3 %collective-permute-start.9 = (bf16[4,128,256]{2,1,0:T(8,128)(2,1)S(1)}, bf16[4,128,256]{2,1,0:T(8,128)(2,1)S(1)}, u32[]{:S(2)}, u32[]{:S(2)}) collective-permute-start(bf16[4,128,256]{2,1,0:T(8,128)(2,1)S(1)} %pad_maximum_fusion.1), channel_id=1, source_target_pairs={{0,2},{1,3},{2,0},{3,1},{4,6},{5,7},{6,4},{7,5},{8,10},{9,11},{10,... | collective-permute-start | bytes 786440 | tf_op jit(solution)/shard_map/ppermute | solution.py:272
  36.3 0.8 collective-permute-start.15
  37.1 8.3 %collective-permute-done.16.refs_12_ = bf16[3,128,512]{2,1,0:T(8,128)(2,1)S(1)} collective-permute-done((bf16[3,128,512]{2,1,0:T(8,128)(2,1)S(1)}, bf16[3,128,512]{2,1,0:T(8,128)(2,1)S(1)}, u32[]{:S(2)}, u32[]{:S(2)}) %collective-permute-start.16) | collective-permute-done | bytes 393248 | tf_op jit(solution)/shard_map/ppermute | solution.py:272
  48.6 1.0 copy-done.1
  49.6 1.0 copy-done.2
  50.7 25.7 %shard_map.84 = (bf16[8,128,256]{2,1,0:T(8,128)(2,1)S(1)}, bf16[4,128,512]{2,1,0:T(8,128)(2,1)S(1)}, bf16[8,128,256]{2,1,0:T(8,128)(2,1)S(1)}, bf16[4,128,512]{2...) custom-call(bf16[8,256,128]{2,1,0:T(8,128)(2,1)S(1)} %copy-done.1, ...), custom_call_target="tpu_custom_call" | custom-call | flops 4831838208 | bytes 46137344 | tf_op jit(solution)/shard_map/pallas_call | solution.py:247
  77.1 1.3 %collective-permute-done.23 = bf16[8,128,256]{2,1,0:T(8,128)(2,1)S(1)} collective-permute-done((bf16[8,128,256]{2,1,0:T(8,128)(2,1)S(1)}, bf16[8,128,256]{2,1,0:T(8,128)(2,1)S(1)}, u32[]{:S(2)}, u32[]{:S(2)}) %collective-permute-start.23) | collective-permute-done | bytes 524320 | tf_op jit(solution)/shard_map/ppermute | solution.py:272
  78.5 1.6 %collective-permute-start.24 = (bf16[8,128,256]{2,1,0:T(8,128)(2,1)S(1)}, bf16[8,128,256]{2,1,0:T(8,128)(2,1)S(1)}, u32[]{:S(2)}, u32[]{:S(2)}) collective-permute-start(bf16[8,128,256]{2,1,0:T(8,128)(2,1)S(1)} %add_convert_fusion.4), channel_id=1, source_target_pairs={{0,2},{1,3},{2,0},{3,1},{4,6},{5,7},{6,4},{7,5},{8,10},{9,11},{10,... | collective-permute-start | bytes 1572872 | tf_op jit(solution)/shard_map/ppermute | solution.py:272
  80.3 1.6 %collective-permute-start.28 = (bf16[4,128,512]{2,1,0:T(8,128)(2,1)S(1)}, bf16[4,128,512]{2,1,0:T(8,128)(2,1)S(1)}, u32[]{:S(2)}, u32[]{:S(2)}) collective-permute-start(bf16[4,128,512]{2,1,0:T(8,128)(2,1)S(1)} %add_convert_fusion.1), channel_id=1, source_target_pairs={{0,4},{4,0},{8,12},{12,8},{16,20},{20,16},{24,28},{28,24},{1,5},{5... | collective-permute-start | bytes 1572872 | tf_op jit(solution)/shard_map/ppermute | solution.py:272
  81.8 10.7 %collective-permute-done.24 = bf16[8,128,256]{2,1,0:T(8,128)(2,1)S(1)} collective-permute-done((bf16[8,128,256]{2,1,0:T(8,128)(2,1)S(1)}, bf16[8,128,256]{2,1,0:T(8,128)(2,1)S(1)}, u32[]{:S(2)}, u32[]{:S(2)}) %collective-permute-start.24) | collective-permute-done | bytes 524320 | tf_op jit(solution)/shard_map/ppermute | solution.py:272
  92.8 1.6 %collective-permute-start.25 = (bf16[4,128,256]{2,1,0:T(8,128)(2,1)S(1)}, bf16[4,128,256]{2,1,0:T(8,128)(2,1)S(1)}, u32[]{:S(2)}, u32[]{:S(2)}) collective-permute-start(bf16[4,128,256]{2,1,0:T(8,128)(2,1)S(1)} %slice_bitcast_fusion), channel_id=1, source_target_pairs={{0,4},{4,0},{8,12},{12,8},{16,20},{20,16},{24,28},{28,24},{1,5},{5... | collective-permute-start | bytes 786440 | tf_op jit(solution)/shard_map/ppermute | solution.py:272
  94.9 1.3 %collective-permute-start.29 = (bf16[4,128,256]{2,1,0:T(8,128)(2,1)S(1)}, bf16[4,128,256]{2,1,0:T(8,128)(2,1)S(1)}, u32[]{:S(2)}, u32[]{:S(2)}) collective-permute-start(bf16[4,128,256]{2,1,0:T(8,128)(2,1)S(1)} %slice.70), channel_id=1, source_target_pairs={{0,2},{1,3},{2,0},{3,1},{4,6},{5,7},{6,4},{7,5},{8,10},{9,11},{10,... | collective-permute-start | bytes 786440 | tf_op jit(solution)/shard_map/ppermute | solution.py:272
  96.2 4.2 %collective-permute-done.25 = bf16[4,128,256]{2,1,0:T(8,128)(2,1)S(1)} collective-permute-done((bf16[4,128,256]{2,1,0:T(8,128)(2,1)S(1)}, bf16[4,128,256]{2,1,0:T(8,128)(2,1)S(1)}, u32[]{:S(2)}, u32[]{:S(2)}) %collective-permute-start.25) | collective-permute-done | bytes 262176 | tf_op jit(solution)/shard_map/ppermute | solution.py:272
  100.5 2.4 %collective-permute-done.29 = bf16[4,128,256]{2,1,0:T(8,128)(2,1)S(1)} collective-permute-done((bf16[4,128,256]{2,1,0:T(8,128)(2,1)S(1)}, bf16[4,128,256]{2,1,0:T(8,128)(2,1)S(1)}, u32[]{:S(2)}, u32[]{:S(2)}) %collective-permute-start.29) | collective-permute-done | bytes 262176 | tf_op jit(solution)/shard_map/ppermute | solution.py:272
  103.1 2.5 %collective-permute-start.32 = (bf16[128,512]{1,0:T(8,128)(2,1)S(1)}, bf16[128,512]{1,0:T(8,128)(2,1)S(1)}, u32[]{:S(2)}, u32[]{:S(2)}) collective-permute-start(bf16[128,512]{1,0:T(8,128)(2,1)S(1)} %get-tuple-element.56), channel_id=1, source_target_pairs={{0,24},{4,28},{8,16},{12,20},{16,8},{20,12},{24,0},{28,4},{1,25},{... | collective-permute-start | bytes 393224 | tf_op jit(solution)/shard_map/ppermute | solution.py:272
  105.6 0.9 collective-permute-start.31
  106.6 3.4 %collective-permute-done.30 = bf16[128,512]{1,0:T(8,128)(2,1)S(1)} collective-permute-done((bf16[128,512]{1,0:T(8,128)(2,1)S(1)}, bf16[128,512]{1,0:T(8,128)(2,1)S(1)}, u32[]{:S(2)}, u32[]{:S(2)}) %collective-permute-start.30) | collective-permute-done | bytes 131104 | tf_op jit(solution)/shard_map/ppermute | solution.py:272
  110.0 2.3 %collective-permute-done.32 = bf16[128,512]{1,0:T(8,128)(2,1)S(1)} collective-permute-done((bf16[128,512]{1,0:T(8,128)(2,1)S(1)}, bf16[128,512]{1,0:T(8,128)(2,1)S(1)}, u32[]{:S(2)}, u32[]{:S(2)}) %collective-permute-start.32) | collective-permute-done | bytes 131104 | tf_op jit(solution)/shard_map/ppermute | solution.py:272
  112.3 4.6 %collective-permute-done.31 = bf16[128,512]{1,0:T(8,128)(2,1)S(1)} collective-permute-done((bf16[128,512]{1,0:T(8,128)(2,1)S(1)}, bf16[128,512]{1,0:T(8,128)(2,1)S(1)}, u32[]{:S(2)}, u32[]{:S(2)}) %collective-permute-start.31) | collective-permute-done | bytes 131104 | tf_op jit(solution)/shard_map/ppermute | solution.py:272
  116.9 0.7 fusion.4
  (74 shorter events, 10.1 us)
Async XLA Ops:
  2.4 7.0 %collective-permute-start.5 = (f32[16,128]{1,0:T(8,128)}, f32[16,128]{1,0:T(8,128)S(1)}, u32[]{:S(2)}, u32[]{:S(2)}) collective-permute-start(f32[16,128]{1,0:T(8,128)} %get-tuple-element.32.refs_0_), channel_id=1, source_target_pairs={{0,24},{4,28},{8,16},{12,20},{16,8},{20,12},{24,0},{28,4},{1,25},{... | collective-permute-start | bytes 24584 | tf_op jit(solution)/shard_map/ppermute | solution.py:272
  7.5 4.8 %collective-permute-start.4 = (f32[16,128]{1,0:T(8,128)}, f32[16,128]{1,0:T(8,128)S(1)}, u32[]{:S(2)}, u32[]{:S(2)}) collective-permute-start(f32[16,128]{1,0:T(8,128)} %get-tuple-element.32.refs_0_), channel_id=1, source_target_pairs={{0,16},{4,20},{8,24},{12,28},{16,0},{20,4},{24,8},{28,12},{1,17},{... | collective-permute-start | bytes 24584 | tf_op jit(solution)/shard_map/ppermute | solution.py:272
  7.5 4.8 %collective-permute-start.3 = (f32[16,128]{1,0:T(8,128)}, f32[16,128]{1,0:T(8,128)S(1)}, u32[]{:S(2)}, u32[]{:S(2)}) collective-permute-start(f32[16,128]{1,0:T(8,128)} %get-tuple-element.32.refs_0_), channel_id=1, source_target_pairs={{0,8},{4,12},{8,0},{12,4},{16,24},{20,28},{24,16},{28,20},{1,9},{5... | collective-permute-start | bytes 24584 | tf_op jit(solution)/shard_map/ppermute | solution.py:272
  13.0 6.4 %collective-permute-start.6 = (f32[4,16,128]{2,1,0:T(8,128)S(1)}, f32[4,16,128]{2,1,0:T(8,128)S(1)}, u32[]{:S(2)}, u32[]{:S(2)}) collective-permute-start(f32[4,16,128]{2,1,0:T(8,128)S(1)} %pad_maximum_fusion.5), channel_id=1, source_target_pairs={{0,4},{4,0},{8,12},{12,8},{16,20},{20,16},{24,28},{28,24},{1,5},{5... | collective-permute-start | bytes 98312 | tf_op jit(solution)/shard_map/ppermute | solution.py:272
  14.5 9.2 %collective-permute-start.2 = (bf16[128,512]{1,0:T(8,128)(2,1)}, bf16[128,512]{1,0:T(8,128)(2,1)S(1)}, u32[]{:S(2)}, u32[]{:S(2)}) collective-permute-start(bf16[128,512]{1,0:T(8,128)(2,1)} %get-tuple-element.31), channel_id=1, source_target_pairs={{0,24},{4,28},{8,16},{12,20},{16,8},{20,12},{24,0},{28,4},{1,25},{... | collective-permute-start | bytes 393224 | tf_op jit(solution)/shard_map/ppermute | solution.py:272
  16.0 11.1 %collective-permute-start.1 = (bf16[128,512]{1,0:T(8,128)(2,1)}, bf16[128,512]{1,0:T(8,128)(2,1)S(1)}, u32[]{:S(2)}, u32[]{:S(2)}) collective-permute-start(bf16[128,512]{1,0:T(8,128)(2,1)} %get-tuple-element.31), channel_id=1, source_target_pairs={{0,16},{4,20},{8,24},{12,28},{16,0},{20,4},{24,8},{28,12},{1,17},{... | collective-permute-start | bytes 393224 | tf_op jit(solution)/shard_map/ppermute | solution.py:272
  16.5 10.6 %collective-permute-start = (bf16[128,512]{1,0:T(8,128)(2,1)}, bf16[128,512]{1,0:T(8,128)(2,1)S(1)}, u32[]{:S(2)}, u32[]{:S(2)}) collective-permute-start(bf16[128,512]{1,0:T(8,128)(2,1)} %get-tuple-element.31), channel_id=1, source_target_pairs={{0,8},{4,12},{8,0},{12,4},{16,24},{20,28},{24,16},{28,20},{1,9},{5... | collective-permute-start | bytes 393224 | tf_op jit(solution)/shard_map/ppermute | solution.py:272
  18.9 10.4 %collective-permute-start.7 = (bf16[128,768]{1,0:T(8,128)(2,1)}, bf16[128,768]{1,0:T(8,128)(2,1)S(1)}, u32[]{:S(2)}, u32[]{:S(2)}) collective-permute-start(bf16[128,768]{1,0:T(8,128)(2,1)} %get-tuple-element.39), channel_id=1, source_target_pairs={{0,4},{4,0},{8,12},{12,8},{16,20},{20,16},{24,28},{28,24},{1,5},{5... | collective-permute-start | bytes 589832 | tf_op jit(solution)/shard_map/ppermute | solution.py:272
  27.1 5.7 %collective-permute-start.8 = (bf16[3,128,256]{2,1,0:T(8,128)(2,1)S(1)}, bf16[3,128,256]{2,1,0:T(8,128)(2,1)S(1)}, u32[]{:S(2)}, u32[]{:S(2)}) collective-permute-start(bf16[3,128,256]{2,1,0:T(8,128)(2,1)S(1)} %pad_maximum_fusion.2), channel_id=1, source_target_pairs={{0,2},{1,3},{2,0},{3,1},{4,6},{5,7},{6,4},{7,5},{8,10},{9,11},{10,... | collective-permute-start | bytes 589832 | tf_op jit(solution)/shard_map/ppermute | solution.py:272
  28.7 5.7 %collective-permute-start.10 = (bf16[3,128,256]{2,1,0:T(8,128)(2,1)S(1)}, bf16[3,128,256]{2,1,0:T(8,128)(2,1)S(1)}, u32[]{:S(2)}, u32[]{:S(2)}) collective-permute-start(bf16[3,128,256]{2,1,0:T(8,128)(2,1)S(1)} %pad_maximum_fusion.3), channel_id=1, source_target_pairs={{0,4},{4,0},{8,12},{12,8},{16,20},{20,16},{24,28},{28,24},{1,5},{5... | collective-permute-start | bytes 589832 | tf_op jit(solution)/shard_map/ppermute | solution.py:272
  29.3 5.2 %collective-permute-start.14 = (bf16[128,768]{1,0:T(8,128)(2,1)S(1)}, bf16[128,768]{1,0:T(8,128)(2,1)S(1)}, u32[]{:S(2)}, u32[]{:S(2)}) collective-permute-start(bf16[128,768]{1,0:T(8,128)(2,1)S(1)} %collective-permute-done.7.refs_7_), channel_id=1, source_target_pairs={{0,1},{1,0},{2,3},{3,2},{4,5},{5,4},{6,7},{7,6},{8,9},{9,8},{10,11... | collective-permute-start | bytes 589832 | tf_op jit(solution)/shard_map/ppermute | solution.py:272
  29.3 3.6 %collective-permute-start.13 = (bf16[128,512]{1,0:T(8,128)(2,1)S(1)}, bf16[128,512]{1,0:T(8,128)(2,1)S(1)}, u32[]{:S(2)}, u32[]{:S(2)}) collective-permute-start(bf16[128,512]{1,0:T(8,128)(2,1)S(1)} %collective-permute-done.2.refs_6_), channel_id=1, source_target_pairs={{0,1},{1,0},{2,3},{3,2},{4,5},{5,4},{6,7},{7,6},{8,9},{9,8},{10,11... | collective-permute-start | bytes 393224 | tf_op jit(solution)/shard_map/ppermute | solution.py:272
  29.8 3.1 %collective-permute-start.12 = (bf16[128,512]{1,0:T(8,128)(2,1)S(1)}, bf16[128,512]{1,0:T(8,128)(2,1)S(1)}, u32[]{:S(2)}, u32[]{:S(2)}) collective-permute-start(bf16[128,512]{1,0:T(8,128)(2,1)S(1)} %collective-permute-done.1.refs_5_), channel_id=1, source_target_pairs={{0,1},{1,0},{2,3},{3,2},{4,5},{5,4},{6,7},{7,6},{8,9},{9,8},{10,11... | collective-permute-start | bytes 393224 | tf_op jit(solution)/shard_map/ppermute | solution.py:272
  34.5 10.9 %collective-permute-start.16 = (bf16[3,128,512]{2,1,0:T(8,128)(2,1)S(1)}, bf16[3,128,512]{2,1,0:T(8,128)(2,1)S(1)}, u32[]{:S(2)}, u32[]{:S(2)}) collective-permute-start(bf16[3,128,512]{2,1,0:T(8,128)(2,1)S(1)} %pad_maximum_fusion), channel_id=1, source_target_pairs={{0,4},{4,0},{8,12},{12,8},{16,20},{20,16},{24,28},{28,24},{1,5},{5... | collective-permute-start | bytes 1179656 | tf_op jit(solution)/shard_map/ppermute | solution.py:272
  35.0 10.4 %collective-permute-start.9 = (bf16[4,128,256]{2,1,0:T(8,128)(2,1)S(1)}, bf16[4,128,256]{2,1,0:T(8,128)(2,1)S(1)}, u32[]{:S(2)}, u32[]{:S(2)}) collective-permute-start(bf16[4,128,256]{2,1,0:T(8,128)(2,1)S(1)} %pad_maximum_fusion.1), channel_id=1, source_target_pairs={{0,2},{1,3},{2,0},{3,1},{4,6},{5,7},{6,4},{7,5},{8,10},{9,11},{10,... | collective-permute-start | bytes 786440 | tf_op jit(solution)/shard_map/ppermute | solution.py:272
  36.3 10.8 %collective-permute-start.15 = (bf16[3,128,256]{2,1,0:T(8,128)(2,1)S(1)}, bf16[3,128,256]{2,1,0:T(8,128)(2,1)S(1)}, u32[]{:S(2)}, u32[]{:S(2)}) collective-permute-start(bf16[3,128,256]{2,1,0:T(8,128)(2,1)S(1)} %collective-permute-done.10.refs_10_), channel_id=1, source_target_pairs={{0,2},{1,3},{2,0},{3,1},{4,6},{5,7},{6,4},{7,5},{8,10},{9,11},{10,... | collective-permute-start | bytes 589832 | tf_op jit(solution)/shard_map/ppermute | solution.py:272
  45.4 3.2 %collective-permute-start.21 = (bf16[3,128,512]{2,1,0:T(8,128)(2,1)S(1)}, bf16[3,128,512]{2,1,0:T(8,128)(2,1)S(1)}, u32[]{:S(2)}, u32[]{:S(2)}) collective-permute-start(bf16[3,128,512]{2,1,0:T(8,128)(2,1)S(1)} %collective-permute-done.16.refs_12_), channel_id=1, source_target_pairs={{0,1},{1,0},{2,3},{3,2},{4,5},{5,4},{6,7},{7,6},{8,9},{9,8},{10,11... | collective-permute-start | bytes 1179656 | tf_op jit(solution)/shard_map/ppermute | solution.py:272
  45.4 2.7 %collective-permute-start.18 = (bf16[4,128,256]{2,1,0:T(8,128)(2,1)S(1)}, bf16[4,128,256]{2,1,0:T(8,128)(2,1)S(1)}, u32[]{:S(2)}, u32[]{:S(2)}) collective-permute-start(bf16[4,128,256]{2,1,0:T(8,128)(2,1)S(1)} %collective-permute-done.9.refs_9_), channel_id=1, source_target_pairs={{0,1},{1,0},{2,3},{3,2},{4,5},{5,4},{6,7},{7,6},{8,9},{9,8},{10,11... | collective-permute-start | bytes 786440 | tf_op jit(solution)/shard_map/ppermute | solution.py:272
  45.9 1.9 %collective-permute-start.17 = (bf16[3,128,256]{2,1,0:T(8,128)(2,1)S(1)}, bf16[3,128,256]{2,1,0:T(8,128)(2,1)S(1)}, u32[]{:S(2)}, u32[]{:S(2)}) collective-permute-start(bf16[3,128,256]{2,1,0:T(8,128)(2,1)S(1)} %collective-permute-done.8.refs_8_), channel_id=1, source_target_pairs={{0,1},{1,0},{2,3},{3,2},{4,5},{5,4},{6,7},{7,6},{8,9},{9,8},{10,11... | collective-permute-start | bytes 589832 | tf_op jit(solution)/shard_map/ppermute | solution.py:272
  45.9 2.1 %collective-permute-start.19 = (bf16[3,128,256]{2,1,0:T(8,128)(2,1)S(1)}, bf16[3,128,256]{2,1,0:T(8,128)(2,1)S(1)}, u32[]{:S(2)}, u32[]{:S(2)}) collective-permute-start(bf16[3,128,256]{2,1,0:T(8,128)(2,1)S(1)} %collective-permute-done.10.refs_10_), channel_id=1, source_target_pairs={{0,1},{1,0},{2,3},{3,2},{4,5},{5,4},{6,7},{7,6},{8,9},{9,8},{10,11... | collective-permute-start | bytes 589832 | tf_op jit(solution)/shard_map/ppermute | solution.py:272
  47.1 1.4 %collective-permute-start.20 = (bf16[3,128,256]{2,1,0:T(8,128)(2,1)S(1)}, bf16[3,128,256]{2,1,0:T(8,128)(2,1)S(1)}, u32[]{:S(2)}, u32[]{:S(2)}) collective-permute-start(bf16[3,128,256]{2,1,0:T(8,128)(2,1)S(1)} %collective-permute-done.15.refs_11_), channel_id=1, source_target_pairs={{0,1},{1,0},{2,3},{3,2},{4,5},{5,4},{6,7},{7,6},{8,9},{9,8},{10,11... | collective-permute-start | bytes 589832 | tf_op jit(solution)/shard_map/ppermute | solution.py:272
  76.4 2.0 %collective-permute-start.23 = (bf16[8,128,256]{2,1,0:T(8,128)(2,1)S(1)}, bf16[8,128,256]{2,1,0:T(8,128)(2,1)S(1)}, u32[]{:S(2)}, u32[]{:S(2)}) collective-permute-start(bf16[8,128,256]{2,1,0:T(8,128)(2,1)S(1)} %get-tuple-element.50), channel_id=1, source_target_pairs={{0,1},{1,0},{2,3},{3,2},{4,5},{5,4},{6,7},{7,6},{8,9},{9,8},{10,11... | collective-permute-start | bytes 1572872 | tf_op jit(solution)/shard_map/ppermute | solution.py:272
  76.6 3.5 %collective-permute-start.27 = (bf16[4,128,512]{2,1,0:T(8,128)(2,1)S(1)}, bf16[4,128,512]{2,1,0:T(8,128)(2,1)S(1)}, u32[]{:S(2)}, u32[]{:S(2)}) collective-permute-start(bf16[4,128,512]{2,1,0:T(8,128)(2,1)S(1)} %get-tuple-element.54), channel_id=1, source_target_pairs={{0,1},{1,0},{2,3},{3,2},{4,5},{5,4},{6,7},{7,6},{8,9},{9,8},{10,11... | collective-permute-start | bytes 1572872 | tf_op jit(solution)/shard_map/ppermute | solution.py:272
  77.0 4.8 %collective-permute-start.22 = (bf16[8,128,256]{2,1,0:T(8,128)(2,1)S(1)}, bf16[8,128,256]{2,1,0:T(8,128)(2,1)S(1)}, u32[]{:S(2)}, u32[]{:S(2)}) collective-permute-start(bf16[8,128,256]{2,1,0:T(8,128)(2,1)S(1)} %get-tuple-element.48), channel_id=1, source_target_pairs={{0,1},{1,0},{2,3},{3,2},{4,5},{5,4},{6,7},{7,6},{8,9},{9,8},{10,11... | collective-permute-start | bytes 1572872 | tf_op jit(solution)/shard_map/ppermute | solution.py:272
  78.5 14.0 %collective-permute-start.24 = (bf16[8,128,256]{2,1,0:T(8,128)(2,1)S(1)}, bf16[8,128,256]{2,1,0:T(8,128)(2,1)S(1)}, u32[]{:S(2)}, u32[]{:S(2)}) collective-permute-start(bf16[8,128,256]{2,1,0:T(8,128)(2,1)S(1)} %add_convert_fusion.4), channel_id=1, source_target_pairs={{0,2},{1,3},{2,0},{3,1},{4,6},{5,7},{6,4},{7,5},{8,10},{9,11},{10,... | collective-permute-start | bytes 1572872 | tf_op jit(solution)/shard_map/ppermute | solution.py:272
  80.1 14.3 %collective-permute-start.26 = (bf16[4,128,512]{2,1,0:T(8,128)(2,1)S(1)}, bf16[4,128,512]{2,1,0:T(8,128)(2,1)S(1)}, u32[]{:S(2)}, u32[]{:S(2)}) collective-permute-start(bf16[4,128,512]{2,1,0:T(8,128)(2,1)S(1)} %get-tuple-element.52), channel_id=1, source_target_pairs={{0,1},{1,0},{2,3},{3,2},{4,5},{5,4},{6,7},{7,6},{8,9},{9,8},{10,11... | collective-permute-start | bytes 1572872 | tf_op jit(solution)/shard_map/ppermute | solution.py:272
  80.3 14.4 %collective-permute-start.28 = (bf16[4,128,512]{2,1,0:T(8,128)(2,1)S(1)}, bf16[4,128,512]{2,1,0:T(8,128)(2,1)S(1)}, u32[]{:S(2)}, u32[]{:S(2)}) collective-permute-start(bf16[4,128,512]{2,1,0:T(8,128)(2,1)S(1)} %add_convert_fusion.1), channel_id=1, source_target_pairs={{0,4},{4,0},{8,12},{12,8},{16,20},{20,16},{24,28},{28,24},{1,5},{5... | collective-permute-start | bytes 1572872 | tf_op jit(solution)/shard_map/ppermute | solution.py:272
  92.8 7.6 %collective-permute-start.25 = (bf16[4,128,256]{2,1,0:T(8,128)(2,1)S(1)}, bf16[4,128,256]{2,1,0:T(8,128)(2,1)S(1)}, u32[]{:S(2)}, u32[]{:S(2)}) collective-permute-start(bf16[4,128,256]{2,1,0:T(8,128)(2,1)S(1)} %slice_bitcast_fusion), channel_id=1, source_target_pairs={{0,4},{4,0},{8,12},{12,8},{16,20},{20,16},{24,28},{28,24},{1,5},{5... | collective-permute-start | bytes 786440 | tf_op jit(solution)/shard_map/ppermute | solution.py:272
  94.9 8.0 %collective-permute-start.29 = (bf16[4,128,256]{2,1,0:T(8,128)(2,1)S(1)}, bf16[4,128,256]{2,1,0:T(8,128)(2,1)S(1)}, u32[]{:S(2)}, u32[]{:S(2)}) collective-permute-start(bf16[4,128,256]{2,1,0:T(8,128)(2,1)S(1)} %slice.70), channel_id=1, source_target_pairs={{0,2},{1,3},{2,0},{3,1},{4,6},{5,7},{6,4},{7,5},{8,10},{9,11},{10,... | collective-permute-start | bytes 786440 | tf_op jit(solution)/shard_map/ppermute | solution.py:272
  103.0 7.0 %collective-permute-start.30 = (bf16[128,512]{1,0:T(8,128)(2,1)S(1)}, bf16[128,512]{1,0:T(8,128)(2,1)S(1)}, u32[]{:S(2)}, u32[]{:S(2)}) collective-permute-start(bf16[128,512]{1,0:T(8,128)(2,1)S(1)} %get-tuple-element.55), channel_id=1, source_target_pairs={{0,8},{4,12},{8,0},{12,4},{16,24},{20,28},{24,16},{28,20},{1,9},{5... | collective-permute-start | bytes 393224 | tf_op jit(solution)/shard_map/ppermute | solution.py:272
  103.1 9.2 %collective-permute-start.32 = (bf16[128,512]{1,0:T(8,128)(2,1)S(1)}, bf16[128,512]{1,0:T(8,128)(2,1)S(1)}, u32[]{:S(2)}, u32[]{:S(2)}) collective-permute-start(bf16[128,512]{1,0:T(8,128)(2,1)S(1)} %get-tuple-element.56), channel_id=1, source_target_pairs={{0,24},{4,28},{8,16},{12,20},{16,8},{20,12},{24,0},{28,4},{1,25},{... | collective-permute-start | bytes 393224 | tf_op jit(solution)/shard_map/ppermute | solution.py:272
  105.6 11.3 %collective-permute-start.31 = (bf16[128,512]{1,0:T(8,128)(2,1)S(1)}, bf16[128,512]{1,0:T(8,128)(2,1)S(1)}, u32[]{:S(2)}, u32[]{:S(2)}) collective-permute-start(bf16[128,512]{1,0:T(8,128)(2,1)S(1)} %get-tuple-element.57), channel_id=1, source_target_pairs={{0,16},{4,20},{8,24},{12,28},{16,0},{20,4},{24,8},{28,12},{1,17},{... | collective-permute-start | bytes 393224 | tf_op jit(solution)/shard_map/ppermute | solution.py:272
  (10 other events, 187.0 us)
where the time goes:
time: 118 us
  waiting for transfers between devices  51.7 us (44%)
  Pallas kernels  31.8 us (27%)
  starting transfers between devices  28.8 us (24%)
  local copies, waits for them, and re-layouts  2.78 us (2%)
  other arithmetic  2.42 us (2%)
    ppermute x33, waiting for transfers between devices, swap(): return lax.ppermute(value, axis, [(i, i ^ distance) for i in range(size)])  51.7 us
    ppermute x33, starting transfers between devices, swap(): return lax.ppermute(value, axis, [(i, i ^ distance) for i in range(size)])  28.8 us
    pallas_call x1, Pallas kernels, moe_partial(): pl.pallas_call(functools.partial(moe_kernel, n_pieces), out_shape=outs, i...  25.7 us
    pallas_call x1, Pallas kernels, route(): pl.pallas_call(functools.partial(route_kernel, exp_dev, n_z), out_shape=[...  3.66 us
    unnamed x18, local copies, waits for them, and re-layouts  2.71 us
    pallas_call x1, Pallas kernels, norm_and_base(): pl.pallas_call(norm_kernel, out_shape=[jax.ShapeDtypeStruct((tok_rows, mo...  2.39 us
  transfers between devices with their start and end apart: 33, of which 19 were waited for; matrix products, arithmetic and copies ran while one was open for 1% of the time, Pallas kernels for 3%

commit v1 on v0

--- a/solution.py
+++ b/solution.py
@@ -38,11 +38,9 @@
     tokens_ref, gain_ref, refusal_ref, ids_ref, probs_ref,
     normed_ref, to_z_ref, to_y_ref, unit_ref, base_ref, meta_ref,
 ):
-    width = tokens_ref.shape[1] // 8
-    top_k = ids_ref.shape[0]
+    tok_rows, model_width = tokens_ref.shape
+    width = model_width // 8
     rep = lax.axis_index("rep")
-    meta_ref[:top_k] = ids_ref[...].astype(jnp.float32)
-    meta_ref[top_k:] = probs_ref[...]
     toks = tokens_ref[...].astype(jnp.float32)
     refusal = refusal_ref[...]
     unit = refusal / jnp.sqrt(jnp.sum(refusal * refusal, axis=1, keepdims=True) + 1e-06)
@@ -50,9 +48,15 @@
     inv_rms = lax.rsqrt(jnp.mean(toks * toks, axis=1, keepdims=True) + 1e-06)
     normed_ref[...] = (toks * inv_rms * gain_ref[...]).astype(jnp.bfloat16)
     own = pl.ds(group_offset(rep, 0, 0, 0, width), 2 * width)
-    to_z_ref[...] = normed_ref[:, own]
-    to_y_ref[:, : 2 * width] = normed_ref[:, own]
-    to_y_ref[:, 2 * width :] = normed_ref[:, pl.ds(group_offset(rep, 1, 1, 0, width), width)]
+    other = pl.ds(group_offset(rep, 1, 1, 0, width), width)
+    meta = jnp.concatenate([ids_ref[...].astype(jnp.float32), probs_ref[...]], axis=0)
+    meta = meta.astype(jnp.bfloat16)
+    meta_ref[...] = meta
+    for ref in (to_z_ref, to_y_ref):
+        ref[:tok_rows, : 2 * width] = normed_ref[:, own]
+        ref[tok_rows:] = jnp.zeros((meta.shape[0], ref.shape[1]), jnp.bfloat16)
+        ref[tok_rows:, :tok_rows] = meta
+    to_y_ref[:tok_rows, 2 * width :] = normed_ref[:, other]
     along = jnp.sum(toks * unit, axis=1, keepdims=True)
     base_ref[...] = tokens_ref[:, own].astype(jnp.float32) - along * unit_ref[:, own]
 
@@ -60,31 +64,26 @@
 def norm_and_base(tokens, norm_gain, refusal_dir, expert_ids, gate_probs):
     tok_rows, model_width = tokens.shape
     width = model_width // 8
+    meta_rows = 2 * expert_ids.shape[1]
     vmem = pl.BlockSpec(memory_space=pltpu.VMEM)
     return pl.pallas_call(
         norm_kernel,
         out_shape=[
             jax.ShapeDtypeStruct((tok_rows, model_width), jnp.bfloat16),
-            jax.ShapeDtypeStruct((tok_rows, 2 * width), jnp.bfloat16),
-            jax.ShapeDtypeStruct((tok_rows, 3 * width), jnp.bfloat16),
+            jax.ShapeDtypeStruct((tok_rows + meta_rows, 2 * width), jnp.bfloat16),
+            jax.ShapeDtypeStruct((tok_rows + meta_rows, 3 * width), jnp.bfloat16),
             jax.ShapeDtypeStruct((1, model_width), jnp.float32),
             jax.ShapeDtypeStruct((tok_rows, 2 * width), jnp.float32),
-            jax.ShapeDtypeStruct((2 * expert_ids.shape[1], tok_rows), jnp.float32),
+            jax.ShapeDtypeStruct((meta_rows, tok_rows), jnp.bfloat16),
         ],
         in_specs=[vmem] * 5,
         out_specs=[vmem] * 6,
     )(tokens, norm_gain[None, :], refusal_dir[None, :], expert_ids.T, gate_probs.T)
 
 
-def route_kernel(exp_dev, n_z, *refs):
-    near_refs, far_ref, picks_ref, weights_ref, meta_ref = (
-        refs[:n_z], refs[n_z], refs[n_z + 1], refs[n_z + 2], refs[n_z + 3]
-    )
+def route_kernel(exp_dev, meta_ref, picks_ref, weights_ref):
     n_seq, twice_k, tok_rows = meta_ref.shape
     top_k = twice_k // 2
-    for d in range(n_z):
-        meta_ref[2 * d] = near_refs[d][...]
-        meta_ref[2 * d + 1] = far_ref[d]
     first = (lax.axis_index("seq") * exp_dev).astype(jnp.float32)
     exp_iota = lax.broadcasted_iota(jnp.int32, (exp_dev, tok_rows), 0).astype(jnp.float32) + first
     earlier = (
@@ -94,7 +93,7 @@
     slot_iota = lax.broadcasted_iota(jnp.int32, (exp_dev, SLOTS, tok_rows), 1).astype(jnp.float32)
 
     def place_block(j, carry):
-        meta = meta_ref[j]
+        meta = meta_ref[j].astype(jnp.float32)
         hit = jnp.zeros((exp_dev, tok_rows), jnp.float32)
         prob = jnp.zeros((exp_dev, tok_rows), jnp.float32)
         for k in range(top_k):
@@ -113,119 +112,149 @@
     lax.fori_loop(0, n_seq, place_block, 0)
 
 
-def route(near, far, exp_dev):
-    n_z, twice_k, tok_rows = far.shape
-    n_seq = 2 * n_z
+def route(meta, exp_dev):
+    n_seq, _, tok_rows = meta.shape
     vmem = pl.BlockSpec(memory_space=pltpu.VMEM)
     return pl.pallas_call(
-        functools.partial(route_kernel, exp_dev, n_z),
+        functools.partial(route_kernel, exp_dev),
         out_shape=[
             jax.ShapeDtypeStruct((n_seq, exp_dev * SLOTS, tok_rows), jnp.bfloat16),
             jax.ShapeDtypeStruct((n_seq, tok_rows, exp_dev * SLOTS), jnp.bfloat16),
         ],
-        in_specs=[vmem] * (n_z + 1),
+        in_specs=[vmem],
         out_specs=[vmem] * 2,
-        scratch_shapes=[pltpu.VMEM((n_seq, twice_k, tok_rows), jnp.float32)],
         cost_estimate=pl.CostEstimate(
             flops=4_000_000_000, bytes_accessed=8 * n_seq * exp_dev * SLOTS * tok_rows,
             transcendentals=0,
         ),
-    )(*near, far)
+    )(meta)
 
 
 def moe_kernel(n_pieces, *refs):
-    picks, weights, unit_ref, own_hbm = refs[:4]
-    pieces_hbm = refs[4 : 4 + n_pieces]
+    picks_hbm, weights_hbm, unit_ref, own_hbm = refs[:4]
+    pieces_in = refs[4 : 4 + n_pieces]
     w_gate_hbm, w_up_hbm, w_down_hbm = refs[4 + n_pieces : 7 + n_pieces]
     out_refs = refs[7 + n_pieces : 15 + n_pieces]
-    (w_in, w_down, toks, rows, mixed, tok_sems, sems) = refs[15 + n_pieces :]
+    (picks, weights, w_in, w_down, toks, rows, hidden, mixed, table_sems, tok_sems, in_sems,
+     down_sems) = refs[15 + n_pieces :]
     n_seq, tok_rows, model_width = toks.shape
     n_z = n_seq // 2
     exp_dev, hid_dev, _ = w_gate_hbm.shape
     width = model_width // 8
     slots_src = exp_dev * SLOTS
     rep = lax.axis_index("rep")
+    tables = [
+        pltpu.make_async_copy(picks_hbm, picks, table_sems.at[0]),
+        pltpu.make_async_copy(weights_hbm, weights, table_sems.at[1]),
+    ]
+    tables[0].start()
 
     pltpu.make_async_copy(own_hbm, toks.at[0], tok_sems.at[0]).start()
     kinds = token_pieces(n_z, width)
-    for i, piece in enumerate(pieces_hbm):
+    for i, piece in enumerate(pieces_in):
         dc = i // len(kinds)
         for at, (j, runs) in enumerate(kinds[i % len(kinds)]):
             block = piece if len(piece.shape) == 2 else piece.at[at]
             for n, (color, dx) in enumerate(runs):
                 cols = pl.ds(group_offset(rep, color, dx, dc, width), width)
                 pltpu.make_async_copy(
-                    block.at[:, pl.ds(n * width, width)], toks.at[j, :, cols], tok_sems.at[j]
+                    block.at[pl.ds(0, tok_rows), pl.ds(n * width, width)],
+                    toks.at[j, :, cols],
+                    tok_sems.at[j],
                 ).start()
 
-    def weight_copies(e):
+    def in_copies(e):
         at = lax.rem(e, RING)
-        gate_at, up_at = pl.ds(0, hid_dev), pl.ds(hid_dev, hid_dev)
         return [
-            pltpu.make_async_copy(w_gate_hbm.at[e], w_in.at[at, gate_at], sems.at[0, at]),
-            pltpu.make_async_copy(w_up_hbm.at[e], w_in.at[at, up_at], sems.at[1, at]),
-            pltpu.make_async_copy(w_down_hbm.at[e], w_down.at[at], sems.at[2, at]),
+            pltpu.make_async_copy(
+                src.at[e], w_in.at[at, pl.ds(i * hid_dev, hid_dev)], in_sems.at[i, at]
+            )
+            for i, src in enumerate((w_gate_hbm, w_up_hbm))
         ]
 
-    def fetch(e, carry):
-        for copy in weight_copies(e):
+    def down_copy(e):
+        return pltpu.make_async_copy(w_down_hbm.at[e], w_down.at[e], down_sems.at[e])
+
+    for e in range(min(RING, exp_dev)):
+        for copy in in_copies(e):
             copy.start()
+    tables[1].start()
+    quarters = [slice(2 * q * width, 2 * (q + 1) * width) for q in range(4)]
+    tables[0].wait()
+
+    def pick(pair, carry):
+        for j in (2 * pair, 2 * pair + 1):
+            pltpu.make_async_copy(toks.at[j], toks.at[j], tok_sems.at[j]).wait()
+        for j in (2 * pair, 2 * pair + 1):
+            onehot = picks[j]
+            for cols in quarters:
+                got = contract(onehot, toks[j, :, cols], 1, 0).astype(jnp.bfloat16)
+                rows[j, :, :, cols] = got.reshape(exp_dev, SLOTS, 2 * width)
         return carry
 
-    lax.fori_loop(0, min(RING, exp_dev), fetch, 0)
-    quarters = [slice(2 * q * width, 2 * (q + 1) * width) for q in range(4)]
-
-    def pick(j, carry):
-        pltpu.make_async_copy(toks.at[j], toks.at[j], tok_sems.at[j]).wait()
-        onehot = picks[j]
-        for cols in quarters:
-            got = contract(onehot, toks[j, :, cols], 1, 0).astype(jnp.bfloat16)
-            rows[j, :, :, cols] = got.reshape(exp_dev, SLOTS, 2 * width)
+    lax.fori_loop(0, n_z, pick, 0)
+
+    def widen(pair, carry):
+        experts = (2 * pair, 2 * pair + 1)
+        for e in experts:
+            for copy in in_copies(e):
+                copy.wait()
+        both = [
+            contract(
+                w_in[lax.rem(e, RING)], rows[:, e].reshape(n_seq * SLOTS, model_width), 1, 1
+            )
+            for e in experts
+        ]
+        for e, value in zip(experts, both):
+            gate_val, up_val = value[:hid_dev], value[hid_dev:]
+            act = gate_val / (1.0 + jnp.exp(-gate_val)) * up_val
+            hidden[e] = act.T.astype(jnp.bfloat16)
+        for e in experts:
+            down_copy(e).start()
+
+            @pl.when(e + RING < exp_dev)
+            def _():
+                for copy in in_copies(e + RING):
+                    copy.start()
+
         return carry
 
-    lax.fori_loop(0, n_seq, pick, 0)
-
-    def expert(e, carry):
-        at = lax.rem(e, RING)
-        for copy in weight_copies(e):
-            copy.wait()
-        taken = rows[:, e].reshape(n_seq * SLOTS, model_width)
-        both = contract(w_in[at], taken, 1, 1)
-        gate_val, up_val = both[:hid_dev], both[hid_dev:]
-        hidden = gate_val / (1.0 + jnp.exp(-gate_val)) * up_val
-        hidden = hidden.T.astype(jnp.bfloat16)
-        for cols in quarters:
-            piece = contract(hidden, w_down[at, :, cols], 1, 0).astype(jnp.bfloat16)
-            rows[:, e, :, cols] = piece.reshape(n_seq, SLOTS, 2 * width)
-
-        @pl.when(e + RING < exp_dev)
-        def _():
-            fetch(e + RING, 0)
-
+    lax.fori_loop(0, exp_dev // 2, widen, 0)
+
+    def narrow(pair, carry):
+        experts = (2 * pair, 2 * pair + 1)
+        for e in experts:
+            down_copy(e).wait()
+        for e in experts:
+            for cols in quarters:
+                piece = contract(hidden[e], w_down[e, :, cols], 1, 0).astype(jnp.bfloat16)
+                rows[:, e, :, cols] = piece.reshape(n_seq, SLOTS, 2 * width)
         return carry
 
-    lax.fori_loop(0, exp_dev, expert, 0)
+    lax.fori_loop(0, exp_dev // 2, narrow, 0)
+    tables[1].wait()
 
     def combine(dz, carry):
+        along = [jnp.zeros((tok_rows, 1), jnp.float32)] * 2
         for dy in range(2):
             j = 2 * dz + dy
             weight = weights[j]
-            along = jnp.zeros((tok_rows, 1), jnp.float32)
             for cols in quarters:
                 got = contract(weight, rows[j, :, :, cols].reshape(slots_src, 2 * width), 1, 0)
-                mixed[:, cols] = got
-                along += jnp.sum(got * unit_ref[:, cols], axis=1, keepdims=True)
+                mixed[dy, :, cols] = got
+                along[dy] += jnp.sum(got * unit_ref[:, cols], axis=1, keepdims=True)
+        for dy in range(2):
             for dc in range(2):
                 first_far, second_far, first_near, second_near = out_refs[4 * dc : 4 * dc + 4]
                 second = second_far if dy else second_near
                 for dst, at, start, color, dx in (
-                    (first_far, j, 0, 0, 1),
-                    (first_near, j, 0, 0, 0),
+                    (first_far, 2 * dz + dy, 0, 0, 1),
+                    (first_near, 2 * dz + dy, 0, 0, 0),
                     (second, dz, 0, 1, 0),
                     (second, dz, width, 1, 1),
                 ):
                     cols = pl.ds(group_offset(rep, color, dx, dc, width), width)
-                    value = mixed[:, cols] - along * unit_ref[:, cols]
+                    value = mixed[dy, :, cols] - along[dy] * unit_ref[:, cols]
                     dst[at, :, start : start + width] = value.astype(jnp.bfloat16)
         return carry
 
@@ -237,8 +266,10 @@
     exp_dev, hid_dev, model_width = w_gate.shape
     width = model_width // 8
     vmem = pl.BlockSpec(memory_space=pltpu.VMEM)
-    hbm = pl.BlockSpec(memory_space=pl.ANY)
+    hbm = pl.BlockSpec(memory_space=pltpu.HBM)
+    whole = pl.BlockSpec(memory_space=pl.ANY)
     n_pieces = len(pieces)
+    pieces = [pltpu.with_memory_space_constraint(piece, pltpu.VMEM) for piece in pieces]
     outs = [
         jax.ShapeDtypeStruct((blocks, tok_rows, runs * width), jnp.bfloat16)
         for _ in range(2)
@@ -247,16 +278,21 @@
     return pl.pallas_call(
         functools.partial(moe_kernel, n_pieces),
         out_shape=outs,
-        in_specs=[vmem] * 3 + [hbm] * (n_pieces + 4),
+        in_specs=[hbm, hbm, vmem, hbm] + [whole] * n_pieces + [hbm] * 3,
         out_specs=[vmem] * len(outs),
         scratch_shapes=[
+            pltpu.VMEM(picks.shape, jnp.bfloat16),
+            pltpu.VMEM(weights.shape, jnp.bfloat16),
             pltpu.VMEM((RING, 2 * hid_dev, model_width), jnp.bfloat16),
-            pltpu.VMEM((RING, hid_dev, model_width), jnp.bfloat16),
+            pltpu.VMEM(w_down.shape, jnp.bfloat16),
             pltpu.VMEM((n_seq, tok_rows, model_width), jnp.bfloat16),
             pltpu.VMEM((n_seq, exp_dev, SLOTS, model_width), jnp.bfloat16),
-            pltpu.VMEM((tok_rows, model_width), jnp.float32),
+            pltpu.VMEM((exp_dev, n_seq * SLOTS, hid_dev), jnp.bfloat16),
+            pltpu.VMEM((2, tok_rows, model_width), jnp.float32),
+            pltpu.SemaphoreType.DMA((2,)),
             pltpu.SemaphoreType.DMA((n_seq,)),
-            pltpu.SemaphoreType.DMA((3, RING)),
+            pltpu.SemaphoreType.DMA((2, RING)),
+            pltpu.SemaphoreType.DMA((exp_dev,)),
         ],
         compiler_params=pltpu.CompilerParams(vmem_limit_bytes=42 * 1024 * 1024),
         cost_estimate=pl.CostEstimate(
@@ -288,21 +324,24 @@
     )
     from_z = [swap(to_z, "seq", 2 * d) for d in others]
     from_y = swap(to_y, "seq", 1)
-    near = [meta] + [swap(meta, "seq", 2 * d) for d in others]
-    picks, weights = route(near, swap(jnp.stack(near), "seq", 1), exp_dev)
-
     first = jnp.stack([piece[:, :width] for piece in from_z])
-    second = jnp.stack([piece[:, width:] for piece in from_z])
-    second, picks, weights = lax.optimization_barrier((second, picks, weights))
+    second = jnp.stack([piece[:tok_rows, width:] for piece in from_z])
     x_two = swap(second, "rep", 2)
     y_two = swap(first, "seq", 1)
-    x_one = swap(jnp.concatenate([first, from_y[None, :, :width]]), "rep", 2)
+    x_one = swap(
+        jnp.concatenate([first[:, :tok_rows], from_y[None, :tok_rows, :width]]), "rep", 2
+    )
     sibling = [swap(piece, "rep", 1) for piece in (*from_z, from_y)]
     to_y, y_two, *sibling = lax.optimization_barrier(
         (jnp.concatenate([second, x_two], axis=2), y_two, *sibling)
     )
     y_three = swap(to_y, "seq", 1)
-    x_three = swap(y_two, "rep", 2)
+    below = [meta, from_y[tok_rows:, :tok_rows]]
+    for d in range(n_z - 1):
+        below += [from_z[d][tok_rows:, :tok_rows], y_two[d, tok_rows:, :tok_rows]]
+    picks, weights = route(jnp.stack(below), exp_dev)
+    to_x, picks, weights = lax.optimization_barrier((y_two[:, :tok_rows], picks, weights))
+    x_three = swap(to_x, "rep", 2)
     last = [x_two, x_one, y_two, x_three, y_three]
     pieces = [*from_z, from_y, *last, *sibling, *[swap(piece, "rep", 1) for piece in last]]
 

time: 118 us -> 107 us (0.907)
  starting transfers between devices: 28.8 us -> 22.5 us
  Pallas kernels: 31.8 us -> 26.1 us
    ppermute x33 -> x29, starting transfers between devices: 28.8 us -> 22.5 us  [swap(): return lax.ppermute(value, axis, [(i, i ^ distance) for i in range(size)])]
    pallas_call x1, Pallas kernels: 25.7 us -> 19.9 us  [moe_partial(): pl.pallas_call(functools.partial(moe_kernel, n_pieces), out_shape=outs, i...]
    unnamed x18 -> x19, local copies, waits for them, and re-layouts: 2.71 us -> 3.44 us
    ppermute x33 -> x29, waiting for transfers between devices: 51.7 us -> 52.1 us  [swap(): return lax.ppermute(value, axis, [(i, i ^ distance) for i in range(size)])]
  transfers between devices with their start and end apart: 33 -> 29, of which waited for: 19 -> 14; matrix products, arithmetic and copies ran while one was open for 1% -> 2% of each run, Pallas kernels for 3% -> 3%
where the time goes in v1:
time: 107 us
  waiting for transfers between devices  52.1 us (49%)
  Pallas kernels  26.1 us (24%)
  starting transfers between devices  22.5 us (21%)
  local copies, waits for them, and re-layouts  3.55 us (3%)
  other arithmetic  2.43 us (2%)
    ppermute x29, waiting for transfers between devices, swap(): return lax.ppermute(value, axis, [(i, i ^ distance) for i in range(size)])  52.1 us
    ppermute x29, starting transfers between devices, swap(): return lax.ppermute(value, axis, [(i, i ^ distance) for i in range(size)])  22.5 us
    pallas_call x1, Pallas kernels, moe_partial(): pl.pallas_call(functools.partial(moe_kernel, n_pieces), out_shape=outs, i...  19.9 us
    pallas_call x1, Pallas kernels, route(): pl.pallas_call(functools.partial(route_kernel, exp_dev), out_shape=[jax.S...  3.64 us
    unnamed x19, local copies, waits for them, and re-layouts  3.44 us
    pallas_call x1, Pallas kernels, norm_and_base(): pl.pallas_call(norm_kernel, out_shape=[jax.ShapeDtypeStruct((tok_rows, mo...  2.48 us
  transfers between devices with their start and end apart: 29, of which 14 were waited for; matrix products, arithmetic and copies ran while one was open for 2% of the time, Pallas kernels for 3%

profile of v1, /device:TPU:0, one launch (start us, length us, event | category | flops | bytes accessed | tf_op | source)
XLA Modules:
  0.0 106.8 jit_solution(7094084941806205519)
XLA Ops:
  0.0 2.5 %shard_map.82 = (bf16[128,2048]{1,0:T(8,128)(2,1)}, bf16[144,512]{1,0:T(8,128)(2,1)}, bf16[144,768]{1,0:T(8,128)(2,1)}, f32[1,2048]{1,0:T(1,128)}, f32[128,512]{1,0:T(8,128)}, /*index=5*/bf16[16,128]{1,0:T(8,128)(2,1)}) custom-call(bf16[128,2048]{1,0:T(8,128)(2,1)} %tokens_ref.1, f32[1,2048]{1,0:T(1,128)} %bitcast.61, f32[1,2048]{1,0:T(1,128)} %bitcast.62, ...), custom_call_target="tpu_custom_call" | custom-call | tf_op jit(solution)/shard_map/pallas_call | solution.py:69
  2.5 5.1 %collective-permute-start.2 = (bf16[144,512]{1,0:T(8,128)(2,1)}, bf16[144,512]{1,0:T(8,128)(2,1)S(1)}, u32[]{:S(2)}, u32[]{:S(2)}) collective-permute-start(bf16[144,512]{1,0:T(8,128)(2,1)} %get-tuple-element.31), channel_id=1, source_target_pairs={{0,24},{4,28},{8,16},{12,20},{16,8},{20,12},{24,0},{28,4},{1,25},{... | collective-permute-start | bytes 442376 | tf_op jit(solution)/shard_map/ppermute | solution.py:308
  7.6 0.6 collective-permute-start
  8.2 1.7 %collective-permute-start.8 = (bf16[144,768]{1,0:T(8,128)(2,1)}, bf16[144,768]{1,0:T(8,128)(2,1)S(1)}, u32[]{:S(2)}, u32[]{:S(2)}) collective-permute-start(bf16[144,768]{1,0:T(8,128)(2,1)} %get-tuple-element.32), channel_id=1, source_target_pairs={{0,4},{4,0},{8,12},{12,8},{16,20},{20,16},{24,28},{28,24},{1,5},{5... | collective-permute-start | bytes 663560 | tf_op jit(solution)/shard_map/ppermute | solution.py:308
  9.9 0.7 constant_dynamic-update-slice_fusion.7
  10.6 2.0 %collective-permute-done.2.refs_6_ = bf16[144,512]{1,0:T(8,128)(2,1)S(1)} collective-permute-done((bf16[144,512]{1,0:T(8,128)(2,1)}, bf16[144,512]{1,0:T(8,128)(2,1)S(1)}, u32[]{:S(2)}, u32[]{:S(2)}) %collective-permute-start.2) | collective-permute-done | bytes 147488 | tf_op jit(solution)/shard_map/ppermute | solution.py:308
  12.6 7.7 %collective-permute-done.1.refs_5_ = bf16[144,512]{1,0:T(8,128)(2,1)S(1)} collective-permute-done((bf16[144,512]{1,0:T(8,128)(2,1)}, bf16[144,512]{1,0:T(8,128)(2,1)S(1)}, u32[]{:S(2)}, u32[]{:S(2)}) %collective-permute-start.1) | collective-permute-done | bytes 147488 | tf_op jit(solution)/shard_map/ppermute | solution.py:308
  20.4 1.6 %collective-permute-start.4 = (bf16[3,144,256]{2,1,0:T(8,128)(2,1)S(1)}, bf16[3,144,256]{2,1,0:T(8,128)(2,1)S(1)}, u32[]{:S(2)}, u32[]{:S(2)}) collective-permute-start(bf16[3,144,256]{2,1,0:T(8,128)(2,1)S(1)} %pad_maximum_fusion.2), channel_id=1, source_target_pairs={{0,4},{4,0},{8,12},{12,8},{16,20},{20,16},{24,28},{28,24},{1,5},{5... | collective-permute-start | bytes 663560 | tf_op jit(solution)/shard_map/ppermute | solution.py:308
  22.0 1.6 %collective-permute-start.3 = (bf16[3,128,256]{2,1,0:T(8,128)(2,1)S(1)}, bf16[3,128,256]{2,1,0:T(8,128)(2,1)S(1)}, u32[]{:S(2)}, u32[]{:S(2)}) collective-permute-start(bf16[3,128,256]{2,1,0:T(8,128)(2,1)S(1)} %pad_maximum_fusion.3), channel_id=1, source_target_pairs={{0,2},{1,3},{2,0},{3,1},{4,6},{5,7},{6,4},{7,5},{8,10},{9,11},{10,... | collective-permute-start | bytes 589832 | tf_op jit(solution)/shard_map/ppermute | solution.py:308
  24.1 3.6 %collective-permute-done.3.refs_8_ = bf16[3,128,256]{2,1,0:T(8,128)(2,1)S(1)} collective-permute-done((bf16[3,128,256]{2,1,0:T(8,128)(2,1)S(1)}, bf16[3,128,256]{2,1,0:T(8,128)(2,1)S(1)}, u32[]{:S(2)}, u32[]{:S(2)}) %collective-permute-start.3) | collective-permute-done | bytes 196640 | tf_op jit(solution)/shard_map/ppermute | solution.py:308
  27.8 0.7 pad_maximum_fusion.1
  28.5 1.6 %collective-permute-start.10 = (bf16[4,128,256]{2,1,0:T(8,128)(2,1)}, bf16[4,128,256]{2,1,0:T(8,128)(2,1)S(1)}, u32[]{:S(2)}, u32[]{:S(2)}) collective-permute-start(bf16[4,128,256]{2,1,0:T(8,128)(2,1)} %pad_maximum_fusion.1), channel_id=1, source_target_pairs={{0,2},{1,3},{2,0},{3,1},{4,6},{5,7},{6,4},{7,5},{8,10},{9,11},{10,... | collective-permute-start | bytes 786440 | tf_op jit(solution)/shard_map/ppermute | solution.py:308
  30.8 0.6 copy-done.5
  31.4 3.6 %shard_map.83 = (bf16[8,256,128]{2,1,0:T(8,128)(2,1)}, bf16[8,128,256]{2,1,0:T(8,128)(2,1)}) custom-call(bf16[8,16,128]{2,1,0:T(8,128)(2,1)} %copy-done.5), custom_call_target="tpu_custom_call" | custom-call | flops 4000000000 | bytes 2097152 | tf_op jit(solution)/shard_map/pallas_call | solution.py:118
  35.0 0.6 collective-permute-start.11
  35.7 5.8 %collective-permute-done.12.refs_12_ = bf16[3,128,512]{2,1,0:T(8,128)(2,1)S(1)} collective-permute-done((bf16[3,128,512]{2,1,0:T(8,128)(2,1)S(1)}, bf16[3,128,512]{2,1,0:T(8,128)(2,1)S(1)}, u32[]{:S(2)}, u32[]{:S(2)}) %collective-permute-start.12) | collective-permute-done | bytes 393248 | tf_op jit(solution)/shard_map/ppermute | solution.py:308
  42.5 1.7 %collective-permute-done.13.refs_17_ = bf16[3,128,256]{2,1,0:T(8,128)(2,1)S(1)} collective-permute-done((bf16[3,128,256]{2,1,0:T(8,128)(2,1)S(1)}, bf16[3,128,256]{2,1,0:T(8,128)(2,1)S(1)}, u32[]{:S(2)}, u32[]{:S(2)}) %collective-permute-start.13) | collective-permute-done | bytes 196640 | tf_op jit(solution)/shard_map/ppermute | solution.py:308
  44.5 1.0 copy-done.1
  45.5 1.0 copy-done.2
  46.6 19.9 %shard_map.84 = (bf16[8,128,256]{2,1,0:T(8,128)(2,1)S(1)}, bf16[4,128,512]{2,1,0:T(8,128)(2,1)S(1)}, bf16[8,128,256]{2,1,0:T(8,128)(2,1)S(1)}, bf16[4,128,512]{2...) custom-call(bf16[8,256,128]{2,1,0:T(8,128)(2,1)S(1)} %copy-done.1, ...), custom_call_target="tpu_custom_call" | custom-call | flops 4831838208 | bytes 46137344 | tf_op jit(solution)/shard_map/pallas_call | solution.py:278
  67.2 1.3 %collective-permute-done.19 = bf16[8,128,256]{2,1,0:T(8,128)(2,1)S(1)} collective-permute-done((bf16[8,128,256]{2,1,0:T(8,128)(2,1)S(1)}, bf16[8,128,256]{2,1,0:T(8,128)(2,1)S(1)}, u32[]{:S(2)}, u32[]{:S(2)}) %collective-permute-start.19) | collective-permute-done | bytes 524320 | tf_op jit(solution)/shard_map/ppermute | solution.py:308
  68.6 0.6 collective-permute-start.20
  70.0 12.7 %collective-permute-done.20 = bf16[8,128,256]{2,1,0:T(8,128)(2,1)S(1)} collective-permute-done((bf16[8,128,256]{2,1,0:T(8,128)(2,1)S(1)}, bf16[8,128,256]{2,1,0:T(8,128)(2,1)S(1)}, u32[]{:S(2)}, u32[]{:S(2)}) %collective-permute-start.20) | collective-permute-done | bytes 524320 | tf_op jit(solution)/shard_map/ppermute | solution.py:308
  84.0 1.5 %collective-permute-start.25 = (bf16[4,128,256]{2,1,0:T(8,128)(2,1)S(1)}, bf16[4,128,256]{2,1,0:T(8,128)(2,1)S(1)}, u32[]{:S(2)}, u32[]{:S(2)}) collective-permute-start(bf16[4,128,256]{2,1,0:T(8,128)(2,1)S(1)} %slice.111), channel_id=1, source_target_pairs={{0,2},{1,3},{2,0},{3,1},{4,6},{5,7},{6,4},{7,5},{8,10},{9,11},{10,... | collective-permute-start | bytes 786440 | tf_op jit(solution)/shard_map/ppermute | solution.py:308
  85.6 5.0 %collective-permute-done.21 = bf16[4,128,256]{2,1,0:T(8,128)(2,1)S(1)} collective-permute-done((bf16[4,128,256]{2,1,0:T(8,128)(2,1)S(1)}, bf16[4,128,256]{2,1,0:T(8,128)(2,1)S(1)}, u32[]{:S(2)}, u32[]{:S(2)}) %collective-permute-start.21) | collective-permute-done | bytes 262176 | tf_op jit(solution)/shard_map/ppermute | solution.py:308
  90.6 1.4 %collective-permute-done.25 = bf16[4,128,256]{2,1,0:T(8,128)(2,1)S(1)} collective-permute-done((bf16[4,128,256]{2,1,0:T(8,128)(2,1)S(1)}, bf16[4,128,256]{2,1,0:T(8,128)(2,1)S(1)}, u32[]{:S(2)}, u32[]{:S(2)}) %collective-permute-start.25) | collective-permute-done | bytes 262176 | tf_op jit(solution)/shard_map/ppermute | solution.py:308
  92.2 2.6 %collective-permute-start.28 = (bf16[128,512]{1,0:T(8,128)(2,1)S(1)}, bf16[128,512]{1,0:T(8,128)(2,1)S(1)}, u32[]{:S(2)}, u32[]{:S(2)}) collective-permute-start(bf16[128,512]{1,0:T(8,128)(2,1)S(1)} %get-tuple-element.56), channel_id=1, source_target_pairs={{0,24},{4,28},{8,16},{12,20},{16,8},{20,12},{24,0},{28,4},{1,25},{... | collective-permute-start | bytes 393224 | tf_op jit(solution)/shard_map/ppermute | solution.py:308
  94.8 0.9 collective-permute-start.27
  95.7 3.4 %collective-permute-done.26 = bf16[128,512]{1,0:T(8,128)(2,1)S(1)} collective-permute-done((bf16[128,512]{1,0:T(8,128)(2,1)S(1)}, bf16[128,512]{1,0:T(8,128)(2,1)S(1)}, u32[]{:S(2)}, u32[]{:S(2)}) %collective-permute-start.26) | collective-permute-done | bytes 131104 | tf_op jit(solution)/shard_map/ppermute | solution.py:308
  99.1 2.3 %collective-permute-done.28 = bf16[128,512]{1,0:T(8,128)(2,1)S(1)} collective-permute-done((bf16[128,512]{1,0:T(8,128)(2,1)S(1)}, bf16[128,512]{1,0:T(8,128)(2,1)S(1)}, u32[]{:S(2)}, u32[]{:S(2)}) %collective-permute-start.28) | collective-permute-done | bytes 131104 | tf_op jit(solution)/shard_map/ppermute | solution.py:308
  101.4 4.6 %collective-permute-done.27 = bf16[128,512]{1,0:T(8,128)(2,1)S(1)} collective-permute-done((bf16[128,512]{1,0:T(8,128)(2,1)S(1)}, bf16[128,512]{1,0:T(8,128)(2,1)S(1)}, u32[]{:S(2)}, u32[]{:S(2)}) %collective-permute-start.27) | collective-permute-done | bytes 131104 | tf_op jit(solution)/shard_map/ppermute | solution.py:308
  106.1 0.7 fusion.4
  (72 shorter events, 5.8 us)
Async XLA Ops:
  2.5 42.0 %copy-start = (bf16[128,2048]{1,0:T(8,128)(2,1)S(1)}, bf16[128,2048]{1,0:T(8,128)(2,1)}, u32[]{:S(2)}) copy-start(bf16[128,2048]{1,0:T(8,128)(2,1)} %get-tuple-element.40.refs_3_) | copy-start | bytes 1572868
  2.5 42.0 %copy-start.3 = (f32[1,2048]{1,0:T(1,128)S(1)}, f32[1,2048]{1,0:T(1,128)}, u32[]{:S(2)}) copy-start(f32[1,2048]{1,0:T(1,128)} %get-tuple-element.39.refs_2_) | copy-start | bytes 24580
  2.5 10.1 %collective-permute-start.2 = (bf16[144,512]{1,0:T(8,128)(2,1)}, bf16[144,512]{1,0:T(8,128)(2,1)S(1)}, u32[]{:S(2)}, u32[]{:S(2)}) collective-permute-start(bf16[144,512]{1,0:T(8,128)(2,1)} %get-tuple-element.31), channel_id=1, source_target_pairs={{0,24},{4,28},{8,16},{12,20},{16,8},{20,12},{24,0},{28,4},{1,25},{... | collective-permute-start | bytes 442376 | tf_op jit(solution)/shard_map/ppermute | solution.py:308
  7.6 12.7 %collective-permute-start.1 = (bf16[144,512]{1,0:T(8,128)(2,1)}, bf16[144,512]{1,0:T(8,128)(2,1)S(1)}, u32[]{:S(2)}, u32[]{:S(2)}) collective-permute-start(bf16[144,512]{1,0:T(8,128)(2,1)} %get-tuple-element.31), channel_id=1, source_target_pairs={{0,16},{4,20},{8,24},{12,28},{16,0},{20,4},{24,8},{28,12},{1,17},{... | collective-permute-start | bytes 442376 | tf_op jit(solution)/shard_map/ppermute | solution.py:308
  7.6 12.7 %collective-permute-start = (bf16[144,512]{1,0:T(8,128)(2,1)}, bf16[144,512]{1,0:T(8,128)(2,1)S(1)}, u32[]{:S(2)}, u32[]{:S(2)}) collective-permute-start(bf16[144,512]{1,0:T(8,128)(2,1)} %get-tuple-element.31), channel_id=1, source_target_pairs={{0,8},{4,12},{8,0},{12,4},{16,24},{20,28},{24,16},{28,20},{1,9},{5... | collective-permute-start | bytes 442376 | tf_op jit(solution)/shard_map/ppermute | solution.py:308
  8.2 15.9 %collective-permute-start.8 = (bf16[144,768]{1,0:T(8,128)(2,1)}, bf16[144,768]{1,0:T(8,128)(2,1)S(1)}, u32[]{:S(2)}, u32[]{:S(2)}) collective-permute-start(bf16[144,768]{1,0:T(8,128)(2,1)} %get-tuple-element.32), channel_id=1, source_target_pairs={{0,4},{4,0},{8,12},{12,8},{16,20},{20,16},{24,28},{28,24},{1,5},{5... | collective-permute-start | bytes 663560 | tf_op jit(solution)/shard_map/ppermute | solution.py:308
  20.4 9.7 %collective-permute-start.4 = (bf16[3,144,256]{2,1,0:T(8,128)(2,1)S(1)}, bf16[3,144,256]{2,1,0:T(8,128)(2,1)S(1)}, u32[]{:S(2)}, u32[]{:S(2)}) collective-permute-start(bf16[3,144,256]{2,1,0:T(8,128)(2,1)S(1)} %pad_maximum_fusion.2), channel_id=1, source_target_pairs={{0,4},{4,0},{8,12},{12,8},{16,20},{20,16},{24,28},{28,24},{1,5},{5... | collective-permute-start | bytes 663560 | tf_op jit(solution)/shard_map/ppermute | solution.py:308
  22.0 5.7 %collective-permute-start.3 = (bf16[3,128,256]{2,1,0:T(8,128)(2,1)S(1)}, bf16[3,128,256]{2,1,0:T(8,128)(2,1)S(1)}, u32[]{:S(2)}, u32[]{:S(2)}) collective-permute-start(bf16[3,128,256]{2,1,0:T(8,128)(2,1)S(1)} %pad_maximum_fusion.3), channel_id=1, source_target_pairs={{0,2},{1,3},{2,0},{3,1},{4,6},{5,7},{6,4},{7,5},{8,10},{9,11},{10,... | collective-permute-start | bytes 589832 | tf_op jit(solution)/shard_map/ppermute | solution.py:308
  23.6 5.0 %collective-permute-start.7 = (bf16[144,512]{1,0:T(8,128)(2,1)S(1)}, bf16[144,512]{1,0:T(8,128)(2,1)S(1)}, u32[]{:S(2)}, u32[]{:S(2)}) collective-permute-start(bf16[144,512]{1,0:T(8,128)(2,1)S(1)} %collective-permute-done.2.refs_6_), channel_id=1, source_target_pairs={{0,1},{1,0},{2,3},{3,2},{4,5},{5,4},{6,7},{7,6},{8,9},{9,8},{10,11... | collective-permute-start | bytes 442376 | tf_op jit(solution)/shard_map/ppermute | solution.py:308
  23.6 6.5 %collective-permute-start.6 = (bf16[144,512]{1,0:T(8,128)(2,1)S(1)}, bf16[144,512]{1,0:T(8,128)(2,1)S(1)}, u32[]{:S(2)}, u32[]{:S(2)}) collective-permute-start(bf16[144,512]{1,0:T(8,128)(2,1)S(1)} %collective-permute-done.1.refs_5_), channel_id=1, source_target_pairs={{0,1},{1,0},{2,3},{3,2},{4,5},{5,4},{6,7},{7,6},{8,9},{9,8},{10,11... | collective-permute-start | bytes 442376 | tf_op jit(solution)/shard_map/ppermute | solution.py:308
  24.1 6.0 %collective-permute-start.5 = (bf16[144,512]{1,0:T(8,128)(2,1)S(1)}, bf16[144,512]{1,0:T(8,128)(2,1)S(1)}, u32[]{:S(2)}, u32[]{:S(2)}) collective-permute-start(bf16[144,512]{1,0:T(8,128)(2,1)S(1)} %collective-permute-done.refs_4_), channel_id=1, source_target_pairs={{0,1},{1,0},{2,3},{3,2},{4,5},{5,4},{6,7},{7,6},{8,9},{9,8},{10,11... | collective-permute-start | bytes 442376 | tf_op jit(solution)/shard_map/ppermute | solution.py:308
  27.8 2.4 %collective-permute-start.9 = (bf16[144,768]{1,0:T(8,128)(2,1)S(1)}, bf16[144,768]{1,0:T(8,128)(2,1)S(1)}, u32[]{:S(2)}, u32[]{:S(2)}) collective-permute-start(bf16[144,768]{1,0:T(8,128)(2,1)S(1)} %collective-permute-done.8.refs_7_), channel_id=1, source_target_pairs={{0,1},{1,0},{2,3},{3,2},{4,5},{5,4},{6,7},{7,6},{8,9},{9,8},{10,11... | collective-permute-start | bytes 663560 | tf_op jit(solution)/shard_map/ppermute | solution.py:308
  28.5 12.9 %collective-permute-start.10 = (bf16[4,128,256]{2,1,0:T(8,128)(2,1)}, bf16[4,128,256]{2,1,0:T(8,128)(2,1)S(1)}, u32[]{:S(2)}, u32[]{:S(2)}) collective-permute-start(bf16[4,128,256]{2,1,0:T(8,128)(2,1)} %pad_maximum_fusion.1), channel_id=1, source_target_pairs={{0,2},{1,3},{2,0},{3,1},{4,6},{5,7},{6,4},{7,5},{8,10},{9,11},{10,... | collective-permute-start | bytes 786440 | tf_op jit(solution)/shard_map/ppermute | solution.py:308
  30.2 11.3 %collective-permute-start.12 = (bf16[3,128,512]{2,1,0:T(8,128)(2,1)S(1)}, bf16[3,128,512]{2,1,0:T(8,128)(2,1)S(1)}, u32[]{:S(2)}, u32[]{:S(2)}) collective-permute-start(bf16[3,128,512]{2,1,0:T(8,128)(2,1)S(1)} %pad_maximum_fusion), channel_id=1, source_target_pairs={{0,4},{4,0},{8,12},{12,8},{16,20},{20,16},{24,28},{28,24},{1,5},{5... | collective-permute-start | bytes 1179656 | tf_op jit(solution)/shard_map/ppermute | solution.py:308
  35.0 7.5 %collective-permute-start.11 = (bf16[3,128,256]{2,1,0:T(8,128)(2,1)S(1)}, bf16[3,128,256]{2,1,0:T(8,128)(2,1)S(1)}, u32[]{:S(2)}, u32[]{:S(2)}) collective-permute-start(bf16[3,128,256]{2,1,0:T(8,128)(2,1)S(1)} %slice.78), channel_id=1, source_target_pairs={{0,2},{1,3},{2,0},{3,1},{4,6},{5,7},{6,4},{7,5},{8,10},{9,11},{10,... | collective-permute-start | bytes 589832 | tf_op jit(solution)/shard_map/ppermute | solution.py:308
  41.5 3.0 %collective-permute-start.17 = (bf16[3,128,512]{2,1,0:T(8,128)(2,1)S(1)}, bf16[3,128,512]{2,1,0:T(8,128)(2,1)S(1)}, u32[]{:S(2)}, u32[]{:S(2)}) collective-permute-start(bf16[3,128,512]{2,1,0:T(8,128)(2,1)S(1)} %collective-permute-done.12.refs_12_), channel_id=1, source_target_pairs={{0,1},{1,0},{2,3},{3,2},{4,5},{5,4},{6,7},{7,6},{8,9},{9,8},{10,11... | collective-permute-start | bytes 1179656 | tf_op jit(solution)/shard_map/ppermute | solution.py:308
  41.5 2.7 %collective-permute-start.14 = (bf16[4,128,256]{2,1,0:T(8,128)(2,1)S(1)}, bf16[4,128,256]{2,1,0:T(8,128)(2,1)S(1)}, u32[]{:S(2)}, u32[]{:S(2)}) collective-permute-start(bf16[4,128,256]{2,1,0:T(8,128)(2,1)S(1)} %collective-permute-done.10.refs_9_), channel_id=1, source_target_pairs={{0,1},{1,0},{2,3},{3,2},{4,5},{5,4},{6,7},{7,6},{8,9},{9,8},{10,11... | collective-permute-start | bytes 786440 | tf_op jit(solution)/shard_map/ppermute | solution.py:308
  42.0 2.2 %collective-permute-start.15 = (bf16[3,144,256]{2,1,0:T(8,128)(2,1)S(1)}, bf16[3,144,256]{2,1,0:T(8,128)(2,1)S(1)}, u32[]{:S(2)}, u32[]{:S(2)}) collective-permute-start(bf16[3,144,256]{2,1,0:T(8,128)(2,1)S(1)} %collective-permute-done.4.refs_10_), channel_id=1, source_target_pairs={{0,1},{1,0},{2,3},{3,2},{4,5},{5,4},{6,7},{7,6},{8,9},{9,8},{10,11... | collective-permute-start | bytes 663560 | tf_op jit(solution)/shard_map/ppermute | solution.py:308
  42.0 2.2 %collective-permute-start.13 = (bf16[3,128,256]{2,1,0:T(8,128)(2,1)S(1)}, bf16[3,128,256]{2,1,0:T(8,128)(2,1)S(1)}, u32[]{:S(2)}, u32[]{:S(2)}) collective-permute-start(bf16[3,128,256]{2,1,0:T(8,128)(2,1)S(1)} %collective-permute-done.3.refs_8_), channel_id=1, source_target_pairs={{0,1},{1,0},{2,3},{3,2},{4,5},{5,4},{6,7},{7,6},{8,9},{9,8},{10,11... | collective-permute-start | bytes 589832 | tf_op jit(solution)/shard_map/ppermute | solution.py:308
  42.5 1.9 %collective-permute-start.16 = (bf16[3,128,256]{2,1,0:T(8,128)(2,1)S(1)}, bf16[3,128,256]{2,1,0:T(8,128)(2,1)S(1)}, u32[]{:S(2)}, u32[]{:S(2)}) collective-permute-start(bf16[3,128,256]{2,1,0:T(8,128)(2,1)S(1)} %collective-permute-done.11.refs_11_), channel_id=1, source_target_pairs={{0,1},{1,0},{2,3},{3,2},{4,5},{5,4},{6,7},{7,6},{8,9},{9,8},{10,11... | collective-permute-start | bytes 589832 | tf_op jit(solution)/shard_map/ppermute | solution.py:308
  46.6 59.5 %copy-start.4 = (f32[128,512]{1,0:T(8,128)S(1)}, f32[128,512]{1,0:T(8,128)}, u32[]{:S(2)}) copy-start(f32[128,512]{1,0:T(8,128)} %get-tuple-element.30) | copy-start | bytes 786436
  66.5 2.0 %collective-permute-start.19 = (bf16[8,128,256]{2,1,0:T(8,128)(2,1)S(1)}, bf16[8,128,256]{2,1,0:T(8,128)(2,1)S(1)}, u32[]{:S(2)}, u32[]{:S(2)}) collective-permute-start(bf16[8,128,256]{2,1,0:T(8,128)(2,1)S(1)} %get-tuple-element.50), channel_id=1, source_target_pairs={{0,1},{1,0},{2,3},{3,2},{4,5},{5,4},{6,7},{7,6},{8,9},{9,8},{10,11... | collective-permute-start | bytes 1572872 | tf_op jit(solution)/shard_map/ppermute | solution.py:308
  66.7 2.5 %collective-permute-start.23 = (bf16[4,128,512]{2,1,0:T(8,128)(2,1)S(1)}, bf16[4,128,512]{2,1,0:T(8,128)(2,1)S(1)}, u32[]{:S(2)}, u32[]{:S(2)}) collective-permute-start(bf16[4,128,512]{2,1,0:T(8,128)(2,1)S(1)} %get-tuple-element.54), channel_id=1, source_target_pairs={{0,1},{1,0},{2,3},{3,2},{4,5},{5,4},{6,7},{7,6},{8,9},{9,8},{10,11... | collective-permute-start | bytes 1572872 | tf_op jit(solution)/shard_map/ppermute | solution.py:308
  67.1 2.9 %collective-permute-start.18 = (bf16[8,128,256]{2,1,0:T(8,128)(2,1)S(1)}, bf16[8,128,256]{2,1,0:T(8,128)(2,1)S(1)}, u32[]{:S(2)}, u32[]{:S(2)}) collective-permute-start(bf16[8,128,256]{2,1,0:T(8,128)(2,1)S(1)} %get-tuple-element.48), channel_id=1, source_target_pairs={{0,1},{1,0},{2,3},{3,2},{4,5},{5,4},{6,7},{7,6},{8,9},{9,8},{10,11... | collective-permute-start | bytes 1572872 | tf_op jit(solution)/shard_map/ppermute | solution.py:308
  68.6 14.0 %collective-permute-start.20 = (bf16[8,128,256]{2,1,0:T(8,128)(2,1)S(1)}, bf16[8,128,256]{2,1,0:T(8,128)(2,1)S(1)}, u32[]{:S(2)}, u32[]{:S(2)}) collective-permute-start(bf16[8,128,256]{2,1,0:T(8,128)(2,1)S(1)} %add_convert_fusion.4), channel_id=1, source_target_pairs={{0,2},{1,3},{2,0},{3,1},{4,6},{5,7},{6,4},{7,5},{8,10},{9,11},{10,... | collective-permute-start | bytes 1572872 | tf_op jit(solution)/shard_map/ppermute | solution.py:308
  69.2 14.3 %collective-permute-start.22 = (bf16[4,128,512]{2,1,0:T(8,128)(2,1)S(1)}, bf16[4,128,512]{2,1,0:T(8,128)(2,1)S(1)}, u32[]{:S(2)}, u32[]{:S(2)}) collective-permute-start(bf16[4,128,512]{2,1,0:T(8,128)(2,1)S(1)} %get-tuple-element.52), channel_id=1, source_target_pairs={{0,1},{1,0},{2,3},{3,2},{4,5},{5,4},{6,7},{7,6},{8,9},{9,8},{10,11... | collective-permute-start | bytes 1572872 | tf_op jit(solution)/shard_map/ppermute | solution.py:308
  69.4 14.4 %collective-permute-start.24 = (bf16[4,128,512]{2,1,0:T(8,128)(2,1)S(1)}, bf16[4,128,512]{2,1,0:T(8,128)(2,1)S(1)}, u32[]{:S(2)}, u32[]{:S(2)}) collective-permute-start(bf16[4,128,512]{2,1,0:T(8,128)(2,1)S(1)} %add_convert_fusion.1), channel_id=1, source_target_pairs={{0,4},{4,0},{8,12},{12,8},{16,20},{20,16},{24,28},{28,24},{1,5},{5... | collective-permute-start | bytes 1572872 | tf_op jit(solution)/shard_map/ppermute | solution.py:308
  82.9 7.6 %collective-permute-start.21 = (bf16[4,128,256]{2,1,0:T(8,128)(2,1)S(1)}, bf16[4,128,256]{2,1,0:T(8,128)(2,1)S(1)}, u32[]{:S(2)}, u32[]{:S(2)}) collective-permute-start(bf16[4,128,256]{2,1,0:T(8,128)(2,1)S(1)} %slice_bitcast_fusion), channel_id=1, source_target_pairs={{0,4},{4,0},{8,12},{12,8},{16,20},{20,16},{24,28},{28,24},{1,5},{5... | collective-permute-start | bytes 786440 | tf_op jit(solution)/shard_map/ppermute | solution.py:308
  84.0 8.0 %collective-permute-start.25 = (bf16[4,128,256]{2,1,0:T(8,128)(2,1)S(1)}, bf16[4,128,256]{2,1,0:T(8,128)(2,1)S(1)}, u32[]{:S(2)}, u32[]{:S(2)}) collective-permute-start(bf16[4,128,256]{2,1,0:T(8,128)(2,1)S(1)} %slice.111), channel_id=1, source_target_pairs={{0,2},{1,3},{2,0},{3,1},{4,6},{5,7},{6,4},{7,5},{8,10},{9,11},{10,... | collective-permute-start | bytes 786440 | tf_op jit(solution)/shard_map/ppermute | solution.py:308
  92.1 7.0 %collective-permute-start.26 = (bf16[128,512]{1,0:T(8,128)(2,1)S(1)}, bf16[128,512]{1,0:T(8,128)(2,1)S(1)}, u32[]{:S(2)}, u32[]{:S(2)}) collective-permute-start(bf16[128,512]{1,0:T(8,128)(2,1)S(1)} %get-tuple-element.55), channel_id=1, source_target_pairs={{0,8},{4,12},{8,0},{12,4},{16,24},{20,28},{24,16},{28,20},{1,9},{5... | collective-permute-start | bytes 393224 | tf_op jit(solution)/shard_map/ppermute | solution.py:308
  92.2 9.2 %collective-permute-start.28 = (bf16[128,512]{1,0:T(8,128)(2,1)S(1)}, bf16[128,512]{1,0:T(8,128)(2,1)S(1)}, u32[]{:S(2)}, u32[]{:S(2)}) collective-permute-start(bf16[128,512]{1,0:T(8,128)(2,1)S(1)} %get-tuple-element.56), channel_id=1, source_target_pairs={{0,24},{4,28},{8,16},{12,20},{16,8},{20,12},{24,0},{28,4},{1,25},{... | collective-permute-start | bytes 393224 | tf_op jit(solution)/shard_map/ppermute | solution.py:308
  94.8 11.3 %collective-permute-start.27 = (bf16[128,512]{1,0:T(8,128)(2,1)S(1)}, bf16[128,512]{1,0:T(8,128)(2,1)S(1)}, u32[]{:S(2)}, u32[]{:S(2)}) collective-permute-start(bf16[128,512]{1,0:T(8,128)(2,1)S(1)} %get-tuple-element.57), channel_id=1, source_target_pairs={{0,16},{4,20},{8,24},{12,28},{16,0},{20,4},{24,8},{28,12},{1,17},{... | collective-permute-start | bytes 393224 | tf_op jit(solution)/shard_map/ppermute | solution.py:308
  (3 other events, 2.7 us)

commit v2 on v1

--- a/solution.py
+++ b/solution.py
@@ -22,21 +22,25 @@
     return pl.multiple_of((rep ^ (2 * dx + dc)) * 2 * width + color * width, width)
 
 
-def token_pieces(n_z, width):
-    others = range(1, n_z)
-    pieces = [[(2 * d, [(0, 0), (1, 0)])] for d in others]
-    pieces.append([(1, [(0, 0), (1, 0), (1, 1)])])
-    pieces.append([(2 * d, [(1, 1)]) for d in others])
-    pieces.append([(2 * d, [(0, 1)]) for d in others] + [(1, [(0, 1)])])
-    pieces.append([(2 * d + 1, [(0, 0)]) for d in others])
-    pieces.append([(2 * d + 1, [(0, 1)]) for d in others])
-    pieces.append([(2 * d + 1, [(1, 0), (1, 1)]) for d in others])
-    return pieces
+def token_pieces(n_z):
+    near = [2 * d for d in range(1, n_z)]
+    far = [2 * d + 1 for d in range(1, n_z)]
+    return [
+        [(j, [(1, 0)]) for j in near],
+        [(j, [(0, 0)]) for j in near],
+        [(1, [(0, 0), (1, 0), (0, 1), (1, 1)])],
+        [(j, [(1, 1)]) for j in near],
+        [(j, [(1, 0)]) for j in far],
+        [(j, [(0, 1)]) for j in near],
+        [(j, [(0, 0)]) for j in far],
+        [(j, [(1, 1)]) for j in far],
+        [(j, [(0, 1)]) for j in far],
+    ]
 
 
 def norm_kernel(
     tokens_ref, gain_ref, refusal_ref, ids_ref, probs_ref,
-    normed_ref, to_z_ref, to_y_ref, unit_ref, base_ref, meta_ref,
+    normed_ref, second_ref, first_ref, to_y_ref, unit_ref, base_ref, meta_ref,
 ):
     tok_rows, model_width = tokens_ref.shape
     width = model_width // 8
@@ -48,15 +52,17 @@
     inv_rms = lax.rsqrt(jnp.mean(toks * toks, axis=1, keepdims=True) + 1e-06)
     normed_ref[...] = (toks * inv_rms * gain_ref[...]).astype(jnp.bfloat16)
     own = pl.ds(group_offset(rep, 0, 0, 0, width), 2 * width)
-    other = pl.ds(group_offset(rep, 1, 1, 0, width), width)
+    other = pl.ds(group_offset(rep, 0, 1, 0, width), 2 * width)
+    first_ref[...] = normed_ref[:, pl.ds(group_offset(rep, 0, 0, 0, width), width)]
+    second_ref[:tok_rows] = normed_ref[:, pl.ds(group_offset(rep, 1, 0, 0, width), width)]
+    to_y_ref[:tok_rows, : 2 * width] = normed_ref[:, own]
+    to_y_ref[:tok_rows, 2 * width :] = normed_ref[:, other]
     meta = jnp.concatenate([ids_ref[...].astype(jnp.float32), probs_ref[...]], axis=0)
     meta = meta.astype(jnp.bfloat16)
     meta_ref[...] = meta
-    for ref in (to_z_ref, to_y_ref):
-        ref[:tok_rows, : 2 * width] = normed_ref[:, own]
+    for ref in (second_ref, to_y_ref):
         ref[tok_rows:] = jnp.zeros((meta.shape[0], ref.shape[1]), jnp.bfloat16)
         ref[tok_rows:, :tok_rows] = meta
-    to_y_ref[:tok_rows, 2 * width :] = normed_ref[:, other]
     along = jnp.sum(toks * unit, axis=1, keepdims=True)
     base_ref[...] = tokens_ref[:, own].astype(jnp.float32) - along * unit_ref[:, own]
 
@@ -70,14 +76,15 @@
         norm_kernel,
         out_shape=[
             jax.ShapeDtypeStruct((tok_rows, model_width), jnp.bfloat16),
-            jax.ShapeDtypeStruct((tok_rows + meta_rows, 2 * width), jnp.bfloat16),
-            jax.ShapeDtypeStruct((tok_rows + meta_rows, 3 * width), jnp.bfloat16),
+            jax.ShapeDtypeStruct((tok_rows + meta_rows, width), jnp.bfloat16),
+            jax.ShapeDtypeStruct((tok_rows, width), jnp.bfloat16),
+            jax.ShapeDtypeStruct((tok_rows + meta_rows, 4 * width), jnp.bfloat16),
             jax.ShapeDtypeStruct((1, model_width), jnp.float32),
             jax.ShapeDtypeStruct((tok_rows, 2 * width), jnp.float32),
             jax.ShapeDtypeStruct((meta_rows, tok_rows), jnp.bfloat16),
         ],
         in_specs=[vmem] * 5,
-        out_specs=[vmem] * 6,
+        out_specs=[vmem] * 7,
     )(tokens, norm_gain[None, :], refusal_dir[None, :], expert_ids.T, gate_probs.T)
 
 
@@ -134,9 +141,9 @@
     picks_hbm, weights_hbm, unit_ref, own_hbm = refs[:4]
     pieces_in = refs[4 : 4 + n_pieces]
     w_gate_hbm, w_up_hbm, w_down_hbm = refs[4 + n_pieces : 7 + n_pieces]
-    out_refs = refs[7 + n_pieces : 15 + n_pieces]
+    out_refs = refs[7 + n_pieces : 11 + n_pieces]
     (picks, weights, w_in, w_down, toks, rows, hidden, mixed, table_sems, tok_sems, in_sems,
-     down_sems) = refs[15 + n_pieces :]
+     down_sems) = refs[11 + n_pieces :]
     n_seq, tok_rows, model_width = toks.shape
     n_z = n_seq // 2
     exp_dev, hid_dev, _ = w_gate_hbm.shape
@@ -150,7 +157,7 @@
     tables[0].start()
 
     pltpu.make_async_copy(own_hbm, toks.at[0], tok_sems.at[0]).start()
-    kinds = token_pieces(n_z, width)
+    kinds = token_pieces(n_z)
     for i, piece in enumerate(pieces_in):
         dc = i // len(kinds)
         for at, (j, runs) in enumerate(kinds[i % len(kinds)]):
@@ -243,19 +250,16 @@
                 got = contract(weight, rows[j, :, :, cols].reshape(slots_src, 2 * width), 1, 0)
                 mixed[dy, :, cols] = got
                 along[dy] += jnp.sum(got * unit_ref[:, cols], axis=1, keepdims=True)
+        half = tok_rows // 2
         for dy in range(2):
             for dc in range(2):
-                first_far, second_far, first_near, second_near = out_refs[4 * dc : 4 * dc + 4]
-                second = second_far if dy else second_near
-                for dst, at, start, color, dx in (
-                    (first_far, 2 * dz + dy, 0, 0, 1),
-                    (first_near, 2 * dz + dy, 0, 0, 0),
-                    (second, dz, 0, 1, 0),
-                    (second, dz, width, 1, 1),
-                ):
+                for n, (color, dx) in enumerate(((0, 1), (0, 0), (1, 0), (1, 1))):
                     cols = pl.ds(group_offset(rep, color, dx, dc, width), width)
                     value = mixed[dy, :, cols] - along[dy] * unit_ref[:, cols]
-                    dst[at, :, start : start + width] = value.astype(jnp.bfloat16)
+                    value = value.astype(jnp.bfloat16)
+                    at = slice(n * width, (n + 1) * width)
+                    out_refs[2 * dc][dy, dz, :, at] = value[:half]
+                    out_refs[2 * dc + 1][dy, dz, :, at] = value[half:]
         return carry
 
     lax.fori_loop(0, n_z, combine, 0)
@@ -270,10 +274,12 @@
     whole = pl.BlockSpec(memory_space=pl.ANY)
     n_pieces = len(pieces)
     pieces = [pltpu.with_memory_space_constraint(piece, pltpu.VMEM) for piece in pieces]
+    picks, weights, own = [
+        pltpu.with_memory_space_constraint(value, pltpu.HBM) for value in (picks, weights, own)
+    ]
     outs = [
-        jax.ShapeDtypeStruct((blocks, tok_rows, runs * width), jnp.bfloat16)
-        for _ in range(2)
-        for blocks, runs in ((n_seq, 1), (n_seq // 2, 2), (n_seq, 1), (n_seq // 2, 2))
+        jax.ShapeDtypeStruct((2, n_seq // 2, tok_rows // 2, 4 * width), jnp.bfloat16)
+        for _ in range(4)
     ]
     return pl.pallas_call(
         functools.partial(moe_kernel, n_pieces),
@@ -319,47 +325,55 @@
     exp_dev = w_gate.shape[0]
     width = model_width // 8
 
-    normed, to_z, to_y, unit_dir, base, meta = norm_and_base(
+    normed, second, first, to_y, unit_dir, base, meta = norm_and_base(
         tokens, norm_gain, refusal_dir, expert_ids, gate_probs
     )
-    from_z = [swap(to_z, "seq", 2 * d) for d in others]
+    second = [swap(second, "seq", 2 * d) for d in others]
     from_y = swap(to_y, "seq", 1)
-    first = jnp.stack([piece[:, :width] for piece in from_z])
-    second = jnp.stack([piece[:tok_rows, width:] for piece in from_z])
-    x_two = swap(second, "rep", 2)
+    first, second, from_y = lax.optimization_barrier((first, jnp.stack(second), from_y))
+    first = jnp.stack([swap(first, "seq", 2 * d) for d in others])
+    x_two = swap(second[:, :tok_rows], "rep", 2)
+    y_one = swap(second, "seq", 1)
     y_two = swap(first, "seq", 1)
-    x_one = swap(
-        jnp.concatenate([first[:, :tok_rows], from_y[None, :tok_rows, :width]]), "rep", 2
-    )
-    sibling = [swap(piece, "rep", 1) for piece in (*from_z, from_y)]
-    to_y, y_two, *sibling = lax.optimization_barrier(
-        (jnp.concatenate([second, x_two], axis=2), y_two, *sibling)
-    )
+    x_one = swap(first, "rep", 2)
+    to_y, to_core, to_core_y = lax.optimization_barrier((x_two, second, from_y))
     y_three = swap(to_y, "seq", 1)
+    early = [swap(piece, "rep", 1) for piece in (to_core, first, to_core_y)]
     below = [meta, from_y[tok_rows:, :tok_rows]]
     for d in range(n_z - 1):
-        below += [from_z[d][tok_rows:, :tok_rows], y_two[d, tok_rows:, :tok_rows]]
+        below += [second[d, tok_rows:, :tok_rows], y_one[d, tok_rows:, :tok_rows]]
     picks, weights = route(jnp.stack(below), exp_dev)
-    to_x, picks, weights = lax.optimization_barrier((y_two[:, :tok_rows], picks, weights))
+    to_x, picks, weights = lax.optimization_barrier((y_two, picks, weights))
     x_three = swap(to_x, "rep", 2)
-    last = [x_two, x_one, y_two, x_three, y_three]
-    pieces = [*from_z, from_y, *last, *sibling, *[swap(piece, "rep", 1) for piece in last]]
-
-    sums = moe_partial(picks, weights, unit_dir, normed, pieces, w_gate, w_up, w_down)
-    kept, sent = sums[:4], sums[4:]
-    first_far, second_far, first_near, second_near = [
-        added(mine, swap(theirs, "rep", 1)) for mine, theirs in zip(kept, sent)
-    ]
-    first_sum = added(first_near, swap(first_far, "rep", 2))
-    second_sum = added(second_near, swap(second_far, "seq", 1))
-    by_y = first_sum.reshape(n_z, 2, tok_rows, width)
-    first_sum = added(by_y[:, 0], swap(by_y[:, 1], "seq", 1))
-    second_sum = added(second_sum[:, :, :width], swap(second_sum[:, :, width:], "rep", 2))
-    blocks = jnp.concatenate([first_sum, second_sum], axis=2)
-    arrived = [swap(blocks[d], "seq", 2 * d) for d in others]
-    summed = sum(term.astype(jnp.float32) for term in [blocks[0], *arrived])
-
+    last = [x_two, y_one, x_one, y_two, y_three, x_three]
+    pieces = [second, first, from_y, *last, *early, *[swap(piece, "rep", 1) for piece in last]]
+
+    kept_0, kept_1, sent_0, sent_1 = moe_partial(
+        picks, weights, unit_dir, normed, pieces, w_gate, w_up, w_down
+    )
+    summed = jnp.concatenate(
+        [summed_up(kept_0, sent_0, width), summed_up(kept_1, sent_1, width)], axis=0
+    )
     return (base + summed).astype(jnp.bfloat16)
+
+
+def summed_up(kept, sent, width):
+    n_z = kept.shape[1]
+    arrived = swap(sent, "rep", 1)
+    x_far = swap(added(kept[..., :width], arrived[..., :width]), "rep", 2)
+    y_far = swap(added(kept[1, ..., 2 * width :], arrived[1, ..., 2 * width :]), "seq", 1)
+    mid = slice(width, 2 * width)
+    first_far = swap(added(kept[1, ..., mid], arrived[1, ..., mid], x_far[1]), "seq", 1)
+    end = slice(3 * width, 4 * width)
+    second_far = swap(
+        added(kept[0, ..., end], arrived[0, ..., end], y_far[..., width:]), "rep", 2
+    )
+    first = added(kept[0, ..., mid], arrived[0, ..., mid], x_far[0], first_far)
+    near = slice(2 * width, 3 * width)
+    second = added(kept[0, ..., near], arrived[0, ..., near], y_far[..., :width], second_far)
+    blocks = jnp.concatenate([first, second], axis=2)
+    terms = [blocks[0]] + [swap(blocks[d], "seq", 2 * d) for d in range(1, n_z)]
+    return sum(term.astype(jnp.float32) for term in terms)
 
 
 def exchanged(tokens, norm_gain, refusal_dir, expert_ids, gate_probs, w_gate, w_up, w_down):

time: 107 us -> 107 us (level)
  starting transfers between devices: 22.5 us -> 39.8 us
  waiting for transfers between devices: 52.1 us -> 37.1 us
  local copies, waits for them, and re-layouts: 3.55 us -> 0.81 us
    ppermute x29 -> x38, starting transfers between devices: 22.5 us -> 39.8 us  [swap(): return lax.ppermute(value, axis, [(i, i ^ distance) for i in range(size)])]
    ppermute x29 -> x38, waiting for transfers between devices: 52.1 us -> 37.1 us  [swap(): return lax.ppermute(value, axis, [(i, i ^ distance) for i in range(size)])]
    unnamed x19 -> x13, local copies, waits for them, and re-layouts: 3.44 us -> 0.78 us
  transfers between devices with their start and end apart: 29 -> 38, of which waited for: 14 -> 14; matrix products, arithmetic and copies ran while one was open for 2% -> 2% of each run, Pallas kernels for 3% -> 3%
where the time goes in v2:
time: 107 us; the launch traced here: 106 us
  starting transfers between devices  39.8 us (37%)
  waiting for transfers between devices  37.1 us (35%)
  Pallas kernels  26.7 us (25%)
  other arithmetic  1.84 us (2%)
    ppermute x38, starting transfers between devices, swap(): return lax.ppermute(value, axis, [(i, i ^ distance) for i in range(size)])  39.8 us
    ppermute x38, waiting for transfers between devices, swap(): return lax.ppermute(value, axis, [(i, i ^ distance) for i in range(size)])  37.1 us
    pallas_call x1, Pallas kernels, moe_partial(): pl.pallas_call(functools.partial(moe_kernel, n_pieces), out_shape=outs, i...  20.6 us
    pallas_call x1, Pallas kernels, route(): pl.pallas_call(functools.partial(route_kernel, exp_dev), out_shape=[jax.S...  3.6 us
    pallas_call x1, Pallas kernels, norm_and_base(): pl.pallas_call(norm_kernel, out_shape=[jax.ShapeDtypeStruct((tok_rows, mo...  2.46 us
  transfers between devices with their start and end apart: 38, of which 14 were waited for; matrix products, arithmetic and copies ran while one was open for 2% of the time, Pallas kernels for 3%

profile of v2, /device:TPU:0, one launch (start us, length us, event | category | flops | bytes accessed | tf_op | source)
XLA Modules:
  0.0 106.4 jit_solution(11203462058431517135)
XLA Ops:
  0.0 2.5 %shard_map.82 = (bf16[128,2048]{1,0:T(8,128)(2,1)}, bf16[144,256]{1,0:T(8,128)(2,1)}, bf16[128,256]{1,0:T(8,128)(2,1)}, bf16[144,1024]{1,0:T(8,128)(2,1)}, f32[1...) custom-call(bf16[128,2048]{1,0:T(8,128)(2,1)} %tokens_ref.1, f32[1,2048]{1,0:T(1,128)} %bitcast.78, ...), custom_call_target="tpu_custom_call" | custom-call | tf_op jit(solution)/shard_map/pallas_call | solution.py:75
  2.5 5.0 %collective-permute-start.2 = (bf16[144,256]{1,0:T(8,128)(2,1)}, bf16[144,256]{1,0:T(8,128)(2,1)S(1)}, u32[]{:S(2)}, u32[]{:S(2)}) collective-permute-start(bf16[144,256]{1,0:T(8,128)(2,1)} %get-tuple-element.29), channel_id=1, source_target_pairs={{0,24},{4,28},{8,16},{12,20},{16,8},{20,12},{24,0},{28,4},{1,25},{... | collective-permute-start | bytes 221192 | tf_op jit(solution)/shard_map/ppermute | solution.py:314
  8.1 1.7 %collective-permute-start.3 = (bf16[144,1024]{1,0:T(8,128)(2,1)}, bf16[144,1024]{1,0:T(8,128)(2,1)S(1)}, u32[]{:S(2)}, u32[]{:S(2)}) collective-permute-start(bf16[144,1024]{1,0:T(8,128)(2,1)} %get-tuple-element.30), channel_id=1, source_target_pairs={{0,4},{4,0},{8,12},{12,8},{16,20},{20,16},{24,28},{28,24},{1,5},{5... | collective-permute-start | bytes 884744 | tf_op jit(solution)/shard_map/ppermute | solution.py:314
  10.5 3.4 %collective-permute-done.1 = bf16[144,256]{1,0:T(8,128)(2,1)S(1)} collective-permute-done((bf16[144,256]{1,0:T(8,128)(2,1)}, bf16[144,256]{1,0:T(8,128)(2,1)S(1)}, u32[]{:S(2)}, u32[]{:S(2)}) %collective-permute-start.1) | collective-permute-done | bytes 73760 | tf_op jit(solution)/shard_map/ppermute | solution.py:314
  14.0 2.6 %collective-permute-done.3.refs_6_ = bf16[144,1024]{1,0:T(8,128)(2,1)S(1)} collective-permute-done((bf16[144,1024]{1,0:T(8,128)(2,1)}, bf16[144,1024]{1,0:T(8,128)(2,1)S(1)}, u32[]{:S(2)}, u32[]{:S(2)}) %collective-permute-start.3) | collective-permute-done | bytes 294944 | tf_op jit(solution)/shard_map/ppermute | solution.py:314
  16.5 3.5 %collective-permute-start.6 = (bf16[128,256]{1,0:T(8,128)(2,1)}, bf16[128,256]{1,0:T(8,128)(2,1)S(1)}, u32[]{:S(2)}, u32[]{:S(2)}) collective-permute-start(bf16[128,256]{1,0:T(8,128)(2,1)} %get-tuple-element.31), channel_id=1, source_target_pairs={{0,24},{4,28},{8,16},{12,20},{16,8},{20,12},{24,0},{28,4},{1,25},{... | collective-permute-start | bytes 196616 | tf_op jit(solution)/shard_map/ppermute | solution.py:314
  21.0 1.6 %collective-permute-start.8 = (bf16[3,144,256]{2,1,0:T(8,128)(2,1)S(1)}, bf16[3,144,256]{2,1,0:T(8,128)(2,1)S(1)}, u32[]{:S(2)}, u32[]{:S(2)}) collective-permute-start(bf16[3,144,256]{2,1,0:T(8,128)(2,1)S(1)} %pad_maximum_fusion.refs_4_), channel_id=1, source_target_pairs={{0,4},{4,0},{8,12},{12,8},{16,20},{20,16},{24,28},{28,24},{1,5},{5... | collective-permute-start | bytes 663560 | tf_op jit(solution)/shard_map/ppermute | solution.py:314
  22.5 1.5 %collective-permute-start.9 = (bf16[3,128,256]{2,1,0:T(8,128)(2,1)S(1)}, bf16[3,128,256]{2,1,0:T(8,128)(2,1)S(1)}, u32[]{:S(2)}, u32[]{:S(2)}) collective-permute-start(bf16[3,128,256]{2,1,0:T(8,128)(2,1)S(1)} %slice.151), channel_id=1, source_target_pairs={{0,2},{1,3},{2,0},{3,1},{4,6},{5,7},{6,4},{7,5},{8,10},{9,11},{10,... | collective-permute-start | bytes 589832 | tf_op jit(solution)/shard_map/ppermute | solution.py:314
  24.1 1.3 %collective-permute-done.5 = bf16[128,256]{1,0:T(8,128)(2,1)S(1)} collective-permute-done((bf16[128,256]{1,0:T(8,128)(2,1)}, bf16[128,256]{1,0:T(8,128)(2,1)S(1)}, u32[]{:S(2)}, u32[]{:S(2)}) %collective-permute-start.5) | collective-permute-done | bytes 65568 | tf_op jit(solution)/shard_map/ppermute | solution.py:314
  25.5 1.6 %collective-permute-start.10 = (bf16[3,128,256]{2,1,0:T(8,128)(2,1)S(1)}, bf16[3,128,256]{2,1,0:T(8,128)(2,1)S(1)}, u32[]{:S(2)}, u32[]{:S(2)}) collective-permute-start(bf16[3,128,256]{2,1,0:T(8,128)(2,1)S(1)} %pad_maximum_fusion.1.refs_5_), channel_id=1, source_target_pairs={{0,2},{1,3},{2,0},{3,1},{4,6},{5,7},{6,4},{7,5},{8,10},{9,11},{10,... | collective-permute-start | bytes 589832 | tf_op jit(solution)/shard_map/ppermute | solution.py:314
  27.1 1.5 %collective-permute-start.7 = (bf16[3,128,256]{2,1,0:T(8,128)(2,1)S(1)}, bf16[3,128,256]{2,1,0:T(8,128)(2,1)S(1)}, u32[]{:S(2)}, u32[]{:S(2)}) collective-permute-start(bf16[3,128,256]{2,1,0:T(8,128)(2,1)S(1)} %pad_maximum_fusion.1.refs_5_), channel_id=1, source_target_pairs={{0,4},{4,0},{8,12},{12,8},{16,20},{20,16},{24,28},{28,24},{1,5},{5... | collective-permute-start | bytes 589832 | tf_op jit(solution)/shard_map/ppermute | solution.py:314
  29.8 3.6 %shard_map.83 = (bf16[8,256,128]{2,1,0:T(8,128)(2,1)}, bf16[8,128,256]{2,1,0:T(8,128)(2,1)}) custom-call(bf16[8,16,128]{2,1,0:T(8,128)(2,1)} %copy-done.2), custom_call_target="tpu_custom_call" | custom-call | flops 4000000000 | bytes 2097152 | tf_op jit(solution)/shard_map/pallas_call | solution.py:125
  33.4 1.4 %collective-permute-done.7.refs_10_ = bf16[3,128,256]{2,1,0:T(8,128)(2,1)S(1)} collective-permute-done((bf16[3,128,256]{2,1,0:T(8,128)(2,1)S(1)}, bf16[3,128,256]{2,1,0:T(8,128)(2,1)S(1)}, u32[]{:S(2)}, u32[]{:S(2)}) %collective-permute-start.7) | collective-permute-done | bytes 196640 | tf_op jit(solution)/shard_map/ppermute | solution.py:314
  35.4 2.9 %collective-permute-done.11.refs_11_ = bf16[3,128,256]{2,1,0:T(8,128)(2,1)S(1)} collective-permute-done((bf16[3,128,256]{2,1,0:T(8,128)(2,1)S(1)}, bf16[3,128,256]{2,1,0:T(8,128)(2,1)S(1)}, u32[]{:S(2)}, u32[]{:S(2)}) %collective-permute-start.11) | collective-permute-done | bytes 196640 | tf_op jit(solution)/shard_map/ppermute | solution.py:314
  39.3 2.8 %collective-permute-done.12.refs_12_ = bf16[3,128,256]{2,1,0:T(8,128)(2,1)S(1)} collective-permute-done((bf16[3,128,256]{2,1,0:T(8,128)(2,1)S(1)}, bf16[3,128,256]{2,1,0:T(8,128)(2,1)S(1)}, u32[]{:S(2)}, u32[]{:S(2)}) %collective-permute-start.12) | collective-permute-done | bytes 196640 | tf_op jit(solution)/shard_map/ppermute | solution.py:314
  42.2 1.4 %collective-permute-done.21.refs_21_ = bf16[3,128,256]{2,1,0:T(8,128)(2,1)S(1)} collective-permute-done((bf16[3,128,256]{2,1,0:T(8,128)(2,1)S(1)}, bf16[3,128,256]{2,1,0:T(8,128)(2,1)S(1)}, u32[]{:S(2)}, u32[]{:S(2)}) %collective-permute-start.21) | collective-permute-done | bytes 196640 | tf_op jit(solution)/shard_map/ppermute | solution.py:314
  43.6 20.6 %shard_map.84 = (bf16[2,4,64,1024]{3,2,1,0:T(8,128)(2,1)S(1)}, bf16[2,4,64,1024]{3,2,1,0:T(8,128)(2,1)S(1)}, bf16[2,4,64,1024]{3,2,1,0:T(8,128)(2,1)S(1)}, bf16[2,4,64,1024]{3,2,1,0:T(8,128)(2,1)S(1)}) custom-call(bf16[8,256,128]{2,1,0:T(8,128)(2,1)} %get-tuple-element.37.refs_0_, bf16[8,128,256]{2,1,0:T(8,128)(2,1)} %get-tuple-element.38.refs_1_, ...), custom_call_target="tpu_custom_call" | custom-call | flops 4831838208 | bytes 46137344 | tf_op jit(solution)/shard_map/pallas_call | solution.py:284
  64.8 2.1 %collective-permute-done.22 = bf16[2,4,64,1024]{3,2,1,0:T(8,128)(2,1)S(1)} collective-permute-done((bf16[2,4,64,1024]{3,2,1,0:T(8,128)(2,1)S(1)}, bf16[2,4,64,1024]{3,2,1,0:T(8,128)(2,1)S(1)}, u32[]{:S(2)}, u32[]{:S(2)}) %collective-permute-start.22) | collective-permute-done | bytes 1048608 | tf_op jit(solution)/shard_map/ppermute | solution.py:314
  67.8 1.6 %collective-permute-start.25 = (bf16[4,64,512]{2,1,0:T(8,128)(2,1)S(1)}, bf16[4,64,512]{2,1,0:T(8,128)(2,1)S(1)}, u32[]{:S(2)}, u32[]{:S(2)}) collective-permute-start(bf16[4,64,512]{2,1,0:T(8,128)(2,1)S(1)} %fusion), channel_id=1, source_target_pairs={{0,4},{4,0},{8,12},{12,8},{16,20},{20,16},{24,28},{28,24},{1,5},{5... | collective-permute-start | bytes 786440 | tf_op jit(solution)/shard_map/ppermute | solution.py:314
  69.5 1.6 %collective-permute-start.31 = (bf16[2,4,64,256]{3,2,1,0:T(8,128)(2,1)S(1)}, bf16[2,4,64,256]{3,2,1,0:T(8,128)(2,1)S(1)}, u32[]{:S(2)}, u32[]{:S(2)}) collective-permute-start(bf16[2,4,64,256]{3,2,1,0:T(8,128)(2,1)S(1)} %add_convert_fusion.1), channel_id=1, source_target_pairs={{0,2},{1,3},{2,0},{3,1},{4,6},{5,7},{6,4},{7,5},{8,10},{9,11},{10,... | collective-permute-start | bytes 786440 | tf_op jit(solution)/shard_map/ppermute | solution.py:314
  71.7 4.6 %collective-permute-done.23 = bf16[2,4,64,256]{3,2,1,0:T(8,128)(2,1)S(1)} collective-permute-done((bf16[2,4,64,256]{3,2,1,0:T(8,128)(2,1)S(1)}, bf16[2,4,64,256]{3,2,1,0:T(8,128)(2,1)S(1)}, u32[]{:S(2)}, u32[]{:S(2)}) %collective-permute-start.23) | collective-permute-done | bytes 262176 | tf_op jit(solution)/shard_map/ppermute | solution.py:314
  76.3 1.6 %collective-permute-start.24 = (bf16[4,64,256]{2,1,0:T(8,128)(2,1)S(1)}, bf16[4,64,256]{2,1,0:T(8,128)(2,1)S(1)}, u32[]{:S(2)}, u32[]{:S(2)}) collective-permute-start(bf16[4,64,256]{2,1,0:T(8,128)(2,1)S(1)} %fusion.11), channel_id=1, source_target_pairs={{0,4},{4,0},{8,12},{12,8},{16,20},{20,16},{24,28},{28,24},{1,5},{5... | collective-permute-start | bytes 393224 | tf_op jit(solution)/shard_map/ppermute | solution.py:314
  77.9 3.2 %collective-permute-done.31 = bf16[2,4,64,256]{3,2,1,0:T(8,128)(2,1)S(1)} collective-permute-done((bf16[2,4,64,256]{3,2,1,0:T(8,128)(2,1)S(1)}, bf16[2,4,64,256]{3,2,1,0:T(8,128)(2,1)S(1)}, u32[]{:S(2)}, u32[]{:S(2)}) %collective-permute-start.31) | collective-permute-done | bytes 262176 | tf_op jit(solution)/shard_map/ppermute | solution.py:314
  81.2 1.6 %collective-permute-start.32 = (bf16[4,64,256]{2,1,0:T(8,128)(2,1)S(1)}, bf16[4,64,256]{2,1,0:T(8,128)(2,1)S(1)}, u32[]{:S(2)}, u32[]{:S(2)}) collective-permute-start(bf16[4,64,256]{2,1,0:T(8,128)(2,1)S(1)} %fusion.12), channel_id=1, source_target_pairs={{0,4},{4,0},{8,12},{12,8},{16,20},{20,16},{24,28},{28,24},{1,5},{5... | collective-permute-start | bytes 393224 | tf_op jit(solution)/shard_map/ppermute | solution.py:314
  82.7 2.7 %collective-permute-done.24 = bf16[4,64,256]{2,1,0:T(8,128)(2,1)S(1)} collective-permute-done((bf16[4,64,256]{2,1,0:T(8,128)(2,1)S(1)}, bf16[4,64,256]{2,1,0:T(8,128)(2,1)S(1)}, u32[]{:S(2)}, u32[]{:S(2)}) %collective-permute-start.24) | collective-permute-done | bytes 131104 | tf_op jit(solution)/shard_map/ppermute | solution.py:314
  85.6 1.5 %collective-permute-start.26 = (bf16[4,64,256]{2,1,0:T(8,128)(2,1)S(1)}, bf16[4,64,256]{2,1,0:T(8,128)(2,1)S(1)}, u32[]{:S(2)}, u32[]{:S(2)}) collective-permute-start(bf16[4,64,256]{2,1,0:T(8,128)(2,1)S(1)} %get-tuple-element.50), channel_id=1, source_target_pairs={{0,2},{1,3},{2,0},{3,1},{4,6},{5,7},{6,4},{7,5},{8,10},{9,11},{10,... | collective-permute-start | bytes 393224 | tf_op jit(solution)/shard_map/ppermute | solution.py:314
  87.3 1.6 %collective-permute-start.34 = (bf16[4,64,256]{2,1,0:T(8,128)(2,1)S(1)}, bf16[4,64,256]{2,1,0:T(8,128)(2,1)S(1)}, u32[]{:S(2)}, u32[]{:S(2)}) collective-permute-start(bf16[4,64,256]{2,1,0:T(8,128)(2,1)S(1)} %get-tuple-element.52), channel_id=1, source_target_pairs={{0,2},{1,3},{2,0},{3,1},{4,6},{5,7},{6,4},{7,5},{8,10},{9,11},{10,... | collective-permute-start | bytes 393224 | tf_op jit(solution)/shard_map/ppermute | solution.py:314
  88.8 2.9 %collective-permute-done.26 = bf16[4,64,256]{2,1,0:T(8,128)(2,1)S(1)} collective-permute-done((bf16[4,64,256]{2,1,0:T(8,128)(2,1)S(1)}, bf16[4,64,256]{2,1,0:T(8,128)(2,1)S(1)}, u32[]{:S(2)}, u32[]{:S(2)}) %collective-permute-start.26) | collective-permute-done | bytes 131104 | tf_op jit(solution)/shard_map/ppermute | solution.py:314
  92.5 2.9 %collective-permute-start.29 = (bf16[64,512]{1,0:T(8,128)(2,1)S(1)}, bf16[64,512]{1,0:T(8,128)(2,1)S(1)}, u32[]{:S(2)}, u32[]{:S(2)}) collective-permute-start(bf16[64,512]{1,0:T(8,128)(2,1)S(1)} %get-tuple-element.54), channel_id=1, source_target_pairs={{0,24},{4,28},{8,16},{12,20},{16,8},{20,12},{24,0},{28,4},{1,25},{... | collective-permute-start | bytes 196616 | tf_op jit(solution)/shard_map/ppermute | solution.py:314
  97.0 2.9 %collective-permute-start.37 = (bf16[64,512]{1,0:T(8,128)(2,1)S(1)}, bf16[64,512]{1,0:T(8,128)(2,1)S(1)}, u32[]{:S(2)}, u32[]{:S(2)}) collective-permute-start(bf16[64,512]{1,0:T(8,128)(2,1)S(1)} %get-tuple-element.57), channel_id=1, source_target_pairs={{0,24},{4,28},{8,16},{12,20},{16,8},{20,12},{24,0},{28,4},{1,25},{... | collective-permute-start | bytes 196616 | tf_op jit(solution)/shard_map/ppermute | solution.py:314
  100.0 3.6 %collective-permute-done.28 = bf16[64,512]{1,0:T(8,128)(2,1)S(1)} collective-permute-done((bf16[64,512]{1,0:T(8,128)(2,1)S(1)}, bf16[64,512]{1,0:T(8,128)(2,1)S(1)}, u32[]{:S(2)}, u32[]{:S(2)}) %collective-permute-start.28) | collective-permute-done | bytes 65568 | tf_op jit(solution)/shard_map/ppermute | solution.py:314
  103.6 2.0 %collective-permute-done.36 = bf16[64,512]{1,0:T(8,128)(2,1)S(1)} collective-permute-done((bf16[64,512]{1,0:T(8,128)(2,1)S(1)}, bf16[64,512]{1,0:T(8,128)(2,1)S(1)}, u32[]{:S(2)}, u32[]{:S(2)}) %collective-permute-start.36) | collective-permute-done | bytes 65568 | tf_op jit(solution)/shard_map/ppermute | solution.py:314
  (79 shorter events, 10.9 us)
Async XLA Ops:
  2.5 8.0 %collective-permute-start.2 = (bf16[144,256]{1,0:T(8,128)(2,1)}, bf16[144,256]{1,0:T(8,128)(2,1)S(1)}, u32[]{:S(2)}, u32[]{:S(2)}) collective-permute-start(bf16[144,256]{1,0:T(8,128)(2,1)} %get-tuple-element.29), channel_id=1, source_target_pairs={{0,24},{4,28},{8,16},{12,20},{16,8},{20,12},{24,0},{28,4},{1,25},{... | collective-permute-start | bytes 221192 | tf_op jit(solution)/shard_map/ppermute | solution.py:314
  7.5 6.4 %collective-permute-start.1 = (bf16[144,256]{1,0:T(8,128)(2,1)}, bf16[144,256]{1,0:T(8,128)(2,1)S(1)}, u32[]{:S(2)}, u32[]{:S(2)}) collective-permute-start(bf16[144,256]{1,0:T(8,128)(2,1)} %get-tuple-element.29), channel_id=1, source_target_pairs={{0,16},{4,20},{8,24},{12,28},{16,0},{20,4},{24,8},{28,12},{1,17},{... | collective-permute-start | bytes 221192 | tf_op jit(solution)/shard_map/ppermute | solution.py:314
  7.5 6.4 %collective-permute-start = (bf16[144,256]{1,0:T(8,128)(2,1)}, bf16[144,256]{1,0:T(8,128)(2,1)S(1)}, u32[]{:S(2)}, u32[]{:S(2)}) collective-permute-start(bf16[144,256]{1,0:T(8,128)(2,1)} %get-tuple-element.29), channel_id=1, source_target_pairs={{0,8},{4,12},{8,0},{12,4},{16,24},{20,28},{24,16},{28,20},{1,9},{5... | collective-permute-start | bytes 221192 | tf_op jit(solution)/shard_map/ppermute | solution.py:314
  8.1 8.4 %collective-permute-start.3 = (bf16[144,1024]{1,0:T(8,128)(2,1)}, bf16[144,1024]{1,0:T(8,128)(2,1)S(1)}, u32[]{:S(2)}, u32[]{:S(2)}) collective-permute-start(bf16[144,1024]{1,0:T(8,128)(2,1)} %get-tuple-element.30), channel_id=1, source_target_pairs={{0,4},{4,0},{8,12},{12,8},{16,20},{20,16},{24,28},{28,24},{1,5},{5... | collective-permute-start | bytes 884744 | tf_op jit(solution)/shard_map/ppermute | solution.py:314
  16.5 7.5 %collective-permute-start.6 = (bf16[128,256]{1,0:T(8,128)(2,1)}, bf16[128,256]{1,0:T(8,128)(2,1)S(1)}, u32[]{:S(2)}, u32[]{:S(2)}) collective-permute-start(bf16[128,256]{1,0:T(8,128)(2,1)} %get-tuple-element.31), channel_id=1, source_target_pairs={{0,24},{4,28},{8,16},{12,20},{16,8},{20,12},{24,0},{28,4},{1,25},{... | collective-permute-start | bytes 196616 | tf_op jit(solution)/shard_map/ppermute | solution.py:314
  20.0 5.4 %collective-permute-start.5 = (bf16[128,256]{1,0:T(8,128)(2,1)}, bf16[128,256]{1,0:T(8,128)(2,1)S(1)}, u32[]{:S(2)}, u32[]{:S(2)}) collective-permute-start(bf16[128,256]{1,0:T(8,128)(2,1)} %get-tuple-element.31), channel_id=1, source_target_pairs={{0,16},{4,20},{8,24},{12,28},{16,0},{20,4},{24,8},{28,12},{1,17},{... | collective-permute-start | bytes 196616 | tf_op jit(solution)/shard_map/ppermute | solution.py:314
  20.0 5.4 %collective-permute-start.4 = (bf16[128,256]{1,0:T(8,128)(2,1)}, bf16[128,256]{1,0:T(8,128)(2,1)S(1)}, u32[]{:S(2)}, u32[]{:S(2)}) collective-permute-start(bf16[128,256]{1,0:T(8,128)(2,1)} %get-tuple-element.31), channel_id=1, source_target_pairs={{0,8},{4,12},{8,0},{12,4},{16,24},{20,28},{24,16},{28,20},{1,9},{5... | collective-permute-start | bytes 196616 | tf_op jit(solution)/shard_map/ppermute | solution.py:314
  21.0 8.1 %collective-permute-start.8 = (bf16[3,144,256]{2,1,0:T(8,128)(2,1)S(1)}, bf16[3,144,256]{2,1,0:T(8,128)(2,1)S(1)}, u32[]{:S(2)}, u32[]{:S(2)}) collective-permute-start(bf16[3,144,256]{2,1,0:T(8,128)(2,1)S(1)} %pad_maximum_fusion.refs_4_), channel_id=1, source_target_pairs={{0,4},{4,0},{8,12},{12,8},{16,20},{20,16},{24,28},{28,24},{1,5},{5... | collective-permute-start | bytes 663560 | tf_op jit(solution)/shard_map/ppermute | solution.py:314
  22.5 6.0 %collective-permute-start.9 = (bf16[3,128,256]{2,1,0:T(8,128)(2,1)S(1)}, bf16[3,128,256]{2,1,0:T(8,128)(2,1)S(1)}, u32[]{:S(2)}, u32[]{:S(2)}) collective-permute-start(bf16[3,128,256]{2,1,0:T(8,128)(2,1)S(1)} %slice.151), channel_id=1, source_target_pairs={{0,2},{1,3},{2,0},{3,1},{4,6},{5,7},{6,4},{7,5},{8,10},{9,11},{10,... | collective-permute-start | bytes 589832 | tf_op jit(solution)/shard_map/ppermute | solution.py:314
  25.5 9.3 %collective-permute-start.10 = (bf16[3,128,256]{2,1,0:T(8,128)(2,1)S(1)}, bf16[3,128,256]{2,1,0:T(8,128)(2,1)S(1)}, u32[]{:S(2)}, u32[]{:S(2)}) collective-permute-start(bf16[3,128,256]{2,1,0:T(8,128)(2,1)S(1)} %pad_maximum_fusion.1.refs_5_), channel_id=1, source_target_pairs={{0,2},{1,3},{2,0},{3,1},{4,6},{5,7},{6,4},{7,5},{8,10},{9,11},{10,... | collective-permute-start | bytes 589832 | tf_op jit(solution)/shard_map/ppermute | solution.py:314
  27.1 7.7 %collective-permute-start.7 = (bf16[3,128,256]{2,1,0:T(8,128)(2,1)S(1)}, bf16[3,128,256]{2,1,0:T(8,128)(2,1)S(1)}, u32[]{:S(2)}, u32[]{:S(2)}) collective-permute-start(bf16[3,128,256]{2,1,0:T(8,128)(2,1)S(1)} %pad_maximum_fusion.1.refs_5_), channel_id=1, source_target_pairs={{0,4},{4,0},{8,12},{12,8},{16,20},{20,16},{24,28},{28,24},{1,5},{5... | collective-permute-start | bytes 589832 | tf_op jit(solution)/shard_map/ppermute | solution.py:314
  28.6 9.7 %collective-permute-start.11 = (bf16[3,128,256]{2,1,0:T(8,128)(2,1)S(1)}, bf16[3,128,256]{2,1,0:T(8,128)(2,1)S(1)}, u32[]{:S(2)}, u32[]{:S(2)}) collective-permute-start(bf16[3,128,256]{2,1,0:T(8,128)(2,1)S(1)} %collective-permute-done.9.refs_7_), channel_id=1, source_target_pairs={{0,4},{4,0},{8,12},{12,8},{16,20},{20,16},{24,28},{28,24},{1,5},{5... | collective-permute-start | bytes 589832 | tf_op jit(solution)/shard_map/ppermute | solution.py:314
  29.1 9.7 %collective-permute-start.13 = (bf16[3,144,256]{2,1,0:T(8,128)(2,1)S(1)}, bf16[3,144,256]{2,1,0:T(8,128)(2,1)S(1)}, u32[]{:S(2)}, u32[]{:S(2)}) collective-permute-start(bf16[3,144,256]{2,1,0:T(8,128)(2,1)S(1)} %pad_maximum_fusion.refs_4_), channel_id=1, source_target_pairs={{0,1},{1,0},{2,3},{3,2},{4,5},{5,4},{6,7},{7,6},{8,9},{9,8},{10,11... | collective-permute-start | bytes 663560 | tf_op jit(solution)/shard_map/ppermute | solution.py:314
  29.2 9.7 %collective-permute-start.17 = (bf16[3,144,256]{2,1,0:T(8,128)(2,1)S(1)}, bf16[3,144,256]{2,1,0:T(8,128)(2,1)S(1)}, u32[]{:S(2)}, u32[]{:S(2)}) collective-permute-start(bf16[3,144,256]{2,1,0:T(8,128)(2,1)S(1)} %collective-permute-done.8.refs_8_), channel_id=1, source_target_pairs={{0,1},{1,0},{2,3},{3,2},{4,5},{5,4},{6,7},{7,6},{8,9},{9,8},{10,11... | collective-permute-start | bytes 663560 | tf_op jit(solution)/shard_map/ppermute | solution.py:314
  34.8 7.3 %collective-permute-start.12 = (bf16[3,128,256]{2,1,0:T(8,128)(2,1)S(1)}, bf16[3,128,256]{2,1,0:T(8,128)(2,1)S(1)}, u32[]{:S(2)}, u32[]{:S(2)}) collective-permute-start(bf16[3,128,256]{2,1,0:T(8,128)(2,1)S(1)} %collective-permute-done.7.refs_10_), channel_id=1, source_target_pairs={{0,2},{1,3},{2,0},{3,1},{4,6},{5,7},{6,4},{7,5},{8,10},{9,11},{10,... | collective-permute-start | bytes 589832 | tf_op jit(solution)/shard_map/ppermute | solution.py:314
  38.2 3.9 %collective-permute-start.15 = (bf16[144,1024]{1,0:T(8,128)(2,1)S(1)}, bf16[144,1024]{1,0:T(8,128)(2,1)S(1)}, u32[]{:S(2)}, u32[]{:S(2)}) collective-permute-start(bf16[144,1024]{1,0:T(8,128)(2,1)S(1)} %collective-permute-done.3.refs_6_), channel_id=1, source_target_pairs={{0,1},{1,0},{2,3},{3,2},{4,5},{5,4},{6,7},{7,6},{8,9},{9,8},{10,11... | collective-permute-start | bytes 884744 | tf_op jit(solution)/shard_map/ppermute | solution.py:314
  38.3 3.9 %collective-permute-start.19 = (bf16[3,128,256]{2,1,0:T(8,128)(2,1)S(1)}, bf16[3,128,256]{2,1,0:T(8,128)(2,1)S(1)}, u32[]{:S(2)}, u32[]{:S(2)}) collective-permute-start(bf16[3,128,256]{2,1,0:T(8,128)(2,1)S(1)} %collective-permute-done.7.refs_10_), channel_id=1, source_target_pairs={{0,1},{1,0},{2,3},{3,2},{4,5},{5,4},{6,7},{7,6},{8,9},{9,8},{10,11... | collective-permute-start | bytes 589832 | tf_op jit(solution)/shard_map/ppermute | solution.py:314
  64.4 4.9 %collective-permute-start.30 = (bf16[2,4,64,1024]{3,2,1,0:T(8,128)(2,1)S(1)}, bf16[2,4,64,1024]{3,2,1,0:T(8,128)(2,1)S(1)}, u32[]{:S(2)}, u32[]{:S(2)}) collective-permute-start(bf16[2,4,64,1024]{3,2,1,0:T(8,128)(2,1)S(1)} %get-tuple-element.48), channel_id=1, source_target_pairs={{0,1},{1,0},{2,3},{3,2},{4,5},{5,4},{6,7},{7,6},{8,9},{9,8},{10,11... | collective-permute-start | bytes 3145736 | tf_op jit(solution)/shard_map/ppermute | solution.py:314
  67.1 9.2 %collective-permute-start.23 = (bf16[2,4,64,256]{3,2,1,0:T(8,128)(2,1)S(1)}, bf16[2,4,64,256]{3,2,1,0:T(8,128)(2,1)S(1)}, u32[]{:S(2)}, u32[]{:S(2)}) collective-permute-start(bf16[2,4,64,256]{3,2,1,0:T(8,128)(2,1)S(1)} %add_convert_fusion.3), channel_id=1, source_target_pairs={{0,2},{1,3},{2,0},{3,1},{4,6},{5,7},{6,4},{7,5},{8,10},{9,11},{10,... | collective-permute-start | bytes 786440 | tf_op jit(solution)/shard_map/ppermute | solution.py:314
  67.8 15.0 %collective-permute-start.25 = (bf16[4,64,512]{2,1,0:T(8,128)(2,1)S(1)}, bf16[4,64,512]{2,1,0:T(8,128)(2,1)S(1)}, u32[]{:S(2)}, u32[]{:S(2)}) collective-permute-start(bf16[4,64,512]{2,1,0:T(8,128)(2,1)S(1)} %fusion), channel_id=1, source_target_pairs={{0,4},{4,0},{8,12},{12,8},{16,20},{20,16},{24,28},{28,24},{1,5},{5... | collective-permute-start | bytes 786440 | tf_op jit(solution)/shard_map/ppermute | solution.py:314
  69.5 11.6 %collective-permute-start.31 = (bf16[2,4,64,256]{3,2,1,0:T(8,128)(2,1)S(1)}, bf16[2,4,64,256]{3,2,1,0:T(8,128)(2,1)S(1)}, u32[]{:S(2)}, u32[]{:S(2)}) collective-permute-start(bf16[2,4,64,256]{3,2,1,0:T(8,128)(2,1)S(1)} %add_convert_fusion.1), channel_id=1, source_target_pairs={{0,2},{1,3},{2,0},{3,1},{4,6},{5,7},{6,4},{7,5},{8,10},{9,11},{10,... | collective-permute-start | bytes 786440 | tf_op jit(solution)/shard_map/ppermute | solution.py:314
  71.1 16.0 %collective-permute-start.33 = (bf16[4,64,512]{2,1,0:T(8,128)(2,1)S(1)}, bf16[4,64,512]{2,1,0:T(8,128)(2,1)S(1)}, u32[]{:S(2)}, u32[]{:S(2)}) collective-permute-start(bf16[4,64,512]{2,1,0:T(8,128)(2,1)S(1)} %fusion.1), channel_id=1, source_target_pairs={{0,4},{4,0},{8,12},{12,8},{16,20},{20,16},{24,28},{28,24},{1,5},{5... | collective-permute-start | bytes 786440 | tf_op jit(solution)/shard_map/ppermute | solution.py:314
  76.3 9.1 %collective-permute-start.24 = (bf16[4,64,256]{2,1,0:T(8,128)(2,1)S(1)}, bf16[4,64,256]{2,1,0:T(8,128)(2,1)S(1)}, u32[]{:S(2)}, u32[]{:S(2)}) collective-permute-start(bf16[4,64,256]{2,1,0:T(8,128)(2,1)S(1)} %fusion.11), channel_id=1, source_target_pairs={{0,4},{4,0},{8,12},{12,8},{16,20},{20,16},{24,28},{28,24},{1,5},{5... | collective-permute-start | bytes 393224 | tf_op jit(solution)/shard_map/ppermute | solution.py:314
  81.2 6.0 %collective-permute-start.32 = (bf16[4,64,256]{2,1,0:T(8,128)(2,1)S(1)}, bf16[4,64,256]{2,1,0:T(8,128)(2,1)S(1)}, u32[]{:S(2)}, u32[]{:S(2)}) collective-permute-start(bf16[4,64,256]{2,1,0:T(8,128)(2,1)S(1)} %fusion.12), channel_id=1, source_target_pairs={{0,4},{4,0},{8,12},{12,8},{16,20},{20,16},{24,28},{28,24},{1,5},{5... | collective-permute-start | bytes 393224 | tf_op jit(solution)/shard_map/ppermute | solution.py:314
  85.6 6.1 %collective-permute-start.26 = (bf16[4,64,256]{2,1,0:T(8,128)(2,1)S(1)}, bf16[4,64,256]{2,1,0:T(8,128)(2,1)S(1)}, u32[]{:S(2)}, u32[]{:S(2)}) collective-permute-start(bf16[4,64,256]{2,1,0:T(8,128)(2,1)S(1)} %get-tuple-element.50), channel_id=1, source_target_pairs={{0,2},{1,3},{2,0},{3,1},{4,6},{5,7},{6,4},{7,5},{8,10},{9,11},{10,... | collective-permute-start | bytes 393224 | tf_op jit(solution)/shard_map/ppermute | solution.py:314
  87.3 8.6 %collective-permute-start.34 = (bf16[4,64,256]{2,1,0:T(8,128)(2,1)S(1)}, bf16[4,64,256]{2,1,0:T(8,128)(2,1)S(1)}, u32[]{:S(2)}, u32[]{:S(2)}) collective-permute-start(bf16[4,64,256]{2,1,0:T(8,128)(2,1)S(1)} %get-tuple-element.52), channel_id=1, source_target_pairs={{0,2},{1,3},{2,0},{3,1},{4,6},{5,7},{6,4},{7,5},{8,10},{9,11},{10,... | collective-permute-start | bytes 393224 | tf_op jit(solution)/shard_map/ppermute | solution.py:314
  91.8 8.1 %collective-permute-start.27 = (bf16[64,512]{1,0:T(8,128)(2,1)S(1)}, bf16[64,512]{1,0:T(8,128)(2,1)S(1)}, u32[]{:S(2)}, u32[]{:S(2)}) collective-permute-start(bf16[64,512]{1,0:T(8,128)(2,1)S(1)} %get-tuple-element.53), channel_id=1, source_target_pairs={{0,8},{4,12},{8,0},{12,4},{16,24},{20,28},{24,16},{28,20},{1,9},{5... | collective-permute-start | bytes 196616 | tf_op jit(solution)/shard_map/ppermute | solution.py:314
  92.5 7.5 %collective-permute-start.29 = (bf16[64,512]{1,0:T(8,128)(2,1)S(1)}, bf16[64,512]{1,0:T(8,128)(2,1)S(1)}, u32[]{:S(2)}, u32[]{:S(2)}) collective-permute-start(bf16[64,512]{1,0:T(8,128)(2,1)S(1)} %get-tuple-element.54), channel_id=1, source_target_pairs={{0,24},{4,28},{8,16},{12,20},{16,8},{20,12},{24,0},{28,4},{1,25},{... | collective-permute-start | bytes 196616 | tf_op jit(solution)/shard_map/ppermute | solution.py:314
  95.4 8.2 %collective-permute-start.28 = (bf16[64,512]{1,0:T(8,128)(2,1)S(1)}, bf16[64,512]{1,0:T(8,128)(2,1)S(1)}, u32[]{:S(2)}, u32[]{:S(2)}) collective-permute-start(bf16[64,512]{1,0:T(8,128)(2,1)S(1)} %get-tuple-element.55), channel_id=1, source_target_pairs={{0,16},{4,20},{8,24},{12,28},{16,0},{20,4},{24,8},{28,12},{1,17},{... | collective-permute-start | bytes 196616 | tf_op jit(solution)/shard_map/ppermute | solution.py:314
  96.0 7.6 %collective-permute-start.35 = (bf16[64,512]{1,0:T(8,128)(2,1)S(1)}, bf16[64,512]{1,0:T(8,128)(2,1)S(1)}, u32[]{:S(2)}, u32[]{:S(2)}) collective-permute-start(bf16[64,512]{1,0:T(8,128)(2,1)S(1)} %get-tuple-element.56), channel_id=1, source_target_pairs={{0,8},{4,12},{8,0},{12,4},{16,24},{20,28},{24,16},{28,20},{1,9},{5... | collective-permute-start | bytes 196616 | tf_op jit(solution)/shard_map/ppermute | solution.py:314
  97.0 6.6 %collective-permute-start.37 = (bf16[64,512]{1,0:T(8,128)(2,1)S(1)}, bf16[64,512]{1,0:T(8,128)(2,1)S(1)}, u32[]{:S(2)}, u32[]{:S(2)}) collective-permute-start(bf16[64,512]{1,0:T(8,128)(2,1)S(1)} %get-tuple-element.57), channel_id=1, source_target_pairs={{0,24},{4,28},{8,16},{12,20},{16,8},{20,12},{24,0},{28,4},{1,25},{... | collective-permute-start | bytes 196616 | tf_op jit(solution)/shard_map/ppermute | solution.py:314
  100.0 5.7 %collective-permute-start.36 = (bf16[64,512]{1,0:T(8,128)(2,1)S(1)}, bf16[64,512]{1,0:T(8,128)(2,1)S(1)}, u32[]{:S(2)}, u32[]{:S(2)}) collective-permute-start(bf16[64,512]{1,0:T(8,128)(2,1)S(1)} %get-tuple-element.58), channel_id=1, source_target_pairs={{0,16},{4,20},{8,24},{12,28},{16,0},{20,4},{24,8},{28,12},{1,17},{... | collective-permute-start | bytes 196616 | tf_op jit(solution)/shard_map/ppermute | solution.py:314
  (9 other events, 121.9 us)

commit v3 on v2

--- a/solution.py
+++ b/solution.py
@@ -137,19 +137,24 @@
     )(meta)
 
 
+def most_rows(tok_rows):
+    return tok_rows // 64 * 48
+
+
 def moe_kernel(n_pieces, *refs):
     picks_hbm, weights_hbm, unit_ref, own_hbm = refs[:4]
     pieces_in = refs[4 : 4 + n_pieces]
     w_gate_hbm, w_up_hbm, w_down_hbm = refs[4 + n_pieces : 7 + n_pieces]
-    out_refs = refs[7 + n_pieces : 11 + n_pieces]
+    out_refs = refs[7 + n_pieces : 13 + n_pieces]
     (picks, weights, w_in, w_down, toks, rows, hidden, mixed, table_sems, tok_sems, in_sems,
-     down_sems) = refs[11 + n_pieces :]
+     down_sems) = refs[13 + n_pieces :]
     n_seq, tok_rows, model_width = toks.shape
     n_z = n_seq // 2
     exp_dev, hid_dev, _ = w_gate_hbm.shape
     width = model_width // 8
     slots_src = exp_dev * SLOTS
     rep = lax.axis_index("rep")
+    split = most_rows(tok_rows)
     tables = [
         pltpu.make_async_copy(picks_hbm, picks, table_sems.at[0]),
         pltpu.make_async_copy(weights_hbm, weights, table_sems.at[1]),
@@ -250,16 +255,16 @@
                 got = contract(weight, rows[j, :, :, cols].reshape(slots_src, 2 * width), 1, 0)
                 mixed[dy, :, cols] = got
                 along[dy] += jnp.sum(got * unit_ref[:, cols], axis=1, keepdims=True)
-        half = tok_rows // 2
         for dy in range(2):
             for dc in range(2):
+                far, near, rest = out_refs[3 * dc : 3 * dc + 3]
                 for n, (color, dx) in enumerate(((0, 1), (0, 0), (1, 0), (1, 1))):
                     cols = pl.ds(group_offset(rep, color, dx, dc, width), width)
                     value = mixed[dy, :, cols] - along[dy] * unit_ref[:, cols]
                     value = value.astype(jnp.bfloat16)
-                    at = slice(n * width, (n + 1) * width)
-                    out_refs[2 * dc][dy, dz, :, at] = value[:half]
-                    out_refs[2 * dc + 1][dy, dz, :, at] = value[half:]
+                    rest[dz, dy, :, n * width : (n + 1) * width] = value[split:]
+                    leaves, kind = (dy, 2 + dx) if color else (dx, dy)
+                    (far if leaves else near)[kind, dz] = value[:split]
         return carry
 
     lax.fori_loop(0, n_z, combine, 0)
@@ -277,9 +282,11 @@
     picks, weights, own = [
         pltpu.with_memory_space_constraint(value, pltpu.HBM) for value in (picks, weights, own)
     ]
+    n_z, split = n_seq // 2, most_rows(tok_rows)
+    most = (4, n_z, split, width)
+    rest = (n_z, 2, tok_rows - split, 4 * width)
     outs = [
-        jax.ShapeDtypeStruct((2, n_seq // 2, tok_rows // 2, 4 * width), jnp.bfloat16)
-        for _ in range(4)
+        jax.ShapeDtypeStruct(shape, jnp.bfloat16) for _ in range(2) for shape in (most, most, rest)
     ]
     return pl.pallas_call(
         functools.partial(moe_kernel, n_pieces),
@@ -348,32 +355,41 @@
     last = [x_two, y_one, x_one, y_two, y_three, x_three]
     pieces = [second, first, from_y, *last, *early, *[swap(piece, "rep", 1) for piece in last]]
 
-    kept_0, kept_1, sent_0, sent_1 = moe_partial(
-        picks, weights, unit_dir, normed, pieces, w_gate, w_up, w_down
-    )
-    summed = jnp.concatenate(
-        [summed_up(kept_0, sent_0, width), summed_up(kept_1, sent_1, width)], axis=0
-    )
-    return (base + summed).astype(jnp.bfloat16)
+    sums = moe_partial(picks, weights, unit_dir, normed, pieces, w_gate, w_up, w_down)
+    return (base + summed_up(sums[:3], sums[3:], width)).astype(jnp.bfloat16)
 
 
 def summed_up(kept, sent, width):
-    n_z = kept.shape[1]
-    arrived = swap(sent, "rep", 1)
-    x_far = swap(added(kept[..., :width], arrived[..., :width]), "rep", 2)
-    y_far = swap(added(kept[1, ..., 2 * width :], arrived[1, ..., 2 * width :]), "seq", 1)
-    mid = slice(width, 2 * width)
-    first_far = swap(added(kept[1, ..., mid], arrived[1, ..., mid], x_far[1]), "seq", 1)
-    end = slice(3 * width, 4 * width)
-    second_far = swap(
-        added(kept[0, ..., end], arrived[0, ..., end], y_far[..., width:]), "rep", 2
-    )
-    first = added(kept[0, ..., mid], arrived[0, ..., mid], x_far[0], first_far)
-    near = slice(2 * width, 3 * width)
-    second = added(kept[0, ..., near], arrived[0, ..., near], y_far[..., :width], second_far)
+    n_z = kept[0].shape[1]
+    others = range(1, n_z)
+    far, near, rest = zip(kept, [swap(piece, "rep", 1) for piece in sent])
+
+    to_x, to_y, rest_kept = lax.optimization_barrier(
+        (added(*[term[:2] for term in far]), added(*[term[2:] for term in far]), rest[0])
+    )
+    by_x, by_y = swap(to_x, "rep", 2), swap(to_y, "seq", 1)
+    rest = added(rest_kept, rest[1])
+    by_z = [swap(rest[d], "seq", 2 * d) for d in others]
+    to_y, to_x, by_z[-1] = lax.optimization_barrier(
+        (
+            added(*[term[1] for term in near], by_x[1]),
+            added(*[term[3] for term in near], by_y[1]),
+            by_z[-1],
+        )
+    )
+    first_far, second_far = swap(to_y, "seq", 1), swap(to_x, "rep", 2)
+    first = added(*[term[0] for term in near], by_x[0], first_far)
+    second = added(*[term[2] for term in near], by_y[0], second_far)
     blocks = jnp.concatenate([first, second], axis=2)
-    terms = [blocks[0]] + [swap(blocks[d], "seq", 2 * d) for d in range(1, n_z)]
-    return sum(term.astype(jnp.float32) for term in terms)
+    most = [blocks[0]] + [swap(blocks[d], "seq", 2 * d) for d in others]
+    most[-1], rest = lax.optimization_barrier((most[-1], rest[0]))
+    rest = added(rest, *by_z)
+    rest = added(rest[0], swap(rest[1], "seq", 1))
+    far = jnp.concatenate([rest[:, :width], rest[:, 3 * width :]], axis=1)
+    rest = [rest[:, width : 3 * width], swap(far, "rep", 2)]
+    return jnp.concatenate(
+        [sum(term.astype(jnp.float32) for term in terms) for terms in (most, rest)], axis=0
+    )
 
 
 def exchanged(tokens, norm_gain, refusal_dir, expert_ids, gate_probs, w_gate, w_up, w_down):

time: 107 us -> 103 us (0.963)
  waiting for transfers between devices: 37.1 us -> 29.2 us
  starting transfers between devices: 39.8 us -> 43.7 us
    ppermute x38 -> x37, waiting for transfers between devices: 37.1 us -> 29.2 us  [swap(): return lax.ppermute(value, axis, [(i, i ^ distance) for i in range(size)])]
    ppermute x38 -> x37, starting transfers between devices: 39.8 us -> 43.7 us  [swap(): return lax.ppermute(value, axis, [(i, i ^ distance) for i in range(size)])]
  transfers between devices with their start and end apart: 38 -> 37, of which waited for: 14 -> 14; matrix products, arithmetic and copies ran while one was open for 2% -> 2% of each run, Pallas kernels for 3% -> 4%
where the time goes in v3:
time: 103 us; the launch traced here: 102 us
  starting transfers between devices  43.7 us (42%)
  waiting for transfers between devices  29.2 us (28%)
  Pallas kernels  26.6 us (26%)
  other arithmetic  1.76 us (2%)
    ppermute x37, starting transfers between devices, swap(): return lax.ppermute(value, axis, [(i, i ^ distance) for i in range(size)])  43.7 us
    ppermute x37, waiting for transfers between devices, swap(): return lax.ppermute(value, axis, [(i, i ^ distance) for i in range(size)])  29.2 us
    pallas_call x1, Pallas kernels, moe_partial(): pl.pallas_call(functools.partial(moe_kernel, n_pieces), out_shape=outs, i...  20.6 us
    pallas_call x1, Pallas kernels, route(): pl.pallas_call(functools.partial(route_kernel, exp_dev), out_shape=[jax.S...  3.59 us
    pallas_call x1, Pallas kernels, norm_and_base(): pl.pallas_call(norm_kernel, out_shape=[jax.ShapeDtypeStruct((tok_rows, mo...  2.45 us
  transfers between devices with their start and end apart: 37, of which 14 were waited for; matrix products, arithmetic and copies ran while one was open for 2% of the time, Pallas kernels for 4%

profile of v3, /device:TPU:0, one launch (start us, length us, event | category | flops | bytes accessed | tf_op | source)
XLA Modules:
  0.0 102.4 jit_solution(10763783556717898580)
XLA Ops:
  0.0 2.5 %shard_map.82 = (bf16[128,2048]{1,0:T(8,128)(2,1)}, bf16[144,256]{1,0:T(8,128)(2,1)}, bf16[128,256]{1,0:T(8,128)(2,1)}, bf16[144,1024]{1,0:T(8,128)(2,1)}, f32[1...) custom-call(bf16[128,2048]{1,0:T(8,128)(2,1)} %tokens_ref.1, f32[1,2048]{1,0:T(1,128)} %bitcast.58, ...), custom_call_target="tpu_custom_call" | custom-call | tf_op jit(solution)/shard_map/pallas_call | solution.py:75
  2.5 5.0 %collective-permute-start.2 = (bf16[144,256]{1,0:T(8,128)(2,1)}, bf16[144,256]{1,0:T(8,128)(2,1)S(1)}, u32[]{:S(2)}, u32[]{:S(2)}) collective-permute-start(bf16[144,256]{1,0:T(8,128)(2,1)} %get-tuple-element.39), channel_id=1, source_target_pairs={{0,24},{4,28},{8,16},{12,20},{16,8},{20,12},{24,0},{28,4},{1,25},{... | collective-permute-start | bytes 221192 | tf_op jit(solution)/shard_map/ppermute | solution.py:321
  8.1 1.7 %collective-permute-start.3 = (bf16[144,1024]{1,0:T(8,128)(2,1)}, bf16[144,1024]{1,0:T(8,128)(2,1)S(1)}, u32[]{:S(2)}, u32[]{:S(2)}) collective-permute-start(bf16[144,1024]{1,0:T(8,128)(2,1)} %get-tuple-element.40), channel_id=1, source_target_pairs={{0,4},{4,0},{8,12},{12,8},{16,20},{20,16},{24,28},{28,24},{1,5},{5... | collective-permute-start | bytes 884744 | tf_op jit(solution)/shard_map/ppermute | solution.py:321
  10.5 3.4 %collective-permute-done.1 = bf16[144,256]{1,0:T(8,128)(2,1)S(1)} collective-permute-done((bf16[144,256]{1,0:T(8,128)(2,1)}, bf16[144,256]{1,0:T(8,128)(2,1)S(1)}, u32[]{:S(2)}, u32[]{:S(2)}) %collective-permute-start.1) | collective-permute-done | bytes 73760 | tf_op jit(solution)/shard_map/ppermute | solution.py:321
  14.0 2.6 %collective-permute-done.3.refs_6_ = bf16[144,1024]{1,0:T(8,128)(2,1)S(1)} collective-permute-done((bf16[144,1024]{1,0:T(8,128)(2,1)}, bf16[144,1024]{1,0:T(8,128)(2,1)S(1)}, u32[]{:S(2)}, u32[]{:S(2)}) %collective-permute-start.3) | collective-permute-done | bytes 294944 | tf_op jit(solution)/shard_map/ppermute | solution.py:321
  16.5 3.5 %collective-permute-start.6 = (bf16[128,256]{1,0:T(8,128)(2,1)}, bf16[128,256]{1,0:T(8,128)(2,1)S(1)}, u32[]{:S(2)}, u32[]{:S(2)}) collective-permute-start(bf16[128,256]{1,0:T(8,128)(2,1)} %get-tuple-element.41), channel_id=1, source_target_pairs={{0,24},{4,28},{8,16},{12,20},{16,8},{20,12},{24,0},{28,4},{1,25},{... | collective-permute-start | bytes 196616 | tf_op jit(solution)/shard_map/ppermute | solution.py:321
  20.0 0.9 collective-permute-start.4
  21.0 1.6 %collective-permute-start.8 = (bf16[3,144,256]{2,1,0:T(8,128)(2,1)S(1)}, bf16[3,144,256]{2,1,0:T(8,128)(2,1)S(1)}, u32[]{:S(2)}, u32[]{:S(2)}) collective-permute-start(bf16[3,144,256]{2,1,0:T(8,128)(2,1)S(1)} %pad_maximum_fusion.refs_4_), channel_id=1, source_target_pairs={{0,4},{4,0},{8,12},{12,8},{16,20},{20,16},{24,28},{28,24},{1,5},{5... | collective-permute-start | bytes 663560 | tf_op jit(solution)/shard_map/ppermute | solution.py:321
  22.5 1.5 %collective-permute-start.9 = (bf16[3,128,256]{2,1,0:T(8,128)(2,1)S(1)}, bf16[3,128,256]{2,1,0:T(8,128)(2,1)S(1)}, u32[]{:S(2)}, u32[]{:S(2)}) collective-permute-start(bf16[3,128,256]{2,1,0:T(8,128)(2,1)S(1)} %slice.118), channel_id=1, source_target_pairs={{0,2},{1,3},{2,0},{3,1},{4,6},{5,7},{6,4},{7,5},{8,10},{9,11},{10,... | collective-permute-start | bytes 589832 | tf_op jit(solution)/shard_map/ppermute | solution.py:321
  24.0 1.3 %collective-permute-done.5 = bf16[128,256]{1,0:T(8,128)(2,1)S(1)} collective-permute-done((bf16[128,256]{1,0:T(8,128)(2,1)}, bf16[128,256]{1,0:T(8,128)(2,1)S(1)}, u32[]{:S(2)}, u32[]{:S(2)}) %collective-permute-start.5) | collective-permute-done | bytes 65568 | tf_op jit(solution)/shard_map/ppermute | solution.py:321
  25.5 1.6 %collective-permute-start.10 = (bf16[3,128,256]{2,1,0:T(8,128)(2,1)S(1)}, bf16[3,128,256]{2,1,0:T(8,128)(2,1)S(1)}, u32[]{:S(2)}, u32[]{:S(2)}) collective-permute-start(bf16[3,128,256]{2,1,0:T(8,128)(2,1)S(1)} %pad_maximum_fusion.1.refs_5_), channel_id=1, source_target_pairs={{0,2},{1,3},{2,0},{3,1},{4,6},{5,7},{6,4},{7,5},{8,10},{9,11},{10,... | collective-permute-start | bytes 589832 | tf_op jit(solution)/shard_map/ppermute | solution.py:321
  27.1 1.5 %collective-permute-start.7 = (bf16[3,128,256]{2,1,0:T(8,128)(2,1)S(1)}, bf16[3,128,256]{2,1,0:T(8,128)(2,1)S(1)}, u32[]{:S(2)}, u32[]{:S(2)}) collective-permute-start(bf16[3,128,256]{2,1,0:T(8,128)(2,1)S(1)} %pad_maximum_fusion.1.refs_5_), channel_id=1, source_target_pairs={{0,4},{4,0},{8,12},{12,8},{16,20},{20,16},{24,28},{28,24},{1,5},{5... | collective-permute-start | bytes 589832 | tf_op jit(solution)/shard_map/ppermute | solution.py:321
  29.8 3.6 %shard_map.83 = (bf16[8,256,128]{2,1,0:T(8,128)(2,1)}, bf16[8,128,256]{2,1,0:T(8,128)(2,1)}) custom-call(bf16[8,16,128]{2,1,0:T(8,128)(2,1)} %copy-done.2), custom_call_target="tpu_custom_call" | custom-call | flops 4000000000 | bytes 2097152 | tf_op jit(solution)/shard_map/pallas_call | solution.py:125
  33.4 1.4 %collective-permute-done.7.refs_10_ = bf16[3,128,256]{2,1,0:T(8,128)(2,1)S(1)} collective-permute-done((bf16[3,128,256]{2,1,0:T(8,128)(2,1)S(1)}, bf16[3,128,256]{2,1,0:T(8,128)(2,1)S(1)}, u32[]{:S(2)}, u32[]{:S(2)}) %collective-permute-start.7) | collective-permute-done | bytes 196640 | tf_op jit(solution)/shard_map/ppermute | solution.py:321
  35.3 2.9 %collective-permute-done.11.refs_11_ = bf16[3,128,256]{2,1,0:T(8,128)(2,1)S(1)} collective-permute-done((bf16[3,128,256]{2,1,0:T(8,128)(2,1)S(1)}, bf16[3,128,256]{2,1,0:T(8,128)(2,1)S(1)}, u32[]{:S(2)}, u32[]{:S(2)}) %collective-permute-start.11) | collective-permute-done | bytes 196640 | tf_op jit(solution)/shard_map/ppermute | solution.py:321
  39.3 2.8 %collective-permute-done.12.refs_12_ = bf16[3,128,256]{2,1,0:T(8,128)(2,1)S(1)} collective-permute-done((bf16[3,128,256]{2,1,0:T(8,128)(2,1)S(1)}, bf16[3,128,256]{2,1,0:T(8,128)(2,1)S(1)}, u32[]{:S(2)}, u32[]{:S(2)}) %collective-permute-start.12) | collective-permute-done | bytes 196640 | tf_op jit(solution)/shard_map/ppermute | solution.py:321
  42.2 1.4 %collective-permute-done.21.refs_21_ = bf16[3,128,256]{2,1,0:T(8,128)(2,1)S(1)} collective-permute-done((bf16[3,128,256]{2,1,0:T(8,128)(2,1)S(1)}, bf16[3,128,256]{2,1,0:T(8,128)(2,1)S(1)}, u32[]{:S(2)}, u32[]{:S(2)}) %collective-permute-start.21) | collective-permute-done | bytes 196640 | tf_op jit(solution)/shard_map/ppermute | solution.py:321
  43.6 20.6 %shard_map.84 = (bf16[4,4,96,256]{3,2,1,0:T(8,128)(2,1)S(1)}, bf16[4,4,96,256]{3,2,1,0:T(8,128)(2,1)S(1)}, bf16[4,2,32,1024]{3,2,1,0:T(8,128)(2,1)S(1)}, bf16[4,...) custom-call(bf16[8,256,128]{2,1,0:T(8,128)(2,1)} %get-tuple-element.47.refs_0, ...), custom_call_target="tpu_custom_call" | custom-call | flops 4831838208 | bytes 46137344 | tf_op jit(solution)/shard_map/pallas_call | solution.py:291
  64.9 1.6 %collective-permute-done.23 = bf16[4,4,96,256]{3,2,1,0:T(8,128)(2,1)S(1)} collective-permute-done((bf16[4,4,96,256]{3,2,1,0:T(8,128)(2,1)S(1)}, bf16[4,4,96,256]{3,2,1,0:T(8,128)(2,1)S(1)}, u32[]{:S(2)}, u32[]{:S(2)}) %collective-permute-start.23) | collective-permute-done | bytes 786464 | tf_op jit(solution)/shard_map/ppermute | solution.py:321
  67.4 1.5 %collective-permute-start.25 = (bf16[2,4,96,256]{3,2,1,0:T(8,128)(2,1)S(1)}, bf16[2,4,96,256]{3,2,1,0:T(8,128)(2,1)S(1)}, u32[]{:S(2)}, u32[]{:S(2)}) collective-permute-start(bf16[2,4,96,256]{3,2,1,0:T(8,128)(2,1)S(1)} %get-tuple-element.61), channel_id=1, source_target_pairs={{0,4},{4,0},{8,12},{12,8},{16,20},{20,16},{24,28},{28,24},{1,5},{5... | collective-permute-start | bytes 1179656 | tf_op jit(solution)/shard_map/ppermute | solution.py:321
  69.2 4.1 %collective-permute-start.27 = (bf16[2,32,1024]{2,1,0:T(8,128)(2,1)S(1)}, bf16[2,32,1024]{2,1,0:T(8,128)(2,1)S(1)}, u32[]{:S(2)}, u32[]{:S(2)}) collective-permute-start(bf16[2,32,1024]{2,1,0:T(8,128)(2,1)S(1)} %get-tuple-element.78), channel_id=1, source_target_pairs={{0,24},{4,28},{8,16},{12,20},{16,8},{20,12},{24,0},{28,4},{1,25},{... | collective-permute-start | bytes 393224 | tf_op jit(solution)/shard_map/ppermute | solution.py:321
  73.2 4.8 %collective-permute-done.24 = bf16[2,4,96,256]{3,2,1,0:T(8,128)(2,1)S(1)} collective-permute-done((bf16[2,4,96,256]{3,2,1,0:T(8,128)(2,1)S(1)}, bf16[2,4,96,256]{3,2,1,0:T(8,128)(2,1)S(1)}, u32[]{:S(2)}, u32[]{:S(2)}) %collective-permute-start.24) | collective-permute-done | bytes 393248 | tf_op jit(solution)/shard_map/ppermute | solution.py:321
  78.5 1.6 %collective-permute-start.28 = (bf16[4,96,256]{2,1,0:T(8,128)(2,1)S(1)}, bf16[4,96,256]{2,1,0:T(8,128)(2,1)S(1)}, u32[]{:S(2)}, u32[]{:S(2)}) collective-permute-start(bf16[4,96,256]{2,1,0:T(8,128)(2,1)S(1)} %get-tuple-element.64), channel_id=1, source_target_pairs={{0,4},{4,0},{8,12},{12,8},{16,20},{20,16},{24,28},{28,24},{1,5},{5... | collective-permute-start | bytes 589832 | tf_op jit(solution)/shard_map/ppermute | solution.py:321
  80.0 1.5 %collective-permute-start.29 = (bf16[4,96,256]{2,1,0:T(8,128)(2,1)S(1)}, bf16[4,96,256]{2,1,0:T(8,128)(2,1)S(1)}, u32[]{:S(2)}, u32[]{:S(2)}) collective-permute-start(bf16[4,96,256]{2,1,0:T(8,128)(2,1)S(1)} %get-tuple-element.65), channel_id=1, source_target_pairs={{0,2},{1,3},{2,0},{3,1},{4,6},{5,7},{6,4},{7,5},{8,10},{9,11},{10,... | collective-permute-start | bytes 589832 | tf_op jit(solution)/shard_map/ppermute | solution.py:321
  81.5 2.0 %collective-permute-start.34 = (bf16[2,32,1024]{2,1,0:T(8,128)(2,1)S(1)}, bf16[2,32,1024]{2,1,0:T(8,128)(2,1)S(1)}, u32[]{:S(2)}, u32[]{:S(2)}) collective-permute-start(bf16[2,32,1024]{2,1,0:T(8,128)(2,1)S(1)} %get-tuple-element.76), channel_id=1, source_target_pairs={{0,16},{4,20},{8,24},{12,28},{16,0},{20,4},{24,8},{28,12},{1,17},{... | collective-permute-start | bytes 393224 | tf_op jit(solution)/shard_map/ppermute | solution.py:321
  83.5 1.4 %collective-permute-start.33 = (bf16[2,32,1024]{2,1,0:T(8,128)(2,1)S(1)}, bf16[2,32,1024]{2,1,0:T(8,128)(2,1)S(1)}, u32[]{:S(2)}, u32[]{:S(2)}) collective-permute-start(bf16[2,32,1024]{2,1,0:T(8,128)(2,1)S(1)} %get-tuple-element.77), channel_id=1, source_target_pairs={{0,8},{4,12},{8,0},{12,4},{16,24},{20,28},{24,16},{28,20},{1,9},{5... | collective-permute-start | bytes 393224 | tf_op jit(solution)/shard_map/ppermute | solution.py:321
  86.0 4.1 %collective-permute-start.32 = (bf16[96,512]{1,0:T(8,128)(2,1)S(1)}, bf16[96,512]{1,0:T(8,128)(2,1)S(1)}, u32[]{:S(2)}, u32[]{:S(2)}) collective-permute-start(bf16[96,512]{1,0:T(8,128)(2,1)S(1)} %get-tuple-element.80), channel_id=1, source_target_pairs={{0,24},{4,28},{8,16},{12,20},{16,8},{20,12},{24,0},{28,4},{1,25},{... | collective-permute-start | bytes 294920 | tf_op jit(solution)/shard_map/ppermute | solution.py:321
  90.0 2.7 %collective-permute-done.32 = bf16[96,512]{1,0:T(8,128)(2,1)S(1)} collective-permute-done((bf16[96,512]{1,0:T(8,128)(2,1)S(1)}, bf16[96,512]{1,0:T(8,128)(2,1)S(1)}, u32[]{:S(2)}, u32[]{:S(2)}) %collective-permute-start.32) | collective-permute-done | bytes 98336 | tf_op jit(solution)/shard_map/ppermute | solution.py:321
  93.3 1.2 %collective-permute-start.30 = (bf16[96,512]{1,0:T(8,128)(2,1)S(1)}, bf16[96,512]{1,0:T(8,128)(2,1)S(1)}, u32[]{:S(2)}, u32[]{:S(2)}) collective-permute-start(bf16[96,512]{1,0:T(8,128)(2,1)S(1)} %get-tuple-element.79), channel_id=1, source_target_pairs={{0,8},{4,12},{8,0},{12,4},{16,24},{20,28},{24,16},{28,20},{1,9},{5... | collective-permute-start | bytes 294920 | tf_op jit(solution)/shard_map/ppermute | solution.py:321
  94.5 3.1 %collective-permute-start.31 = (bf16[96,512]{1,0:T(8,128)(2,1)S(1)}, bf16[96,512]{1,0:T(8,128)(2,1)S(1)}, u32[]{:S(2)}, u32[]{:S(2)}) collective-permute-start(bf16[96,512]{1,0:T(8,128)(2,1)S(1)} %get-tuple-element.81), channel_id=1, source_target_pairs={{0,16},{4,20},{8,24},{12,28},{16,0},{20,4},{24,8},{28,12},{1,17},{... | collective-permute-start | bytes 294920 | tf_op jit(solution)/shard_map/ppermute | solution.py:321
  97.7 0.8 collective-permute-start.36
  98.5 2.8 %collective-permute-done.31 = bf16[96,512]{1,0:T(8,128)(2,1)S(1)} collective-permute-done((bf16[96,512]{1,0:T(8,128)(2,1)S(1)}, bf16[96,512]{1,0:T(8,128)(2,1)S(1)}, u32[]{:S(2)}, u32[]{:S(2)}) %collective-permute-start.31) | collective-permute-done | bytes 98336 | tf_op jit(solution)/shard_map/ppermute | solution.py:321
  (76 shorter events, 9.2 us)
Async XLA Ops:
  2.5 8.0 %collective-permute-start.2 = (bf16[144,256]{1,0:T(8,128)(2,1)}, bf16[144,256]{1,0:T(8,128)(2,1)S(1)}, u32[]{:S(2)}, u32[]{:S(2)}) collective-permute-start(bf16[144,256]{1,0:T(8,128)(2,1)} %get-tuple-element.39), channel_id=1, source_target_pairs={{0,24},{4,28},{8,16},{12,20},{16,8},{20,12},{24,0},{28,4},{1,25},{... | collective-permute-start | bytes 221192 | tf_op jit(solution)/shard_map/ppermute | solution.py:321
  7.5 6.4 %collective-permute-start.1 = (bf16[144,256]{1,0:T(8,128)(2,1)}, bf16[144,256]{1,0:T(8,128)(2,1)S(1)}, u32[]{:S(2)}, u32[]{:S(2)}) collective-permute-start(bf16[144,256]{1,0:T(8,128)(2,1)} %get-tuple-element.39), channel_id=1, source_target_pairs={{0,16},{4,20},{8,24},{12,28},{16,0},{20,4},{24,8},{28,12},{1,17},{... | collective-permute-start | bytes 221192 | tf_op jit(solution)/shard_map/ppermute | solution.py:321
  7.5 6.4 %collective-permute-start = (bf16[144,256]{1,0:T(8,128)(2,1)}, bf16[144,256]{1,0:T(8,128)(2,1)S(1)}, u32[]{:S(2)}, u32[]{:S(2)}) collective-permute-start(bf16[144,256]{1,0:T(8,128)(2,1)} %get-tuple-element.39), channel_id=1, source_target_pairs={{0,8},{4,12},{8,0},{12,4},{16,24},{20,28},{24,16},{28,20},{1,9},{5... | collective-permute-start | bytes 221192 | tf_op jit(solution)/shard_map/ppermute | solution.py:321
  8.1 8.4 %collective-permute-start.3 = (bf16[144,1024]{1,0:T(8,128)(2,1)}, bf16[144,1024]{1,0:T(8,128)(2,1)S(1)}, u32[]{:S(2)}, u32[]{:S(2)}) collective-permute-start(bf16[144,1024]{1,0:T(8,128)(2,1)} %get-tuple-element.40), channel_id=1, source_target_pairs={{0,4},{4,0},{8,12},{12,8},{16,20},{20,16},{24,28},{28,24},{1,5},{5... | collective-permute-start | bytes 884744 | tf_op jit(solution)/shard_map/ppermute | solution.py:321
  16.5 7.5 %collective-permute-start.6 = (bf16[128,256]{1,0:T(8,128)(2,1)}, bf16[128,256]{1,0:T(8,128)(2,1)S(1)}, u32[]{:S(2)}, u32[]{:S(2)}) collective-permute-start(bf16[128,256]{1,0:T(8,128)(2,1)} %get-tuple-element.41), channel_id=1, source_target_pairs={{0,24},{4,28},{8,16},{12,20},{16,8},{20,12},{24,0},{28,4},{1,25},{... | collective-permute-start | bytes 196616 | tf_op jit(solution)/shard_map/ppermute | solution.py:321
  20.0 5.4 %collective-permute-start.5 = (bf16[128,256]{1,0:T(8,128)(2,1)}, bf16[128,256]{1,0:T(8,128)(2,1)S(1)}, u32[]{:S(2)}, u32[]{:S(2)}) collective-permute-start(bf16[128,256]{1,0:T(8,128)(2,1)} %get-tuple-element.41), channel_id=1, source_target_pairs={{0,16},{4,20},{8,24},{12,28},{16,0},{20,4},{24,8},{28,12},{1,17},{... | collective-permute-start | bytes 196616 | tf_op jit(solution)/shard_map/ppermute | solution.py:321
  20.0 5.4 %collective-permute-start.4 = (bf16[128,256]{1,0:T(8,128)(2,1)}, bf16[128,256]{1,0:T(8,128)(2,1)S(1)}, u32[]{:S(2)}, u32[]{:S(2)}) collective-permute-start(bf16[128,256]{1,0:T(8,128)(2,1)} %get-tuple-element.41), channel_id=1, source_target_pairs={{0,8},{4,12},{8,0},{12,4},{16,24},{20,28},{24,16},{28,20},{1,9},{5... | collective-permute-start | bytes 196616 | tf_op jit(solution)/shard_map/ppermute | solution.py:321
  21.0 8.1 %collective-permute-start.8 = (bf16[3,144,256]{2,1,0:T(8,128)(2,1)S(1)}, bf16[3,144,256]{2,1,0:T(8,128)(2,1)S(1)}, u32[]{:S(2)}, u32[]{:S(2)}) collective-permute-start(bf16[3,144,256]{2,1,0:T(8,128)(2,1)S(1)} %pad_maximum_fusion.refs_4_), channel_id=1, source_target_pairs={{0,4},{4,0},{8,12},{12,8},{16,20},{20,16},{24,28},{28,24},{1,5},{5... | collective-permute-start | bytes 663560 | tf_op jit(solution)/shard_map/ppermute | solution.py:321
  22.5 6.0 %collective-permute-start.9 = (bf16[3,128,256]{2,1,0:T(8,128)(2,1)S(1)}, bf16[3,128,256]{2,1,0:T(8,128)(2,1)S(1)}, u32[]{:S(2)}, u32[]{:S(2)}) collective-permute-start(bf16[3,128,256]{2,1,0:T(8,128)(2,1)S(1)} %slice.118), channel_id=1, source_target_pairs={{0,2},{1,3},{2,0},{3,1},{4,6},{5,7},{6,4},{7,5},{8,10},{9,11},{10,... | collective-permute-start | bytes 589832 | tf_op jit(solution)/shard_map/ppermute | solution.py:321
  25.4 3.7 %collective-permute-start.14 = (bf16[3,128,256]{2,1,0:T(8,128)(2,1)S(1)}, bf16[3,128,256]{2,1,0:T(8,128)(2,1)S(1)}, u32[]{:S(2)}, u32[]{:S(2)}) collective-permute-start(bf16[3,128,256]{2,1,0:T(8,128)(2,1)S(1)} %pad_maximum_fusion.1.refs_5_), channel_id=1, source_target_pairs={{0,1},{1,0},{2,3},{3,2},{4,5},{5,4},{6,7},{7,6},{8,9},{9,8},{10,11... | collective-permute-start | bytes 589832 | tf_op jit(solution)/shard_map/ppermute | solution.py:321
  25.5 9.3 %collective-permute-start.10 = (bf16[3,128,256]{2,1,0:T(8,128)(2,1)S(1)}, bf16[3,128,256]{2,1,0:T(8,128)(2,1)S(1)}, u32[]{:S(2)}, u32[]{:S(2)}) collective-permute-start(bf16[3,128,256]{2,1,0:T(8,128)(2,1)S(1)} %pad_maximum_fusion.1.refs_5_), channel_id=1, source_target_pairs={{0,2},{1,3},{2,0},{3,1},{4,6},{5,7},{6,4},{7,5},{8,10},{9,11},{10,... | collective-permute-start | bytes 589832 | tf_op jit(solution)/shard_map/ppermute | solution.py:321
  27.1 7.7 %collective-permute-start.7 = (bf16[3,128,256]{2,1,0:T(8,128)(2,1)S(1)}, bf16[3,128,256]{2,1,0:T(8,128)(2,1)S(1)}, u32[]{:S(2)}, u32[]{:S(2)}) collective-permute-start(bf16[3,128,256]{2,1,0:T(8,128)(2,1)S(1)} %pad_maximum_fusion.1.refs_5_), channel_id=1, source_target_pairs={{0,4},{4,0},{8,12},{12,8},{16,20},{20,16},{24,28},{28,24},{1,5},{5... | collective-permute-start | bytes 589832 | tf_op jit(solution)/shard_map/ppermute | solution.py:321
  28.6 9.7 %collective-permute-start.11 = (bf16[3,128,256]{2,1,0:T(8,128)(2,1)S(1)}, bf16[3,128,256]{2,1,0:T(8,128)(2,1)S(1)}, u32[]{:S(2)}, u32[]{:S(2)}) collective-permute-start(bf16[3,128,256]{2,1,0:T(8,128)(2,1)S(1)} %collective-permute-done.9.refs_7_), channel_id=1, source_target_pairs={{0,4},{4,0},{8,12},{12,8},{16,20},{20,16},{24,28},{28,24},{1,5},{5... | collective-permute-start | bytes 589832 | tf_op jit(solution)/shard_map/ppermute | solution.py:321
  29.1 9.7 %collective-permute-start.13 = (bf16[3,144,256]{2,1,0:T(8,128)(2,1)S(1)}, bf16[3,144,256]{2,1,0:T(8,128)(2,1)S(1)}, u32[]{:S(2)}, u32[]{:S(2)}) collective-permute-start(bf16[3,144,256]{2,1,0:T(8,128)(2,1)S(1)} %pad_maximum_fusion.refs_4_), channel_id=1, source_target_pairs={{0,1},{1,0},{2,3},{3,2},{4,5},{5,4},{6,7},{7,6},{8,9},{9,8},{10,11... | collective-permute-start | bytes 663560 | tf_op jit(solution)/shard_map/ppermute | solution.py:321
  29.2 9.7 %collective-permute-start.17 = (bf16[3,144,256]{2,1,0:T(8,128)(2,1)S(1)}, bf16[3,144,256]{2,1,0:T(8,128)(2,1)S(1)}, u32[]{:S(2)}, u32[]{:S(2)}) collective-permute-start(bf16[3,144,256]{2,1,0:T(8,128)(2,1)S(1)} %collective-permute-done.8.refs_8_), channel_id=1, source_target_pairs={{0,1},{1,0},{2,3},{3,2},{4,5},{5,4},{6,7},{7,6},{8,9},{9,8},{10,11... | collective-permute-start | bytes 663560 | tf_op jit(solution)/shard_map/ppermute | solution.py:321
  34.8 7.3 %collective-permute-start.12 = (bf16[3,128,256]{2,1,0:T(8,128)(2,1)S(1)}, bf16[3,128,256]{2,1,0:T(8,128)(2,1)S(1)}, u32[]{:S(2)}, u32[]{:S(2)}) collective-permute-start(bf16[3,128,256]{2,1,0:T(8,128)(2,1)S(1)} %collective-permute-done.7.refs_10_), channel_id=1, source_target_pairs={{0,2},{1,3},{2,0},{3,1},{4,6},{5,7},{6,4},{7,5},{8,10},{9,11},{10,... | collective-permute-start | bytes 589832 | tf_op jit(solution)/shard_map/ppermute | solution.py:321
  38.2 3.9 %collective-permute-start.15 = (bf16[144,1024]{1,0:T(8,128)(2,1)S(1)}, bf16[144,1024]{1,0:T(8,128)(2,1)S(1)}, u32[]{:S(2)}, u32[]{:S(2)}) collective-permute-start(bf16[144,1024]{1,0:T(8,128)(2,1)S(1)} %collective-permute-done.3.refs_6_), channel_id=1, source_target_pairs={{0,1},{1,0},{2,3},{3,2},{4,5},{5,4},{6,7},{7,6},{8,9},{9,8},{10,11... | collective-permute-start | bytes 884744 | tf_op jit(solution)/shard_map/ppermute | solution.py:321
  38.3 3.9 %collective-permute-start.19 = (bf16[3,128,256]{2,1,0:T(8,128)(2,1)S(1)}, bf16[3,128,256]{2,1,0:T(8,128)(2,1)S(1)}, u32[]{:S(2)}, u32[]{:S(2)}) collective-permute-start(bf16[3,128,256]{2,1,0:T(8,128)(2,1)S(1)} %collective-permute-done.7.refs_10_), channel_id=1, source_target_pairs={{0,1},{1,0},{2,3},{3,2},{4,5},{5,4},{6,7},{7,6},{8,9},{9,8},{10,11... | collective-permute-start | bytes 589832 | tf_op jit(solution)/shard_map/ppermute | solution.py:321
  64.4 4.5 %collective-permute-start.26 = (bf16[4,2,32,1024]{3,2,1,0:T(8,128)(2,1)S(1)}, bf16[4,2,32,1024]{3,2,1,0:T(8,128)(2,1)S(1)}, u32[]{:S(2)}, u32[]{:S(2)}) collective-permute-start(bf16[4,2,32,1024]{3,2,1,0:T(8,128)(2,1)S(1)} %get-tuple-element.63), channel_id=1, source_target_pairs={{0,1},{1,0},{2,3},{3,2},{4,5},{5,4},{6,7},{7,6},{8,9},{9,8},{10,11... | collective-permute-start | bytes 1572872 | tf_op jit(solution)/shard_map/ppermute | solution.py:321
  64.8 8.5 %collective-permute-start.22 = (bf16[4,4,96,256]{3,2,1,0:T(8,128)(2,1)S(1)}, bf16[4,4,96,256]{3,2,1,0:T(8,128)(2,1)S(1)}, u32[]{:S(2)}, u32[]{:S(2)}) collective-permute-start(bf16[4,4,96,256]{3,2,1,0:T(8,128)(2,1)S(1)} %get-tuple-element.56), channel_id=1, source_target_pairs={{0,1},{1,0},{2,3},{3,2},{4,5},{5,4},{6,7},{7,6},{8,9},{9,8},{10,11... | collective-permute-start | bytes 2359304 | tf_op jit(solution)/shard_map/ppermute | solution.py:321
  66.8 11.2 %collective-permute-start.24 = (bf16[2,4,96,256]{3,2,1,0:T(8,128)(2,1)S(1)}, bf16[2,4,96,256]{3,2,1,0:T(8,128)(2,1)S(1)}, u32[]{:S(2)}, u32[]{:S(2)}) collective-permute-start(bf16[2,4,96,256]{3,2,1,0:T(8,128)(2,1)S(1)} %get-tuple-element.60), channel_id=1, source_target_pairs={{0,2},{1,3},{2,0},{3,1},{4,6},{5,7},{6,4},{7,5},{8,10},{9,11},{10,... | collective-permute-start | bytes 1179656 | tf_op jit(solution)/shard_map/ppermute | solution.py:321
  67.4 10.9 %collective-permute-start.25 = (bf16[2,4,96,256]{3,2,1,0:T(8,128)(2,1)S(1)}, bf16[2,4,96,256]{3,2,1,0:T(8,128)(2,1)S(1)}, u32[]{:S(2)}, u32[]{:S(2)}) collective-permute-start(bf16[2,4,96,256]{3,2,1,0:T(8,128)(2,1)S(1)} %get-tuple-element.61), channel_id=1, source_target_pairs={{0,4},{4,0},{8,12},{12,8},{16,20},{20,16},{24,28},{28,24},{1,5},{5... | collective-permute-start | bytes 1179656 | tf_op jit(solution)/shard_map/ppermute | solution.py:321
  69.2 9.3 %collective-permute-start.27 = (bf16[2,32,1024]{2,1,0:T(8,128)(2,1)S(1)}, bf16[2,32,1024]{2,1,0:T(8,128)(2,1)S(1)}, u32[]{:S(2)}, u32[]{:S(2)}) collective-permute-start(bf16[2,32,1024]{2,1,0:T(8,128)(2,1)S(1)} %get-tuple-element.78), channel_id=1, source_target_pairs={{0,24},{4,28},{8,16},{12,20},{16,8},{20,12},{24,0},{28,4},{1,25},{... | collective-permute-start | bytes 393224 | tf_op jit(solution)/shard_map/ppermute | solution.py:321
  78.5 6.5 %collective-permute-start.28 = (bf16[4,96,256]{2,1,0:T(8,128)(2,1)S(1)}, bf16[4,96,256]{2,1,0:T(8,128)(2,1)S(1)}, u32[]{:S(2)}, u32[]{:S(2)}) collective-permute-start(bf16[4,96,256]{2,1,0:T(8,128)(2,1)S(1)} %get-tuple-element.64), channel_id=1, source_target_pairs={{0,4},{4,0},{8,12},{12,8},{16,20},{20,16},{24,28},{28,24},{1,5},{5... | collective-permute-start | bytes 589832 | tf_op jit(solution)/shard_map/ppermute | solution.py:321
  80.0 5.7 %collective-permute-start.29 = (bf16[4,96,256]{2,1,0:T(8,128)(2,1)S(1)}, bf16[4,96,256]{2,1,0:T(8,128)(2,1)S(1)}, u32[]{:S(2)}, u32[]{:S(2)}) collective-permute-start(bf16[4,96,256]{2,1,0:T(8,128)(2,1)S(1)} %get-tuple-element.65), channel_id=1, source_target_pairs={{0,2},{1,3},{2,0},{3,1},{4,6},{5,7},{6,4},{7,5},{8,10},{9,11},{10,... | collective-permute-start | bytes 589832 | tf_op jit(solution)/shard_map/ppermute | solution.py:321
  81.5 11.2 %collective-permute-start.34 = (bf16[2,32,1024]{2,1,0:T(8,128)(2,1)S(1)}, bf16[2,32,1024]{2,1,0:T(8,128)(2,1)S(1)}, u32[]{:S(2)}, u32[]{:S(2)}) collective-permute-start(bf16[2,32,1024]{2,1,0:T(8,128)(2,1)S(1)} %get-tuple-element.76), channel_id=1, source_target_pairs={{0,16},{4,20},{8,24},{12,28},{16,0},{20,4},{24,8},{28,12},{1,17},{... | collective-permute-start | bytes 393224 | tf_op jit(solution)/shard_map/ppermute | solution.py:321
  83.5 9.2 %collective-permute-start.33 = (bf16[2,32,1024]{2,1,0:T(8,128)(2,1)S(1)}, bf16[2,32,1024]{2,1,0:T(8,128)(2,1)S(1)}, u32[]{:S(2)}, u32[]{:S(2)}) collective-permute-start(bf16[2,32,1024]{2,1,0:T(8,128)(2,1)S(1)} %get-tuple-element.77), channel_id=1, source_target_pairs={{0,8},{4,12},{8,0},{12,4},{16,24},{20,28},{24,16},{28,20},{1,9},{5... | collective-permute-start | bytes 393224 | tf_op jit(solution)/shard_map/ppermute | solution.py:321
  86.0 6.8 %collective-permute-start.32 = (bf16[96,512]{1,0:T(8,128)(2,1)S(1)}, bf16[96,512]{1,0:T(8,128)(2,1)S(1)}, u32[]{:S(2)}, u32[]{:S(2)}) collective-permute-start(bf16[96,512]{1,0:T(8,128)(2,1)S(1)} %get-tuple-element.80), channel_id=1, source_target_pairs={{0,24},{4,28},{8,16},{12,20},{16,8},{20,12},{24,0},{28,4},{1,25},{... | collective-permute-start | bytes 294920 | tf_op jit(solution)/shard_map/ppermute | solution.py:321
  92.8 4.8 %collective-permute-start.35 = (bf16[32,1024]{1,0:T(8,128)(2,1)S(1)}, bf16[32,1024]{1,0:T(8,128)(2,1)S(1)}, u32[]{:S(2)}, u32[]{:S(2)}) collective-permute-start(bf16[32,1024]{1,0:T(8,128)(2,1)S(1)} %slice_bitcast_fusion.4), channel_id=1, source_target_pairs={{0,4},{4,0},{8,12},{12,8},{16,20},{20,16},{24,28},{28,24},{1,5},{5... | collective-permute-start | bytes 196616 | tf_op jit(solution)/shard_map/ppermute | solution.py:321
  93.3 5.1 %collective-permute-start.30 = (bf16[96,512]{1,0:T(8,128)(2,1)S(1)}, bf16[96,512]{1,0:T(8,128)(2,1)S(1)}, u32[]{:S(2)}, u32[]{:S(2)}) collective-permute-start(bf16[96,512]{1,0:T(8,128)(2,1)S(1)} %get-tuple-element.79), channel_id=1, source_target_pairs={{0,8},{4,12},{8,0},{12,4},{16,24},{20,28},{24,16},{28,20},{1,9},{5... | collective-permute-start | bytes 294920 | tf_op jit(solution)/shard_map/ppermute | solution.py:321
  94.5 6.7 %collective-permute-start.31 = (bf16[96,512]{1,0:T(8,128)(2,1)S(1)}, bf16[96,512]{1,0:T(8,128)(2,1)S(1)}, u32[]{:S(2)}, u32[]{:S(2)}) collective-permute-start(bf16[96,512]{1,0:T(8,128)(2,1)S(1)} %get-tuple-element.81), channel_id=1, source_target_pairs={{0,16},{4,20},{8,24},{12,28},{16,0},{20,4},{24,8},{28,12},{1,17},{... | collective-permute-start | bytes 294920 | tf_op jit(solution)/shard_map/ppermute | solution.py:321
  97.7 4.0 %collective-permute-start.36 = (bf16[32,512]{1,0:T(8,128)(2,1)S(1)}, bf16[32,512]{1,0:T(8,128)(2,1)S(1)}, u32[]{:S(2)}, u32[]{:S(2)}) collective-permute-start(bf16[32,512]{1,0:T(8,128)(2,1)S(1)} %pad_maximum_fusion.3), channel_id=1, source_target_pairs={{0,2},{1,3},{2,0},{3,1},{4,6},{5,7},{6,4},{7,5},{8,10},{9,11},{10,... | collective-permute-start | bytes 98312 | tf_op jit(solution)/shard_map/ppermute | solution.py:321
  (8 other events, 113.7 us)

commit v4 on v3

--- a/solution.py
+++ b/solution.py
@@ -28,10 +28,10 @@
     return [
         [(j, [(1, 0)]) for j in near],
         [(j, [(0, 0)]) for j in near],
-        [(1, [(0, 0), (1, 0), (0, 1), (1, 1)])],
+        [(1, [(0, 0), (1, 0), (1, 1)])],
         [(j, [(1, 1)]) for j in near],
         [(j, [(1, 0)]) for j in far],
-        [(j, [(0, 1)]) for j in near],
+        [(j, [(0, 1)]) for j in (*near, 1)],
         [(j, [(0, 0)]) for j in far],
         [(j, [(1, 1)]) for j in far],
         [(j, [(0, 1)]) for j in far],
@@ -52,7 +52,7 @@
     inv_rms = lax.rsqrt(jnp.mean(toks * toks, axis=1, keepdims=True) + 1e-06)
     normed_ref[...] = (toks * inv_rms * gain_ref[...]).astype(jnp.bfloat16)
     own = pl.ds(group_offset(rep, 0, 0, 0, width), 2 * width)
-    other = pl.ds(group_offset(rep, 0, 1, 0, width), 2 * width)
+    other = pl.ds(group_offset(rep, 1, 1, 0, width), width)
     first_ref[...] = normed_ref[:, pl.ds(group_offset(rep, 0, 0, 0, width), width)]
     second_ref[:tok_rows] = normed_ref[:, pl.ds(group_offset(rep, 1, 0, 0, width), width)]
     to_y_ref[:tok_rows, : 2 * width] = normed_ref[:, own]
@@ -78,7 +78,7 @@
             jax.ShapeDtypeStruct((tok_rows, model_width), jnp.bfloat16),
             jax.ShapeDtypeStruct((tok_rows + meta_rows, width), jnp.bfloat16),
             jax.ShapeDtypeStruct((tok_rows, width), jnp.bfloat16),
-            jax.ShapeDtypeStruct((tok_rows + meta_rows, 4 * width), jnp.bfloat16),
+            jax.ShapeDtypeStruct((tok_rows + meta_rows, 3 * width), jnp.bfloat16),
             jax.ShapeDtypeStruct((1, model_width), jnp.float32),
             jax.ShapeDtypeStruct((tok_rows, 2 * width), jnp.float32),
             jax.ShapeDtypeStruct((meta_rows, tok_rows), jnp.bfloat16),
@@ -99,24 +99,32 @@
     ).astype(jnp.float32).astype(jnp.bfloat16)
     slot_iota = lax.broadcasted_iota(jnp.int32, (exp_dev, SLOTS, tok_rows), 1).astype(jnp.float32)
 
-    def place_block(j, carry):
-        meta = meta_ref[j].astype(jnp.float32)
-        hit = jnp.zeros((exp_dev, tok_rows), jnp.float32)
-        prob = jnp.zeros((exp_dev, tok_rows), jnp.float32)
-        for k in range(top_k):
-            same = meta[k : k + 1, :] == exp_iota
-            hit = jnp.where(same, 1.0, hit)
-            prob = jnp.where(same, meta[top_k + k : top_k + k + 1, :], prob)
-        rank = contract(hit.astype(jnp.bfloat16), earlier, 1, 0)
-        slot = jnp.where(hit > 0.0, rank, -1.0)
-        here = slot[:, None, :] == slot_iota
-        onehot = jnp.where(here, 1.0, 0.0).reshape(exp_dev * SLOTS, tok_rows)
-        weight = jnp.where(here, prob[:, None, :], 0.0).reshape(exp_dev * SLOTS, tok_rows)
-        picks_ref[j] = onehot.astype(jnp.bfloat16)
-        weights_ref[j] = weight.T.astype(jnp.bfloat16)
+    def place_pair(pair, carry):
+        blocks = (2 * pair, 2 * pair + 1)
+        hits, probs = [], []
+        for j in blocks:
+            meta = meta_ref[j].astype(jnp.float32)
+            hit = jnp.zeros((exp_dev, tok_rows), jnp.float32)
+            prob = jnp.zeros((exp_dev, tok_rows), jnp.float32)
+            for k in range(top_k):
+                same = meta[k : k + 1, :] == exp_iota
+                hit = jnp.where(same, 1.0, hit)
+                prob = jnp.where(same, meta[top_k + k : top_k + k + 1, :], prob)
+            hits.append(hit)
+            probs.append(prob)
+        ranks = contract(jnp.concatenate(hits, axis=0).astype(jnp.bfloat16), earlier, 1, 0)
+        for n, j in enumerate(blocks):
+            rank = ranks[n * exp_dev : (n + 1) * exp_dev]
+            slot = jnp.where(hits[n] > 0.0, rank, -1.0)
+            here = slot[:, None, :] == slot_iota
+            onehot = jnp.where(here, 1.0, 0.0).reshape(exp_dev * SLOTS, tok_rows)
+            weight = jnp.where(here, probs[n][:, None, :], 0.0)
+            weight = weight.reshape(exp_dev * SLOTS, tok_rows)
+            picks_ref[j] = onehot.astype(jnp.bfloat16)
+            weights_ref[j] = weight.T.astype(jnp.bfloat16)
         return carry
 
-    lax.fori_loop(0, n_seq, place_block, 0)
+    lax.fori_loop(0, n_seq // 2, place_pair, 0)
 
 
 def route(meta, exp_dev):
@@ -138,7 +146,7 @@
 
 
 def most_rows(tok_rows):
-    return tok_rows // 64 * 48
+    return tok_rows // 128 * 112
 
 
 def moe_kernel(n_pieces, *refs):
@@ -342,7 +350,7 @@
     x_two = swap(second[:, :tok_rows], "rep", 2)
     y_one = swap(second, "seq", 1)
     y_two = swap(first, "seq", 1)
-    x_one = swap(first, "rep", 2)
+    x_one = swap(jnp.concatenate([first, from_y[None, :tok_rows, :width]]), "rep", 2)
     to_y, to_core, to_core_y = lax.optimization_barrier((x_two, second, from_y))
     y_three = swap(to_y, "seq", 1)
     early = [swap(piece, "rep", 1) for piece in (to_core, first, to_core_y)]
@@ -370,11 +378,11 @@
     by_x, by_y = swap(to_x, "rep", 2), swap(to_y, "seq", 1)
     rest = added(rest_kept, rest[1])
     by_z = [swap(rest[d], "seq", 2 * d) for d in others]
-    to_y, to_x, by_z[-1] = lax.optimization_barrier(
+    to_y, to_x, *by_z = lax.optimization_barrier(
         (
             added(*[term[1] for term in near], by_x[1]),
             added(*[term[3] for term in near], by_y[1]),
-            by_z[-1],
+            *by_z,
         )
     )
     first_far, second_far = swap(to_y, "seq", 1), swap(to_x, "rep", 2)
@@ -382,8 +390,7 @@
     second = added(*[term[2] for term in near], by_y[0], second_far)
     blocks = jnp.concatenate([first, second], axis=2)
     most = [blocks[0]] + [swap(blocks[d], "seq", 2 * d) for d in others]
-    most[-1], rest = lax.optimization_barrier((most[-1], rest[0]))
-    rest = added(rest, *by_z)
+    rest = added(rest[0], *by_z)
     rest = added(rest[0], swap(rest[1], "seq", 1))
     far = jnp.concatenate([rest[:, :width], rest[:, 3 * width :]], axis=1)
     rest = [rest[:, width : 3 * width], swap(far, "rep", 2)]

time: 103 us -> 102 us (level)
  waiting for transfers between devices: 29.2 us -> 36.8 us
  starting transfers between devices: 43.7 us -> 36.7 us
    ppermute x37, waiting for transfers between devices: 29.2 us -> 36.8 us  [swap(): return lax.ppermute(value, axis, [(i, i ^ distance) for i in range(size)])]
    ppermute x37, starting transfers between devices: 43.7 us -> 36.7 us  [swap(): return lax.ppermute(value, axis, [(i, i ^ distance) for i in range(size)])]
  transfers between devices with their start and end apart: 37 -> 37, of which waited for: 14 -> 15; matrix products, arithmetic and copies ran while one was open for 2% -> 2% of each run, Pallas kernels for 4% -> 3%
where the time goes in v4:
time: 102 us
  waiting for transfers between devices  36.8 us (36%)
  starting transfers between devices  36.7 us (36%)
  Pallas kernels  25.8 us (25%)
  other arithmetic  1.62 us (2%)
    ppermute x37, waiting for transfers between devices, swap(): return lax.ppermute(value, axis, [(i, i ^ distance) for i in range(size)])  36.8 us
    ppermute x37, starting transfers between devices, swap(): return lax.ppermute(value, axis, [(i, i ^ distance) for i in range(size)])  36.7 us
    pallas_call x1, Pallas kernels, moe_partial(): pl.pallas_call(functools.partial(moe_kernel, n_pieces), out_shape=outs, i...  20.6 us
    pallas_call x1, Pallas kernels, route(): pl.pallas_call(functools.partial(route_kernel, exp_dev), out_shape=[jax.S...  2.72 us
    pallas_call x1, Pallas kernels, norm_and_base(): pl.pallas_call(norm_kernel, out_shape=[jax.ShapeDtypeStruct((tok_rows, mo...  2.46 us
  transfers between devices with their start and end apart: 37, of which 15 were waited for; matrix products, arithmetic and copies ran while one was open for 2% of the time, Pallas kernels for 3%

profile of v4, /device:TPU:0, one launch (start us, length us, event | category | flops | bytes accessed | tf_op | source)
XLA Modules:
  0.0 102.0 jit_solution(17791340795540246574)
XLA Ops:
  0.0 2.5 %shard_map.82 = (bf16[128,2048]{1,0:T(8,128)(2,1)}, bf16[144,256]{1,0:T(8,128)(2,1)}, bf16[128,256]{1,0:T(8,128)(2,1)}, bf16[144,768]{1,0:T(8,128)(2,1)}, f32[1,...) custom-call(bf16[128,2048]{1,0:T(8,128)(2,1)} %tokens_ref.1, f32[1,2048]{1,0:T(1,128)} %bitcast.66, ...), custom_call_target="tpu_custom_call" | custom-call | tf_op jit(solution)/shard_map/pallas_call | solution.py:75
  2.5 5.1 %collective-permute-start.2 = (bf16[144,256]{1,0:T(8,128)(2,1)}, bf16[144,256]{1,0:T(8,128)(2,1)S(1)}, u32[]{:S(2)}, u32[]{:S(2)}) collective-permute-start(bf16[144,256]{1,0:T(8,128)(2,1)} %get-tuple-element.39), channel_id=1, source_target_pairs={{0,24},{4,28},{8,16},{12,20},{16,8},{20,12},{24,0},{28,4},{1,25},{... | collective-permute-start | bytes 221192 | tf_op jit(solution)/shard_map/ppermute | solution.py:329
  8.2 1.7 %collective-permute-start.3 = (bf16[144,768]{1,0:T(8,128)(2,1)}, bf16[144,768]{1,0:T(8,128)(2,1)S(1)}, u32[]{:S(2)}, u32[]{:S(2)}) collective-permute-start(bf16[144,768]{1,0:T(8,128)(2,1)} %get-tuple-element.40), channel_id=1, source_target_pairs={{0,4},{4,0},{8,12},{12,8},{16,20},{20,16},{24,28},{28,24},{1,5},{5... | collective-permute-start | bytes 663560 | tf_op jit(solution)/shard_map/ppermute | solution.py:329
  10.5 3.4 %collective-permute-done.1 = bf16[144,256]{1,0:T(8,128)(2,1)S(1)} collective-permute-done((bf16[144,256]{1,0:T(8,128)(2,1)}, bf16[144,256]{1,0:T(8,128)(2,1)S(1)}, u32[]{:S(2)}, u32[]{:S(2)}) %collective-permute-start.1) | collective-permute-done | bytes 73760 | tf_op jit(solution)/shard_map/ppermute | solution.py:329
  14.0 1.0 collective-permute-done.3.refs_6_
  15.0 3.5 %collective-permute-start.6 = (bf16[128,256]{1,0:T(8,128)(2,1)}, bf16[128,256]{1,0:T(8,128)(2,1)S(1)}, u32[]{:S(2)}, u32[]{:S(2)}) collective-permute-start(bf16[128,256]{1,0:T(8,128)(2,1)} %get-tuple-element.41), channel_id=1, source_target_pairs={{0,24},{4,28},{8,16},{12,20},{16,8},{20,12},{24,0},{28,4},{1,25},{... | collective-permute-start | bytes 196616 | tf_op jit(solution)/shard_map/ppermute | solution.py:329
  18.5 0.9 collective-permute-start.4
  19.4 1.6 %collective-permute-start.8 = (bf16[3,144,256]{2,1,0:T(8,128)(2,1)S(1)}, bf16[3,144,256]{2,1,0:T(8,128)(2,1)S(1)}, u32[]{:S(2)}, u32[]{:S(2)}) collective-permute-start(bf16[3,144,256]{2,1,0:T(8,128)(2,1)S(1)} %pad_maximum_fusion.1.refs_4_), channel_id=1, source_target_pairs={{0,4},{4,0},{8,12},{12,8},{16,20},{20,16},{24,28},{28,24},{1,5},{5... | collective-permute-start | bytes 663560 | tf_op jit(solution)/shard_map/ppermute | solution.py:329
  21.0 1.6 %collective-permute-start.9 = (bf16[3,128,256]{2,1,0:T(8,128)(2,1)S(1)}, bf16[3,128,256]{2,1,0:T(8,128)(2,1)S(1)}, u32[]{:S(2)}, u32[]{:S(2)}) collective-permute-start(bf16[3,128,256]{2,1,0:T(8,128)(2,1)S(1)} %slice.121), channel_id=1, source_target_pairs={{0,2},{1,3},{2,0},{3,1},{4,6},{5,7},{6,4},{7,5},{8,10},{9,11},{10,... | collective-permute-start | bytes 589832 | tf_op jit(solution)/shard_map/ppermute | solution.py:329
  22.6 1.3 %collective-permute-done.5 = bf16[128,256]{1,0:T(8,128)(2,1)S(1)} collective-permute-done((bf16[128,256]{1,0:T(8,128)(2,1)}, bf16[128,256]{1,0:T(8,128)(2,1)S(1)}, u32[]{:S(2)}, u32[]{:S(2)}) %collective-permute-start.5) | collective-permute-done | bytes 65568 | tf_op jit(solution)/shard_map/ppermute | solution.py:329
  23.9 1.6 %collective-permute-start.7 = (bf16[3,128,256]{2,1,0:T(8,128)(2,1)S(1)}, bf16[3,128,256]{2,1,0:T(8,128)(2,1)S(1)}, u32[]{:S(2)}, u32[]{:S(2)}) collective-permute-start(bf16[3,128,256]{2,1,0:T(8,128)(2,1)S(1)} %pad_maximum_fusion.2.refs_5_), channel_id=1, source_target_pairs={{0,4},{4,0},{8,12},{12,8},{16,20},{20,16},{24,28},{28,24},{1,5},{5... | collective-permute-start | bytes 589832 | tf_op jit(solution)/shard_map/ppermute | solution.py:329
  25.6 1.6 %collective-permute-start.10 = (bf16[4,128,256]{2,1,0:T(8,128)(2,1)S(1)}, bf16[4,128,256]{2,1,0:T(8,128)(2,1)S(1)}, u32[]{:S(2)}, u32[]{:S(2)}) collective-permute-start(bf16[4,128,256]{2,1,0:T(8,128)(2,1)S(1)} %pad_maximum_fusion), channel_id=1, source_target_pairs={{0,2},{1,3},{2,0},{3,1},{4,6},{5,7},{6,4},{7,5},{8,10},{9,11},{10,... | collective-permute-start | bytes 786440 | tf_op jit(solution)/shard_map/ppermute | solution.py:329
  28.3 3.4 %collective-permute-done.7.refs_10_ = bf16[3,128,256]{2,1,0:T(8,128)(2,1)S(1)} collective-permute-done((bf16[3,128,256]{2,1,0:T(8,128)(2,1)S(1)}, bf16[3,128,256]{2,1,0:T(8,128)(2,1)S(1)}, u32[]{:S(2)}, u32[]{:S(2)}) %collective-permute-start.7) | collective-permute-done | bytes 196640 | tf_op jit(solution)/shard_map/ppermute | solution.py:329
  31.7 2.7 %shard_map.83 = (bf16[8,256,128]{2,1,0:T(8,128)(2,1)}, bf16[8,128,256]{2,1,0:T(8,128)(2,1)}) custom-call(bf16[8,16,128]{2,1,0:T(8,128)(2,1)} %copy-done.2), custom_call_target="tpu_custom_call" | custom-call | flops 4000000000 | bytes 2097152 | tf_op jit(solution)/shard_map/pallas_call | solution.py:133
  34.4 1.5 %collective-permute-start.12 = (bf16[3,128,256]{2,1,0:T(8,128)(2,1)S(1)}, bf16[3,128,256]{2,1,0:T(8,128)(2,1)S(1)}, u32[]{:S(2)}, u32[]{:S(2)}) collective-permute-start(bf16[3,128,256]{2,1,0:T(8,128)(2,1)S(1)} %collective-permute-done.7.refs_10_), channel_id=1, source_target_pairs={{0,2},{1,3},{2,0},{3,1},{4,6},{5,7},{6,4},{7,5},{8,10},{9,11},{10,... | collective-permute-start | bytes 589832 | tf_op jit(solution)/shard_map/ppermute | solution.py:329
  37.0 4.8 %collective-permute-done.12.refs_12_ = bf16[3,128,256]{2,1,0:T(8,128)(2,1)S(1)} collective-permute-done((bf16[3,128,256]{2,1,0:T(8,128)(2,1)S(1)}, bf16[3,128,256]{2,1,0:T(8,128)(2,1)S(1)}, u32[]{:S(2)}, u32[]{:S(2)}) %collective-permute-start.12) | collective-permute-done | bytes 196640 | tf_op jit(solution)/shard_map/ppermute | solution.py:329
  41.8 1.4 %collective-permute-done.21.refs_21_ = bf16[3,128,256]{2,1,0:T(8,128)(2,1)S(1)} collective-permute-done((bf16[3,128,256]{2,1,0:T(8,128)(2,1)S(1)}, bf16[3,128,256]{2,1,0:T(8,128)(2,1)S(1)}, u32[]{:S(2)}, u32[]{:S(2)}) %collective-permute-start.21) | collective-permute-done | bytes 196640 | tf_op jit(solution)/shard_map/ppermute | solution.py:329
  43.2 20.6 %shard_map.84 = (bf16[4,4,112,256]{3,2,1,0:T(8,128)(2,1)S(1)}, bf16[4,4,112,256]{3,2,1,0:T(8,128)(2,1)S(1)}, bf16[4,2,16,1024]{3,2,1,0:T(8,128)(2,1)S(1)}, bf16[...) custom-call(bf16[8,256,128]{2,1,0:T(8,128)(2,1)} %get-tuple-element.47.re, ...), custom_call_target="tpu_custom_call" | custom-call | flops 4831838208 | bytes 46137344 | tf_op jit(solution)/shard_map/pallas_call | solution.py:299
  64.5 1.8 %collective-permute-done.23 = bf16[4,4,112,256]{3,2,1,0:T(8,128)(2,1)S(1)} collective-permute-done((bf16[4,4,112,256]{3,2,1,0:T(8,128)(2,1)S(1)}, bf16[4,4,112,256]{3,2,1,0:T(8,128)(2,1)S(1)}, u32[]{:S(2)}, u32[]{:S(2)}) %collective-permute-start.23) | collective-permute-done | bytes 917536 | tf_op jit(solution)/shard_map/ppermute | solution.py:329
  66.6 1.6 %collective-permute-start.24 = (bf16[2,4,112,256]{3,2,1,0:T(8,128)(2,1)S(1)}, bf16[2,4,112,256]{3,2,1,0:T(8,128)(2,1)S(1)}, u32[]{:S(2)}, u32[]{:S(2)}) collective-permute-start(bf16[2,4,112,256]{3,2,1,0:T(8,128)(2,1)S(1)} %get-tuple-element.60), channel_id=1, source_target_pairs={{0,2},{1,3},{2,0},{3,1},{4,6},{5,7},{6,4},{7,5},{8,10},{9,11},{10,... | collective-permute-start | bytes 1376264 | tf_op jit(solution)/shard_map/ppermute | solution.py:329
  68.1 1.5 %collective-permute-start.25 = (bf16[2,4,112,256]{3,2,1,0:T(8,128)(2,1)S(1)}, bf16[2,4,112,256]{3,2,1,0:T(8,128)(2,1)S(1)}, u32[]{:S(2)}, u32[]{:S(2)}) collective-permute-start(bf16[2,4,112,256]{3,2,1,0:T(8,128)(2,1)S(1)} %get-tuple-element.61), channel_id=1, source_target_pairs={{0,4},{4,0},{8,12},{12,8},{16,20},{20,16},{24,28},{28,24},{1,5},{5... | collective-permute-start | bytes 1376264 | tf_op jit(solution)/shard_map/ppermute | solution.py:329
  69.8 2.1 %collective-permute-start.29 = (bf16[2,16,1024]{2,1,0:T(8,128)(2,1)S(1)}, bf16[2,16,1024]{2,1,0:T(8,128)(2,1)S(1)}, u32[]{:S(2)}, u32[]{:S(2)}) collective-permute-start(bf16[2,16,1024]{2,1,0:T(8,128)(2,1)S(1)} %get-tuple-element.78), channel_id=1, source_target_pairs={{0,24},{4,28},{8,16},{12,20},{16,8},{20,12},{24,0},{28,4},{1,25},{... | collective-permute-start | bytes 196616 | tf_op jit(solution)/shard_map/ppermute | solution.py:329
  71.9 2.3 %collective-permute-start.27 = (bf16[2,16,1024]{2,1,0:T(8,128)(2,1)S(1)}, bf16[2,16,1024]{2,1,0:T(8,128)(2,1)S(1)}, u32[]{:S(2)}, u32[]{:S(2)}) collective-permute-start(bf16[2,16,1024]{2,1,0:T(8,128)(2,1)S(1)} %get-tuple-element.80), channel_id=1, source_target_pairs={{0,8},{4,12},{8,0},{12,4},{16,24},{20,28},{24,16},{28,20},{1,9},{5... | collective-permute-start | bytes 196616 | tf_op jit(solution)/shard_map/ppermute | solution.py:329
  74.2 5.0 %collective-permute-done.24 = bf16[2,4,112,256]{3,2,1,0:T(8,128)(2,1)S(1)} collective-permute-done((bf16[2,4,112,256]{3,2,1,0:T(8,128)(2,1)S(1)}, bf16[2,4,112,256]{3,2,1,0:T(8,128)(2,1)S(1)}, u32[]{:S(2)}, u32[]{:S(2)}) %collective-permute-start.24) | collective-permute-done | bytes 458784 | tf_op jit(solution)/shard_map/ppermute | solution.py:329
  79.2 1.2 %collective-permute-done.25 = bf16[2,4,112,256]{3,2,1,0:T(8,128)(2,1)S(1)} collective-permute-done((bf16[2,4,112,256]{3,2,1,0:T(8,128)(2,1)S(1)}, bf16[2,4,112,256]{3,2,1,0:T(8,128)(2,1)S(1)}, u32[]{:S(2)}, u32[]{:S(2)}) %collective-permute-start.25) | collective-permute-done | bytes 458784 | tf_op jit(solution)/shard_map/ppermute | solution.py:329
  80.7 1.6 %collective-permute-start.35 = (bf16[16,1024]{1,0:T(8,128)(2,1)S(1)}, bf16[16,1024]{1,0:T(8,128)(2,1)S(1)}, u32[]{:S(2)}, u32[]{:S(2)}) collective-permute-start(bf16[16,1024]{1,0:T(8,128)(2,1)S(1)} %slice_bitcast_fusion.5), channel_id=1, source_target_pairs={{0,4},{4,0},{8,12},{12,8},{16,20},{20,16},{24,28},{28,24},{1,5},{5... | collective-permute-start | bytes 98312 | tf_op jit(solution)/shard_map/ppermute | solution.py:329
  83.3 1.7 %collective-permute-done.35 = bf16[16,1024]{1,0:T(8,128)(2,1)S(1)} collective-permute-done((bf16[16,1024]{1,0:T(8,128)(2,1)S(1)}, bf16[16,1024]{1,0:T(8,128)(2,1)S(1)}, u32[]{:S(2)}, u32[]{:S(2)}) %collective-permute-start.35) | collective-permute-done | bytes 32800 | tf_op jit(solution)/shard_map/ppermute | solution.py:329
  85.6 3.2 %collective-permute-done.30 = bf16[4,112,256]{2,1,0:T(8,128)(2,1)S(1)} collective-permute-done((bf16[4,112,256]{2,1,0:T(8,128)(2,1)S(1)}, bf16[4,112,256]{2,1,0:T(8,128)(2,1)S(1)}, u32[]{:S(2)}, u32[]{:S(2)}) %collective-permute-start.30) | collective-permute-done | bytes 229408 | tf_op jit(solution)/shard_map/ppermute | solution.py:329
  89.8 2.9 %collective-permute-start.34 = (bf16[112,512]{1,0:T(8,128)(2,1)S(1)}, bf16[112,512]{1,0:T(8,128)(2,1)S(1)}, u32[]{:S(2)}, u32[]{:S(2)}) collective-permute-start(bf16[112,512]{1,0:T(8,128)(2,1)S(1)} %get-tuple-element.76), channel_id=1, source_target_pairs={{0,24},{4,28},{8,16},{12,20},{16,8},{20,12},{24,0},{28,4},{1,25},{... | collective-permute-start | bytes 344072 | tf_op jit(solution)/shard_map/ppermute | solution.py:329
  92.7 2.6 %collective-permute-done.32 = bf16[112,512]{1,0:T(8,128)(2,1)S(1)} collective-permute-done((bf16[112,512]{1,0:T(8,128)(2,1)S(1)}, bf16[112,512]{1,0:T(8,128)(2,1)S(1)}, u32[]{:S(2)}, u32[]{:S(2)}) %collective-permute-start.32) | collective-permute-done | bytes 114720 | tf_op jit(solution)/shard_map/ppermute | solution.py:329
  95.3 2.3 %collective-permute-done.34 = bf16[112,512]{1,0:T(8,128)(2,1)S(1)} collective-permute-done((bf16[112,512]{1,0:T(8,128)(2,1)S(1)}, bf16[112,512]{1,0:T(8,128)(2,1)S(1)}, u32[]{:S(2)}, u32[]{:S(2)}) %collective-permute-start.34) | collective-permute-done | bytes 114720 | tf_op jit(solution)/shard_map/ppermute | solution.py:329
  97.6 3.6 %collective-permute-done.33 = bf16[112,512]{1,0:T(8,128)(2,1)S(1)} collective-permute-done((bf16[112,512]{1,0:T(8,128)(2,1)S(1)}, bf16[112,512]{1,0:T(8,128)(2,1)S(1)}, u32[]{:S(2)}, u32[]{:S(2)}) %collective-permute-start.33) | collective-permute-done | bytes 114720 | tf_op jit(solution)/shard_map/ppermute | solution.py:329
  (78 shorter events, 8.4 us)
Async XLA Ops:
  2.5 8.1 %collective-permute-start.2 = (bf16[144,256]{1,0:T(8,128)(2,1)}, bf16[144,256]{1,0:T(8,128)(2,1)S(1)}, u32[]{:S(2)}, u32[]{:S(2)}) collective-permute-start(bf16[144,256]{1,0:T(8,128)(2,1)} %get-tuple-element.39), channel_id=1, source_target_pairs={{0,24},{4,28},{8,16},{12,20},{16,8},{20,12},{24,0},{28,4},{1,25},{... | collective-permute-start | bytes 221192 | tf_op jit(solution)/shard_map/ppermute | solution.py:329
  7.5 6.4 %collective-permute-start.1 = (bf16[144,256]{1,0:T(8,128)(2,1)}, bf16[144,256]{1,0:T(8,128)(2,1)S(1)}, u32[]{:S(2)}, u32[]{:S(2)}) collective-permute-start(bf16[144,256]{1,0:T(8,128)(2,1)} %get-tuple-element.39), channel_id=1, source_target_pairs={{0,16},{4,20},{8,24},{12,28},{16,0},{20,4},{24,8},{28,12},{1,17},{... | collective-permute-start | bytes 221192 | tf_op jit(solution)/shard_map/ppermute | solution.py:329
  7.5 6.4 %collective-permute-start = (bf16[144,256]{1,0:T(8,128)(2,1)}, bf16[144,256]{1,0:T(8,128)(2,1)S(1)}, u32[]{:S(2)}, u32[]{:S(2)}) collective-permute-start(bf16[144,256]{1,0:T(8,128)(2,1)} %get-tuple-element.39), channel_id=1, source_target_pairs={{0,8},{4,12},{8,0},{12,4},{16,24},{20,28},{24,16},{28,20},{1,9},{5... | collective-permute-start | bytes 221192 | tf_op jit(solution)/shard_map/ppermute | solution.py:329
  8.2 6.8 %collective-permute-start.3 = (bf16[144,768]{1,0:T(8,128)(2,1)}, bf16[144,768]{1,0:T(8,128)(2,1)S(1)}, u32[]{:S(2)}, u32[]{:S(2)}) collective-permute-start(bf16[144,768]{1,0:T(8,128)(2,1)} %get-tuple-element.40), channel_id=1, source_target_pairs={{0,4},{4,0},{8,12},{12,8},{16,20},{20,16},{24,28},{28,24},{1,5},{5... | collective-permute-start | bytes 663560 | tf_op jit(solution)/shard_map/ppermute | solution.py:329
  15.0 7.6 %collective-permute-start.6 = (bf16[128,256]{1,0:T(8,128)(2,1)}, bf16[128,256]{1,0:T(8,128)(2,1)S(1)}, u32[]{:S(2)}, u32[]{:S(2)}) collective-permute-start(bf16[128,256]{1,0:T(8,128)(2,1)} %get-tuple-element.41), channel_id=1, source_target_pairs={{0,24},{4,28},{8,16},{12,20},{16,8},{20,12},{24,0},{28,4},{1,25},{... | collective-permute-start | bytes 196616 | tf_op jit(solution)/shard_map/ppermute | solution.py:329
  18.5 5.4 %collective-permute-start.5 = (bf16[128,256]{1,0:T(8,128)(2,1)}, bf16[128,256]{1,0:T(8,128)(2,1)S(1)}, u32[]{:S(2)}, u32[]{:S(2)}) collective-permute-start(bf16[128,256]{1,0:T(8,128)(2,1)} %get-tuple-element.41), channel_id=1, source_target_pairs={{0,16},{4,20},{8,24},{12,28},{16,0},{20,4},{24,8},{28,12},{1,17},{... | collective-permute-start | bytes 196616 | tf_op jit(solution)/shard_map/ppermute | solution.py:329
  18.5 5.4 %collective-permute-start.4 = (bf16[128,256]{1,0:T(8,128)(2,1)}, bf16[128,256]{1,0:T(8,128)(2,1)S(1)}, u32[]{:S(2)}, u32[]{:S(2)}) collective-permute-start(bf16[128,256]{1,0:T(8,128)(2,1)} %get-tuple-element.41), channel_id=1, source_target_pairs={{0,8},{4,12},{8,0},{12,4},{16,24},{20,28},{24,16},{28,20},{1,9},{5... | collective-permute-start | bytes 196616 | tf_op jit(solution)/shard_map/ppermute | solution.py:329
  19.4 8.2 %collective-permute-start.8 = (bf16[3,144,256]{2,1,0:T(8,128)(2,1)S(1)}, bf16[3,144,256]{2,1,0:T(8,128)(2,1)S(1)}, u32[]{:S(2)}, u32[]{:S(2)}) collective-permute-start(bf16[3,144,256]{2,1,0:T(8,128)(2,1)S(1)} %pad_maximum_fusion.1.refs_4_), channel_id=1, source_target_pairs={{0,4},{4,0},{8,12},{12,8},{16,20},{20,16},{24,28},{28,24},{1,5},{5... | collective-permute-start | bytes 663560 | tf_op jit(solution)/shard_map/ppermute | solution.py:329
  21.0 6.1 %collective-permute-start.9 = (bf16[3,128,256]{2,1,0:T(8,128)(2,1)S(1)}, bf16[3,128,256]{2,1,0:T(8,128)(2,1)S(1)}, u32[]{:S(2)}, u32[]{:S(2)}) collective-permute-start(bf16[3,128,256]{2,1,0:T(8,128)(2,1)S(1)} %slice.121), channel_id=1, source_target_pairs={{0,2},{1,3},{2,0},{3,1},{4,6},{5,7},{6,4},{7,5},{8,10},{9,11},{10,... | collective-permute-start | bytes 589832 | tf_op jit(solution)/shard_map/ppermute | solution.py:329
  23.9 7.8 %collective-permute-start.7 = (bf16[3,128,256]{2,1,0:T(8,128)(2,1)S(1)}, bf16[3,128,256]{2,1,0:T(8,128)(2,1)S(1)}, u32[]{:S(2)}, u32[]{:S(2)}) collective-permute-start(bf16[3,128,256]{2,1,0:T(8,128)(2,1)S(1)} %pad_maximum_fusion.2.refs_5_), channel_id=1, source_target_pairs={{0,4},{4,0},{8,12},{12,8},{16,20},{20,16},{24,28},{28,24},{1,5},{5... | collective-permute-start | bytes 589832 | tf_op jit(solution)/shard_map/ppermute | solution.py:329
  25.6 8.9 %collective-permute-start.10 = (bf16[4,128,256]{2,1,0:T(8,128)(2,1)S(1)}, bf16[4,128,256]{2,1,0:T(8,128)(2,1)S(1)}, u32[]{:S(2)}, u32[]{:S(2)}) collective-permute-start(bf16[4,128,256]{2,1,0:T(8,128)(2,1)S(1)} %pad_maximum_fusion), channel_id=1, source_target_pairs={{0,2},{1,3},{2,0},{3,1},{4,6},{5,7},{6,4},{7,5},{8,10},{9,11},{10,... | collective-permute-start | bytes 786440 | tf_op jit(solution)/shard_map/ppermute | solution.py:329
  27.1 8.8 %collective-permute-start.11 = (bf16[3,128,256]{2,1,0:T(8,128)(2,1)S(1)}, bf16[3,128,256]{2,1,0:T(8,128)(2,1)S(1)}, u32[]{:S(2)}, u32[]{:S(2)}) collective-permute-start(bf16[3,128,256]{2,1,0:T(8,128)(2,1)S(1)} %collective-permute-done.9.refs_7_), channel_id=1, source_target_pairs={{0,4},{4,0},{8,12},{12,8},{16,20},{20,16},{24,28},{28,24},{1,5},{5... | collective-permute-start | bytes 589832 | tf_op jit(solution)/shard_map/ppermute | solution.py:329
  27.6 8.8 %collective-permute-start.13 = (bf16[3,144,256]{2,1,0:T(8,128)(2,1)S(1)}, bf16[3,144,256]{2,1,0:T(8,128)(2,1)S(1)}, u32[]{:S(2)}, u32[]{:S(2)}) collective-permute-start(bf16[3,144,256]{2,1,0:T(8,128)(2,1)S(1)} %pad_maximum_fusion.1.refs_4_), channel_id=1, source_target_pairs={{0,1},{1,0},{2,3},{3,2},{4,5},{5,4},{6,7},{7,6},{8,9},{9,8},{10,11... | collective-permute-start | bytes 663560 | tf_op jit(solution)/shard_map/ppermute | solution.py:329
  27.7 9.0 %collective-permute-start.15 = (bf16[144,768]{1,0:T(8,128)(2,1)S(1)}, bf16[144,768]{1,0:T(8,128)(2,1)S(1)}, u32[]{:S(2)}, u32[]{:S(2)}) collective-permute-start(bf16[144,768]{1,0:T(8,128)(2,1)S(1)} %collective-permute-done.3.refs_6_), channel_id=1, source_target_pairs={{0,1},{1,0},{2,3},{3,2},{4,5},{5,4},{6,7},{7,6},{8,9},{9,8},{10,11... | collective-permute-start | bytes 663560 | tf_op jit(solution)/shard_map/ppermute | solution.py:329
  34.4 7.3 %collective-permute-start.12 = (bf16[3,128,256]{2,1,0:T(8,128)(2,1)S(1)}, bf16[3,128,256]{2,1,0:T(8,128)(2,1)S(1)}, u32[]{:S(2)}, u32[]{:S(2)}) collective-permute-start(bf16[3,128,256]{2,1,0:T(8,128)(2,1)S(1)} %collective-permute-done.7.refs_10_), channel_id=1, source_target_pairs={{0,2},{1,3},{2,0},{3,1},{4,6},{5,7},{6,4},{7,5},{8,10},{9,11},{10,... | collective-permute-start | bytes 589832 | tf_op jit(solution)/shard_map/ppermute | solution.py:329
  35.9 5.8 %collective-permute-start.18 = (bf16[4,128,256]{2,1,0:T(8,128)(2,1)S(1)}, bf16[4,128,256]{2,1,0:T(8,128)(2,1)S(1)}, u32[]{:S(2)}, u32[]{:S(2)}) collective-permute-start(bf16[4,128,256]{2,1,0:T(8,128)(2,1)S(1)} %collective-permute-done.10.refs_9_), channel_id=1, source_target_pairs={{0,1},{1,0},{2,3},{3,2},{4,5},{5,4},{6,7},{7,6},{8,9},{9,8},{10,11... | collective-permute-start | bytes 786440 | tf_op jit(solution)/shard_map/ppermute | solution.py:329
  36.2 5.6 %collective-permute-start.17 = (bf16[3,144,256]{2,1,0:T(8,128)(2,1)S(1)}, bf16[3,144,256]{2,1,0:T(8,128)(2,1)S(1)}, u32[]{:S(2)}, u32[]{:S(2)}) collective-permute-start(bf16[3,144,256]{2,1,0:T(8,128)(2,1)S(1)} %collective-permute-done.8.refs_8_), channel_id=1, source_target_pairs={{0,1},{1,0},{2,3},{3,2},{4,5},{5,4},{6,7},{7,6},{8,9},{9,8},{10,11... | collective-permute-start | bytes 663560 | tf_op jit(solution)/shard_map/ppermute | solution.py:329
  36.5 5.3 %collective-permute-start.19 = (bf16[3,128,256]{2,1,0:T(8,128)(2,1)S(1)}, bf16[3,128,256]{2,1,0:T(8,128)(2,1)S(1)}, u32[]{:S(2)}, u32[]{:S(2)}) collective-permute-start(bf16[3,128,256]{2,1,0:T(8,128)(2,1)S(1)} %collective-permute-done.7.refs_10_), channel_id=1, source_target_pairs={{0,1},{1,0},{2,3},{3,2},{4,5},{5,4},{6,7},{7,6},{8,9},{9,8},{10,11... | collective-permute-start | bytes 589832 | tf_op jit(solution)/shard_map/ppermute | solution.py:329
  36.7 5.1 %collective-permute-start.20 = (bf16[3,128,256]{2,1,0:T(8,128)(2,1)S(1)}, bf16[3,128,256]{2,1,0:T(8,128)(2,1)S(1)}, u32[]{:S(2)}, u32[]{:S(2)}) collective-permute-start(bf16[3,128,256]{2,1,0:T(8,128)(2,1)S(1)} %collective-permute-done.11.refs_11_), channel_id=1, source_target_pairs={{0,1},{1,0},{2,3},{3,2},{4,5},{5,4},{6,7},{7,6},{8,9},{9,8},{10,11... | collective-permute-start | bytes 589832 | tf_op jit(solution)/shard_map/ppermute | solution.py:329
  64.0 7.9 %collective-permute-start.22 = (bf16[4,4,112,256]{3,2,1,0:T(8,128)(2,1)S(1)}, bf16[4,4,112,256]{3,2,1,0:T(8,128)(2,1)S(1)}, u32[]{:S(2)}, u32[]{:S(2)}) collective-permute-start(bf16[4,4,112,256]{3,2,1,0:T(8,128)(2,1)S(1)} %get-tuple-element.56), channel_id=1, source_target_pairs={{0,1},{1,0},{2,3},{3,2},{4,5},{5,4},{6,7},{7,6},{8,9},{9,8},{10,11... | collective-permute-start | bytes 2752520 | tf_op jit(solution)/shard_map/ppermute | solution.py:329
  64.4 5.3 %collective-permute-start.26 = (bf16[4,2,16,1024]{3,2,1,0:T(8,128)(2,1)S(1)}, bf16[4,2,16,1024]{3,2,1,0:T(8,128)(2,1)S(1)}, u32[]{:S(2)}, u32[]{:S(2)}) collective-permute-start(bf16[4,2,16,1024]{3,2,1,0:T(8,128)(2,1)S(1)} %get-tuple-element.63), channel_id=1, source_target_pairs={{0,1},{1,0},{2,3},{3,2},{4,5},{5,4},{6,7},{7,6},{8,9},{9,8},{10,11... | collective-permute-start | bytes 786440 | tf_op jit(solution)/shard_map/ppermute | solution.py:329
  66.6 12.6 %collective-permute-start.24 = (bf16[2,4,112,256]{3,2,1,0:T(8,128)(2,1)S(1)}, bf16[2,4,112,256]{3,2,1,0:T(8,128)(2,1)S(1)}, u32[]{:S(2)}, u32[]{:S(2)}) collective-permute-start(bf16[2,4,112,256]{3,2,1,0:T(8,128)(2,1)S(1)} %get-tuple-element.60), channel_id=1, source_target_pairs={{0,2},{1,3},{2,0},{3,1},{4,6},{5,7},{6,4},{7,5},{8,10},{9,11},{10,... | collective-permute-start | bytes 1376264 | tf_op jit(solution)/shard_map/ppermute | solution.py:329
  68.1 12.3 %collective-permute-start.25 = (bf16[2,4,112,256]{3,2,1,0:T(8,128)(2,1)S(1)}, bf16[2,4,112,256]{3,2,1,0:T(8,128)(2,1)S(1)}, u32[]{:S(2)}, u32[]{:S(2)}) collective-permute-start(bf16[2,4,112,256]{3,2,1,0:T(8,128)(2,1)S(1)} %get-tuple-element.61), channel_id=1, source_target_pairs={{0,4},{4,0},{8,12},{12,8},{16,20},{20,16},{24,28},{28,24},{1,5},{5... | collective-permute-start | bytes 1376264 | tf_op jit(solution)/shard_map/ppermute | solution.py:329
  69.8 10.8 %collective-permute-start.29 = (bf16[2,16,1024]{2,1,0:T(8,128)(2,1)S(1)}, bf16[2,16,1024]{2,1,0:T(8,128)(2,1)S(1)}, u32[]{:S(2)}, u32[]{:S(2)}) collective-permute-start(bf16[2,16,1024]{2,1,0:T(8,128)(2,1)S(1)} %get-tuple-element.78), channel_id=1, source_target_pairs={{0,24},{4,28},{8,16},{12,20},{16,8},{20,12},{24,0},{28,4},{1,25},{... | collective-permute-start | bytes 196616 | tf_op jit(solution)/shard_map/ppermute | solution.py:329
  71.9 8.7 %collective-permute-start.28 = (bf16[2,16,1024]{2,1,0:T(8,128)(2,1)S(1)}, bf16[2,16,1024]{2,1,0:T(8,128)(2,1)S(1)}, u32[]{:S(2)}, u32[]{:S(2)}) collective-permute-start(bf16[2,16,1024]{2,1,0:T(8,128)(2,1)S(1)} %get-tuple-element.79), channel_id=1, source_target_pairs={{0,16},{4,20},{8,24},{12,28},{16,0},{20,4},{24,8},{28,12},{1,17},{... | collective-permute-start | bytes 196616 | tf_op jit(solution)/shard_map/ppermute | solution.py:329
  71.9 8.7 %collective-permute-start.27 = (bf16[2,16,1024]{2,1,0:T(8,128)(2,1)S(1)}, bf16[2,16,1024]{2,1,0:T(8,128)(2,1)S(1)}, u32[]{:S(2)}, u32[]{:S(2)}) collective-permute-start(bf16[2,16,1024]{2,1,0:T(8,128)(2,1)S(1)} %get-tuple-element.80), channel_id=1, source_target_pairs={{0,8},{4,12},{8,0},{12,4},{16,24},{20,28},{24,16},{28,20},{1,9},{5... | collective-permute-start | bytes 196616 | tf_op jit(solution)/shard_map/ppermute | solution.py:329
  82.3 6.6 %collective-permute-start.30 = (bf16[4,112,256]{2,1,0:T(8,128)(2,1)S(1)}, bf16[4,112,256]{2,1,0:T(8,128)(2,1)S(1)}, u32[]{:S(2)}, u32[]{:S(2)}) collective-permute-start(bf16[4,112,256]{2,1,0:T(8,128)(2,1)S(1)} %get-tuple-element.64), channel_id=1, source_target_pairs={{0,4},{4,0},{8,12},{12,8},{16,20},{20,16},{24,28},{28,24},{1,5},{5... | collective-permute-start | bytes 688136 | tf_op jit(solution)/shard_map/ppermute | solution.py:329
  82.8 6.1 %collective-permute-start.31 = (bf16[4,112,256]{2,1,0:T(8,128)(2,1)S(1)}, bf16[4,112,256]{2,1,0:T(8,128)(2,1)S(1)}, u32[]{:S(2)}, u32[]{:S(2)}) collective-permute-start(bf16[4,112,256]{2,1,0:T(8,128)(2,1)S(1)} %get-tuple-element.65), channel_id=1, source_target_pairs={{0,2},{1,3},{2,0},{3,1},{4,6},{5,7},{6,4},{7,5},{8,10},{9,11},{10,... | collective-permute-start | bytes 688136 | tf_op jit(solution)/shard_map/ppermute | solution.py:329
  85.0 7.7 %collective-permute-start.36 = (bf16[16,512]{1,0:T(8,128)(2,1)S(1)}, bf16[16,512]{1,0:T(8,128)(2,1)S(1)}, u32[]{:S(2)}, u32[]{:S(2)}) collective-permute-start(bf16[16,512]{1,0:T(8,128)(2,1)S(1)} %pad_maximum_fusion.4), channel_id=1, source_target_pairs={{0,2},{1,3},{2,0},{3,1},{4,6},{5,7},{6,4},{7,5},{8,10},{9,11},{10,... | collective-permute-start | bytes 49160 | tf_op jit(solution)/shard_map/ppermute | solution.py:329
  89.2 6.2 %collective-permute-start.32 = (bf16[112,512]{1,0:T(8,128)(2,1)S(1)}, bf16[112,512]{1,0:T(8,128)(2,1)S(1)}, u32[]{:S(2)}, u32[]{:S(2)}) collective-permute-start(bf16[112,512]{1,0:T(8,128)(2,1)S(1)} %get-tuple-element.75), channel_id=1, source_target_pairs={{0,8},{4,12},{8,0},{12,4},{16,24},{20,28},{24,16},{28,20},{1,9},{5... | collective-permute-start | bytes 344072 | tf_op jit(solution)/shard_map/ppermute | solution.py:329
  89.8 7.8 %collective-permute-start.34 = (bf16[112,512]{1,0:T(8,128)(2,1)S(1)}, bf16[112,512]{1,0:T(8,128)(2,1)S(1)}, u32[]{:S(2)}, u32[]{:S(2)}) collective-permute-start(bf16[112,512]{1,0:T(8,128)(2,1)S(1)} %get-tuple-element.76), channel_id=1, source_target_pairs={{0,24},{4,28},{8,16},{12,20},{16,8},{20,12},{24,0},{28,4},{1,25},{... | collective-permute-start | bytes 344072 | tf_op jit(solution)/shard_map/ppermute | solution.py:329
  92.7 8.5 %collective-permute-start.33 = (bf16[112,512]{1,0:T(8,128)(2,1)S(1)}, bf16[112,512]{1,0:T(8,128)(2,1)S(1)}, u32[]{:S(2)}, u32[]{:S(2)}) collective-permute-start(bf16[112,512]{1,0:T(8,128)(2,1)S(1)} %get-tuple-element.77), channel_id=1, source_target_pairs={{0,16},{4,20},{8,24},{12,28},{16,0},{20,4},{24,8},{28,12},{1,17},{... | collective-permute-start | bytes 344072 | tf_op jit(solution)/shard_map/ppermute | solution.py:329
  (8 other events, 119.4 us)

commit v5 on v4

--- a/solution.py
+++ b/solution.py
@@ -9,7 +9,7 @@
 
 CAP = 12
 SLOTS = 16
-RING = 6
+RING = 8
 
 
 def contract(lhs, rhs, lhs_dim, rhs_dim):
@@ -163,6 +163,25 @@
     slots_src = exp_dev * SLOTS
     rep = lax.axis_index("rep")
     split = most_rows(tok_rows)
+    def in_copies(e):
+        at = lax.rem(e, RING)
+        return [
+            pltpu.make_async_copy(
+                src.at[e], w_in.at[at, pl.ds(i * hid_dev, hid_dev)], in_sems.at[i, at]
+            )
+            for i, src in enumerate((w_gate_hbm, w_up_hbm))
+        ]
+
+    def down_copy(e):
+        return pltpu.make_async_copy(w_down_hbm.at[e], w_down.at[e], down_sems.at[e])
+
+    def start_down(e, carry):
+        down_copy(e).start()
+        return carry
+
+    for e in range(min(RING, exp_dev)):
+        for copy in in_copies(e):
+            copy.start()
     tables = [
         pltpu.make_async_copy(picks_hbm, picks, table_sems.at[0]),
         pltpu.make_async_copy(weights_hbm, weights, table_sems.at[1]),
@@ -183,21 +202,6 @@
                     tok_sems.at[j],
                 ).start()
 
-    def in_copies(e):
-        at = lax.rem(e, RING)
-        return [
-            pltpu.make_async_copy(
-                src.at[e], w_in.at[at, pl.ds(i * hid_dev, hid_dev)], in_sems.at[i, at]
-            )
-            for i, src in enumerate((w_gate_hbm, w_up_hbm))
-        ]
-
-    def down_copy(e):
-        return pltpu.make_async_copy(w_down_hbm.at[e], w_down.at[e], down_sems.at[e])
-
-    for e in range(min(RING, exp_dev)):
-        for copy in in_copies(e):
-            copy.start()
     tables[1].start()
     quarters = [slice(2 * q * width, 2 * (q + 1) * width) for q in range(4)]
     tables[0].wait()
@@ -230,12 +234,15 @@
             act = gate_val / (1.0 + jnp.exp(-gate_val)) * up_val
             hidden[e] = act.T.astype(jnp.bfloat16)
         for e in experts:
-            down_copy(e).start()
 
             @pl.when(e + RING < exp_dev)
             def _():
                 for copy in in_copies(e + RING):
                     copy.start()
+
+        @pl.when(pair == max((exp_dev - RING) // 2 - 1, 0))
+        def _():
+            lax.fori_loop(0, exp_dev, start_down, 0)
 
         return carry
 
@@ -315,7 +322,7 @@
             pltpu.SemaphoreType.DMA((2, RING)),
             pltpu.SemaphoreType.DMA((exp_dev,)),
         ],
-        compiler_params=pltpu.CompilerParams(vmem_limit_bytes=42 * 1024 * 1024),
+        compiler_params=pltpu.CompilerParams(vmem_limit_bytes=46 * 1024 * 1024),
         cost_estimate=pl.CostEstimate(
             flops=6 * n_seq * SLOTS * exp_dev * hid_dev * model_width,
             bytes_accessed=6 * exp_dev * hid_dev * model_width + 4 * n_seq * own.size,
@@ -351,15 +358,15 @@
     y_one = swap(second, "seq", 1)
     y_two = swap(first, "seq", 1)
     x_one = swap(jnp.concatenate([first, from_y[None, :tok_rows, :width]]), "rep", 2)
-    to_y, to_core, to_core_y = lax.optimization_barrier((x_two, second, from_y))
+    to_y, to_core = lax.optimization_barrier((x_two, second))
     y_three = swap(to_y, "seq", 1)
-    early = [swap(piece, "rep", 1) for piece in (to_core, first, to_core_y)]
     below = [meta, from_y[tok_rows:, :tok_rows]]
     for d in range(n_z - 1):
         below += [second[d, tok_rows:, :tok_rows], y_one[d, tok_rows:, :tok_rows]]
     picks, weights = route(jnp.stack(below), exp_dev)
-    to_x, picks, weights = lax.optimization_barrier((y_two, picks, weights))
-    x_three = swap(to_x, "rep", 2)
+    to_core_y, picks, weights = lax.optimization_barrier((from_y, picks, weights))
+    early = [swap(piece, "rep", 1) for piece in (to_core, first, to_core_y)]
+    x_three = swap(y_two, "rep", 2)
     last = [x_two, y_one, x_one, y_two, y_three, x_three]
     pieces = [second, first, from_y, *last, *early, *[swap(piece, "rep", 1) for piece in last]]
 
@@ -389,7 +396,7 @@
     first = added(*[term[0] for term in near], by_x[0], first_far)
     second = added(*[term[2] for term in near], by_y[0], second_far)
     blocks = jnp.concatenate([first, second], axis=2)
-    most = [blocks[0]] + [swap(blocks[d], "seq", 2 * d) for d in others]
+    most = [swap(blocks[d], "seq", 2 * d) for d in reversed(others)] + [blocks[0]]
     rest = added(rest[0], *by_z)
     rest = added(rest[0], swap(rest[1], "seq", 1))
     far = jnp.concatenate([rest[:, :width], rest[:, 3 * width :]], axis=1)

time: 102 us -> 102 us (level)
  waiting for transfers between devices: 36.8 us -> 33.9 us
  Pallas kernels: 25.8 us -> 28.4 us
    ppermute x37, waiting for transfers between devices: 36.8 us -> 33.9 us  [swap(): return lax.ppermute(value, axis, [(i, i ^ distance) for i in range(size)])]
    pallas_call x1, Pallas kernels: 20.6 us -> 23.2 us  [moe_partial(): pl.pallas_call(functools.partial(moe_kernel, n_pieces), out_shape=outs, i...]
  transfers between devices with their start and end apart: 37 -> 37, of which waited for: 15 -> 16; matrix products, arithmetic and copies ran while one was open for 2% -> 2% of each run, Pallas kernels for 3% -> 3%
where the time goes in v5:
time: 102 us
  starting transfers between devices  36.8 us (36%)
  waiting for transfers between devices  33.9 us (33%)
  Pallas kernels  28.4 us (28%)
  other arithmetic  1.62 us (2%)
    ppermute x37, starting transfers between devices, swap(): return lax.ppermute(value, axis, [(i, i ^ distance) for i in range(size)])  36.8 us
    ppermute x37, waiting for transfers between devices, swap(): return lax.ppermute(value, axis, [(i, i ^ distance) for i in range(size)])  33.9 us
    pallas_call x1, Pallas kernels, moe_partial(): pl.pallas_call(functools.partial(moe_kernel, n_pieces), out_shape=outs, i...  23.2 us
    pallas_call x1, Pallas kernels, route(): pl.pallas_call(functools.partial(route_kernel, exp_dev), out_shape=[jax.S...  2.72 us
    pallas_call x1, Pallas kernels, norm_and_base(): pl.pallas_call(norm_kernel, out_shape=[jax.ShapeDtypeStruct((tok_rows, mo...  2.46 us
  transfers between devices with their start and end apart: 37, of which 16 were waited for; matrix products, arithmetic and copies ran while one was open for 2% of the time, Pallas kernels for 3%

profile of v5, /device:TPU:0, one launch (start us, length us, event | category | flops | bytes accessed | tf_op | source)
XLA Modules:
  0.0 101.7 jit_solution(17779205606089147176)
XLA Ops:
  0.0 2.5 %shard_map.82 = (bf16[128,2048]{1,0:T(8,128)(2,1)}, bf16[144,256]{1,0:T(8,128)(2,1)}, bf16[128,256]{1,0:T(8,128)(2,1)}, bf16[144,768]{1,0:T(8,128)(2,1)}, f32[1,...) custom-call(bf16[128,2048]{1,0:T(8,128)(2,1)} %tokens_ref.1, f32[1,2048]{1,0:T(1,128)} %bitcast.66, ...), custom_call_target="tpu_custom_call" | custom-call | tf_op jit(solution)/shard_map/pallas_call | solution.py:75
  2.5 5.1 %collective-permute-start.2 = (bf16[144,256]{1,0:T(8,128)(2,1)}, bf16[144,256]{1,0:T(8,128)(2,1)S(1)}, u32[]{:S(2)}, u32[]{:S(2)}) collective-permute-start(bf16[144,256]{1,0:T(8,128)(2,1)} %get-tuple-element.38), channel_id=1, source_target_pairs={{0,24},{4,28},{8,16},{12,20},{16,8},{20,12},{24,0},{28,4},{1,25},{... | collective-permute-start | bytes 221192 | tf_op jit(solution)/shard_map/ppermute | solution.py:336
  8.2 1.7 %collective-permute-start.3 = (bf16[144,768]{1,0:T(8,128)(2,1)}, bf16[144,768]{1,0:T(8,128)(2,1)S(1)}, u32[]{:S(2)}, u32[]{:S(2)}) collective-permute-start(bf16[144,768]{1,0:T(8,128)(2,1)} %get-tuple-element.39), channel_id=1, source_target_pairs={{0,4},{4,0},{8,12},{12,8},{16,20},{20,16},{24,28},{28,24},{1,5},{5... | collective-permute-start | bytes 663560 | tf_op jit(solution)/shard_map/ppermute | solution.py:336
  10.5 3.4 %collective-permute-done.1 = bf16[144,256]{1,0:T(8,128)(2,1)S(1)} collective-permute-done((bf16[144,256]{1,0:T(8,128)(2,1)}, bf16[144,256]{1,0:T(8,128)(2,1)S(1)}, u32[]{:S(2)}, u32[]{:S(2)}) %collective-permute-start.1) | collective-permute-done | bytes 73760 | tf_op jit(solution)/shard_map/ppermute | solution.py:336
  14.0 1.0 collective-permute-done.3.refs_6_
  15.0 3.5 %collective-permute-start.7 = (bf16[128,256]{1,0:T(8,128)(2,1)}, bf16[128,256]{1,0:T(8,128)(2,1)S(1)}, u32[]{:S(2)}, u32[]{:S(2)}) collective-permute-start(bf16[128,256]{1,0:T(8,128)(2,1)} %get-tuple-element.49), channel_id=1, source_target_pairs={{0,24},{4,28},{8,16},{12,20},{16,8},{20,12},{24,0},{28,4},{1,25},{... | collective-permute-start | bytes 196616 | tf_op jit(solution)/shard_map/ppermute | solution.py:336
  18.5 0.9 collective-permute-start.5
  19.4 1.6 %collective-permute-start.4 = (bf16[3,144,256]{2,1,0:T(8,128)(2,1)S(1)}, bf16[3,144,256]{2,1,0:T(8,128)(2,1)S(1)}, u32[]{:S(2)}, u32[]{:S(2)}) collective-permute-start(bf16[3,144,256]{2,1,0:T(8,128)(2,1)S(1)} %pad_maximum_fusion.1.refs_4_), channel_id=1, source_target_pairs={{0,4},{4,0},{8,12},{12,8},{16,20},{20,16},{24,28},{28,24},{1,5},{5... | collective-permute-start | bytes 663560 | tf_op jit(solution)/shard_map/ppermute | solution.py:336
  21.0 1.6 %collective-permute-start.8 = (bf16[3,128,256]{2,1,0:T(8,128)(2,1)S(1)}, bf16[3,128,256]{2,1,0:T(8,128)(2,1)S(1)}, u32[]{:S(2)}, u32[]{:S(2)}) collective-permute-start(bf16[3,128,256]{2,1,0:T(8,128)(2,1)S(1)} %slice.121), channel_id=1, source_target_pairs={{0,2},{1,3},{2,0},{3,1},{4,6},{5,7},{6,4},{7,5},{8,10},{9,11},{10,... | collective-permute-start | bytes 589832 | tf_op jit(solution)/shard_map/ppermute | solution.py:336
  22.6 1.3 %collective-permute-done.6 = bf16[128,256]{1,0:T(8,128)(2,1)S(1)} collective-permute-done((bf16[128,256]{1,0:T(8,128)(2,1)}, bf16[128,256]{1,0:T(8,128)(2,1)S(1)}, u32[]{:S(2)}, u32[]{:S(2)}) %collective-permute-start.6) | collective-permute-done | bytes 65568 | tf_op jit(solution)/shard_map/ppermute | solution.py:336
  23.9 1.6 %collective-permute-start.10 = (bf16[3,128,256]{2,1,0:T(8,128)(2,1)S(1)}, bf16[3,128,256]{2,1,0:T(8,128)(2,1)S(1)}, u32[]{:S(2)}, u32[]{:S(2)}) collective-permute-start(bf16[3,128,256]{2,1,0:T(8,128)(2,1)S(1)} %pad_maximum_fusion.2.refs_5_), channel_id=1, source_target_pairs={{0,4},{4,0},{8,12},{12,8},{16,20},{20,16},{24,28},{28,24},{1,5},{5... | collective-permute-start | bytes 589832 | tf_op jit(solution)/shard_map/ppermute | solution.py:336
  25.6 1.6 %collective-permute-start.9 = (bf16[4,128,256]{2,1,0:T(8,128)(2,1)S(1)}, bf16[4,128,256]{2,1,0:T(8,128)(2,1)S(1)}, u32[]{:S(2)}, u32[]{:S(2)}) collective-permute-start(bf16[4,128,256]{2,1,0:T(8,128)(2,1)S(1)} %pad_maximum_fusion), channel_id=1, source_target_pairs={{0,2},{1,3},{2,0},{3,1},{4,6},{5,7},{6,4},{7,5},{8,10},{9,11},{10,... | collective-permute-start | bytes 786440 | tf_op jit(solution)/shard_map/ppermute | solution.py:336
  28.3 3.4 %collective-permute-done.10.refs_10_ = bf16[3,128,256]{2,1,0:T(8,128)(2,1)S(1)} collective-permute-done((bf16[3,128,256]{2,1,0:T(8,128)(2,1)S(1)}, bf16[3,128,256]{2,1,0:T(8,128)(2,1)S(1)}, u32[]{:S(2)}, u32[]{:S(2)}) %collective-permute-start.10) | collective-permute-done | bytes 196640 | tf_op jit(solution)/shard_map/ppermute | solution.py:336
  31.7 2.3 %collective-permute-done.9.refs_9_ = bf16[4,128,256]{2,1,0:T(8,128)(2,1)S(1)} collective-permute-done((bf16[4,128,256]{2,1,0:T(8,128)(2,1)S(1)}, bf16[4,128,256]{2,1,0:T(8,128)(2,1)S(1)}, u32[]{:S(2)}, u32[]{:S(2)}) %collective-permute-start.9) | collective-permute-done | bytes 262176 | tf_op jit(solution)/shard_map/ppermute | solution.py:336
  34.0 1.5 %collective-permute-start.12 = (bf16[3,128,256]{2,1,0:T(8,128)(2,1)S(1)}, bf16[3,128,256]{2,1,0:T(8,128)(2,1)S(1)}, u32[]{:S(2)}, u32[]{:S(2)}) collective-permute-start(bf16[3,128,256]{2,1,0:T(8,128)(2,1)S(1)} %collective-permute-done.10.refs_10_), channel_id=1, source_target_pairs={{0,2},{1,3},{2,0},{3,1},{4,6},{5,7},{6,4},{7,5},{8,10},{9,11},{10,... | collective-permute-start | bytes 589832 | tf_op jit(solution)/shard_map/ppermute | solution.py:336
  35.5 2.7 %shard_map.83 = (bf16[8,256,128]{2,1,0:T(8,128)(2,1)}, bf16[8,128,256]{2,1,0:T(8,128)(2,1)}) custom-call(bf16[8,16,128]{2,1,0:T(8,128)(2,1)} %copy-done.2), custom_call_target="tpu_custom_call" | custom-call | flops 4000000000 | bytes 2097152 | tf_op jit(solution)/shard_map/pallas_call | solution.py:133
  39.3 0.9 collective-permute-done.12.refs_12_
  40.5 1.1 %collective-permute-done.21.refs_21_ = bf16[3,128,256]{2,1,0:T(8,128)(2,1)S(1)} collective-permute-done((bf16[3,128,256]{2,1,0:T(8,128)(2,1)S(1)}, bf16[3,128,256]{2,1,0:T(8,128)(2,1)S(1)}, u32[]{:S(2)}, u32[]{:S(2)}) %collective-permute-start.21) | collective-permute-done | bytes 196640 | tf_op jit(solution)/shard_map/ppermute | solution.py:336
  41.6 23.2 %shard_map.84 = (bf16[4,4,112,256]{3,2,1,0:T(8,128)(2,1)S(1)}, bf16[4,4,112,256]{3,2,1,0:T(8,128)(2,1)S(1)}, bf16[4,2,16,1024]{3,2,1,0:T(8,128)(2,1)S(1)}, bf16[...) custom-call(bf16[8,256,128]{2,1,0:T(8,128)(2,1)} %get-tuple-element.45.re, ...), custom_call_target="tpu_custom_call" | custom-call | flops 4831838208 | bytes 46137344 | tf_op jit(solution)/shard_map/pallas_call | solution.py:306
  65.5 1.8 %collective-permute-done.23 = bf16[4,4,112,256]{3,2,1,0:T(8,128)(2,1)S(1)} collective-permute-done((bf16[4,4,112,256]{3,2,1,0:T(8,128)(2,1)S(1)}, bf16[4,4,112,256]{3,2,1,0:T(8,128)(2,1)S(1)}, u32[]{:S(2)}, u32[]{:S(2)}) %collective-permute-start.23) | collective-permute-done | bytes 917536 | tf_op jit(solution)/shard_map/ppermute | solution.py:336
  67.6 1.5 %collective-permute-start.24 = (bf16[2,4,112,256]{3,2,1,0:T(8,128)(2,1)S(1)}, bf16[2,4,112,256]{3,2,1,0:T(8,128)(2,1)S(1)}, u32[]{:S(2)}, u32[]{:S(2)}) collective-permute-start(bf16[2,4,112,256]{3,2,1,0:T(8,128)(2,1)S(1)} %get-tuple-element.58), channel_id=1, source_target_pairs={{0,2},{1,3},{2,0},{3,1},{4,6},{5,7},{6,4},{7,5},{8,10},{9,11},{10,... | collective-permute-start | bytes 1376264 | tf_op jit(solution)/shard_map/ppermute | solution.py:336
  69.9 2.1 %collective-permute-start.29 = (bf16[2,16,1024]{2,1,0:T(8,128)(2,1)S(1)}, bf16[2,16,1024]{2,1,0:T(8,128)(2,1)S(1)}, u32[]{:S(2)}, u32[]{:S(2)}) collective-permute-start(bf16[2,16,1024]{2,1,0:T(8,128)(2,1)S(1)} %get-tuple-element.76), channel_id=1, source_target_pairs={{0,24},{4,28},{8,16},{12,20},{16,8},{20,12},{24,0},{28,4},{1,25},{... | collective-permute-start | bytes 196616 | tf_op jit(solution)/shard_map/ppermute | solution.py:336
  72.0 2.3 %collective-permute-start.27 = (bf16[2,16,1024]{2,1,0:T(8,128)(2,1)S(1)}, bf16[2,16,1024]{2,1,0:T(8,128)(2,1)S(1)}, u32[]{:S(2)}, u32[]{:S(2)}) collective-permute-start(bf16[2,16,1024]{2,1,0:T(8,128)(2,1)S(1)} %get-tuple-element.78), channel_id=1, source_target_pairs={{0,8},{4,12},{8,0},{12,4},{16,24},{20,28},{24,16},{28,20},{1,9},{5... | collective-permute-start | bytes 196616 | tf_op jit(solution)/shard_map/ppermute | solution.py:336
  74.4 5.9 %collective-permute-done.24 = bf16[2,4,112,256]{3,2,1,0:T(8,128)(2,1)S(1)} collective-permute-done((bf16[2,4,112,256]{3,2,1,0:T(8,128)(2,1)S(1)}, bf16[2,4,112,256]{3,2,1,0:T(8,128)(2,1)S(1)}, u32[]{:S(2)}, u32[]{:S(2)}) %collective-permute-start.24) | collective-permute-done | bytes 458784 | tf_op jit(solution)/shard_map/ppermute | solution.py:336
  80.2 1.2 %collective-permute-done.25 = bf16[2,4,112,256]{3,2,1,0:T(8,128)(2,1)S(1)} collective-permute-done((bf16[2,4,112,256]{3,2,1,0:T(8,128)(2,1)S(1)}, bf16[2,4,112,256]{3,2,1,0:T(8,128)(2,1)S(1)}, u32[]{:S(2)}, u32[]{:S(2)}) %collective-permute-start.25) | collective-permute-done | bytes 458784 | tf_op jit(solution)/shard_map/ppermute | solution.py:336
  82.5 1.2 %collective-permute-start.30 = (bf16[4,112,256]{2,1,0:T(8,128)(2,1)S(1)}, bf16[4,112,256]{2,1,0:T(8,128)(2,1)S(1)}, u32[]{:S(2)}, u32[]{:S(2)}) collective-permute-start(bf16[4,112,256]{2,1,0:T(8,128)(2,1)S(1)} %get-tuple-element.62), channel_id=1, source_target_pairs={{0,4},{4,0},{8,12},{12,8},{16,20},{20,16},{24,28},{28,24},{1,5},{5... | collective-permute-start | bytes 688136 | tf_op jit(solution)/shard_map/ppermute | solution.py:336
  84.3 1.7 %collective-permute-done.35 = bf16[16,1024]{1,0:T(8,128)(2,1)S(1)} collective-permute-done((bf16[16,1024]{1,0:T(8,128)(2,1)S(1)}, bf16[16,1024]{1,0:T(8,128)(2,1)S(1)}, u32[]{:S(2)}, u32[]{:S(2)}) %collective-permute-start.35) | collective-permute-done | bytes 32800 | tf_op jit(solution)/shard_map/ppermute | solution.py:336
  86.7 2.6 %collective-permute-done.30 = bf16[4,112,256]{2,1,0:T(8,128)(2,1)S(1)} collective-permute-done((bf16[4,112,256]{2,1,0:T(8,128)(2,1)S(1)}, bf16[4,112,256]{2,1,0:T(8,128)(2,1)S(1)}, u32[]{:S(2)}, u32[]{:S(2)}) %collective-permute-start.30) | collective-permute-done | bytes 229408 | tf_op jit(solution)/shard_map/ppermute | solution.py:336
  90.1 2.1 %collective-permute-start.32 = (bf16[112,512]{1,0:T(8,128)(2,1)S(1)}, bf16[112,512]{1,0:T(8,128)(2,1)S(1)}, u32[]{:S(2)}, u32[]{:S(2)}) collective-permute-start(bf16[112,512]{1,0:T(8,128)(2,1)S(1)} %get-tuple-element.73), channel_id=1, source_target_pairs={{0,24},{4,28},{8,16},{12,20},{16,8},{20,12},{24,0},{28,4},{1,25},{... | collective-permute-start | bytes 344072 | tf_op jit(solution)/shard_map/ppermute | solution.py:336
  92.3 2.3 %collective-permute-start.34 = (bf16[112,512]{1,0:T(8,128)(2,1)S(1)}, bf16[112,512]{1,0:T(8,128)(2,1)S(1)}, u32[]{:S(2)}, u32[]{:S(2)}) collective-permute-start(bf16[112,512]{1,0:T(8,128)(2,1)S(1)} %get-tuple-element.75), channel_id=1, source_target_pairs={{0,8},{4,12},{8,0},{12,4},{16,24},{20,28},{24,16},{28,20},{1,9},{5... | collective-permute-start | bytes 344072 | tf_op jit(solution)/shard_map/ppermute | solution.py:336
  94.6 2.8 %collective-permute-done.32 = bf16[112,512]{1,0:T(8,128)(2,1)S(1)} collective-permute-done((bf16[112,512]{1,0:T(8,128)(2,1)S(1)}, bf16[112,512]{1,0:T(8,128)(2,1)S(1)}, u32[]{:S(2)}, u32[]{:S(2)}) %collective-permute-start.32) | collective-permute-done | bytes 114720 | tf_op jit(solution)/shard_map/ppermute | solution.py:336
  97.4 3.5 %collective-permute-done.33 = bf16[112,512]{1,0:T(8,128)(2,1)S(1)} collective-permute-done((bf16[112,512]{1,0:T(8,128)(2,1)S(1)}, bf16[112,512]{1,0:T(8,128)(2,1)S(1)}, u32[]{:S(2)}, u32[]{:S(2)}) %collective-permute-start.33) | collective-permute-done | bytes 114720 | tf_op jit(solution)/shard_map/ppermute | solution.py:336
  (78 shorter events, 9.7 us)
Async XLA Ops:
  2.5 8.1 %collective-permute-start.2 = (bf16[144,256]{1,0:T(8,128)(2,1)}, bf16[144,256]{1,0:T(8,128)(2,1)S(1)}, u32[]{:S(2)}, u32[]{:S(2)}) collective-permute-start(bf16[144,256]{1,0:T(8,128)(2,1)} %get-tuple-element.38), channel_id=1, source_target_pairs={{0,24},{4,28},{8,16},{12,20},{16,8},{20,12},{24,0},{28,4},{1,25},{... | collective-permute-start | bytes 221192 | tf_op jit(solution)/shard_map/ppermute | solution.py:336
  7.5 6.4 %collective-permute-start.1 = (bf16[144,256]{1,0:T(8,128)(2,1)}, bf16[144,256]{1,0:T(8,128)(2,1)S(1)}, u32[]{:S(2)}, u32[]{:S(2)}) collective-permute-start(bf16[144,256]{1,0:T(8,128)(2,1)} %get-tuple-element.38), channel_id=1, source_target_pairs={{0,16},{4,20},{8,24},{12,28},{16,0},{20,4},{24,8},{28,12},{1,17},{... | collective-permute-start | bytes 221192 | tf_op jit(solution)/shard_map/ppermute | solution.py:336
  7.5 6.4 %collective-permute-start = (bf16[144,256]{1,0:T(8,128)(2,1)}, bf16[144,256]{1,0:T(8,128)(2,1)S(1)}, u32[]{:S(2)}, u32[]{:S(2)}) collective-permute-start(bf16[144,256]{1,0:T(8,128)(2,1)} %get-tuple-element.38), channel_id=1, source_target_pairs={{0,8},{4,12},{8,0},{12,4},{16,24},{20,28},{24,16},{28,20},{1,9},{5... | collective-permute-start | bytes 221192 | tf_op jit(solution)/shard_map/ppermute | solution.py:336
  8.2 6.8 %collective-permute-start.3 = (bf16[144,768]{1,0:T(8,128)(2,1)}, bf16[144,768]{1,0:T(8,128)(2,1)S(1)}, u32[]{:S(2)}, u32[]{:S(2)}) collective-permute-start(bf16[144,768]{1,0:T(8,128)(2,1)} %get-tuple-element.39), channel_id=1, source_target_pairs={{0,4},{4,0},{8,12},{12,8},{16,20},{20,16},{24,28},{28,24},{1,5},{5... | collective-permute-start | bytes 663560 | tf_op jit(solution)/shard_map/ppermute | solution.py:336
  15.0 7.6 %collective-permute-start.7 = (bf16[128,256]{1,0:T(8,128)(2,1)}, bf16[128,256]{1,0:T(8,128)(2,1)S(1)}, u32[]{:S(2)}, u32[]{:S(2)}) collective-permute-start(bf16[128,256]{1,0:T(8,128)(2,1)} %get-tuple-element.49), channel_id=1, source_target_pairs={{0,24},{4,28},{8,16},{12,20},{16,8},{20,12},{24,0},{28,4},{1,25},{... | collective-permute-start | bytes 196616 | tf_op jit(solution)/shard_map/ppermute | solution.py:336
  18.5 5.4 %collective-permute-start.6 = (bf16[128,256]{1,0:T(8,128)(2,1)}, bf16[128,256]{1,0:T(8,128)(2,1)S(1)}, u32[]{:S(2)}, u32[]{:S(2)}) collective-permute-start(bf16[128,256]{1,0:T(8,128)(2,1)} %get-tuple-element.49), channel_id=1, source_target_pairs={{0,16},{4,20},{8,24},{12,28},{16,0},{20,4},{24,8},{28,12},{1,17},{... | collective-permute-start | bytes 196616 | tf_op jit(solution)/shard_map/ppermute | solution.py:336
  18.5 5.4 %collective-permute-start.5 = (bf16[128,256]{1,0:T(8,128)(2,1)}, bf16[128,256]{1,0:T(8,128)(2,1)S(1)}, u32[]{:S(2)}, u32[]{:S(2)}) collective-permute-start(bf16[128,256]{1,0:T(8,128)(2,1)} %get-tuple-element.49), channel_id=1, source_target_pairs={{0,8},{4,12},{8,0},{12,4},{16,24},{20,28},{24,16},{28,20},{1,9},{5... | collective-permute-start | bytes 196616 | tf_op jit(solution)/shard_map/ppermute | solution.py:336
  19.4 8.2 %collective-permute-start.4 = (bf16[3,144,256]{2,1,0:T(8,128)(2,1)S(1)}, bf16[3,144,256]{2,1,0:T(8,128)(2,1)S(1)}, u32[]{:S(2)}, u32[]{:S(2)}) collective-permute-start(bf16[3,144,256]{2,1,0:T(8,128)(2,1)S(1)} %pad_maximum_fusion.1.refs_4_), channel_id=1, source_target_pairs={{0,4},{4,0},{8,12},{12,8},{16,20},{20,16},{24,28},{28,24},{1,5},{5... | collective-permute-start | bytes 663560 | tf_op jit(solution)/shard_map/ppermute | solution.py:336
  21.0 6.1 %collective-permute-start.8 = (bf16[3,128,256]{2,1,0:T(8,128)(2,1)S(1)}, bf16[3,128,256]{2,1,0:T(8,128)(2,1)S(1)}, u32[]{:S(2)}, u32[]{:S(2)}) collective-permute-start(bf16[3,128,256]{2,1,0:T(8,128)(2,1)S(1)} %slice.121), channel_id=1, source_target_pairs={{0,2},{1,3},{2,0},{3,1},{4,6},{5,7},{6,4},{7,5},{8,10},{9,11},{10,... | collective-permute-start | bytes 589832 | tf_op jit(solution)/shard_map/ppermute | solution.py:336
  23.9 3.8 %collective-permute-start.14 = (bf16[3,128,256]{2,1,0:T(8,128)(2,1)S(1)}, bf16[3,128,256]{2,1,0:T(8,128)(2,1)S(1)}, u32[]{:S(2)}, u32[]{:S(2)}) collective-permute-start(bf16[3,128,256]{2,1,0:T(8,128)(2,1)S(1)} %pad_maximum_fusion.2.refs_5_), channel_id=1, source_target_pairs={{0,1},{1,0},{2,3},{3,2},{4,5},{5,4},{6,7},{7,6},{8,9},{9,8},{10,11... | collective-permute-start | bytes 589832 | tf_op jit(solution)/shard_map/ppermute | solution.py:336
  23.9 7.8 %collective-permute-start.10 = (bf16[3,128,256]{2,1,0:T(8,128)(2,1)S(1)}, bf16[3,128,256]{2,1,0:T(8,128)(2,1)S(1)}, u32[]{:S(2)}, u32[]{:S(2)}) collective-permute-start(bf16[3,128,256]{2,1,0:T(8,128)(2,1)S(1)} %pad_maximum_fusion.2.refs_5_), channel_id=1, source_target_pairs={{0,4},{4,0},{8,12},{12,8},{16,20},{20,16},{24,28},{28,24},{1,5},{5... | collective-permute-start | bytes 589832 | tf_op jit(solution)/shard_map/ppermute | solution.py:336
  25.6 8.4 %collective-permute-start.9 = (bf16[4,128,256]{2,1,0:T(8,128)(2,1)S(1)}, bf16[4,128,256]{2,1,0:T(8,128)(2,1)S(1)}, u32[]{:S(2)}, u32[]{:S(2)}) collective-permute-start(bf16[4,128,256]{2,1,0:T(8,128)(2,1)S(1)} %pad_maximum_fusion), channel_id=1, source_target_pairs={{0,2},{1,3},{2,0},{3,1},{4,6},{5,7},{6,4},{7,5},{8,10},{9,11},{10,... | collective-permute-start | bytes 786440 | tf_op jit(solution)/shard_map/ppermute | solution.py:336
  27.1 8.4 %collective-permute-start.11 = (bf16[3,128,256]{2,1,0:T(8,128)(2,1)S(1)}, bf16[3,128,256]{2,1,0:T(8,128)(2,1)S(1)}, u32[]{:S(2)}, u32[]{:S(2)}) collective-permute-start(bf16[3,128,256]{2,1,0:T(8,128)(2,1)S(1)} %collective-permute-done.8.refs_7_), channel_id=1, source_target_pairs={{0,4},{4,0},{8,12},{12,8},{16,20},{20,16},{24,28},{28,24},{1,5},{5... | collective-permute-start | bytes 589832 | tf_op jit(solution)/shard_map/ppermute | solution.py:336
  27.6 11.1 %collective-permute-start.13 = (bf16[3,144,256]{2,1,0:T(8,128)(2,1)S(1)}, bf16[3,144,256]{2,1,0:T(8,128)(2,1)S(1)}, u32[]{:S(2)}, u32[]{:S(2)}) collective-permute-start(bf16[3,144,256]{2,1,0:T(8,128)(2,1)S(1)} %pad_maximum_fusion.1.refs_4_), channel_id=1, source_target_pairs={{0,1},{1,0},{2,3},{3,2},{4,5},{5,4},{6,7},{7,6},{8,9},{9,8},{10,11... | collective-permute-start | bytes 663560 | tf_op jit(solution)/shard_map/ppermute | solution.py:336
  27.7 10.5 %collective-permute-start.16 = (bf16[3,128,256]{2,1,0:T(8,128)(2,1)S(1)}, bf16[3,128,256]{2,1,0:T(8,128)(2,1)S(1)}, u32[]{:S(2)}, u32[]{:S(2)}) collective-permute-start(bf16[3,128,256]{2,1,0:T(8,128)(2,1)S(1)} %collective-permute-done.8.refs_7_), channel_id=1, source_target_pairs={{0,1},{1,0},{2,3},{3,2},{4,5},{5,4},{6,7},{7,6},{8,9},{9,8},{10,11... | collective-permute-start | bytes 589832 | tf_op jit(solution)/shard_map/ppermute | solution.py:336
  31.7 7.1 %collective-permute-start.17 = (bf16[3,144,256]{2,1,0:T(8,128)(2,1)S(1)}, bf16[3,144,256]{2,1,0:T(8,128)(2,1)S(1)}, u32[]{:S(2)}, u32[]{:S(2)}) collective-permute-start(bf16[3,144,256]{2,1,0:T(8,128)(2,1)S(1)} %collective-permute-done.4.refs_8_), channel_id=1, source_target_pairs={{0,1},{1,0},{2,3},{3,2},{4,5},{5,4},{6,7},{7,6},{8,9},{9,8},{10,11... | collective-permute-start | bytes 663560 | tf_op jit(solution)/shard_map/ppermute | solution.py:336
  34.0 6.1 %collective-permute-start.12 = (bf16[3,128,256]{2,1,0:T(8,128)(2,1)S(1)}, bf16[3,128,256]{2,1,0:T(8,128)(2,1)S(1)}, u32[]{:S(2)}, u32[]{:S(2)}) collective-permute-start(bf16[3,128,256]{2,1,0:T(8,128)(2,1)S(1)} %collective-permute-done.10.refs_10_), channel_id=1, source_target_pairs={{0,2},{1,3},{2,0},{3,1},{4,6},{5,7},{6,4},{7,5},{8,10},{9,11},{10,... | collective-permute-start | bytes 589832 | tf_op jit(solution)/shard_map/ppermute | solution.py:336
  35.5 5.0 %collective-permute-start.18 = (bf16[4,128,256]{2,1,0:T(8,128)(2,1)S(1)}, bf16[4,128,256]{2,1,0:T(8,128)(2,1)S(1)}, u32[]{:S(2)}, u32[]{:S(2)}) collective-permute-start(bf16[4,128,256]{2,1,0:T(8,128)(2,1)S(1)} %collective-permute-done.9.refs_9_), channel_id=1, source_target_pairs={{0,1},{1,0},{2,3},{3,2},{4,5},{5,4},{6,7},{7,6},{8,9},{9,8},{10,11... | collective-permute-start | bytes 786440 | tf_op jit(solution)/shard_map/ppermute | solution.py:336
  65.0 7.0 %collective-permute-start.22 = (bf16[4,4,112,256]{3,2,1,0:T(8,128)(2,1)S(1)}, bf16[4,4,112,256]{3,2,1,0:T(8,128)(2,1)S(1)}, u32[]{:S(2)}, u32[]{:S(2)}) collective-permute-start(bf16[4,4,112,256]{3,2,1,0:T(8,128)(2,1)S(1)} %get-tuple-element.54), channel_id=1, source_target_pairs={{0,1},{1,0},{2,3},{3,2},{4,5},{5,4},{6,7},{7,6},{8,9},{9,8},{10,11... | collective-permute-start | bytes 2752520 | tf_op jit(solution)/shard_map/ppermute | solution.py:336
  65.4 4.4 %collective-permute-start.26 = (bf16[4,2,16,1024]{3,2,1,0:T(8,128)(2,1)S(1)}, bf16[4,2,16,1024]{3,2,1,0:T(8,128)(2,1)S(1)}, u32[]{:S(2)}, u32[]{:S(2)}) collective-permute-start(bf16[4,2,16,1024]{3,2,1,0:T(8,128)(2,1)S(1)} %get-tuple-element.61), channel_id=1, source_target_pairs={{0,1},{1,0},{2,3},{3,2},{4,5},{5,4},{6,7},{7,6},{8,9},{9,8},{10,11... | collective-permute-start | bytes 786440 | tf_op jit(solution)/shard_map/ppermute | solution.py:336
  67.6 12.6 %collective-permute-start.24 = (bf16[2,4,112,256]{3,2,1,0:T(8,128)(2,1)S(1)}, bf16[2,4,112,256]{3,2,1,0:T(8,128)(2,1)S(1)}, u32[]{:S(2)}, u32[]{:S(2)}) collective-permute-start(bf16[2,4,112,256]{3,2,1,0:T(8,128)(2,1)S(1)} %get-tuple-element.58), channel_id=1, source_target_pairs={{0,2},{1,3},{2,0},{3,1},{4,6},{5,7},{6,4},{7,5},{8,10},{9,11},{10,... | collective-permute-start | bytes 1376264 | tf_op jit(solution)/shard_map/ppermute | solution.py:336
  69.1 12.3 %collective-permute-start.25 = (bf16[2,4,112,256]{3,2,1,0:T(8,128)(2,1)S(1)}, bf16[2,4,112,256]{3,2,1,0:T(8,128)(2,1)S(1)}, u32[]{:S(2)}, u32[]{:S(2)}) collective-permute-start(bf16[2,4,112,256]{3,2,1,0:T(8,128)(2,1)S(1)} %get-tuple-element.59), channel_id=1, source_target_pairs={{0,4},{4,0},{8,12},{12,8},{16,20},{20,16},{24,28},{28,24},{1,5},{5... | collective-permute-start | bytes 1376264 | tf_op jit(solution)/shard_map/ppermute | solution.py:336
  69.9 11.7 %collective-permute-start.29 = (bf16[2,16,1024]{2,1,0:T(8,128)(2,1)S(1)}, bf16[2,16,1024]{2,1,0:T(8,128)(2,1)S(1)}, u32[]{:S(2)}, u32[]{:S(2)}) collective-permute-start(bf16[2,16,1024]{2,1,0:T(8,128)(2,1)S(1)} %get-tuple-element.76), channel_id=1, source_target_pairs={{0,24},{4,28},{8,16},{12,20},{16,8},{20,12},{24,0},{28,4},{1,25},{... | collective-permute-start | bytes 196616 | tf_op jit(solution)/shard_map/ppermute | solution.py:336
  72.0 9.6 %collective-permute-start.28 = (bf16[2,16,1024]{2,1,0:T(8,128)(2,1)S(1)}, bf16[2,16,1024]{2,1,0:T(8,128)(2,1)S(1)}, u32[]{:S(2)}, u32[]{:S(2)}) collective-permute-start(bf16[2,16,1024]{2,1,0:T(8,128)(2,1)S(1)} %get-tuple-element.77), channel_id=1, source_target_pairs={{0,16},{4,20},{8,24},{12,28},{16,0},{20,4},{24,8},{28,12},{1,17},{... | collective-permute-start | bytes 196616 | tf_op jit(solution)/shard_map/ppermute | solution.py:336
  72.0 9.6 %collective-permute-start.27 = (bf16[2,16,1024]{2,1,0:T(8,128)(2,1)S(1)}, bf16[2,16,1024]{2,1,0:T(8,128)(2,1)S(1)}, u32[]{:S(2)}, u32[]{:S(2)}) collective-permute-start(bf16[2,16,1024]{2,1,0:T(8,128)(2,1)S(1)} %get-tuple-element.78), channel_id=1, source_target_pairs={{0,8},{4,12},{8,0},{12,4},{16,24},{20,28},{24,16},{28,20},{1,9},{5... | collective-permute-start | bytes 196616 | tf_op jit(solution)/shard_map/ppermute | solution.py:336
  81.7 4.4 %collective-permute-start.35 = (bf16[16,1024]{1,0:T(8,128)(2,1)S(1)}, bf16[16,1024]{1,0:T(8,128)(2,1)S(1)}, u32[]{:S(2)}, u32[]{:S(2)}) collective-permute-start(bf16[16,1024]{1,0:T(8,128)(2,1)S(1)} %slice_bitcast_fusion.5), channel_id=1, source_target_pairs={{0,4},{4,0},{8,12},{12,8},{16,20},{20,16},{24,28},{28,24},{1,5},{5... | collective-permute-start | bytes 98312 | tf_op jit(solution)/shard_map/ppermute | solution.py:336
  82.5 6.7 %collective-permute-start.30 = (bf16[4,112,256]{2,1,0:T(8,128)(2,1)S(1)}, bf16[4,112,256]{2,1,0:T(8,128)(2,1)S(1)}, u32[]{:S(2)}, u32[]{:S(2)}) collective-permute-start(bf16[4,112,256]{2,1,0:T(8,128)(2,1)S(1)} %get-tuple-element.62), channel_id=1, source_target_pairs={{0,4},{4,0},{8,12},{12,8},{16,20},{20,16},{24,28},{28,24},{1,5},{5... | collective-permute-start | bytes 688136 | tf_op jit(solution)/shard_map/ppermute | solution.py:336
  83.8 6.1 %collective-permute-start.31 = (bf16[4,112,256]{2,1,0:T(8,128)(2,1)S(1)}, bf16[4,112,256]{2,1,0:T(8,128)(2,1)S(1)}, u32[]{:S(2)}, u32[]{:S(2)}) collective-permute-start(bf16[4,112,256]{2,1,0:T(8,128)(2,1)S(1)} %get-tuple-element.63), channel_id=1, source_target_pairs={{0,2},{1,3},{2,0},{3,1},{4,6},{5,7},{6,4},{7,5},{8,10},{9,11},{10,... | collective-permute-start | bytes 688136 | tf_op jit(solution)/shard_map/ppermute | solution.py:336
  86.1 8.5 %collective-permute-start.36 = (bf16[16,512]{1,0:T(8,128)(2,1)S(1)}, bf16[16,512]{1,0:T(8,128)(2,1)S(1)}, u32[]{:S(2)}, u32[]{:S(2)}) collective-permute-start(bf16[16,512]{1,0:T(8,128)(2,1)S(1)} %pad_maximum_fusion.4), channel_id=1, source_target_pairs={{0,2},{1,3},{2,0},{3,1},{4,6},{5,7},{6,4},{7,5},{8,10},{9,11},{10,... | collective-permute-start | bytes 49160 | tf_op jit(solution)/shard_map/ppermute | solution.py:336
  90.1 7.2 %collective-permute-start.32 = (bf16[112,512]{1,0:T(8,128)(2,1)S(1)}, bf16[112,512]{1,0:T(8,128)(2,1)S(1)}, u32[]{:S(2)}, u32[]{:S(2)}) collective-permute-start(bf16[112,512]{1,0:T(8,128)(2,1)S(1)} %get-tuple-element.73), channel_id=1, source_target_pairs={{0,24},{4,28},{8,16},{12,20},{16,8},{20,12},{24,0},{28,4},{1,25},{... | collective-permute-start | bytes 344072 | tf_op jit(solution)/shard_map/ppermute | solution.py:336
  92.3 8.6 %collective-permute-start.33 = (bf16[112,512]{1,0:T(8,128)(2,1)S(1)}, bf16[112,512]{1,0:T(8,128)(2,1)S(1)}, u32[]{:S(2)}, u32[]{:S(2)}) collective-permute-start(bf16[112,512]{1,0:T(8,128)(2,1)S(1)} %get-tuple-element.74), channel_id=1, source_target_pairs={{0,16},{4,20},{8,24},{12,28},{16,0},{20,4},{24,8},{28,12},{1,17},{... | collective-permute-start | bytes 344072 | tf_op jit(solution)/shard_map/ppermute | solution.py:336
  92.3 8.6 %collective-permute-start.34 = (bf16[112,512]{1,0:T(8,128)(2,1)S(1)}, bf16[112,512]{1,0:T(8,128)(2,1)S(1)}, u32[]{:S(2)}, u32[]{:S(2)}) collective-permute-start(bf16[112,512]{1,0:T(8,128)(2,1)S(1)} %get-tuple-element.75), channel_id=1, source_target_pairs={{0,8},{4,12},{8,0},{12,4},{16,24},{20,28},{24,16},{28,20},{1,9},{5... | collective-permute-start | bytes 344072 | tf_op jit(solution)/shard_map/ppermute | solution.py:336
  (8 other events, 115.3 us)

commit v6 on v5

--- a/solution.py
+++ b/solution.py
@@ -9,7 +9,7 @@
 
 CAP = 12
 SLOTS = 16
-RING = 8
+RING = 6
 
 
 def contract(lhs, rhs, lhs_dim, rhs_dim):
@@ -40,7 +40,7 @@
 
 def norm_kernel(
     tokens_ref, gain_ref, refusal_ref, ids_ref, probs_ref,
-    normed_ref, second_ref, first_ref, to_y_ref, unit_ref, base_ref, meta_ref,
+    normed_ref, second_ref, first_ref, to_y_ref, rest_ref, unit_ref, base_ref, meta_ref,
 ):
     tok_rows, model_width = tokens_ref.shape
     width = model_width // 8
@@ -52,17 +52,22 @@
     inv_rms = lax.rsqrt(jnp.mean(toks * toks, axis=1, keepdims=True) + 1e-06)
     normed_ref[...] = (toks * inv_rms * gain_ref[...]).astype(jnp.bfloat16)
     own = pl.ds(group_offset(rep, 0, 0, 0, width), 2 * width)
-    other = pl.ds(group_offset(rep, 1, 1, 0, width), width)
-    first_ref[...] = normed_ref[:, pl.ds(group_offset(rep, 0, 0, 0, width), width)]
-    second_ref[:tok_rows] = normed_ref[:, pl.ds(group_offset(rep, 1, 0, 0, width), width)]
-    to_y_ref[:tok_rows, : 2 * width] = normed_ref[:, own]
-    to_y_ref[:tok_rows, 2 * width :] = normed_ref[:, other]
+    other = pl.ds(group_offset(rep, 0, 1, 0, width), 2 * width)
+    split = most_rows(tok_rows)
+    first_ref[...] = normed_ref[:split, pl.ds(group_offset(rep, 0, 0, 0, width), width)]
+    second_ref[:split] = normed_ref[:split, pl.ds(group_offset(rep, 1, 0, 0, width), width)]
+    to_y_ref[:split, : 2 * width] = normed_ref[:split, own]
+    to_y_ref[:split, 2 * width :] = normed_ref[
+        :split, pl.ds(group_offset(rep, 1, 1, 0, width), width)
+    ]
+    rest_ref[:, : 2 * width] = normed_ref[split:, own]
+    rest_ref[:, 2 * width :] = normed_ref[split:, other]
     meta = jnp.concatenate([ids_ref[...].astype(jnp.float32), probs_ref[...]], axis=0)
     meta = meta.astype(jnp.bfloat16)
     meta_ref[...] = meta
     for ref in (second_ref, to_y_ref):
-        ref[tok_rows:] = jnp.zeros((meta.shape[0], ref.shape[1]), jnp.bfloat16)
-        ref[tok_rows:, :tok_rows] = meta
+        ref[split:] = jnp.zeros((meta.shape[0], ref.shape[1]), jnp.bfloat16)
+        ref[split:, :tok_rows] = meta
     along = jnp.sum(toks * unit, axis=1, keepdims=True)
     base_ref[...] = tokens_ref[:, own].astype(jnp.float32) - along * unit_ref[:, own]
 
@@ -71,20 +76,22 @@
     tok_rows, model_width = tokens.shape
     width = model_width // 8
     meta_rows = 2 * expert_ids.shape[1]
+    split = most_rows(tok_rows)
     vmem = pl.BlockSpec(memory_space=pltpu.VMEM)
     return pl.pallas_call(
         norm_kernel,
         out_shape=[
             jax.ShapeDtypeStruct((tok_rows, model_width), jnp.bfloat16),
-            jax.ShapeDtypeStruct((tok_rows + meta_rows, width), jnp.bfloat16),
-            jax.ShapeDtypeStruct((tok_rows, width), jnp.bfloat16),
-            jax.ShapeDtypeStruct((tok_rows + meta_rows, 3 * width), jnp.bfloat16),
+            jax.ShapeDtypeStruct((split + meta_rows, width), jnp.bfloat16),
+            jax.ShapeDtypeStruct((split, width), jnp.bfloat16),
+            jax.ShapeDtypeStruct((split + meta_rows, 3 * width), jnp.bfloat16),
+            jax.ShapeDtypeStruct((tok_rows - split, 4 * width), jnp.bfloat16),
             jax.ShapeDtypeStruct((1, model_width), jnp.float32),
             jax.ShapeDtypeStruct((tok_rows, 2 * width), jnp.float32),
             jax.ShapeDtypeStruct((meta_rows, tok_rows), jnp.bfloat16),
         ],
         in_specs=[vmem] * 5,
-        out_specs=[vmem] * 7,
+        out_specs=[vmem] * 8,
     )(tokens, norm_gain[None, :], refusal_dir[None, :], expert_ids.T, gate_probs.T)
 
 
@@ -146,22 +153,23 @@
 
 
 def most_rows(tok_rows):
-    return tok_rows // 128 * 112
+    return tok_rows // 4 * 3
 
 
 def moe_kernel(n_pieces, *refs):
     picks_hbm, weights_hbm, unit_ref, own_hbm = refs[:4]
     pieces_in = refs[4 : 4 + n_pieces]
-    w_gate_hbm, w_up_hbm, w_down_hbm = refs[4 + n_pieces : 7 + n_pieces]
-    out_refs = refs[7 + n_pieces : 13 + n_pieces]
+    rest_in = refs[4 + n_pieces : 6 + n_pieces]
+    w_gate_hbm, w_up_hbm, w_down_hbm = refs[6 + n_pieces : 9 + n_pieces]
+    out_refs = refs[9 + n_pieces : 15 + n_pieces]
     (picks, weights, w_in, w_down, toks, rows, hidden, mixed, table_sems, tok_sems, in_sems,
-     down_sems) = refs[13 + n_pieces :]
+     down_sems) = refs[15 + n_pieces :]
     n_seq, tok_rows, model_width = toks.shape
     n_z = n_seq // 2
     exp_dev, hid_dev, _ = w_gate_hbm.shape
     width = model_width // 8
     slots_src = exp_dev * SLOTS
-    rep = lax.axis_index("rep")
+    rep, z = lax.axis_index("rep"), lax.axis_index("seq") // 2
     split = most_rows(tok_rows)
     def in_copies(e):
         at = lax.rem(e, RING)
@@ -175,10 +183,6 @@
     def down_copy(e):
         return pltpu.make_async_copy(w_down_hbm.at[e], w_down.at[e], down_sems.at[e])
 
-    def start_down(e, carry):
-        down_copy(e).start()
-        return carry
-
     for e in range(min(RING, exp_dev)):
         for copy in in_copies(e):
             copy.start()
@@ -197,10 +201,24 @@
             for n, (color, dx) in enumerate(runs):
                 cols = pl.ds(group_offset(rep, color, dx, dc, width), width)
                 pltpu.make_async_copy(
-                    block.at[pl.ds(0, tok_rows), pl.ds(n * width, width)],
-                    toks.at[j, :, cols],
+                    block.at[pl.ds(0, split), pl.ds(n * width, width)],
+                    toks.at[j, pl.ds(0, split), cols],
                     tok_sems.at[j],
                 ).start()
+    for at in range(n_z):
+        for dy in range(2):
+            j = 2 * (at ^ z) + dy
+
+            @pl.when(j > 0)
+            def _():
+                for dc in range(2):
+                    for dx in range(2):
+                        cols = pl.ds(group_offset(rep, 0, dx, dc, width), 2 * width)
+                        pltpu.make_async_copy(
+                            rest_in[dc].at[at, dy, :, pl.ds(2 * dx * width, 2 * width)],
+                            toks.at[j, pl.ds(split, tok_rows - split), cols],
+                            tok_sems.at[j],
+                        ).start()
 
     tables[1].start()
     quarters = [slice(2 * q * width, 2 * (q + 1) * width) for q in range(4)]
@@ -234,15 +252,12 @@
             act = gate_val / (1.0 + jnp.exp(-gate_val)) * up_val
             hidden[e] = act.T.astype(jnp.bfloat16)
         for e in experts:
+            down_copy(e).start()
 
             @pl.when(e + RING < exp_dev)
             def _():
                 for copy in in_copies(e + RING):
                     copy.start()
-
-        @pl.when(pair == max((exp_dev - RING) // 2 - 1, 0))
-        def _():
-            lax.fori_loop(0, exp_dev, start_down, 0)
 
         return carry
 
@@ -277,7 +292,7 @@
                     cols = pl.ds(group_offset(rep, color, dx, dc, width), width)
                     value = mixed[dy, :, cols] - along[dy] * unit_ref[:, cols]
                     value = value.astype(jnp.bfloat16)
-                    rest[dz, dy, :, n * width : (n + 1) * width] = value[split:]
+                    rest[dz ^ z, dy, :, n * width : (n + 1) * width] = value[split:]
                     leaves, kind = (dy, 2 + dx) if color else (dx, dy)
                     (far if leaves else near)[kind, dz] = value[:split]
         return carry
@@ -285,7 +300,7 @@
     lax.fori_loop(0, n_z, combine, 0)
 
 
-def moe_partial(picks, weights, unit_dir, own, pieces, w_gate, w_up, w_down):
+def moe_partial(picks, weights, unit_dir, own, pieces, rest, w_gate, w_up, w_down):
     n_seq, _, tok_rows = picks.shape
     exp_dev, hid_dev, model_width = w_gate.shape
     width = model_width // 8
@@ -299,14 +314,14 @@
     ]
     n_z, split = n_seq // 2, most_rows(tok_rows)
     most = (4, n_z, split, width)
-    rest = (n_z, 2, tok_rows - split, 4 * width)
+    shapes = [most, most, (n_z, 2, tok_rows - split, 4 * width)]
     outs = [
-        jax.ShapeDtypeStruct(shape, jnp.bfloat16) for _ in range(2) for shape in (most, most, rest)
+        jax.ShapeDtypeStruct(shape, jnp.bfloat16) for _ in range(2) for shape in shapes
     ]
     return pl.pallas_call(
         functools.partial(moe_kernel, n_pieces),
         out_shape=outs,
-        in_specs=[hbm, hbm, vmem, hbm] + [whole] * n_pieces + [hbm] * 3,
+        in_specs=[hbm, hbm, vmem, hbm] + [whole] * (n_pieces + 2) + [hbm] * 3,
         out_specs=[vmem] * len(outs),
         scratch_shapes=[
             pltpu.VMEM(picks.shape, jnp.bfloat16),
@@ -322,13 +337,13 @@
             pltpu.SemaphoreType.DMA((2, RING)),
             pltpu.SemaphoreType.DMA((exp_dev,)),
         ],
-        compiler_params=pltpu.CompilerParams(vmem_limit_bytes=46 * 1024 * 1024),
+        compiler_params=pltpu.CompilerParams(vmem_limit_bytes=42 * 1024 * 1024),
         cost_estimate=pl.CostEstimate(
             flops=6 * n_seq * SLOTS * exp_dev * hid_dev * model_width,
             bytes_accessed=6 * exp_dev * hid_dev * model_width + 4 * n_seq * own.size,
             transcendentals=0,
         ),
-    )(picks, weights, unit_dir, own, *pieces, w_gate, w_up, w_down)
+    )(picks, weights, unit_dir, own, *pieces, *rest, w_gate, w_up, w_down)
 
 
 def swap(value, axis, distance):
@@ -347,22 +362,25 @@
     exp_dev = w_gate.shape[0]
     width = model_width // 8
 
-    normed, second, first, to_y, unit_dir, base, meta = norm_and_base(
+    normed, second, first, to_y, rest, unit_dir, base, meta = norm_and_base(
         tokens, norm_gain, refusal_dir, expert_ids, gate_probs
     )
+    split = most_rows(tok_rows)
+    groups = z_groups(n_z)
     second = [swap(second, "seq", 2 * d) for d in others]
     from_y = swap(to_y, "seq", 1)
+    rest = lax.all_gather(jnp.stack([rest, swap(rest, "seq", 1)]), "seq", axis_index_groups=groups)
     first, second, from_y = lax.optimization_barrier((first, jnp.stack(second), from_y))
     first = jnp.stack([swap(first, "seq", 2 * d) for d in others])
-    x_two = swap(second[:, :tok_rows], "rep", 2)
+    x_two = swap(second[:, :split], "rep", 2)
     y_one = swap(second, "seq", 1)
     y_two = swap(first, "seq", 1)
-    x_one = swap(jnp.concatenate([first, from_y[None, :tok_rows, :width]]), "rep", 2)
+    x_one = swap(jnp.concatenate([first, from_y[None, :split, :width]]), "rep", 2)
     to_y, to_core = lax.optimization_barrier((x_two, second))
     y_three = swap(to_y, "seq", 1)
-    below = [meta, from_y[tok_rows:, :tok_rows]]
+    below = [meta, from_y[split:, :tok_rows]]
     for d in range(n_z - 1):
-        below += [second[d, tok_rows:, :tok_rows], y_one[d, tok_rows:, :tok_rows]]
+        below += [second[d, split:, :tok_rows], y_one[d, split:, :tok_rows]]
     picks, weights = route(jnp.stack(below), exp_dev)
     to_core_y, picks, weights = lax.optimization_barrier((from_y, picks, weights))
     early = [swap(piece, "rep", 1) for piece in (to_core, first, to_core_y)]
@@ -370,8 +388,13 @@
     last = [x_two, y_one, x_one, y_two, y_three, x_three]
     pieces = [second, first, from_y, *last, *early, *[swap(piece, "rep", 1) for piece in last]]
 
-    sums = moe_partial(picks, weights, unit_dir, normed, pieces, w_gate, w_up, w_down)
+    rest = [rest, swap(rest, "rep", 1)]
+    sums = moe_partial(picks, weights, unit_dir, normed, pieces, rest, w_gate, w_up, w_down)
     return (base + summed_up(sums[:3], sums[3:], width)).astype(jnp.bfloat16)
+
+
+def z_groups(n_z):
+    return [[2 * z + y for z in range(n_z)] for y in range(2)]
 
 
 def summed_up(kept, sent, width):
@@ -379,26 +402,18 @@
     others = range(1, n_z)
     far, near, rest = zip(kept, [swap(piece, "rep", 1) for piece in sent])
 
-    to_x, to_y, rest_kept = lax.optimization_barrier(
-        (added(*[term[:2] for term in far]), added(*[term[2:] for term in far]), rest[0])
-    )
-    by_x, by_y = swap(to_x, "rep", 2), swap(to_y, "seq", 1)
-    rest = added(rest_kept, rest[1])
-    by_z = [swap(rest[d], "seq", 2 * d) for d in others]
-    to_y, to_x, *by_z = lax.optimization_barrier(
-        (
-            added(*[term[1] for term in near], by_x[1]),
-            added(*[term[3] for term in near], by_y[1]),
-            *by_z,
-        )
-    )
-    first_far, second_far = swap(to_y, "seq", 1), swap(to_x, "rep", 2)
+    by_x = swap(added(*[term[:2] for term in far]), "rep", 2)
+    by_y = swap(added(*[term[2:] for term in far]), "seq", 1)
+    rest = lax.psum_scatter(added(*rest), "seq", axis_index_groups=z_groups(n_z))
+    first_far = swap(added(*[term[1] for term in near], by_x[1]), "seq", 1)
+    second_far = swap(added(*[term[3] for term in near], by_y[1]), "rep", 2)
+    first_far, second_far, rest = lax.optimization_barrier((first_far, second_far, rest))
     first = added(*[term[0] for term in near], by_x[0], first_far)
     second = added(*[term[2] for term in near], by_y[0], second_far)
     blocks = jnp.concatenate([first, second], axis=2)
     most = [swap(blocks[d], "seq", 2 * d) for d in reversed(others)] + [blocks[0]]
-    rest = added(rest[0], *by_z)
     rest = added(rest[0], swap(rest[1], "seq", 1))
+    most[0], rest = lax.optimization_barrier((most[0], rest))
     far = jnp.concatenate([rest[:, :width], rest[:, 3 * width :]], axis=1)
     rest = [rest[:, width : 3 * width], swap(far, "rep", 2)]
     return jnp.concatenate(

time: 102 us -> 148 us (1.45)
  local copies, waits for them, and re-layouts: 0.79 us -> 17.3 us
  blocking collectives: 0 us -> 16.1 us
  between operations: 0.21 us -> 13.6 us
  other arithmetic: 1.62 us -> 7.15 us
  starting transfers between devices: 36.8 us -> 32.6 us
  waiting for transfers between devices: 33.9 us -> 31.1 us
    all_gather x0 -> x1, blocking collectives: none -> 16.1 us  [gathered(): lax.all_gather(jnp.stack([rest, swap(rest, 'seq', 1)]), 'seq', axis_index...]
    unnamed x13 -> x51, local copies, waits for them, and re-layouts: 0.74 us -> 16.4 us
    ppermute x37 -> x36, starting transfers between devices: 36.8 us -> 32.6 us  [swap(): return lax.ppermute(value, axis, [(i, i ^ distance) for i in range(size)])]
    convert_element_type x6 -> x5, other arithmetic: 0.74 us -> 4.49 us  [added(): sum((term.astype(jnp.float32) for term in terms)).astype(jnp.bfloat16)]
    ppermute x37 -> x36, waiting for transfers between devices: 33.9 us -> 31 us  [swap(): return lax.ppermute(value, axis, [(i, i ^ distance) for i in range(size)])]
  transfers between devices with their start and end apart: 37 -> 37, of which waited for: 16 -> 15; matrix products, arithmetic and copies ran while one was open for 2% -> 4% of each run, Pallas kernels for 3% -> 2%
where the time goes in v6:
time: 148 us; the launch traced here: 147 us
  starting transfers between devices  32.6 us (22%)
  waiting for transfers between devices  31.1 us (21%)
  Pallas kernels  29.6 us (20%)
  local copies, waits for them, and re-layouts  17.3 us (12%)
  blocking collectives  16.1 us (11%)
  between operations  13.6 us (9%)
  other arithmetic  7.15 us (5%)
    ppermute x36, starting transfers between devices, swap(): return lax.ppermute(value, axis, [(i, i ^ distance) for i in range(size)])  32.6 us
    ppermute x36, waiting for transfers between devices, swap(): return lax.ppermute(value, axis, [(i, i ^ distance) for i in range(size)])  31 us
    pallas_call x1, Pallas kernels, moe_partial(): pl.pallas_call(functools.partial(moe_kernel, n_pieces), out_shape=outs, i...  24.5 us
    unnamed x51, local copies, waits for them, and re-layouts  16.4 us
    all_gather x1, blocking collectives, gathered(): lax.all_gather(jnp.stack([rest, swap(rest, 'seq', 1)]), 'seq', axis_index...  16.1 us
    convert_element_type x5, other arithmetic, added(): sum((term.astype(jnp.float32) for term in terms)).astype(jnp.bfloat16)  4.49 us
  transfers between devices with their start and end apart: 37, of which 15 were waited for; matrix products, arithmetic and copies ran while one was open for 4% of the time, Pallas kernels for 2%

profile of v6, /device:TPU:0, one launch (start us, length us, event | category | flops | bytes accessed | tf_op | source)
XLA Modules:
  0.0 147.3 jit_solution(6573743147106699477)
XLA Ops:
  6.5 2.4 %shard_map.82 = (bf16[128,2048]{1,0:T(8,128)(2,1)}, bf16[112,256]{1,0:T(8,128)(2,1)}, bf16[96,256]{1,0:T(8,128)(2,1)}, bf16[112,768]{1,0:T(8,128)(2,1)}, bf16[32...) custom-call(bf16[128,2048]{1,0:T(8,128)(2,1)} %tokens_ref.1, ...), custom_call_target="tpu_custom_call" | custom-call | tf_op jit(solution)/shard_map/pallas_call | solution.py:81
  9.0 5.1 %collective-permute-start.2 = (bf16[112,256]{1,0:T(8,128)(2,1)}, bf16[112,256]{1,0:T(8,128)(2,1)S(1)}, u32[]{:S(2)}, u32[]{:S(2)}) collective-permute-start(bf16[112,256]{1,0:T(8,128)(2,1)} %get-tuple-element.36), channel_id=1, source_target_pairs={{0,24},{4,28},{8,16},{12,20},{16,8},{20,12},{24,0},{28,4},{1,25},{... | collective-permute-start | bytes 172040 | tf_op jit(solution)/shard_map/ppermute | solution.py:351
  14.7 1.7 %collective-permute-start.22 = (bf16[32,1024]{1,0:T(8,128)(2,1)}, bf16[32,1024]{1,0:T(8,128)(2,1)S(1)}, u32[]{:S(2)}, u32[]{:S(2)}) collective-permute-start(bf16[32,1024]{1,0:T(8,128)(2,1)} %get-tuple-element.51), channel_id=1, source_target_pairs={{0,4},{4,0},{8,12},{12,8},{16,20},{20,16},{24,28},{28,24},{1,5},{5... | collective-permute-start | bytes 196616 | tf_op jit(solution)/shard_map/ppermute | solution.py:351
  17.4 1.9 %collective-permute-done.1 = bf16[112,256]{1,0:T(8,128)(2,1)S(1)} collective-permute-done((bf16[112,256]{1,0:T(8,128)(2,1)}, bf16[112,256]{1,0:T(8,128)(2,1)S(1)}, u32[]{:S(2)}, u32[]{:S(2)}) %collective-permute-start.1) | collective-permute-done | bytes 57376 | tf_op jit(solution)/shard_map/ppermute | solution.py:351
  20.7 16.1 %all-gather = bf16[8,32,1024]{2,1,0:T(8,128)(2,1)S(1)} all-gather(bf16[2,32,1024]{2,1,0:T(8,128)(2,1)S(1)} %pad_maximum_fusion.3), channel_id=2, replica_groups={{0,8,16,24},{4,12,20,28},{1,9,17,25},{5,13,21,29},{2,10,18,26},{6,14,22..., dimensions={0}, use_global_device_ids=true | all-gather | bytes 655360 | tf_op jit(solution)/shard_map/all_gather | solution.py:372
  36.7 2.7 %collective-permute-start.7 = (bf16[96,256]{1,0:T(8,128)(2,1)}, bf16[96,256]{1,0:T(8,128)(2,1)S(1)}, u32[]{:S(2)}, u32[]{:S(2)}) collective-permute-start(bf16[96,256]{1,0:T(8,128)(2,1)} %get-tuple-element.47), channel_id=1, source_target_pairs={{0,24},{4,28},{8,16},{12,20},{16,8},{20,12},{24,0},{28,4},{1,25},{... | collective-permute-start | bytes 147464 | tf_op jit(solution)/shard_map/ppermute | solution.py:351
  39.7 1.4 collective-permute-start.5
  41.1 1.8 %collective-permute-start.4 = (bf16[3,112,256]{2,1,0:T(8,128)(2,1)S(1)}, bf16[3,112,256]{2,1,0:T(8,128)(2,1)S(1)}, u32[]{:S(2)}, u32[]{:S(2)}) collective-permute-start(bf16[3,112,256]{2,1,0:T(8,128)(2,1)S(1)} %pad_maximum_fusion.1.refs_4_), channel_id=1, source_target_pairs={{0,4},{4,0},{8,12},{12,8},{16,20},{20,16},{24,28},{28,24},{1,5},{5... | collective-permute-start | bytes 516104 | tf_op jit(solution)/shard_map/ppermute | solution.py:351
  42.9 1.6 %collective-permute-start.8 = (bf16[3,96,256]{2,1,0:T(8,128)(2,1)S(1)}, bf16[3,96,256]{2,1,0:T(8,128)(2,1)S(1)}, u32[]{:S(2)}, u32[]{:S(2)}) collective-permute-start(bf16[3,96,256]{2,1,0:T(8,128)(2,1)S(1)} %slice.109), channel_id=1, source_target_pairs={{0,2},{1,3},{2,0},{3,1},{4,6},{5,7},{6,4},{7,5},{8,10},{9,11},{10,... | collective-permute-start | bytes 442376 | tf_op jit(solution)/shard_map/ppermute | solution.py:351
  44.8 1.7 %collective-permute-start.10 = (bf16[3,96,256]{2,1,0:T(8,128)(2,1)S(1)}, bf16[3,96,256]{2,1,0:T(8,128)(2,1)S(1)}, u32[]{:S(2)}, u32[]{:S(2)}) collective-permute-start(bf16[3,96,256]{2,1,0:T(8,128)(2,1)S(1)} %pad_maximum_fusion.2.refs_5_), channel_id=1, source_target_pairs={{0,4},{4,0},{8,12},{12,8},{16,20},{20,16},{24,28},{28,24},{1,5},{5... | collective-permute-start | bytes 442376 | tf_op jit(solution)/shard_map/ppermute | solution.py:351
  46.5 1.6 %collective-permute-start.9 = (bf16[4,96,256]{2,1,0:T(8,128)(2,1)S(1)}, bf16[4,96,256]{2,1,0:T(8,128)(2,1)S(1)}, u32[]{:S(2)}, u32[]{:S(2)}) collective-permute-start(bf16[4,96,256]{2,1,0:T(8,128)(2,1)S(1)} %pad_maximum_fusion), channel_id=1, source_target_pairs={{0,2},{1,3},{2,0},{3,1},{4,6},{5,7},{6,4},{7,5},{8,10},{9,11},{10,... | collective-permute-start | bytes 589832 | tf_op jit(solution)/shard_map/ppermute | solution.py:351
  50.4 1.1 collective-permute-done.10.refs_10_
  51.5 2.0 %collective-permute-done.9.refs_9_ = bf16[4,96,256]{2,1,0:T(8,128)(2,1)S(1)} collective-permute-done((bf16[4,96,256]{2,1,0:T(8,128)(2,1)S(1)}, bf16[4,96,256]{2,1,0:T(8,128)(2,1)S(1)}, u32[]{:S(2)}, u32[]{:S(2)}) %collective-permute-start.9) | collective-permute-done | bytes 196640 | tf_op jit(solution)/shard_map/ppermute | solution.py:351
  54.9 1.6 %collective-permute-start.12 = (bf16[3,96,256]{2,1,0:T(8,128)(2,1)S(1)}, bf16[3,96,256]{2,1,0:T(8,128)(2,1)S(1)}, u32[]{:S(2)}, u32[]{:S(2)}) collective-permute-start(bf16[3,96,256]{2,1,0:T(8,128)(2,1)S(1)} %collective-permute-done.10.refs_10_), channel_id=1, source_target_pairs={{0,2},{1,3},{2,0},{3,1},{4,6},{5,7},{6,4},{7,5},{8,10},{9,11},{10,... | collective-permute-start | bytes 442376 | tf_op jit(solution)/shard_map/ppermute | solution.py:351
  58.0 2.7 %shard_map.83 = (bf16[8,256,128]{2,1,0:T(8,128)(2,1)}, bf16[8,128,256]{2,1,0:T(8,128)(2,1)}) custom-call(bf16[8,16,128]{2,1,0:T(8,128)(2,1)} %copy-done.21), custom_call_target="tpu_custom_call" | custom-call | flops 4000000000 | bytes 2097152 | tf_op jit(solution)/shard_map/pallas_call | solution.py:140
  74.0 24.5 %shard_map.84 = (bf16[4,4,96,256]{3,2,1,0:T(8,128)(2,1)S(1)}, bf16[4,4,96,256]{3,2,1,0:T(8,128)(2,1)S(1)}, bf16[4,2,32,1024]{3,2,1,0:T(8,128)(2,1)S(1)}, bf16[4,...) custom-call(bf16[8,256,128]{2,1,0:T(8,128)(2,1)} %get-tuple-element.43.refs_0_, ...), custom_call_target="tpu_custom_call" | custom-call | flops 4831838208 | bytes 46137344 | tf_op jit(solution)/shard_map/pallas_call | solution.py:321
  99.3 1.2 collective-permute-done.30
  100.5 1.0 add_convert_fusion
  101.5 1.4 collective-permute-done.25
  103.2 1.6 %collective-permute-start.28 = (bf16[2,4,96,256]{3,2,1,0:T(8,128)(2,1)S(1)}, bf16[2,4,96,256]{3,2,1,0:T(8,128)(2,1)S(1)}, u32[]{:S(2)}, u32[]{:S(2)}) collective-permute-start(bf16[2,4,96,256]{3,2,1,0:T(8,128)(2,1)S(1)} %get-tuple-element.67), channel_id=1, source_target_pairs={{0,4},{4,0},{8,12},{12,8},{16,20},{20,16},{24,28},{28,24},{1,5},{5... | collective-permute-start | bytes 1179656 | tf_op jit(solution)/shard_map/ppermute | solution.py:351
  104.8 1.0 collective-permute-start.26
  105.8 8.7 %collective-permute-done.28 = bf16[2,4,96,256]{3,2,1,0:T(8,128)(2,1)S(1)} collective-permute-done((bf16[2,4,96,256]{3,2,1,0:T(8,128)(2,1)S(1)}, bf16[2,4,96,256]{3,2,1,0:T(8,128)(2,1)S(1)}, u32[]{:S(2)}, u32[]{:S(2)}) %collective-permute-start.28) | collective-permute-done | bytes 393248 | tf_op jit(solution)/shard_map/ppermute | solution.py:351
  114.5 1.3 collective-permute-done.26
  115.7 1.2 fusion.4
  118.4 4.6 %collective-permute-done.29 = bf16[4,96,256]{2,1,0:T(8,128)(2,1)S(1)} collective-permute-done((bf16[4,96,256]{2,1,0:T(8,128)(2,1)S(1)}, bf16[4,96,256]{2,1,0:T(8,128)(2,1)S(1)}, u32[]{:S(2)}, u32[]{:S(2)}) %collective-permute-start.29) | collective-permute-done | bytes 196640 | tf_op jit(solution)/shard_map/ppermute | solution.py:351
  125.0 1.2 fusion
  126.2 2.1 %collective-permute-start.33 = (bf16[96,512]{1,0:T(8,128)(2,1)S(1)}, bf16[96,512]{1,0:T(8,128)(2,1)S(1)}, u32[]{:S(2)}, u32[]{:S(2)}) collective-permute-start(bf16[96,512]{1,0:T(8,128)(2,1)S(1)} %get-tuple-element.69), channel_id=1, source_target_pairs={{0,16},{4,20},{8,24},{12,28},{16,0},{20,4},{24,8},{28,12},{1,17},{... | collective-permute-start | bytes 294920 | tf_op jit(solution)/shard_map/ppermute | solution.py:351
  128.3 1.2 collective-permute-start.31
  130.6 4.2 %collective-permute-done.31 = bf16[96,512]{1,0:T(8,128)(2,1)S(1)} collective-permute-done((bf16[96,512]{1,0:T(8,128)(2,1)S(1)}, bf16[96,512]{1,0:T(8,128)(2,1)S(1)}, u32[]{:S(2)}, u32[]{:S(2)}) %collective-permute-start.31) | collective-permute-done | bytes 98336 | tf_op jit(solution)/shard_map/ppermute | solution.py:351
  134.9 1.3 collective-permute-start.35
  136.2 2.6 %collective-permute-done.35 = bf16[32,512]{1,0:T(8,128)(2,1)S(1)} collective-permute-done((bf16[32,512]{1,0:T(8,128)(2,1)S(1)}, bf16[32,512]{1,0:T(8,128)(2,1)S(1)}, u32[]{:S(2)}, u32[]{:S(2)}) %collective-permute-start.35) | collective-permute-done | bytes 32800 | tf_op jit(solution)/shard_map/ppermute | solution.py:351
  138.8 1.6 %fusion.2 = bf16[128,512]{1,0:T(8,128)(2,1)} fusion(f32[128,512]{1,0:T(8,128)} %get-tuple-element.34, f32[32,512]{1,0:T(8,128)S(1)} %convert_add_fusion.2, f32[96,512]{1,0:T(8,128)S(1)} %convert_add_fusion), kind=kLoop, calls=%fused_computation.16 | loop fusion | flops 196608 | bytes 655360 | tf_op jit(solution)/shard_map/convert_element_type | solution.py:393
  (117 shorter events, 27.8 us)
Async XLA Ops:
  6.5 117.0 %reduce-scatter.2.cloned.1.call-start = ((), (), s32[]{:S(2)}) async-start(), calls=%async_computation.1 | async-start | bytes 655360 | tf_op jit(solution)/shard_map/reduce_scatter | solution.py:407
  9.0 8.5 %collective-permute-start.2 = (bf16[112,256]{1,0:T(8,128)(2,1)}, bf16[112,256]{1,0:T(8,128)(2,1)S(1)}, u32[]{:S(2)}, u32[]{:S(2)}) collective-permute-start(bf16[112,256]{1,0:T(8,128)(2,1)} %get-tuple-element.36), channel_id=1, source_target_pairs={{0,24},{4,28},{8,16},{12,20},{16,8},{20,12},{24,0},{28,4},{1,25},{... | collective-permute-start | bytes 172040 | tf_op jit(solution)/shard_map/ppermute | solution.py:351
  14.1 5.3 %collective-permute-start.1 = (bf16[112,256]{1,0:T(8,128)(2,1)}, bf16[112,256]{1,0:T(8,128)(2,1)S(1)}, u32[]{:S(2)}, u32[]{:S(2)}) collective-permute-start(bf16[112,256]{1,0:T(8,128)(2,1)} %get-tuple-element.36), channel_id=1, source_target_pairs={{0,16},{4,20},{8,24},{12,28},{16,0},{20,4},{24,8},{28,12},{1,17},{... | collective-permute-start | bytes 172040 | tf_op jit(solution)/shard_map/ppermute | solution.py:351
  14.1 5.3 %collective-permute-start = (bf16[112,256]{1,0:T(8,128)(2,1)}, bf16[112,256]{1,0:T(8,128)(2,1)S(1)}, u32[]{:S(2)}, u32[]{:S(2)}) collective-permute-start(bf16[112,256]{1,0:T(8,128)(2,1)} %get-tuple-element.36), channel_id=1, source_target_pairs={{0,8},{4,12},{8,0},{12,4},{16,24},{20,28},{24,16},{28,20},{1,9},{5... | collective-permute-start | bytes 172040 | tf_op jit(solution)/shard_map/ppermute | solution.py:351
  14.7 5.1 %collective-permute-start.22 = (bf16[32,1024]{1,0:T(8,128)(2,1)}, bf16[32,1024]{1,0:T(8,128)(2,1)S(1)}, u32[]{:S(2)}, u32[]{:S(2)}) collective-permute-start(bf16[32,1024]{1,0:T(8,128)(2,1)} %get-tuple-element.51), channel_id=1, source_target_pairs={{0,4},{4,0},{8,12},{12,8},{16,20},{20,16},{24,28},{28,24},{1,5},{5... | collective-permute-start | bytes 196616 | tf_op jit(solution)/shard_map/ppermute | solution.py:351
  16.4 20.3 %collective-permute-start.3 = (bf16[112,768]{1,0:T(8,128)(2,1)}, bf16[112,768]{1,0:T(8,128)(2,1)S(1)}, u32[]{:S(2)}, u32[]{:S(2)}) collective-permute-start(bf16[112,768]{1,0:T(8,128)(2,1)} %get-tuple-element.37), channel_id=1, source_target_pairs={{0,4},{4,0},{8,12},{12,8},{16,20},{20,16},{24,28},{28,24},{1,5},{5... | collective-permute-start | bytes 516104 | tf_op jit(solution)/shard_map/ppermute | solution.py:351
  36.7 7.7 %collective-permute-start.7 = (bf16[96,256]{1,0:T(8,128)(2,1)}, bf16[96,256]{1,0:T(8,128)(2,1)S(1)}, u32[]{:S(2)}, u32[]{:S(2)}) collective-permute-start(bf16[96,256]{1,0:T(8,128)(2,1)} %get-tuple-element.47), channel_id=1, source_target_pairs={{0,24},{4,28},{8,16},{12,20},{16,8},{20,12},{24,0},{28,4},{1,25},{... | collective-permute-start | bytes 147464 | tf_op jit(solution)/shard_map/ppermute | solution.py:351
  39.5 5.2 %collective-permute-start.6 = (bf16[96,256]{1,0:T(8,128)(2,1)}, bf16[96,256]{1,0:T(8,128)(2,1)S(1)}, u32[]{:S(2)}, u32[]{:S(2)}) collective-permute-start(bf16[96,256]{1,0:T(8,128)(2,1)} %get-tuple-element.47), channel_id=1, source_target_pairs={{0,16},{4,20},{8,24},{12,28},{16,0},{20,4},{24,8},{28,12},{1,17},{... | collective-permute-start | bytes 147464 | tf_op jit(solution)/shard_map/ppermute | solution.py:351
  39.7 5.0 %collective-permute-start.5 = (bf16[96,256]{1,0:T(8,128)(2,1)}, bf16[96,256]{1,0:T(8,128)(2,1)S(1)}, u32[]{:S(2)}, u32[]{:S(2)}) collective-permute-start(bf16[96,256]{1,0:T(8,128)(2,1)} %get-tuple-element.47), channel_id=1, source_target_pairs={{0,8},{4,12},{8,0},{12,4},{16,24},{20,28},{24,16},{28,20},{1,9},{5... | collective-permute-start | bytes 147464 | tf_op jit(solution)/shard_map/ppermute | solution.py:351
  41.1 7.4 %collective-permute-start.4 = (bf16[3,112,256]{2,1,0:T(8,128)(2,1)S(1)}, bf16[3,112,256]{2,1,0:T(8,128)(2,1)S(1)}, u32[]{:S(2)}, u32[]{:S(2)}) collective-permute-start(bf16[3,112,256]{2,1,0:T(8,128)(2,1)S(1)} %pad_maximum_fusion.1.refs_4_), channel_id=1, source_target_pairs={{0,4},{4,0},{8,12},{12,8},{16,20},{20,16},{24,28},{28,24},{1,5},{5... | collective-permute-start | bytes 516104 | tf_op jit(solution)/shard_map/ppermute | solution.py:351
  42.9 5.2 %collective-permute-start.8 = (bf16[3,96,256]{2,1,0:T(8,128)(2,1)S(1)}, bf16[3,96,256]{2,1,0:T(8,128)(2,1)S(1)}, u32[]{:S(2)}, u32[]{:S(2)}) collective-permute-start(bf16[3,96,256]{2,1,0:T(8,128)(2,1)S(1)} %slice.109), channel_id=1, source_target_pairs={{0,2},{1,3},{2,0},{3,1},{4,6},{5,7},{6,4},{7,5},{8,10},{9,11},{10,... | collective-permute-start | bytes 442376 | tf_op jit(solution)/shard_map/ppermute | solution.py:351
  44.8 6.7 %collective-permute-start.10 = (bf16[3,96,256]{2,1,0:T(8,128)(2,1)S(1)}, bf16[3,96,256]{2,1,0:T(8,128)(2,1)S(1)}, u32[]{:S(2)}, u32[]{:S(2)}) collective-permute-start(bf16[3,96,256]{2,1,0:T(8,128)(2,1)S(1)} %pad_maximum_fusion.2.refs_5_), channel_id=1, source_target_pairs={{0,4},{4,0},{8,12},{12,8},{16,20},{20,16},{24,28},{28,24},{1,5},{5... | collective-permute-start | bytes 442376 | tf_op jit(solution)/shard_map/ppermute | solution.py:351
  46.5 7.0 %collective-permute-start.9 = (bf16[4,96,256]{2,1,0:T(8,128)(2,1)S(1)}, bf16[4,96,256]{2,1,0:T(8,128)(2,1)S(1)}, u32[]{:S(2)}, u32[]{:S(2)}) collective-permute-start(bf16[4,96,256]{2,1,0:T(8,128)(2,1)S(1)} %pad_maximum_fusion), channel_id=1, source_target_pairs={{0,2},{1,3},{2,0},{3,1},{4,6},{5,7},{6,4},{7,5},{8,10},{9,11},{10,... | collective-permute-start | bytes 589832 | tf_op jit(solution)/shard_map/ppermute | solution.py:351
  48.1 6.1 %collective-permute-start.11 = (bf16[3,96,256]{2,1,0:T(8,128)(2,1)S(1)}, bf16[3,96,256]{2,1,0:T(8,128)(2,1)S(1)}, u32[]{:S(2)}, u32[]{:S(2)}) collective-permute-start(bf16[3,96,256]{2,1,0:T(8,128)(2,1)S(1)} %collective-permute-done.8.refs_7_), channel_id=1, source_target_pairs={{0,4},{4,0},{8,12},{12,8},{16,20},{20,16},{24,28},{28,24},{1,5},{5... | collective-permute-start | bytes 442376 | tf_op jit(solution)/shard_map/ppermute | solution.py:351
  48.5 8.6 %collective-permute-start.13 = (bf16[3,112,256]{2,1,0:T(8,128)(2,1)S(1)}, bf16[3,112,256]{2,1,0:T(8,128)(2,1)S(1)}, u32[]{:S(2)}, u32[]{:S(2)}) collective-permute-start(bf16[3,112,256]{2,1,0:T(8,128)(2,1)S(1)} %pad_maximum_fusion.1.refs_4_), channel_id=1, source_target_pairs={{0,1},{1,0},{2,3},{3,2},{4,5},{5,4},{6,7},{7,6},{8,9},{9,8},{10,11... | collective-permute-start | bytes 516104 | tf_op jit(solution)/shard_map/ppermute | solution.py:351
  49.3 4.9 %collective-permute-start.16 = (bf16[3,96,256]{2,1,0:T(8,128)(2,1)S(1)}, bf16[3,96,256]{2,1,0:T(8,128)(2,1)S(1)}, u32[]{:S(2)}, u32[]{:S(2)}) collective-permute-start(bf16[3,96,256]{2,1,0:T(8,128)(2,1)S(1)} %collective-permute-done.8.refs_7_), channel_id=1, source_target_pairs={{0,1},{1,0},{2,3},{3,2},{4,5},{5,4},{6,7},{7,6},{8,9},{9,8},{10,11... | collective-permute-start | bytes 442376 | tf_op jit(solution)/shard_map/ppermute | solution.py:351
  51.5 12.7 %collective-permute-start.23 = (bf16[4,2,32,1024]{3,2,1,0:T(8,128)(2,1)S(1)}, bf16[4,2,32,1024]{3,2,1,0:T(8,128)(2,1)S(1)}, u32[]{:S(2)}, u32[]{:S(2)}) collective-permute-start(bf16[4,2,32,1024]{3,2,1,0:T(8,128)(2,1)S(1)} %bitcast.48), channel_id=1, source_target_pairs={{0,1},{1,0},{2,3},{3,2},{4,5},{5,4},{6,7},{7,6},{8,9},{9,8},{10,11... | collective-permute-start | bytes 1572872 | tf_op jit(solution)/shard_map/ppermute | solution.py:351
  53.5 9.0 %collective-permute-start.17 = (bf16[3,112,256]{2,1,0:T(8,128)(2,1)S(1)}, bf16[3,112,256]{2,1,0:T(8,128)(2,1)S(1)}, u32[]{:S(2)}, u32[]{:S(2)}) collective-permute-start(bf16[3,112,256]{2,1,0:T(8,128)(2,1)S(1)} %collective-permute-done.4.refs_8_), channel_id=1, source_target_pairs={{0,1},{1,0},{2,3},{3,2},{4,5},{5,4},{6,7},{7,6},{8,9},{9,8},{10,11... | collective-permute-start | bytes 516104 | tf_op jit(solution)/shard_map/ppermute | solution.py:351
  54.2 6.5 %collective-permute-start.19 = (bf16[3,96,256]{2,1,0:T(8,128)(2,1)S(1)}, bf16[3,96,256]{2,1,0:T(8,128)(2,1)S(1)}, u32[]{:S(2)}, u32[]{:S(2)}) collective-permute-start(bf16[3,96,256]{2,1,0:T(8,128)(2,1)S(1)} %collective-permute-done.10.refs_10_), channel_id=1, source_target_pairs={{0,1},{1,0},{2,3},{3,2},{4,5},{5,4},{6,7},{7,6},{8,9},{9,8},{10,11... | collective-permute-start | bytes 442376 | tf_op jit(solution)/shard_map/ppermute | solution.py:351
  54.9 6.8 %collective-permute-start.12 = (bf16[3,96,256]{2,1,0:T(8,128)(2,1)S(1)}, bf16[3,96,256]{2,1,0:T(8,128)(2,1)S(1)}, u32[]{:S(2)}, u32[]{:S(2)}) collective-permute-start(bf16[3,96,256]{2,1,0:T(8,128)(2,1)S(1)} %collective-permute-done.10.refs_10_), channel_id=1, source_target_pairs={{0,2},{1,3},{2,0},{3,1},{4,6},{5,7},{6,4},{7,5},{8,10},{9,11},{10,... | collective-permute-start | bytes 442376 | tf_op jit(solution)/shard_map/ppermute | solution.py:351
  57.8 6.4 %collective-permute-start.18 = (bf16[4,96,256]{2,1,0:T(8,128)(2,1)S(1)}, bf16[4,96,256]{2,1,0:T(8,128)(2,1)S(1)}, u32[]{:S(2)}, u32[]{:S(2)}) collective-permute-start(bf16[4,96,256]{2,1,0:T(8,128)(2,1)S(1)} %collective-permute-done.9.refs_9_), channel_id=1, source_target_pairs={{0,1},{1,0},{2,3},{3,2},{4,5},{5,4},{6,7},{7,6},{8,9},{9,8},{10,11... | collective-permute-start | bytes 589832 | tf_op jit(solution)/shard_map/ppermute | solution.py:351
  98.8 4.1 %collective-permute-start.25 = (bf16[4,4,96,256]{3,2,1,0:T(8,128)(2,1)}, bf16[4,4,96,256]{3,2,1,0:T(8,128)(2,1)S(1)}, u32[]{:S(2)}, u32[]{:S(2)}) collective-permute-start(bf16[4,4,96,256]{3,2,1,0:T(8,128)(2,1)} %get-tuple-element.55), channel_id=1, source_target_pairs={{0,1},{1,0},{2,3},{3,2},{4,5},{5,4},{6,7},{7,6},{8,9},{9,8},{10,11... | collective-permute-start | bytes 2359304 | tf_op jit(solution)/shard_map/ppermute | solution.py:351
  99.1 6.7 %collective-permute-start.24 = (bf16[4,4,96,256]{3,2,1,0:T(8,128)(2,1)}, bf16[4,4,96,256]{3,2,1,0:T(8,128)(2,1)}, u32[]{:S(2)}, u32[]{:S(2)}) collective-permute-start(bf16[4,4,96,256]{3,2,1,0:T(8,128)(2,1)} %get-tuple-element.53), channel_id=1, source_target_pairs={{0,1},{1,0},{2,3},{3,2},{4,5},{5,4},{6,7},{7,6},{8,9},{9,8},{10,11... | collective-permute-start | bytes 2359304 | tf_op jit(solution)/shard_map/ppermute | solution.py:351
  103.2 11.3 %collective-permute-start.28 = (bf16[2,4,96,256]{3,2,1,0:T(8,128)(2,1)S(1)}, bf16[2,4,96,256]{3,2,1,0:T(8,128)(2,1)S(1)}, u32[]{:S(2)}, u32[]{:S(2)}) collective-permute-start(bf16[2,4,96,256]{3,2,1,0:T(8,128)(2,1)S(1)} %get-tuple-element.67), channel_id=1, source_target_pairs={{0,4},{4,0},{8,12},{12,8},{16,20},{20,16},{24,28},{28,24},{1,5},{5... | collective-permute-start | bytes 1179656 | tf_op jit(solution)/shard_map/ppermute | solution.py:351
  104.8 11.0 %collective-permute-start.26 = (bf16[2,4,96,256]{3,2,1,0:T(8,128)(2,1)S(1)}, bf16[2,4,96,256]{3,2,1,0:T(8,128)(2,1)S(1)}, u32[]{:S(2)}, u32[]{:S(2)}) collective-permute-start(bf16[2,4,96,256]{3,2,1,0:T(8,128)(2,1)S(1)} %get-tuple-element.68), channel_id=1, source_target_pairs={{0,2},{1,3},{2,0},{3,1},{4,6},{5,7},{6,4},{7,5},{8,10},{9,11},{10,... | collective-permute-start | bytes 1179656 | tf_op jit(solution)/shard_map/ppermute | solution.py:351
  116.9 6.1 %collective-permute-start.29 = (bf16[4,96,256]{2,1,0:T(8,128)(2,1)S(1)}, bf16[4,96,256]{2,1,0:T(8,128)(2,1)S(1)}, u32[]{:S(2)}, u32[]{:S(2)}) collective-permute-start(bf16[4,96,256]{2,1,0:T(8,128)(2,1)S(1)} %get-tuple-element.65), channel_id=1, source_target_pairs={{0,2},{1,3},{2,0},{3,1},{4,6},{5,7},{6,4},{7,5},{8,10},{9,11},{10,... | collective-permute-start | bytes 589832 | tf_op jit(solution)/shard_map/ppermute | solution.py:351
  117.9 5.7 %collective-permute-start.27 = (bf16[4,96,256]{2,1,0:T(8,128)(2,1)S(1)}, bf16[4,96,256]{2,1,0:T(8,128)(2,1)S(1)}, u32[]{:S(2)}, u32[]{:S(2)}) collective-permute-start(bf16[4,96,256]{2,1,0:T(8,128)(2,1)S(1)} %get-tuple-element.66), channel_id=1, source_target_pairs={{0,4},{4,0},{8,12},{12,8},{16,20},{20,16},{24,28},{28,24},{1,5},{5... | collective-permute-start | bytes 589832 | tf_op jit(solution)/shard_map/ppermute | solution.py:351
  124.4 5.4 %collective-permute-start.32 = (bf16[32,1024]{1,0:T(8,128)(2,1)S(1)}, bf16[32,1024]{1,0:T(8,128)(2,1)S(1)}, u32[]{:S(2)}, u32[]{:S(2)}) collective-permute-start(bf16[32,1024]{1,0:T(8,128)(2,1)S(1)} %slice_bitcast_fusion), channel_id=1, source_target_pairs={{0,4},{4,0},{8,12},{12,8},{16,20},{20,16},{24,28},{28,24},{1,5},{5... | collective-permute-start | bytes 196616 | tf_op jit(solution)/shard_map/ppermute | solution.py:351
  126.2 9.9 %collective-permute-start.33 = (bf16[96,512]{1,0:T(8,128)(2,1)S(1)}, bf16[96,512]{1,0:T(8,128)(2,1)S(1)}, u32[]{:S(2)}, u32[]{:S(2)}) collective-permute-start(bf16[96,512]{1,0:T(8,128)(2,1)S(1)} %get-tuple-element.69), channel_id=1, source_target_pairs={{0,16},{4,20},{8,24},{12,28},{16,0},{20,4},{24,8},{28,12},{1,17},{... | collective-permute-start | bytes 294920 | tf_op jit(solution)/shard_map/ppermute | solution.py:351
  128.3 6.6 %collective-permute-start.31 = (bf16[96,512]{1,0:T(8,128)(2,1)S(1)}, bf16[96,512]{1,0:T(8,128)(2,1)S(1)}, u32[]{:S(2)}, u32[]{:S(2)}) collective-permute-start(bf16[96,512]{1,0:T(8,128)(2,1)S(1)} %get-tuple-element.70), channel_id=1, source_target_pairs={{0,24},{4,28},{8,16},{12,20},{16,8},{20,12},{24,0},{28,4},{1,25},{... | collective-permute-start | bytes 294920 | tf_op jit(solution)/shard_map/ppermute | solution.py:351
  129.4 6.7 %collective-permute-start.34 = (bf16[96,512]{1,0:T(8,128)(2,1)S(1)}, bf16[96,512]{1,0:T(8,128)(2,1)S(1)}, u32[]{:S(2)}, u32[]{:S(2)}) collective-permute-start(bf16[96,512]{1,0:T(8,128)(2,1)S(1)} %get-tuple-element.71), channel_id=1, source_target_pairs={{0,8},{4,12},{8,0},{12,4},{16,24},{20,28},{24,16},{28,20},{1,9},{5... | collective-permute-start | bytes 294920 | tf_op jit(solution)/shard_map/ppermute | solution.py:351
  134.9 4.0 %collective-permute-start.35 = (bf16[32,512]{1,0:T(8,128)(2,1)S(1)}, bf16[32,512]{1,0:T(8,128)(2,1)S(1)}, u32[]{:S(2)}, u32[]{:S(2)}) collective-permute-start(bf16[32,512]{1,0:T(8,128)(2,1)S(1)} %pad_maximum_fusion.5), channel_id=1, source_target_pairs={{0,2},{1,3},{2,0},{3,1},{4,6},{5,7},{6,4},{7,5},{8,10},{9,11},{10,... | collective-permute-start | bytes 98312 | tf_op jit(solution)/shard_map/ppermute | solution.py:351
  (27 other events, 92.7 us)
Sparse Core Ops, SparseCore 0:
  101.6 20.8 reduce-scatter.1

commit v7 on v5

--- a/solution.py
+++ b/solution.py
@@ -9,7 +9,7 @@
 
 CAP = 12
 SLOTS = 16
-RING = 8
+RING = 6
 
 
 def contract(lhs, rhs, lhs_dim, rhs_dim):
@@ -23,18 +23,17 @@
 
 
 def token_pieces(n_z):
-    near = [2 * d for d in range(1, n_z)]
-    far = [2 * d + 1 for d in range(1, n_z)]
+    near, far = (0, 1, n_z - 1, 0), (0, 1, n_z - 1, 1)
     return [
-        [(j, [(1, 0)]) for j in near],
-        [(j, [(0, 0)]) for j in near],
-        [(1, [(0, 0), (1, 0), (1, 1)])],
-        [(j, [(1, 1)]) for j in near],
-        [(j, [(1, 0)]) for j in far],
-        [(j, [(0, 1)]) for j in (*near, 1)],
-        [(j, [(0, 0)]) for j in far],
-        [(j, [(1, 1)]) for j in far],
-        [(j, [(0, 1)]) for j in far],
+        ([near], [(1, 0)]),
+        ([near], [(0, 0)]),
+        ([(0, 0, 1, 1)], [(0, 0), (1, 0), (1, 1)]),
+        ([near], [(1, 1)]),
+        ([far], [(1, 0)]),
+        ([(0, 0, 1, 1), (1, 1, n_z - 1, 0)], [(0, 1)]),
+        ([far], [(0, 0)]),
+        ([far], [(1, 1)]),
+        ([far], [(0, 1)]),
     ]
 
 
@@ -156,8 +155,8 @@
     out_refs = refs[7 + n_pieces : 13 + n_pieces]
     (picks, weights, w_in, w_down, toks, rows, hidden, mixed, table_sems, tok_sems, in_sems,
      down_sems) = refs[13 + n_pieces :]
-    n_seq, tok_rows, model_width = toks.shape
-    n_z = n_seq // 2
+    n_z, _, tok_rows, model_width = toks.shape
+    n_seq = 2 * n_z
     exp_dev, hid_dev, _ = w_gate_hbm.shape
     width = model_width // 8
     slots_src = exp_dev * SLOTS
@@ -175,48 +174,51 @@
     def down_copy(e):
         return pltpu.make_async_copy(w_down_hbm.at[e], w_down.at[e], down_sems.at[e])
 
-    def start_down(e, carry):
-        down_copy(e).start()
-        return carry
-
-    for e in range(min(RING, exp_dev)):
-        for copy in in_copies(e):
-            copy.start()
     tables = [
         pltpu.make_async_copy(picks_hbm, picks, table_sems.at[0]),
         pltpu.make_async_copy(weights_hbm, weights, table_sems.at[1]),
     ]
     tables[0].start()
 
-    pltpu.make_async_copy(own_hbm, toks.at[0], tok_sems.at[0]).start()
     kinds = token_pieces(n_z)
+    tok_copies = [pltpu.make_async_copy(own_hbm, toks.at[0, 0], tok_sems.at[0])]
     for i, piece in enumerate(pieces_in):
-        dc = i // len(kinds)
-        for at, (j, runs) in enumerate(kinds[i % len(kinds)]):
-            block = piece if len(piece.shape) == 2 else piece.at[at]
-            for n, (color, dx) in enumerate(runs):
-                cols = pl.ds(group_offset(rep, color, dx, dc, width), width)
-                pltpu.make_async_copy(
-                    block.at[pl.ds(0, tok_rows), pl.ds(n * width, width)],
-                    toks.at[j, :, cols],
-                    tok_sems.at[j],
-                ).start()
-
+        blocks, runs = kinds[i % len(kinds)]
+        for n, (color, dx) in enumerate(runs):
+            cols = pl.ds(group_offset(rep, color, dx, i // len(kinds), width), width)
+            for at, dz, count, dy in blocks:
+                tok_copies.append(
+                    pltpu.make_async_copy(
+                        piece.at[pl.ds(at, count), pl.ds(0, tok_rows), pl.ds(n * width, width)],
+                        toks.at[pl.ds(dz, count), dy, :, cols],
+                        tok_sems.at[len(tok_copies)],
+                    )
+                )
+    for copy in tok_copies:
+        copy.start()
+
+    for e in range(min(RING, exp_dev)):
+        for copy in in_copies(e):
+            copy.start()
     tables[1].start()
     quarters = [slice(2 * q * width, 2 * (q + 1) * width) for q in range(4)]
     tables[0].wait()
 
-    def pick(pair, carry):
-        for j in (2 * pair, 2 * pair + 1):
-            pltpu.make_async_copy(toks.at[j], toks.at[j], tok_sems.at[j]).wait()
-        for j in (2 * pair, 2 * pair + 1):
-            onehot = picks[j]
-            for cols in quarters:
-                got = contract(onehot, toks[j, :, cols], 1, 0).astype(jnp.bfloat16)
-                rows[j, :, :, cols] = got.reshape(exp_dev, SLOTS, 2 * width)
+    tok_copies[0].wait()
+
+    def pick(j, carry):
+        @pl.when(j == 1)
+        def _():
+            for copy in tok_copies[1:]:
+                copy.wait()
+
+        onehot = picks[j]
+        for cols in quarters:
+            got = contract(onehot, toks[j // 2, j % 2, :, cols], 1, 0).astype(jnp.bfloat16)
+            rows[j, :, :, cols] = got.reshape(exp_dev, SLOTS, 2 * width)
         return carry
 
-    lax.fori_loop(0, n_z, pick, 0)
+    lax.fori_loop(0, n_seq, pick, 0)
 
     def widen(pair, carry):
         experts = (2 * pair, 2 * pair + 1)
@@ -234,15 +236,12 @@
             act = gate_val / (1.0 + jnp.exp(-gate_val)) * up_val
             hidden[e] = act.T.astype(jnp.bfloat16)
         for e in experts:
+            down_copy(e).start()
 
             @pl.when(e + RING < exp_dev)
             def _():
                 for copy in in_copies(e + RING):
                     copy.start()
-
-        @pl.when(pair == max((exp_dev - RING) // 2 - 1, 0))
-        def _():
-            lax.fori_loop(0, exp_dev, start_down, 0)
 
         return carry
 
@@ -313,16 +312,16 @@
             pltpu.VMEM(weights.shape, jnp.bfloat16),
             pltpu.VMEM((RING, 2 * hid_dev, model_width), jnp.bfloat16),
             pltpu.VMEM(w_down.shape, jnp.bfloat16),
-            pltpu.VMEM((n_seq, tok_rows, model_width), jnp.bfloat16),
+            pltpu.VMEM((n_z, 2, tok_rows, model_width), jnp.bfloat16),
             pltpu.VMEM((n_seq, exp_dev, SLOTS, model_width), jnp.bfloat16),
             pltpu.VMEM((exp_dev, n_seq * SLOTS, hid_dev), jnp.bfloat16),
             pltpu.VMEM((2, tok_rows, model_width), jnp.float32),
             pltpu.SemaphoreType.DMA((2,)),
-            pltpu.SemaphoreType.DMA((n_seq,)),
+            pltpu.SemaphoreType.DMA((len(pieces) + 7,)),
             pltpu.SemaphoreType.DMA((2, RING)),
             pltpu.SemaphoreType.DMA((exp_dev,)),
         ],
-        compiler_params=pltpu.CompilerParams(vmem_limit_bytes=46 * 1024 * 1024),
+        compiler_params=pltpu.CompilerParams(vmem_limit_bytes=42 * 1024 * 1024),
         cost_estimate=pl.CostEstimate(
             flops=6 * n_seq * SLOTS * exp_dev * hid_dev * model_width,
             bytes_accessed=6 * exp_dev * hid_dev * model_width + 4 * n_seq * own.size,
@@ -351,16 +350,16 @@
         tokens, norm_gain, refusal_dir, expert_ids, gate_probs
     )
     second = [swap(second, "seq", 2 * d) for d in others]
-    from_y = swap(to_y, "seq", 1)
+    from_y = swap(to_y[None], "seq", 1)
     first, second, from_y = lax.optimization_barrier((first, jnp.stack(second), from_y))
     first = jnp.stack([swap(first, "seq", 2 * d) for d in others])
     x_two = swap(second[:, :tok_rows], "rep", 2)
     y_one = swap(second, "seq", 1)
     y_two = swap(first, "seq", 1)
-    x_one = swap(jnp.concatenate([first, from_y[None, :tok_rows, :width]]), "rep", 2)
+    x_one = swap(jnp.concatenate([from_y[:, :tok_rows, :width], first]), "rep", 2)
     to_y, to_core = lax.optimization_barrier((x_two, second))
     y_three = swap(to_y, "seq", 1)
-    below = [meta, from_y[tok_rows:, :tok_rows]]
+    below = [meta, from_y[0, tok_rows:, :tok_rows]]
     for d in range(n_z - 1):
         below += [second[d, tok_rows:, :tok_rows], y_one[d, tok_rows:, :tok_rows]]
     picks, weights = route(jnp.stack(below), exp_dev)

time: 102 us -> 100 us (0.980)
  Pallas kernels: 28.4 us -> 26.7 us
    pallas_call x1, Pallas kernels: 23.2 us -> 21.5 us  [moe_partial(): pl.pallas_call(functools.partial(moe_kernel, n_pieces), out_shape=outs, i...]
where the time goes in v7:
time: 100 us
  starting transfers between devices  36.7 us (37%)
  waiting for transfers between devices  34.1 us (34%)
  Pallas kernels  26.7 us (27%)
  other arithmetic  1.62 us (2%)
    ppermute x37, starting transfers between devices, swap(): return lax.ppermute(value, axis, [(i, i ^ distance) for i in range(size)])  36.7 us
    ppermute x37, waiting for transfers between devices, swap(): return lax.ppermute(value, axis, [(i, i ^ distance) for i in range(size)])  34.1 us
    pallas_call x1, Pallas kernels, moe_partial(): pl.pallas_call(functools.partial(moe_kernel, n_pieces), out_shape=outs, i...  21.5 us
    pallas_call x1, Pallas kernels, route(): pl.pallas_call(functools.partial(route_kernel, exp_dev), out_shape=[jax.S...  2.72 us
    pallas_call x1, Pallas kernels, norm_and_base(): pl.pallas_call(norm_kernel, out_shape=[jax.ShapeDtypeStruct((tok_rows, mo...  2.46 us
  transfers between devices with their start and end apart: 37, of which 16 were waited for; matrix products, arithmetic and copies ran while one was open for 2% of the time, Pallas kernels for 3%

profile of v7, /device:TPU:0, one launch (start us, length us, event | category | flops | bytes accessed | tf_op | source)
XLA Modules:
  0.0 100.1 jit_solution(1457613446905582605)
XLA Ops:
  0.0 2.5 %shard_map.82 = (bf16[128,2048]{1,0:T(8,128)(2,1)}, bf16[144,256]{1,0:T(8,128)(2,1)}, bf16[128,256]{1,0:T(8,128)(2,1)}, bf16[144,768]{1,0:T(8,128)(2,1)}, f32[1,...) custom-call(bf16[128,2048]{1,0:T(8,128)(2,1)} %tokens_ref.1, f32[1,2048]{1,0:T(1,128)} %bitcast.63, ...), custom_call_target="tpu_custom_call" | custom-call | tf_op jit(solution)/shard_map/pallas_call | solution.py:74
  2.5 5.1 %collective-permute-start.2 = (bf16[144,256]{1,0:T(8,128)(2,1)}, bf16[144,256]{1,0:T(8,128)(2,1)S(1)}, u32[]{:S(2)}, u32[]{:S(2)}) collective-permute-start(bf16[144,256]{1,0:T(8,128)(2,1)} %get-tuple-element.38), channel_id=1, source_target_pairs={{0,24},{4,28},{8,16},{12,20},{16,8},{20,12},{24,0},{28,4},{1,25},{... | collective-permute-start | bytes 221192 | tf_op jit(solution)/shard_map/ppermute | solution.py:335
  8.2 1.7 %collective-permute-start.3 = (bf16[1,144,768]{2,1,0:T(8,128)(2,1)}, bf16[1,144,768]{2,1,0:T(8,128)(2,1)S(1)}, u32[]{:S(2)}, u32[]{:S(2)}) collective-permute-start(bf16[1,144,768]{2,1,0:T(8,128)(2,1)} %bitcast.67), channel_id=1, source_target_pairs={{0,4},{4,0},{8,12},{12,8},{16,20},{20,16},{24,28},{28,24},{1,5},{5... | collective-permute-start | bytes 663560 | tf_op jit(solution)/shard_map/ppermute | solution.py:335
  10.5 3.4 %collective-permute-done.1 = bf16[144,256]{1,0:T(8,128)(2,1)S(1)} collective-permute-done((bf16[144,256]{1,0:T(8,128)(2,1)}, bf16[144,256]{1,0:T(8,128)(2,1)S(1)}, u32[]{:S(2)}, u32[]{:S(2)}) %collective-permute-start.1) | collective-permute-done | bytes 73760 | tf_op jit(solution)/shard_map/ppermute | solution.py:335
  14.0 1.0 collective-permute-done.3.refs_6_
  15.0 3.5 %collective-permute-start.7 = (bf16[128,256]{1,0:T(8,128)(2,1)}, bf16[128,256]{1,0:T(8,128)(2,1)S(1)}, u32[]{:S(2)}, u32[]{:S(2)}) collective-permute-start(bf16[128,256]{1,0:T(8,128)(2,1)} %get-tuple-element.49), channel_id=1, source_target_pairs={{0,24},{4,28},{8,16},{12,20},{16,8},{20,12},{24,0},{28,4},{1,25},{... | collective-permute-start | bytes 196616 | tf_op jit(solution)/shard_map/ppermute | solution.py:335
  18.5 0.9 collective-permute-start.5
  19.4 1.6 %collective-permute-start.4 = (bf16[3,144,256]{2,1,0:T(8,128)(2,1)S(1)}, bf16[3,144,256]{2,1,0:T(8,128)(2,1)S(1)}, u32[]{:S(2)}, u32[]{:S(2)}) collective-permute-start(bf16[3,144,256]{2,1,0:T(8,128)(2,1)S(1)} %pad_maximum_fusion.1.refs_4_), channel_id=1, source_target_pairs={{0,4},{4,0},{8,12},{12,8},{16,20},{20,16},{24,28},{28,24},{1,5},{5... | collective-permute-start | bytes 663560 | tf_op jit(solution)/shard_map/ppermute | solution.py:335
  21.0 1.5 %collective-permute-start.8 = (bf16[3,128,256]{2,1,0:T(8,128)(2,1)S(1)}, bf16[3,128,256]{2,1,0:T(8,128)(2,1)S(1)}, u32[]{:S(2)}, u32[]{:S(2)}) collective-permute-start(bf16[3,128,256]{2,1,0:T(8,128)(2,1)S(1)} %slice.121), channel_id=1, source_target_pairs={{0,2},{1,3},{2,0},{3,1},{4,6},{5,7},{6,4},{7,5},{8,10},{9,11},{10,... | collective-permute-start | bytes 589832 | tf_op jit(solution)/shard_map/ppermute | solution.py:335
  22.5 1.3 %collective-permute-done.6 = bf16[128,256]{1,0:T(8,128)(2,1)S(1)} collective-permute-done((bf16[128,256]{1,0:T(8,128)(2,1)}, bf16[128,256]{1,0:T(8,128)(2,1)S(1)}, u32[]{:S(2)}, u32[]{:S(2)}) %collective-permute-start.6) | collective-permute-done | bytes 65568 | tf_op jit(solution)/shard_map/ppermute | solution.py:335
  23.9 1.6 %collective-permute-start.10 = (bf16[3,128,256]{2,1,0:T(8,128)(2,1)S(1)}, bf16[3,128,256]{2,1,0:T(8,128)(2,1)S(1)}, u32[]{:S(2)}, u32[]{:S(2)}) collective-permute-start(bf16[3,128,256]{2,1,0:T(8,128)(2,1)S(1)} %pad_maximum_fusion.2.refs_5_), channel_id=1, source_target_pairs={{0,4},{4,0},{8,12},{12,8},{16,20},{20,16},{24,28},{28,24},{1,5},{5... | collective-permute-start | bytes 589832 | tf_op jit(solution)/shard_map/ppermute | solution.py:335
  25.6 1.6 %collective-permute-start.9 = (bf16[4,128,256]{2,1,0:T(8,128)(2,1)S(1)}, bf16[4,128,256]{2,1,0:T(8,128)(2,1)S(1)}, u32[]{:S(2)}, u32[]{:S(2)}) collective-permute-start(bf16[4,128,256]{2,1,0:T(8,128)(2,1)S(1)} %pad_maximum_fusion), channel_id=1, source_target_pairs={{0,2},{1,3},{2,0},{3,1},{4,6},{5,7},{6,4},{7,5},{8,10},{9,11},{10,... | collective-permute-start | bytes 786440 | tf_op jit(solution)/shard_map/ppermute | solution.py:335
  28.3 3.4 %collective-permute-done.10.refs_10_ = bf16[3,128,256]{2,1,0:T(8,128)(2,1)S(1)} collective-permute-done((bf16[3,128,256]{2,1,0:T(8,128)(2,1)S(1)}, bf16[3,128,256]{2,1,0:T(8,128)(2,1)S(1)}, u32[]{:S(2)}, u32[]{:S(2)}) %collective-permute-start.10) | collective-permute-done | bytes 196640 | tf_op jit(solution)/shard_map/ppermute | solution.py:335
  31.7 2.3 %collective-permute-done.9.refs_9_ = bf16[4,128,256]{2,1,0:T(8,128)(2,1)S(1)} collective-permute-done((bf16[4,128,256]{2,1,0:T(8,128)(2,1)S(1)}, bf16[4,128,256]{2,1,0:T(8,128)(2,1)S(1)}, u32[]{:S(2)}, u32[]{:S(2)}) %collective-permute-start.9) | collective-permute-done | bytes 262176 | tf_op jit(solution)/shard_map/ppermute | solution.py:335
  34.0 1.5 %collective-permute-start.12 = (bf16[3,128,256]{2,1,0:T(8,128)(2,1)S(1)}, bf16[3,128,256]{2,1,0:T(8,128)(2,1)S(1)}, u32[]{:S(2)}, u32[]{:S(2)}) collective-permute-start(bf16[3,128,256]{2,1,0:T(8,128)(2,1)S(1)} %collective-permute-done.10.refs_10_), channel_id=1, source_target_pairs={{0,2},{1,3},{2,0},{3,1},{4,6},{5,7},{6,4},{7,5},{8,10},{9,11},{10,... | collective-permute-start | bytes 589832 | tf_op jit(solution)/shard_map/ppermute | solution.py:335
  35.5 2.7 %shard_map.83 = (bf16[8,256,128]{2,1,0:T(8,128)(2,1)}, bf16[8,128,256]{2,1,0:T(8,128)(2,1)}) custom-call(bf16[8,16,128]{2,1,0:T(8,128)(2,1)} %copy-done.2), custom_call_target="tpu_custom_call" | custom-call | flops 4000000000 | bytes 2097152 | tf_op jit(solution)/shard_map/pallas_call | solution.py:132
  39.3 0.9 collective-permute-done.12.refs_12_
  40.5 1.1 %collective-permute-done.21.refs_21_ = bf16[3,128,256]{2,1,0:T(8,128)(2,1)S(1)} collective-permute-done((bf16[3,128,256]{2,1,0:T(8,128)(2,1)S(1)}, bf16[3,128,256]{2,1,0:T(8,128)(2,1)S(1)}, u32[]{:S(2)}, u32[]{:S(2)}) %collective-permute-start.21) | collective-permute-done | bytes 196640 | tf_op jit(solution)/shard_map/ppermute | solution.py:335
  41.6 21.5 %shard_map.84 = (bf16[4,4,112,256]{3,2,1,0:T(8,128)(2,1)S(1)}, bf16[4,4,112,256]{3,2,1,0:T(8,128)(2,1)S(1)}, bf16[4,2,16,1024]{3,2,1,0:T(8,128)(2,1)S(1)}, bf16[...) custom-call(bf16[8,256,128]{2,1,0:T(8,128)(2,1)} %get-tuple-element.45.re, ...), custom_call_target="tpu_custom_call" | custom-call | flops 4831838208 | bytes 46137344 | tf_op jit(solution)/shard_map/pallas_call | solution.py:305
  63.8 1.8 %collective-permute-done.23 = bf16[4,4,112,256]{3,2,1,0:T(8,128)(2,1)S(1)} collective-permute-done((bf16[4,4,112,256]{3,2,1,0:T(8,128)(2,1)S(1)}, bf16[4,4,112,256]{3,2,1,0:T(8,128)(2,1)S(1)}, u32[]{:S(2)}, u32[]{:S(2)}) %collective-permute-start.23) | collective-permute-done | bytes 917536 | tf_op jit(solution)/shard_map/ppermute | solution.py:335
  65.9 1.6 %collective-permute-start.24 = (bf16[2,4,112,256]{3,2,1,0:T(8,128)(2,1)S(1)}, bf16[2,4,112,256]{3,2,1,0:T(8,128)(2,1)S(1)}, u32[]{:S(2)}, u32[]{:S(2)}) collective-permute-start(bf16[2,4,112,256]{3,2,1,0:T(8,128)(2,1)S(1)} %get-tuple-element.58), channel_id=1, source_target_pairs={{0,2},{1,3},{2,0},{3,1},{4,6},{5,7},{6,4},{7,5},{8,10},{9,11},{10,... | collective-permute-start | bytes 1376264 | tf_op jit(solution)/shard_map/ppermute | solution.py:335
  68.2 2.1 %collective-permute-start.29 = (bf16[2,16,1024]{2,1,0:T(8,128)(2,1)S(1)}, bf16[2,16,1024]{2,1,0:T(8,128)(2,1)S(1)}, u32[]{:S(2)}, u32[]{:S(2)}) collective-permute-start(bf16[2,16,1024]{2,1,0:T(8,128)(2,1)S(1)} %get-tuple-element.76), channel_id=1, source_target_pairs={{0,24},{4,28},{8,16},{12,20},{16,8},{20,12},{24,0},{28,4},{1,25},{... | collective-permute-start | bytes 196616 | tf_op jit(solution)/shard_map/ppermute | solution.py:335
  70.3 2.3 %collective-permute-start.27 = (bf16[2,16,1024]{2,1,0:T(8,128)(2,1)S(1)}, bf16[2,16,1024]{2,1,0:T(8,128)(2,1)S(1)}, u32[]{:S(2)}, u32[]{:S(2)}) collective-permute-start(bf16[2,16,1024]{2,1,0:T(8,128)(2,1)S(1)} %get-tuple-element.78), channel_id=1, source_target_pairs={{0,8},{4,12},{8,0},{12,4},{16,24},{20,28},{24,16},{28,20},{1,9},{5... | collective-permute-start | bytes 196616 | tf_op jit(solution)/shard_map/ppermute | solution.py:335
  72.6 5.9 %collective-permute-done.24 = bf16[2,4,112,256]{3,2,1,0:T(8,128)(2,1)S(1)} collective-permute-done((bf16[2,4,112,256]{3,2,1,0:T(8,128)(2,1)S(1)}, bf16[2,4,112,256]{3,2,1,0:T(8,128)(2,1)S(1)}, u32[]{:S(2)}, u32[]{:S(2)}) %collective-permute-start.24) | collective-permute-done | bytes 458784 | tf_op jit(solution)/shard_map/ppermute | solution.py:335
  78.5 1.2 %collective-permute-done.25 = bf16[2,4,112,256]{3,2,1,0:T(8,128)(2,1)S(1)} collective-permute-done((bf16[2,4,112,256]{3,2,1,0:T(8,128)(2,1)S(1)}, bf16[2,4,112,256]{3,2,1,0:T(8,128)(2,1)S(1)}, u32[]{:S(2)}, u32[]{:S(2)}) %collective-permute-start.25) | collective-permute-done | bytes 458784 | tf_op jit(solution)/shard_map/ppermute | solution.py:335
  80.9 1.2 %collective-permute-start.30 = (bf16[4,112,256]{2,1,0:T(8,128)(2,1)S(1)}, bf16[4,112,256]{2,1,0:T(8,128)(2,1)S(1)}, u32[]{:S(2)}, u32[]{:S(2)}) collective-permute-start(bf16[4,112,256]{2,1,0:T(8,128)(2,1)S(1)} %get-tuple-element.62), channel_id=1, source_target_pairs={{0,4},{4,0},{8,12},{12,8},{16,20},{20,16},{24,28},{28,24},{1,5},{5... | collective-permute-start | bytes 688136 | tf_op jit(solution)/shard_map/ppermute | solution.py:335
  82.6 1.7 %collective-permute-done.35 = bf16[16,1024]{1,0:T(8,128)(2,1)S(1)} collective-permute-done((bf16[16,1024]{1,0:T(8,128)(2,1)S(1)}, bf16[16,1024]{1,0:T(8,128)(2,1)S(1)}, u32[]{:S(2)}, u32[]{:S(2)}) %collective-permute-start.35) | collective-permute-done | bytes 32800 | tf_op jit(solution)/shard_map/ppermute | solution.py:335
  85.0 2.7 %collective-permute-done.30 = bf16[4,112,256]{2,1,0:T(8,128)(2,1)S(1)} collective-permute-done((bf16[4,112,256]{2,1,0:T(8,128)(2,1)S(1)}, bf16[4,112,256]{2,1,0:T(8,128)(2,1)S(1)}, u32[]{:S(2)}, u32[]{:S(2)}) %collective-permute-start.30) | collective-permute-done | bytes 229408 | tf_op jit(solution)/shard_map/ppermute | solution.py:335
  88.5 2.1 %collective-permute-start.32 = (bf16[112,512]{1,0:T(8,128)(2,1)S(1)}, bf16[112,512]{1,0:T(8,128)(2,1)S(1)}, u32[]{:S(2)}, u32[]{:S(2)}) collective-permute-start(bf16[112,512]{1,0:T(8,128)(2,1)S(1)} %get-tuple-element.73), channel_id=1, source_target_pairs={{0,24},{4,28},{8,16},{12,20},{16,8},{20,12},{24,0},{28,4},{1,25},{... | collective-permute-start | bytes 344072 | tf_op jit(solution)/shard_map/ppermute | solution.py:335
  90.6 2.3 %collective-permute-start.34 = (bf16[112,512]{1,0:T(8,128)(2,1)S(1)}, bf16[112,512]{1,0:T(8,128)(2,1)S(1)}, u32[]{:S(2)}, u32[]{:S(2)}) collective-permute-start(bf16[112,512]{1,0:T(8,128)(2,1)S(1)} %get-tuple-element.75), channel_id=1, source_target_pairs={{0,8},{4,12},{8,0},{12,4},{16,24},{20,28},{24,16},{28,20},{1,9},{5... | collective-permute-start | bytes 344072 | tf_op jit(solution)/shard_map/ppermute | solution.py:335
  92.9 2.9 %collective-permute-done.32 = bf16[112,512]{1,0:T(8,128)(2,1)S(1)} collective-permute-done((bf16[112,512]{1,0:T(8,128)(2,1)S(1)}, bf16[112,512]{1,0:T(8,128)(2,1)S(1)}, u32[]{:S(2)}, u32[]{:S(2)}) %collective-permute-start.32) | collective-permute-done | bytes 114720 | tf_op jit(solution)/shard_map/ppermute | solution.py:335
  95.8 3.5 %collective-permute-done.33 = bf16[112,512]{1,0:T(8,128)(2,1)S(1)} collective-permute-done((bf16[112,512]{1,0:T(8,128)(2,1)S(1)}, bf16[112,512]{1,0:T(8,128)(2,1)S(1)}, u32[]{:S(2)}, u32[]{:S(2)}) %collective-permute-start.33) | collective-permute-done | bytes 114720 | tf_op jit(solution)/shard_map/ppermute | solution.py:335
  (78 shorter events, 9.6 us)
Async XLA Ops:
  2.5 8.1 %collective-permute-start.2 = (bf16[144,256]{1,0:T(8,128)(2,1)}, bf16[144,256]{1,0:T(8,128)(2,1)S(1)}, u32[]{:S(2)}, u32[]{:S(2)}) collective-permute-start(bf16[144,256]{1,0:T(8,128)(2,1)} %get-tuple-element.38), channel_id=1, source_target_pairs={{0,24},{4,28},{8,16},{12,20},{16,8},{20,12},{24,0},{28,4},{1,25},{... | collective-permute-start | bytes 221192 | tf_op jit(solution)/shard_map/ppermute | solution.py:335
  7.5 6.4 %collective-permute-start.1 = (bf16[144,256]{1,0:T(8,128)(2,1)}, bf16[144,256]{1,0:T(8,128)(2,1)S(1)}, u32[]{:S(2)}, u32[]{:S(2)}) collective-permute-start(bf16[144,256]{1,0:T(8,128)(2,1)} %get-tuple-element.38), channel_id=1, source_target_pairs={{0,16},{4,20},{8,24},{12,28},{16,0},{20,4},{24,8},{28,12},{1,17},{... | collective-permute-start | bytes 221192 | tf_op jit(solution)/shard_map/ppermute | solution.py:335
  7.5 6.4 %collective-permute-start = (bf16[144,256]{1,0:T(8,128)(2,1)}, bf16[144,256]{1,0:T(8,128)(2,1)S(1)}, u32[]{:S(2)}, u32[]{:S(2)}) collective-permute-start(bf16[144,256]{1,0:T(8,128)(2,1)} %get-tuple-element.38), channel_id=1, source_target_pairs={{0,8},{4,12},{8,0},{12,4},{16,24},{20,28},{24,16},{28,20},{1,9},{5... | collective-permute-start | bytes 221192 | tf_op jit(solution)/shard_map/ppermute | solution.py:335
  8.2 6.8 %collective-permute-start.3 = (bf16[1,144,768]{2,1,0:T(8,128)(2,1)}, bf16[1,144,768]{2,1,0:T(8,128)(2,1)S(1)}, u32[]{:S(2)}, u32[]{:S(2)}) collective-permute-start(bf16[1,144,768]{2,1,0:T(8,128)(2,1)} %bitcast.67), channel_id=1, source_target_pairs={{0,4},{4,0},{8,12},{12,8},{16,20},{20,16},{24,28},{28,24},{1,5},{5... | collective-permute-start | bytes 663560 | tf_op jit(solution)/shard_map/ppermute | solution.py:335
  15.0 7.5 %collective-permute-start.7 = (bf16[128,256]{1,0:T(8,128)(2,1)}, bf16[128,256]{1,0:T(8,128)(2,1)S(1)}, u32[]{:S(2)}, u32[]{:S(2)}) collective-permute-start(bf16[128,256]{1,0:T(8,128)(2,1)} %get-tuple-element.49), channel_id=1, source_target_pairs={{0,24},{4,28},{8,16},{12,20},{16,8},{20,12},{24,0},{28,4},{1,25},{... | collective-permute-start | bytes 196616 | tf_op jit(solution)/shard_map/ppermute | solution.py:335
  18.5 5.4 %collective-permute-start.6 = (bf16[128,256]{1,0:T(8,128)(2,1)}, bf16[128,256]{1,0:T(8,128)(2,1)S(1)}, u32[]{:S(2)}, u32[]{:S(2)}) collective-permute-start(bf16[128,256]{1,0:T(8,128)(2,1)} %get-tuple-element.49), channel_id=1, source_target_pairs={{0,16},{4,20},{8,24},{12,28},{16,0},{20,4},{24,8},{28,12},{1,17},{... | collective-permute-start | bytes 196616 | tf_op jit(solution)/shard_map/ppermute | solution.py:335
  18.5 5.4 %collective-permute-start.5 = (bf16[128,256]{1,0:T(8,128)(2,1)}, bf16[128,256]{1,0:T(8,128)(2,1)S(1)}, u32[]{:S(2)}, u32[]{:S(2)}) collective-permute-start(bf16[128,256]{1,0:T(8,128)(2,1)} %get-tuple-element.49), channel_id=1, source_target_pairs={{0,8},{4,12},{8,0},{12,4},{16,24},{20,28},{24,16},{28,20},{1,9},{5... | collective-permute-start | bytes 196616 | tf_op jit(solution)/shard_map/ppermute | solution.py:335
  19.4 8.2 %collective-permute-start.4 = (bf16[3,144,256]{2,1,0:T(8,128)(2,1)S(1)}, bf16[3,144,256]{2,1,0:T(8,128)(2,1)S(1)}, u32[]{:S(2)}, u32[]{:S(2)}) collective-permute-start(bf16[3,144,256]{2,1,0:T(8,128)(2,1)S(1)} %pad_maximum_fusion.1.refs_4_), channel_id=1, source_target_pairs={{0,4},{4,0},{8,12},{12,8},{16,20},{20,16},{24,28},{28,24},{1,5},{5... | collective-permute-start | bytes 663560 | tf_op jit(solution)/shard_map/ppermute | solution.py:335
  21.0 6.1 %collective-permute-start.8 = (bf16[3,128,256]{2,1,0:T(8,128)(2,1)S(1)}, bf16[3,128,256]{2,1,0:T(8,128)(2,1)S(1)}, u32[]{:S(2)}, u32[]{:S(2)}) collective-permute-start(bf16[3,128,256]{2,1,0:T(8,128)(2,1)S(1)} %slice.121), channel_id=1, source_target_pairs={{0,2},{1,3},{2,0},{3,1},{4,6},{5,7},{6,4},{7,5},{8,10},{9,11},{10,... | collective-permute-start | bytes 589832 | tf_op jit(solution)/shard_map/ppermute | solution.py:335
  23.9 3.8 %collective-permute-start.14 = (bf16[3,128,256]{2,1,0:T(8,128)(2,1)S(1)}, bf16[3,128,256]{2,1,0:T(8,128)(2,1)S(1)}, u32[]{:S(2)}, u32[]{:S(2)}) collective-permute-start(bf16[3,128,256]{2,1,0:T(8,128)(2,1)S(1)} %pad_maximum_fusion.2.refs_5_), channel_id=1, source_target_pairs={{0,1},{1,0},{2,3},{3,2},{4,5},{5,4},{6,7},{7,6},{8,9},{9,8},{10,11... | collective-permute-start | bytes 589832 | tf_op jit(solution)/shard_map/ppermute | solution.py:335
  23.9 7.8 %collective-permute-start.10 = (bf16[3,128,256]{2,1,0:T(8,128)(2,1)S(1)}, bf16[3,128,256]{2,1,0:T(8,128)(2,1)S(1)}, u32[]{:S(2)}, u32[]{:S(2)}) collective-permute-start(bf16[3,128,256]{2,1,0:T(8,128)(2,1)S(1)} %pad_maximum_fusion.2.refs_5_), channel_id=1, source_target_pairs={{0,4},{4,0},{8,12},{12,8},{16,20},{20,16},{24,28},{28,24},{1,5},{5... | collective-permute-start | bytes 589832 | tf_op jit(solution)/shard_map/ppermute | solution.py:335
  25.6 8.4 %collective-permute-start.9 = (bf16[4,128,256]{2,1,0:T(8,128)(2,1)S(1)}, bf16[4,128,256]{2,1,0:T(8,128)(2,1)S(1)}, u32[]{:S(2)}, u32[]{:S(2)}) collective-permute-start(bf16[4,128,256]{2,1,0:T(8,128)(2,1)S(1)} %pad_maximum_fusion), channel_id=1, source_target_pairs={{0,2},{1,3},{2,0},{3,1},{4,6},{5,7},{6,4},{7,5},{8,10},{9,11},{10,... | collective-permute-start | bytes 786440 | tf_op jit(solution)/shard_map/ppermute | solution.py:335
  27.1 8.4 %collective-permute-start.11 = (bf16[3,128,256]{2,1,0:T(8,128)(2,1)S(1)}, bf16[3,128,256]{2,1,0:T(8,128)(2,1)S(1)}, u32[]{:S(2)}, u32[]{:S(2)}) collective-permute-start(bf16[3,128,256]{2,1,0:T(8,128)(2,1)S(1)} %collective-permute-done.8.refs_7_), channel_id=1, source_target_pairs={{0,4},{4,0},{8,12},{12,8},{16,20},{20,16},{24,28},{28,24},{1,5},{5... | collective-permute-start | bytes 589832 | tf_op jit(solution)/shard_map/ppermute | solution.py:335
  27.6 11.1 %collective-permute-start.13 = (bf16[3,144,256]{2,1,0:T(8,128)(2,1)S(1)}, bf16[3,144,256]{2,1,0:T(8,128)(2,1)S(1)}, u32[]{:S(2)}, u32[]{:S(2)}) collective-permute-start(bf16[3,144,256]{2,1,0:T(8,128)(2,1)S(1)} %pad_maximum_fusion.1.refs_4_), channel_id=1, source_target_pairs={{0,1},{1,0},{2,3},{3,2},{4,5},{5,4},{6,7},{7,6},{8,9},{9,8},{10,11... | collective-permute-start | bytes 663560 | tf_op jit(solution)/shard_map/ppermute | solution.py:335
  27.7 10.5 %collective-permute-start.16 = (bf16[3,128,256]{2,1,0:T(8,128)(2,1)S(1)}, bf16[3,128,256]{2,1,0:T(8,128)(2,1)S(1)}, u32[]{:S(2)}, u32[]{:S(2)}) collective-permute-start(bf16[3,128,256]{2,1,0:T(8,128)(2,1)S(1)} %collective-permute-done.8.refs_7_), channel_id=1, source_target_pairs={{0,1},{1,0},{2,3},{3,2},{4,5},{5,4},{6,7},{7,6},{8,9},{9,8},{10,11... | collective-permute-start | bytes 589832 | tf_op jit(solution)/shard_map/ppermute | solution.py:335
  31.7 7.1 %collective-permute-start.17 = (bf16[3,144,256]{2,1,0:T(8,128)(2,1)S(1)}, bf16[3,144,256]{2,1,0:T(8,128)(2,1)S(1)}, u32[]{:S(2)}, u32[]{:S(2)}) collective-permute-start(bf16[3,144,256]{2,1,0:T(8,128)(2,1)S(1)} %collective-permute-done.4.refs_8_), channel_id=1, source_target_pairs={{0,1},{1,0},{2,3},{3,2},{4,5},{5,4},{6,7},{7,6},{8,9},{9,8},{10,11... | collective-permute-start | bytes 663560 | tf_op jit(solution)/shard_map/ppermute | solution.py:335
  34.0 6.1 %collective-permute-start.12 = (bf16[3,128,256]{2,1,0:T(8,128)(2,1)S(1)}, bf16[3,128,256]{2,1,0:T(8,128)(2,1)S(1)}, u32[]{:S(2)}, u32[]{:S(2)}) collective-permute-start(bf16[3,128,256]{2,1,0:T(8,128)(2,1)S(1)} %collective-permute-done.10.refs_10_), channel_id=1, source_target_pairs={{0,2},{1,3},{2,0},{3,1},{4,6},{5,7},{6,4},{7,5},{8,10},{9,11},{10,... | collective-permute-start | bytes 589832 | tf_op jit(solution)/shard_map/ppermute | solution.py:335
  35.5 5.0 %collective-permute-start.18 = (bf16[4,128,256]{2,1,0:T(8,128)(2,1)S(1)}, bf16[4,128,256]{2,1,0:T(8,128)(2,1)S(1)}, u32[]{:S(2)}, u32[]{:S(2)}) collective-permute-start(bf16[4,128,256]{2,1,0:T(8,128)(2,1)S(1)} %collective-permute-done.9.refs_9_), channel_id=1, source_target_pairs={{0,1},{1,0},{2,3},{3,2},{4,5},{5,4},{6,7},{7,6},{8,9},{9,8},{10,11... | collective-permute-start | bytes 786440 | tf_op jit(solution)/shard_map/ppermute | solution.py:335
  63.3 7.0 %collective-permute-start.22 = (bf16[4,4,112,256]{3,2,1,0:T(8,128)(2,1)S(1)}, bf16[4,4,112,256]{3,2,1,0:T(8,128)(2,1)S(1)}, u32[]{:S(2)}, u32[]{:S(2)}) collective-permute-start(bf16[4,4,112,256]{3,2,1,0:T(8,128)(2,1)S(1)} %get-tuple-element.54), channel_id=1, source_target_pairs={{0,1},{1,0},{2,3},{3,2},{4,5},{5,4},{6,7},{7,6},{8,9},{9,8},{10,11... | collective-permute-start | bytes 2752520 | tf_op jit(solution)/shard_map/ppermute | solution.py:335
  63.7 4.4 %collective-permute-start.26 = (bf16[4,2,16,1024]{3,2,1,0:T(8,128)(2,1)S(1)}, bf16[4,2,16,1024]{3,2,1,0:T(8,128)(2,1)S(1)}, u32[]{:S(2)}, u32[]{:S(2)}) collective-permute-start(bf16[4,2,16,1024]{3,2,1,0:T(8,128)(2,1)S(1)} %get-tuple-element.61), channel_id=1, source_target_pairs={{0,1},{1,0},{2,3},{3,2},{4,5},{5,4},{6,7},{7,6},{8,9},{9,8},{10,11... | collective-permute-start | bytes 786440 | tf_op jit(solution)/shard_map/ppermute | solution.py:335
  65.9 12.6 %collective-permute-start.24 = (bf16[2,4,112,256]{3,2,1,0:T(8,128)(2,1)S(1)}, bf16[2,4,112,256]{3,2,1,0:T(8,128)(2,1)S(1)}, u32[]{:S(2)}, u32[]{:S(2)}) collective-permute-start(bf16[2,4,112,256]{3,2,1,0:T(8,128)(2,1)S(1)} %get-tuple-element.58), channel_id=1, source_target_pairs={{0,2},{1,3},{2,0},{3,1},{4,6},{5,7},{6,4},{7,5},{8,10},{9,11},{10,... | collective-permute-start | bytes 1376264 | tf_op jit(solution)/shard_map/ppermute | solution.py:335
  67.4 12.3 %collective-permute-start.25 = (bf16[2,4,112,256]{3,2,1,0:T(8,128)(2,1)S(1)}, bf16[2,4,112,256]{3,2,1,0:T(8,128)(2,1)S(1)}, u32[]{:S(2)}, u32[]{:S(2)}) collective-permute-start(bf16[2,4,112,256]{3,2,1,0:T(8,128)(2,1)S(1)} %get-tuple-element.59), channel_id=1, source_target_pairs={{0,4},{4,0},{8,12},{12,8},{16,20},{20,16},{24,28},{28,24},{1,5},{5... | collective-permute-start | bytes 1376264 | tf_op jit(solution)/shard_map/ppermute | solution.py:335
  68.2 11.7 %collective-permute-start.29 = (bf16[2,16,1024]{2,1,0:T(8,128)(2,1)S(1)}, bf16[2,16,1024]{2,1,0:T(8,128)(2,1)S(1)}, u32[]{:S(2)}, u32[]{:S(2)}) collective-permute-start(bf16[2,16,1024]{2,1,0:T(8,128)(2,1)S(1)} %get-tuple-element.76), channel_id=1, source_target_pairs={{0,24},{4,28},{8,16},{12,20},{16,8},{20,12},{24,0},{28,4},{1,25},{... | collective-permute-start | bytes 196616 | tf_op jit(solution)/shard_map/ppermute | solution.py:335
  70.3 9.6 %collective-permute-start.28 = (bf16[2,16,1024]{2,1,0:T(8,128)(2,1)S(1)}, bf16[2,16,1024]{2,1,0:T(8,128)(2,1)S(1)}, u32[]{:S(2)}, u32[]{:S(2)}) collective-permute-start(bf16[2,16,1024]{2,1,0:T(8,128)(2,1)S(1)} %get-tuple-element.77), channel_id=1, source_target_pairs={{0,16},{4,20},{8,24},{12,28},{16,0},{20,4},{24,8},{28,12},{1,17},{... | collective-permute-start | bytes 196616 | tf_op jit(solution)/shard_map/ppermute | solution.py:335
  70.3 9.6 %collective-permute-start.27 = (bf16[2,16,1024]{2,1,0:T(8,128)(2,1)S(1)}, bf16[2,16,1024]{2,1,0:T(8,128)(2,1)S(1)}, u32[]{:S(2)}, u32[]{:S(2)}) collective-permute-start(bf16[2,16,1024]{2,1,0:T(8,128)(2,1)S(1)} %get-tuple-element.78), channel_id=1, source_target_pairs={{0,8},{4,12},{8,0},{12,4},{16,24},{20,28},{24,16},{28,20},{1,9},{5... | collective-permute-start | bytes 196616 | tf_op jit(solution)/shard_map/ppermute | solution.py:335
  80.0 4.4 %collective-permute-start.35 = (bf16[16,1024]{1,0:T(8,128)(2,1)S(1)}, bf16[16,1024]{1,0:T(8,128)(2,1)S(1)}, u32[]{:S(2)}, u32[]{:S(2)}) collective-permute-start(bf16[16,1024]{1,0:T(8,128)(2,1)S(1)} %slice_bitcast_fusion.4), channel_id=1, source_target_pairs={{0,4},{4,0},{8,12},{12,8},{16,20},{20,16},{24,28},{28,24},{1,5},{5... | collective-permute-start | bytes 98312 | tf_op jit(solution)/shard_map/ppermute | solution.py:335
  80.9 6.8 %collective-permute-start.30 = (bf16[4,112,256]{2,1,0:T(8,128)(2,1)S(1)}, bf16[4,112,256]{2,1,0:T(8,128)(2,1)S(1)}, u32[]{:S(2)}, u32[]{:S(2)}) collective-permute-start(bf16[4,112,256]{2,1,0:T(8,128)(2,1)S(1)} %get-tuple-element.62), channel_id=1, source_target_pairs={{0,4},{4,0},{8,12},{12,8},{16,20},{20,16},{24,28},{28,24},{1,5},{5... | collective-permute-start | bytes 688136 | tf_op jit(solution)/shard_map/ppermute | solution.py:335
  82.1 6.1 %collective-permute-start.31 = (bf16[4,112,256]{2,1,0:T(8,128)(2,1)S(1)}, bf16[4,112,256]{2,1,0:T(8,128)(2,1)S(1)}, u32[]{:S(2)}, u32[]{:S(2)}) collective-permute-start(bf16[4,112,256]{2,1,0:T(8,128)(2,1)S(1)} %get-tuple-element.63), channel_id=1, source_target_pairs={{0,2},{1,3},{2,0},{3,1},{4,6},{5,7},{6,4},{7,5},{8,10},{9,11},{10,... | collective-permute-start | bytes 688136 | tf_op jit(solution)/shard_map/ppermute | solution.py:335
  84.4 8.5 %collective-permute-start.36 = (bf16[16,512]{1,0:T(8,128)(2,1)S(1)}, bf16[16,512]{1,0:T(8,128)(2,1)S(1)}, u32[]{:S(2)}, u32[]{:S(2)}) collective-permute-start(bf16[16,512]{1,0:T(8,128)(2,1)S(1)} %pad_maximum_fusion.4), channel_id=1, source_target_pairs={{0,2},{1,3},{2,0},{3,1},{4,6},{5,7},{6,4},{7,5},{8,10},{9,11},{10,... | collective-permute-start | bytes 49160 | tf_op jit(solution)/shard_map/ppermute | solution.py:335
  88.5 7.3 %collective-permute-start.32 = (bf16[112,512]{1,0:T(8,128)(2,1)S(1)}, bf16[112,512]{1,0:T(8,128)(2,1)S(1)}, u32[]{:S(2)}, u32[]{:S(2)}) collective-permute-start(bf16[112,512]{1,0:T(8,128)(2,1)S(1)} %get-tuple-element.73), channel_id=1, source_target_pairs={{0,24},{4,28},{8,16},{12,20},{16,8},{20,12},{24,0},{28,4},{1,25},{... | collective-permute-start | bytes 344072 | tf_op jit(solution)/shard_map/ppermute | solution.py:335
  90.6 8.7 %collective-permute-start.33 = (bf16[112,512]{1,0:T(8,128)(2,1)S(1)}, bf16[112,512]{1,0:T(8,128)(2,1)S(1)}, u32[]{:S(2)}, u32[]{:S(2)}) collective-permute-start(bf16[112,512]{1,0:T(8,128)(2,1)S(1)} %get-tuple-element.74), channel_id=1, source_target_pairs={{0,16},{4,20},{8,24},{12,28},{16,0},{20,4},{24,8},{28,12},{1,17},{... | collective-permute-start | bytes 344072 | tf_op jit(solution)/shard_map/ppermute | solution.py:335
  90.6 8.7 %collective-permute-start.34 = (bf16[112,512]{1,0:T(8,128)(2,1)S(1)}, bf16[112,512]{1,0:T(8,128)(2,1)S(1)}, u32[]{:S(2)}, u32[]{:S(2)}) collective-permute-start(bf16[112,512]{1,0:T(8,128)(2,1)S(1)} %get-tuple-element.75), channel_id=1, source_target_pairs={{0,8},{4,12},{8,0},{12,4},{16,24},{20,28},{24,16},{28,20},{1,9},{5... | collective-permute-start | bytes 344072 | tf_op jit(solution)/shard_map/ppermute | solution.py:335
  (8 other events, 113.7 us)

commit v8 on v7

--- a/solution.py
+++ b/solution.py
@@ -153,8 +153,8 @@
     pieces_in = refs[4 : 4 + n_pieces]
     w_gate_hbm, w_up_hbm, w_down_hbm = refs[4 + n_pieces : 7 + n_pieces]
     out_refs = refs[7 + n_pieces : 13 + n_pieces]
-    (picks, weights, w_in, w_down, toks, rows, hidden, mixed, table_sems, tok_sems, in_sems,
-     down_sems) = refs[13 + n_pieces :]
+    (picks, weights, w_in, w_down, toks, rows, both, hidden, mixed, along, table_sems, tok_sems,
+     in_sems, down_sems) = refs[13 + n_pieces :]
     n_z, _, tok_rows, model_width = toks.shape
     n_seq = 2 * n_z
     exp_dev, hid_dev, _ = w_gate_hbm.shape
@@ -204,37 +204,35 @@
     quarters = [slice(2 * q * width, 2 * (q + 1) * width) for q in range(4)]
     tables[0].wait()
 
-    tok_copies[0].wait()
-
-    def pick(j, carry):
-        @pl.when(j == 1)
-        def _():
-            for copy in tok_copies[1:]:
-                copy.wait()
-
-        onehot = picks[j]
-        for cols in quarters:
-            got = contract(onehot, toks[j // 2, j % 2, :, cols], 1, 0).astype(jnp.bfloat16)
-            rows[j, :, :, cols] = got.reshape(exp_dev, SLOTS, 2 * width)
+    for copy in tok_copies:
+        copy.wait()
+
+    def pick(dz, carry):
+        for dy in range(2):
+            onehot = picks[2 * dz + dy]
+            for cols in quarters:
+                got = contract(onehot, toks[dz, dy, :, cols], 1, 0).astype(jnp.bfloat16)
+                rows[2 * dz + dy, :, :, cols] = got.reshape(exp_dev, SLOTS, 2 * width)
         return carry
 
-    lax.fori_loop(0, n_seq, pick, 0)
+    lax.fori_loop(0, n_z, pick, 0)
+
+    def activate(pair):
+        for i in range(2):
+            gate_val, up_val = both[i, :hid_dev], both[i, hid_dev:]
+            act = gate_val / (1.0 + jnp.exp(-gate_val)) * up_val
+            hidden[2 * pair + i] = act.T.astype(jnp.bfloat16)
 
     def widen(pair, carry):
         experts = (2 * pair, 2 * pair + 1)
         for e in experts:
             for copy in in_copies(e):
                 copy.wait()
-        both = [
-            contract(
+        activate(jnp.maximum(pair - 1, 0))
+        for i, e in enumerate(experts):
+            both[i] = contract(
                 w_in[lax.rem(e, RING)], rows[:, e].reshape(n_seq * SLOTS, model_width), 1, 1
             )
-            for e in experts
-        ]
-        for e, value in zip(experts, both):
-            gate_val, up_val = value[:hid_dev], value[hid_dev:]
-            act = gate_val / (1.0 + jnp.exp(-gate_val)) * up_val
-            hidden[e] = act.T.astype(jnp.bfloat16)
         for e in experts:
             down_copy(e).start()
 
@@ -246,6 +244,7 @@
         return carry
 
     lax.fori_loop(0, exp_dev // 2, widen, 0)
+    activate(exp_dev // 2 - 1)
 
     def narrow(pair, carry):
         experts = (2 * pair, 2 * pair + 1)
@@ -260,15 +259,7 @@
     lax.fori_loop(0, exp_dev // 2, narrow, 0)
     tables[1].wait()
 
-    def combine(dz, carry):
-        along = [jnp.zeros((tok_rows, 1), jnp.float32)] * 2
-        for dy in range(2):
-            j = 2 * dz + dy
-            weight = weights[j]
-            for cols in quarters:
-                got = contract(weight, rows[j, :, :, cols].reshape(slots_src, 2 * width), 1, 0)
-                mixed[dy, :, cols] = got
-                along[dy] += jnp.sum(got * unit_ref[:, cols], axis=1, keepdims=True)
+    def project(dz):
         for dy in range(2):
             for dc in range(2):
                 far, near, rest = out_refs[3 * dc : 3 * dc + 3]
@@ -279,9 +270,23 @@
                     rest[dz, dy, :, n * width : (n + 1) * width] = value[split:]
                     leaves, kind = (dy, 2 + dx) if color else (dx, dy)
                     (far if leaves else near)[kind, dz] = value[:split]
+
+    def combine(dz, carry):
+        project(jnp.maximum(dz - 1, 0))
+        for dy in range(2):
+            j = 2 * dz + dy
+            total = jnp.zeros((tok_rows, 1), jnp.float32)
+            for cols in quarters:
+                got = contract(
+                    weights[j], rows[j, :, :, cols].reshape(slots_src, 2 * width), 1, 0
+                )
+                mixed[dy, :, cols] = got
+                total += jnp.sum(got * unit_ref[:, cols], axis=1, keepdims=True)
+            along[dy] = total
         return carry
 
     lax.fori_loop(0, n_z, combine, 0)
+    project(n_z - 1)
 
 
 def moe_partial(picks, weights, unit_dir, own, pieces, w_gate, w_up, w_down):
@@ -314,8 +319,10 @@
             pltpu.VMEM(w_down.shape, jnp.bfloat16),
             pltpu.VMEM((n_z, 2, tok_rows, model_width), jnp.bfloat16),
             pltpu.VMEM((n_seq, exp_dev, SLOTS, model_width), jnp.bfloat16),
+            pltpu.VMEM((2, 2 * hid_dev, n_seq * SLOTS), jnp.float32),
             pltpu.VMEM((exp_dev, n_seq * SLOTS, hid_dev), jnp.bfloat16),
             pltpu.VMEM((2, tok_rows, model_width), jnp.float32),
+            pltpu.VMEM((2, tok_rows, 1), jnp.float32),
             pltpu.SemaphoreType.DMA((2,)),
             pltpu.SemaphoreType.DMA((len(pieces) + 7,)),
             pltpu.SemaphoreType.DMA((2, RING)),

time: 100 us -> 100 us (level)
  no operation moved by 1% of the time
where the time goes in v8:
time: 100 us
  starting transfers between devices  36.6 us (37%)
  waiting for transfers between devices  34.1 us (34%)
  Pallas kernels  26.7 us (27%)
  other arithmetic  1.62 us (2%)
    ppermute x37, starting transfers between devices, swap(): return lax.ppermute(value, axis, [(i, i ^ distance) for i in range(size)])  36.6 us
    ppermute x37, waiting for transfers between devices, swap(): return lax.ppermute(value, axis, [(i, i ^ distance) for i in range(size)])  34.1 us
    pallas_call x1, Pallas kernels, moe_partial(): pl.pallas_call(functools.partial(moe_kernel, n_pieces), out_shape=outs, i...  21.6 us
    pallas_call x1, Pallas kernels, route(): pl.pallas_call(functools.partial(route_kernel, exp_dev), out_shape=[jax.S...  2.72 us
    pallas_call x1, Pallas kernels, norm_and_base(): pl.pallas_call(norm_kernel, out_shape=[jax.ShapeDtypeStruct((tok_rows, mo...  2.46 us
  transfers between devices with their start and end apart: 37, of which 16 were waited for; matrix products, arithmetic and copies ran while one was open for 2% of the time, Pallas kernels for 3%

profile of v8, /device:TPU:0, one launch (start us, length us, event | category | flops | bytes accessed | tf_op | source)
XLA Modules:
  0.0 100.1 jit_solution(12161601446833820322)
XLA Ops:
  0.0 2.5 %shard_map.82 = (bf16[128,2048]{1,0:T(8,128)(2,1)}, bf16[144,256]{1,0:T(8,128)(2,1)}, bf16[128,256]{1,0:T(8,128)(2,1)}, bf16[144,768]{1,0:T(8,128)(2,1)}, f32[1,...) custom-call(bf16[128,2048]{1,0:T(8,128)(2,1)} %tokens_ref.1, f32[1,2048]{1,0:T(1,128)} %bitcast.63, ...), custom_call_target="tpu_custom_call" | custom-call | tf_op jit(solution)/shard_map/pallas_call | solution.py:74
  2.5 5.1 %collective-permute-start.2 = (bf16[144,256]{1,0:T(8,128)(2,1)}, bf16[144,256]{1,0:T(8,128)(2,1)S(1)}, u32[]{:S(2)}, u32[]{:S(2)}) collective-permute-start(bf16[144,256]{1,0:T(8,128)(2,1)} %get-tuple-element.38), channel_id=1, source_target_pairs={{0,24},{4,28},{8,16},{12,20},{16,8},{20,12},{24,0},{28,4},{1,25},{... | collective-permute-start | bytes 221192 | tf_op jit(solution)/shard_map/ppermute | solution.py:342
  8.2 1.7 %collective-permute-start.3 = (bf16[1,144,768]{2,1,0:T(8,128)(2,1)}, bf16[1,144,768]{2,1,0:T(8,128)(2,1)S(1)}, u32[]{:S(2)}, u32[]{:S(2)}) collective-permute-start(bf16[1,144,768]{2,1,0:T(8,128)(2,1)} %bitcast.67), channel_id=1, source_target_pairs={{0,4},{4,0},{8,12},{12,8},{16,20},{20,16},{24,28},{28,24},{1,5},{5... | collective-permute-start | bytes 663560 | tf_op jit(solution)/shard_map/ppermute | solution.py:342
  10.5 3.4 %collective-permute-done.1 = bf16[144,256]{1,0:T(8,128)(2,1)S(1)} collective-permute-done((bf16[144,256]{1,0:T(8,128)(2,1)}, bf16[144,256]{1,0:T(8,128)(2,1)S(1)}, u32[]{:S(2)}, u32[]{:S(2)}) %collective-permute-start.1) | collective-permute-done | bytes 73760 | tf_op jit(solution)/shard_map/ppermute | solution.py:342
  14.0 1.0 collective-permute-done.3.refs_6_
  15.0 3.5 %collective-permute-start.7 = (bf16[128,256]{1,0:T(8,128)(2,1)}, bf16[128,256]{1,0:T(8,128)(2,1)S(1)}, u32[]{:S(2)}, u32[]{:S(2)}) collective-permute-start(bf16[128,256]{1,0:T(8,128)(2,1)} %get-tuple-element.49), channel_id=1, source_target_pairs={{0,24},{4,28},{8,16},{12,20},{16,8},{20,12},{24,0},{28,4},{1,25},{... | collective-permute-start | bytes 196616 | tf_op jit(solution)/shard_map/ppermute | solution.py:342
  18.5 0.9 collective-permute-start.5
  19.4 1.6 %collective-permute-start.4 = (bf16[3,144,256]{2,1,0:T(8,128)(2,1)S(1)}, bf16[3,144,256]{2,1,0:T(8,128)(2,1)S(1)}, u32[]{:S(2)}, u32[]{:S(2)}) collective-permute-start(bf16[3,144,256]{2,1,0:T(8,128)(2,1)S(1)} %pad_maximum_fusion.1.refs_4_), channel_id=1, source_target_pairs={{0,4},{4,0},{8,12},{12,8},{16,20},{20,16},{24,28},{28,24},{1,5},{5... | collective-permute-start | bytes 663560 | tf_op jit(solution)/shard_map/ppermute | solution.py:342
  21.0 1.5 %collective-permute-start.8 = (bf16[3,128,256]{2,1,0:T(8,128)(2,1)S(1)}, bf16[3,128,256]{2,1,0:T(8,128)(2,1)S(1)}, u32[]{:S(2)}, u32[]{:S(2)}) collective-permute-start(bf16[3,128,256]{2,1,0:T(8,128)(2,1)S(1)} %slice.121), channel_id=1, source_target_pairs={{0,2},{1,3},{2,0},{3,1},{4,6},{5,7},{6,4},{7,5},{8,10},{9,11},{10,... | collective-permute-start | bytes 589832 | tf_op jit(solution)/shard_map/ppermute | solution.py:342
  22.5 1.3 %collective-permute-done.6 = bf16[128,256]{1,0:T(8,128)(2,1)S(1)} collective-permute-done((bf16[128,256]{1,0:T(8,128)(2,1)}, bf16[128,256]{1,0:T(8,128)(2,1)S(1)}, u32[]{:S(2)}, u32[]{:S(2)}) %collective-permute-start.6) | collective-permute-done | bytes 65568 | tf_op jit(solution)/shard_map/ppermute | solution.py:342
  23.9 1.6 %collective-permute-start.10 = (bf16[3,128,256]{2,1,0:T(8,128)(2,1)S(1)}, bf16[3,128,256]{2,1,0:T(8,128)(2,1)S(1)}, u32[]{:S(2)}, u32[]{:S(2)}) collective-permute-start(bf16[3,128,256]{2,1,0:T(8,128)(2,1)S(1)} %pad_maximum_fusion.2.refs_5_), channel_id=1, source_target_pairs={{0,4},{4,0},{8,12},{12,8},{16,20},{20,16},{24,28},{28,24},{1,5},{5... | collective-permute-start | bytes 589832 | tf_op jit(solution)/shard_map/ppermute | solution.py:342
  25.6 1.6 %collective-permute-start.9 = (bf16[4,128,256]{2,1,0:T(8,128)(2,1)S(1)}, bf16[4,128,256]{2,1,0:T(8,128)(2,1)S(1)}, u32[]{:S(2)}, u32[]{:S(2)}) collective-permute-start(bf16[4,128,256]{2,1,0:T(8,128)(2,1)S(1)} %pad_maximum_fusion), channel_id=1, source_target_pairs={{0,2},{1,3},{2,0},{3,1},{4,6},{5,7},{6,4},{7,5},{8,10},{9,11},{10,... | collective-permute-start | bytes 786440 | tf_op jit(solution)/shard_map/ppermute | solution.py:342
  28.3 3.4 %collective-permute-done.10.refs_10_ = bf16[3,128,256]{2,1,0:T(8,128)(2,1)S(1)} collective-permute-done((bf16[3,128,256]{2,1,0:T(8,128)(2,1)S(1)}, bf16[3,128,256]{2,1,0:T(8,128)(2,1)S(1)}, u32[]{:S(2)}, u32[]{:S(2)}) %collective-permute-start.10) | collective-permute-done | bytes 196640 | tf_op jit(solution)/shard_map/ppermute | solution.py:342
  31.7 2.3 %collective-permute-done.9.refs_9_ = bf16[4,128,256]{2,1,0:T(8,128)(2,1)S(1)} collective-permute-done((bf16[4,128,256]{2,1,0:T(8,128)(2,1)S(1)}, bf16[4,128,256]{2,1,0:T(8,128)(2,1)S(1)}, u32[]{:S(2)}, u32[]{:S(2)}) %collective-permute-start.9) | collective-permute-done | bytes 262176 | tf_op jit(solution)/shard_map/ppermute | solution.py:342
  34.0 1.5 %collective-permute-start.12 = (bf16[3,128,256]{2,1,0:T(8,128)(2,1)S(1)}, bf16[3,128,256]{2,1,0:T(8,128)(2,1)S(1)}, u32[]{:S(2)}, u32[]{:S(2)}) collective-permute-start(bf16[3,128,256]{2,1,0:T(8,128)(2,1)S(1)} %collective-permute-done.10.refs_10_), channel_id=1, source_target_pairs={{0,2},{1,3},{2,0},{3,1},{4,6},{5,7},{6,4},{7,5},{8,10},{9,11},{10,... | collective-permute-start | bytes 589832 | tf_op jit(solution)/shard_map/ppermute | solution.py:342
  35.5 2.7 %shard_map.83 = (bf16[8,256,128]{2,1,0:T(8,128)(2,1)}, bf16[8,128,256]{2,1,0:T(8,128)(2,1)}) custom-call(bf16[8,16,128]{2,1,0:T(8,128)(2,1)} %copy-done.2), custom_call_target="tpu_custom_call" | custom-call | flops 4000000000 | bytes 2097152 | tf_op jit(solution)/shard_map/pallas_call | solution.py:132
  39.3 0.9 collective-permute-done.12.refs_12_
  40.5 1.1 %collective-permute-done.21.refs_21_ = bf16[3,128,256]{2,1,0:T(8,128)(2,1)S(1)} collective-permute-done((bf16[3,128,256]{2,1,0:T(8,128)(2,1)S(1)}, bf16[3,128,256]{2,1,0:T(8,128)(2,1)S(1)}, u32[]{:S(2)}, u32[]{:S(2)}) %collective-permute-start.21) | collective-permute-done | bytes 196640 | tf_op jit(solution)/shard_map/ppermute | solution.py:342
  41.6 21.6 %shard_map.84 = (bf16[4,4,112,256]{3,2,1,0:T(8,128)(2,1)S(1)}, bf16[4,4,112,256]{3,2,1,0:T(8,128)(2,1)S(1)}, bf16[4,2,16,1024]{3,2,1,0:T(8,128)(2,1)S(1)}, bf16[...) custom-call(bf16[8,256,128]{2,1,0:T(8,128)(2,1)} %get-tuple-element.45.re, ...), custom_call_target="tpu_custom_call" | custom-call | flops 4831838208 | bytes 46137344 | tf_op jit(solution)/shard_map/pallas_call | solution.py:310
  63.9 1.8 %collective-permute-done.23 = bf16[4,4,112,256]{3,2,1,0:T(8,128)(2,1)S(1)} collective-permute-done((bf16[4,4,112,256]{3,2,1,0:T(8,128)(2,1)S(1)}, bf16[4,4,112,256]{3,2,1,0:T(8,128)(2,1)S(1)}, u32[]{:S(2)}, u32[]{:S(2)}) %collective-permute-start.23) | collective-permute-done | bytes 917536 | tf_op jit(solution)/shard_map/ppermute | solution.py:342
  65.9 1.6 %collective-permute-start.24 = (bf16[2,4,112,256]{3,2,1,0:T(8,128)(2,1)S(1)}, bf16[2,4,112,256]{3,2,1,0:T(8,128)(2,1)S(1)}, u32[]{:S(2)}, u32[]{:S(2)}) collective-permute-start(bf16[2,4,112,256]{3,2,1,0:T(8,128)(2,1)S(1)} %get-tuple-element.58), channel_id=1, source_target_pairs={{0,2},{1,3},{2,0},{3,1},{4,6},{5,7},{6,4},{7,5},{8,10},{9,11},{10,... | collective-permute-start | bytes 1376264 | tf_op jit(solution)/shard_map/ppermute | solution.py:342
  68.2 2.1 %collective-permute-start.29 = (bf16[2,16,1024]{2,1,0:T(8,128)(2,1)S(1)}, bf16[2,16,1024]{2,1,0:T(8,128)(2,1)S(1)}, u32[]{:S(2)}, u32[]{:S(2)}) collective-permute-start(bf16[2,16,1024]{2,1,0:T(8,128)(2,1)S(1)} %get-tuple-element.76), channel_id=1, source_target_pairs={{0,24},{4,28},{8,16},{12,20},{16,8},{20,12},{24,0},{28,4},{1,25},{... | collective-permute-start | bytes 196616 | tf_op jit(solution)/shard_map/ppermute | solution.py:342
  70.4 2.3 %collective-permute-start.27 = (bf16[2,16,1024]{2,1,0:T(8,128)(2,1)S(1)}, bf16[2,16,1024]{2,1,0:T(8,128)(2,1)S(1)}, u32[]{:S(2)}, u32[]{:S(2)}) collective-permute-start(bf16[2,16,1024]{2,1,0:T(8,128)(2,1)S(1)} %get-tuple-element.78), channel_id=1, source_target_pairs={{0,8},{4,12},{8,0},{12,4},{16,24},{20,28},{24,16},{28,20},{1,9},{5... | collective-permute-start | bytes 196616 | tf_op jit(solution)/shard_map/ppermute | solution.py:342
  72.7 5.9 %collective-permute-done.24 = bf16[2,4,112,256]{3,2,1,0:T(8,128)(2,1)S(1)} collective-permute-done((bf16[2,4,112,256]{3,2,1,0:T(8,128)(2,1)S(1)}, bf16[2,4,112,256]{3,2,1,0:T(8,128)(2,1)S(1)}, u32[]{:S(2)}, u32[]{:S(2)}) %collective-permute-start.24) | collective-permute-done | bytes 458784 | tf_op jit(solution)/shard_map/ppermute | solution.py:342
  78.6 1.2 %collective-permute-done.25 = bf16[2,4,112,256]{3,2,1,0:T(8,128)(2,1)S(1)} collective-permute-done((bf16[2,4,112,256]{3,2,1,0:T(8,128)(2,1)S(1)}, bf16[2,4,112,256]{3,2,1,0:T(8,128)(2,1)S(1)}, u32[]{:S(2)}, u32[]{:S(2)}) %collective-permute-start.25) | collective-permute-done | bytes 458784 | tf_op jit(solution)/shard_map/ppermute | solution.py:342
  80.9 1.2 %collective-permute-start.30 = (bf16[4,112,256]{2,1,0:T(8,128)(2,1)S(1)}, bf16[4,112,256]{2,1,0:T(8,128)(2,1)S(1)}, u32[]{:S(2)}, u32[]{:S(2)}) collective-permute-start(bf16[4,112,256]{2,1,0:T(8,128)(2,1)S(1)} %get-tuple-element.62), channel_id=1, source_target_pairs={{0,4},{4,0},{8,12},{12,8},{16,20},{20,16},{24,28},{28,24},{1,5},{5... | collective-permute-start | bytes 688136 | tf_op jit(solution)/shard_map/ppermute | solution.py:342
  82.7 1.7 %collective-permute-done.35 = bf16[16,1024]{1,0:T(8,128)(2,1)S(1)} collective-permute-done((bf16[16,1024]{1,0:T(8,128)(2,1)S(1)}, bf16[16,1024]{1,0:T(8,128)(2,1)S(1)}, u32[]{:S(2)}, u32[]{:S(2)}) %collective-permute-start.35) | collective-permute-done | bytes 32800 | tf_op jit(solution)/shard_map/ppermute | solution.py:342
  85.0 2.6 %collective-permute-done.30 = bf16[4,112,256]{2,1,0:T(8,128)(2,1)S(1)} collective-permute-done((bf16[4,112,256]{2,1,0:T(8,128)(2,1)S(1)}, bf16[4,112,256]{2,1,0:T(8,128)(2,1)S(1)}, u32[]{:S(2)}, u32[]{:S(2)}) %collective-permute-start.30) | collective-permute-done | bytes 229408 | tf_op jit(solution)/shard_map/ppermute | solution.py:342
  88.5 2.1 %collective-permute-start.32 = (bf16[112,512]{1,0:T(8,128)(2,1)S(1)}, bf16[112,512]{1,0:T(8,128)(2,1)S(1)}, u32[]{:S(2)}, u32[]{:S(2)}) collective-permute-start(bf16[112,512]{1,0:T(8,128)(2,1)S(1)} %get-tuple-element.73), channel_id=1, source_target_pairs={{0,24},{4,28},{8,16},{12,20},{16,8},{20,12},{24,0},{28,4},{1,25},{... | collective-permute-start | bytes 344072 | tf_op jit(solution)/shard_map/ppermute | solution.py:342
  90.7 2.3 %collective-permute-start.34 = (bf16[112,512]{1,0:T(8,128)(2,1)S(1)}, bf16[112,512]{1,0:T(8,128)(2,1)S(1)}, u32[]{:S(2)}, u32[]{:S(2)}) collective-permute-start(bf16[112,512]{1,0:T(8,128)(2,1)S(1)} %get-tuple-element.75), channel_id=1, source_target_pairs={{0,8},{4,12},{8,0},{12,4},{16,24},{20,28},{24,16},{28,20},{1,9},{5... | collective-permute-start | bytes 344072 | tf_op jit(solution)/shard_map/ppermute | solution.py:342
  93.0 2.8 %collective-permute-done.32 = bf16[112,512]{1,0:T(8,128)(2,1)S(1)} collective-permute-done((bf16[112,512]{1,0:T(8,128)(2,1)S(1)}, bf16[112,512]{1,0:T(8,128)(2,1)S(1)}, u32[]{:S(2)}, u32[]{:S(2)}) %collective-permute-start.32) | collective-permute-done | bytes 114720 | tf_op jit(solution)/shard_map/ppermute | solution.py:342
  95.8 3.5 %collective-permute-done.33 = bf16[112,512]{1,0:T(8,128)(2,1)S(1)} collective-permute-done((bf16[112,512]{1,0:T(8,128)(2,1)S(1)}, bf16[112,512]{1,0:T(8,128)(2,1)S(1)}, u32[]{:S(2)}, u32[]{:S(2)}) %collective-permute-start.33) | collective-permute-done | bytes 114720 | tf_op jit(solution)/shard_map/ppermute | solution.py:342
  (78 shorter events, 9.5 us)
Async XLA Ops:
  2.5 8.1 %collective-permute-start.2 = (bf16[144,256]{1,0:T(8,128)(2,1)}, bf16[144,256]{1,0:T(8,128)(2,1)S(1)}, u32[]{:S(2)}, u32[]{:S(2)}) collective-permute-start(bf16[144,256]{1,0:T(8,128)(2,1)} %get-tuple-element.38), channel_id=1, source_target_pairs={{0,24},{4,28},{8,16},{12,20},{16,8},{20,12},{24,0},{28,4},{1,25},{... | collective-permute-start | bytes 221192 | tf_op jit(solution)/shard_map/ppermute | solution.py:342
  7.5 6.4 %collective-permute-start.1 = (bf16[144,256]{1,0:T(8,128)(2,1)}, bf16[144,256]{1,0:T(8,128)(2,1)S(1)}, u32[]{:S(2)}, u32[]{:S(2)}) collective-permute-start(bf16[144,256]{1,0:T(8,128)(2,1)} %get-tuple-element.38), channel_id=1, source_target_pairs={{0,16},{4,20},{8,24},{12,28},{16,0},{20,4},{24,8},{28,12},{1,17},{... | collective-permute-start | bytes 221192 | tf_op jit(solution)/shard_map/ppermute | solution.py:342
  7.5 6.4 %collective-permute-start = (bf16[144,256]{1,0:T(8,128)(2,1)}, bf16[144,256]{1,0:T(8,128)(2,1)S(1)}, u32[]{:S(2)}, u32[]{:S(2)}) collective-permute-start(bf16[144,256]{1,0:T(8,128)(2,1)} %get-tuple-element.38), channel_id=1, source_target_pairs={{0,8},{4,12},{8,0},{12,4},{16,24},{20,28},{24,16},{28,20},{1,9},{5... | collective-permute-start | bytes 221192 | tf_op jit(solution)/shard_map/ppermute | solution.py:342
  8.2 6.8 %collective-permute-start.3 = (bf16[1,144,768]{2,1,0:T(8,128)(2,1)}, bf16[1,144,768]{2,1,0:T(8,128)(2,1)S(1)}, u32[]{:S(2)}, u32[]{:S(2)}) collective-permute-start(bf16[1,144,768]{2,1,0:T(8,128)(2,1)} %bitcast.67), channel_id=1, source_target_pairs={{0,4},{4,0},{8,12},{12,8},{16,20},{20,16},{24,28},{28,24},{1,5},{5... | collective-permute-start | bytes 663560 | tf_op jit(solution)/shard_map/ppermute | solution.py:342
  15.0 7.5 %collective-permute-start.7 = (bf16[128,256]{1,0:T(8,128)(2,1)}, bf16[128,256]{1,0:T(8,128)(2,1)S(1)}, u32[]{:S(2)}, u32[]{:S(2)}) collective-permute-start(bf16[128,256]{1,0:T(8,128)(2,1)} %get-tuple-element.49), channel_id=1, source_target_pairs={{0,24},{4,28},{8,16},{12,20},{16,8},{20,12},{24,0},{28,4},{1,25},{... | collective-permute-start | bytes 196616 | tf_op jit(solution)/shard_map/ppermute | solution.py:342
  18.5 5.4 %collective-permute-start.6 = (bf16[128,256]{1,0:T(8,128)(2,1)}, bf16[128,256]{1,0:T(8,128)(2,1)S(1)}, u32[]{:S(2)}, u32[]{:S(2)}) collective-permute-start(bf16[128,256]{1,0:T(8,128)(2,1)} %get-tuple-element.49), channel_id=1, source_target_pairs={{0,16},{4,20},{8,24},{12,28},{16,0},{20,4},{24,8},{28,12},{1,17},{... | collective-permute-start | bytes 196616 | tf_op jit(solution)/shard_map/ppermute | solution.py:342
  18.5 5.4 %collective-permute-start.5 = (bf16[128,256]{1,0:T(8,128)(2,1)}, bf16[128,256]{1,0:T(8,128)(2,1)S(1)}, u32[]{:S(2)}, u32[]{:S(2)}) collective-permute-start(bf16[128,256]{1,0:T(8,128)(2,1)} %get-tuple-element.49), channel_id=1, source_target_pairs={{0,8},{4,12},{8,0},{12,4},{16,24},{20,28},{24,16},{28,20},{1,9},{5... | collective-permute-start | bytes 196616 | tf_op jit(solution)/shard_map/ppermute | solution.py:342
  19.4 8.2 %collective-permute-start.4 = (bf16[3,144,256]{2,1,0:T(8,128)(2,1)S(1)}, bf16[3,144,256]{2,1,0:T(8,128)(2,1)S(1)}, u32[]{:S(2)}, u32[]{:S(2)}) collective-permute-start(bf16[3,144,256]{2,1,0:T(8,128)(2,1)S(1)} %pad_maximum_fusion.1.refs_4_), channel_id=1, source_target_pairs={{0,4},{4,0},{8,12},{12,8},{16,20},{20,16},{24,28},{28,24},{1,5},{5... | collective-permute-start | bytes 663560 | tf_op jit(solution)/shard_map/ppermute | solution.py:342
  21.0 6.1 %collective-permute-start.8 = (bf16[3,128,256]{2,1,0:T(8,128)(2,1)S(1)}, bf16[3,128,256]{2,1,0:T(8,128)(2,1)S(1)}, u32[]{:S(2)}, u32[]{:S(2)}) collective-permute-start(bf16[3,128,256]{2,1,0:T(8,128)(2,1)S(1)} %slice.121), channel_id=1, source_target_pairs={{0,2},{1,3},{2,0},{3,1},{4,6},{5,7},{6,4},{7,5},{8,10},{9,11},{10,... | collective-permute-start | bytes 589832 | tf_op jit(solution)/shard_map/ppermute | solution.py:342
  23.9 3.8 %collective-permute-start.14 = (bf16[3,128,256]{2,1,0:T(8,128)(2,1)S(1)}, bf16[3,128,256]{2,1,0:T(8,128)(2,1)S(1)}, u32[]{:S(2)}, u32[]{:S(2)}) collective-permute-start(bf16[3,128,256]{2,1,0:T(8,128)(2,1)S(1)} %pad_maximum_fusion.2.refs_5_), channel_id=1, source_target_pairs={{0,1},{1,0},{2,3},{3,2},{4,5},{5,4},{6,7},{7,6},{8,9},{9,8},{10,11... | collective-permute-start | bytes 589832 | tf_op jit(solution)/shard_map/ppermute | solution.py:342
  23.9 7.8 %collective-permute-start.10 = (bf16[3,128,256]{2,1,0:T(8,128)(2,1)S(1)}, bf16[3,128,256]{2,1,0:T(8,128)(2,1)S(1)}, u32[]{:S(2)}, u32[]{:S(2)}) collective-permute-start(bf16[3,128,256]{2,1,0:T(8,128)(2,1)S(1)} %pad_maximum_fusion.2.refs_5_), channel_id=1, source_target_pairs={{0,4},{4,0},{8,12},{12,8},{16,20},{20,16},{24,28},{28,24},{1,5},{5... | collective-permute-start | bytes 589832 | tf_op jit(solution)/shard_map/ppermute | solution.py:342
  25.6 8.4 %collective-permute-start.9 = (bf16[4,128,256]{2,1,0:T(8,128)(2,1)S(1)}, bf16[4,128,256]{2,1,0:T(8,128)(2,1)S(1)}, u32[]{:S(2)}, u32[]{:S(2)}) collective-permute-start(bf16[4,128,256]{2,1,0:T(8,128)(2,1)S(1)} %pad_maximum_fusion), channel_id=1, source_target_pairs={{0,2},{1,3},{2,0},{3,1},{4,6},{5,7},{6,4},{7,5},{8,10},{9,11},{10,... | collective-permute-start | bytes 786440 | tf_op jit(solution)/shard_map/ppermute | solution.py:342
  27.1 8.4 %collective-permute-start.11 = (bf16[3,128,256]{2,1,0:T(8,128)(2,1)S(1)}, bf16[3,128,256]{2,1,0:T(8,128)(2,1)S(1)}, u32[]{:S(2)}, u32[]{:S(2)}) collective-permute-start(bf16[3,128,256]{2,1,0:T(8,128)(2,1)S(1)} %collective-permute-done.8.refs_7_), channel_id=1, source_target_pairs={{0,4},{4,0},{8,12},{12,8},{16,20},{20,16},{24,28},{28,24},{1,5},{5... | collective-permute-start | bytes 589832 | tf_op jit(solution)/shard_map/ppermute | solution.py:342
  27.6 11.1 %collective-permute-start.13 = (bf16[3,144,256]{2,1,0:T(8,128)(2,1)S(1)}, bf16[3,144,256]{2,1,0:T(8,128)(2,1)S(1)}, u32[]{:S(2)}, u32[]{:S(2)}) collective-permute-start(bf16[3,144,256]{2,1,0:T(8,128)(2,1)S(1)} %pad_maximum_fusion.1.refs_4_), channel_id=1, source_target_pairs={{0,1},{1,0},{2,3},{3,2},{4,5},{5,4},{6,7},{7,6},{8,9},{9,8},{10,11... | collective-permute-start | bytes 663560 | tf_op jit(solution)/shard_map/ppermute | solution.py:342
  27.7 10.5 %collective-permute-start.16 = (bf16[3,128,256]{2,1,0:T(8,128)(2,1)S(1)}, bf16[3,128,256]{2,1,0:T(8,128)(2,1)S(1)}, u32[]{:S(2)}, u32[]{:S(2)}) collective-permute-start(bf16[3,128,256]{2,1,0:T(8,128)(2,1)S(1)} %collective-permute-done.8.refs_7_), channel_id=1, source_target_pairs={{0,1},{1,0},{2,3},{3,2},{4,5},{5,4},{6,7},{7,6},{8,9},{9,8},{10,11... | collective-permute-start | bytes 589832 | tf_op jit(solution)/shard_map/ppermute | solution.py:342
  31.7 7.1 %collective-permute-start.17 = (bf16[3,144,256]{2,1,0:T(8,128)(2,1)S(1)}, bf16[3,144,256]{2,1,0:T(8,128)(2,1)S(1)}, u32[]{:S(2)}, u32[]{:S(2)}) collective-permute-start(bf16[3,144,256]{2,1,0:T(8,128)(2,1)S(1)} %collective-permute-done.4.refs_8_), channel_id=1, source_target_pairs={{0,1},{1,0},{2,3},{3,2},{4,5},{5,4},{6,7},{7,6},{8,9},{9,8},{10,11... | collective-permute-start | bytes 663560 | tf_op jit(solution)/shard_map/ppermute | solution.py:342
  34.0 6.1 %collective-permute-start.12 = (bf16[3,128,256]{2,1,0:T(8,128)(2,1)S(1)}, bf16[3,128,256]{2,1,0:T(8,128)(2,1)S(1)}, u32[]{:S(2)}, u32[]{:S(2)}) collective-permute-start(bf16[3,128,256]{2,1,0:T(8,128)(2,1)S(1)} %collective-permute-done.10.refs_10_), channel_id=1, source_target_pairs={{0,2},{1,3},{2,0},{3,1},{4,6},{5,7},{6,4},{7,5},{8,10},{9,11},{10,... | collective-permute-start | bytes 589832 | tf_op jit(solution)/shard_map/ppermute | solution.py:342
  35.5 5.0 %collective-permute-start.18 = (bf16[4,128,256]{2,1,0:T(8,128)(2,1)S(1)}, bf16[4,128,256]{2,1,0:T(8,128)(2,1)S(1)}, u32[]{:S(2)}, u32[]{:S(2)}) collective-permute-start(bf16[4,128,256]{2,1,0:T(8,128)(2,1)S(1)} %collective-permute-done.9.refs_9_), channel_id=1, source_target_pairs={{0,1},{1,0},{2,3},{3,2},{4,5},{5,4},{6,7},{7,6},{8,9},{9,8},{10,11... | collective-permute-start | bytes 786440 | tf_op jit(solution)/shard_map/ppermute | solution.py:342
  63.4 7.0 %collective-permute-start.22 = (bf16[4,4,112,256]{3,2,1,0:T(8,128)(2,1)S(1)}, bf16[4,4,112,256]{3,2,1,0:T(8,128)(2,1)S(1)}, u32[]{:S(2)}, u32[]{:S(2)}) collective-permute-start(bf16[4,4,112,256]{3,2,1,0:T(8,128)(2,1)S(1)} %get-tuple-element.54), channel_id=1, source_target_pairs={{0,1},{1,0},{2,3},{3,2},{4,5},{5,4},{6,7},{7,6},{8,9},{9,8},{10,11... | collective-permute-start | bytes 2752520 | tf_op jit(solution)/shard_map/ppermute | solution.py:342
  63.7 4.4 %collective-permute-start.26 = (bf16[4,2,16,1024]{3,2,1,0:T(8,128)(2,1)S(1)}, bf16[4,2,16,1024]{3,2,1,0:T(8,128)(2,1)S(1)}, u32[]{:S(2)}, u32[]{:S(2)}) collective-permute-start(bf16[4,2,16,1024]{3,2,1,0:T(8,128)(2,1)S(1)} %get-tuple-element.61), channel_id=1, source_target_pairs={{0,1},{1,0},{2,3},{3,2},{4,5},{5,4},{6,7},{7,6},{8,9},{9,8},{10,11... | collective-permute-start | bytes 786440 | tf_op jit(solution)/shard_map/ppermute | solution.py:342
  65.9 12.6 %collective-permute-start.24 = (bf16[2,4,112,256]{3,2,1,0:T(8,128)(2,1)S(1)}, bf16[2,4,112,256]{3,2,1,0:T(8,128)(2,1)S(1)}, u32[]{:S(2)}, u32[]{:S(2)}) collective-permute-start(bf16[2,4,112,256]{3,2,1,0:T(8,128)(2,1)S(1)} %get-tuple-element.58), channel_id=1, source_target_pairs={{0,2},{1,3},{2,0},{3,1},{4,6},{5,7},{6,4},{7,5},{8,10},{9,11},{10,... | collective-permute-start | bytes 1376264 | tf_op jit(solution)/shard_map/ppermute | solution.py:342
  67.5 12.3 %collective-permute-start.25 = (bf16[2,4,112,256]{3,2,1,0:T(8,128)(2,1)S(1)}, bf16[2,4,112,256]{3,2,1,0:T(8,128)(2,1)S(1)}, u32[]{:S(2)}, u32[]{:S(2)}) collective-permute-start(bf16[2,4,112,256]{3,2,1,0:T(8,128)(2,1)S(1)} %get-tuple-element.59), channel_id=1, source_target_pairs={{0,4},{4,0},{8,12},{12,8},{16,20},{20,16},{24,28},{28,24},{1,5},{5... | collective-permute-start | bytes 1376264 | tf_op jit(solution)/shard_map/ppermute | solution.py:342
  68.2 11.7 %collective-permute-start.29 = (bf16[2,16,1024]{2,1,0:T(8,128)(2,1)S(1)}, bf16[2,16,1024]{2,1,0:T(8,128)(2,1)S(1)}, u32[]{:S(2)}, u32[]{:S(2)}) collective-permute-start(bf16[2,16,1024]{2,1,0:T(8,128)(2,1)S(1)} %get-tuple-element.76), channel_id=1, source_target_pairs={{0,24},{4,28},{8,16},{12,20},{16,8},{20,12},{24,0},{28,4},{1,25},{... | collective-permute-start | bytes 196616 | tf_op jit(solution)/shard_map/ppermute | solution.py:342
  70.3 9.6 %collective-permute-start.28 = (bf16[2,16,1024]{2,1,0:T(8,128)(2,1)S(1)}, bf16[2,16,1024]{2,1,0:T(8,128)(2,1)S(1)}, u32[]{:S(2)}, u32[]{:S(2)}) collective-permute-start(bf16[2,16,1024]{2,1,0:T(8,128)(2,1)S(1)} %get-tuple-element.77), channel_id=1, source_target_pairs={{0,16},{4,20},{8,24},{12,28},{16,0},{20,4},{24,8},{28,12},{1,17},{... | collective-permute-start | bytes 196616 | tf_op jit(solution)/shard_map/ppermute | solution.py:342
  70.4 9.6 %collective-permute-start.27 = (bf16[2,16,1024]{2,1,0:T(8,128)(2,1)S(1)}, bf16[2,16,1024]{2,1,0:T(8,128)(2,1)S(1)}, u32[]{:S(2)}, u32[]{:S(2)}) collective-permute-start(bf16[2,16,1024]{2,1,0:T(8,128)(2,1)S(1)} %get-tuple-element.78), channel_id=1, source_target_pairs={{0,8},{4,12},{8,0},{12,4},{16,24},{20,28},{24,16},{28,20},{1,9},{5... | collective-permute-start | bytes 196616 | tf_op jit(solution)/shard_map/ppermute | solution.py:342
  80.0 4.4 %collective-permute-start.35 = (bf16[16,1024]{1,0:T(8,128)(2,1)S(1)}, bf16[16,1024]{1,0:T(8,128)(2,1)S(1)}, u32[]{:S(2)}, u32[]{:S(2)}) collective-permute-start(bf16[16,1024]{1,0:T(8,128)(2,1)S(1)} %slice_bitcast_fusion.4), channel_id=1, source_target_pairs={{0,4},{4,0},{8,12},{12,8},{16,20},{20,16},{24,28},{28,24},{1,5},{5... | collective-permute-start | bytes 98312 | tf_op jit(solution)/shard_map/ppermute | solution.py:342
  80.9 6.8 %collective-permute-start.30 = (bf16[4,112,256]{2,1,0:T(8,128)(2,1)S(1)}, bf16[4,112,256]{2,1,0:T(8,128)(2,1)S(1)}, u32[]{:S(2)}, u32[]{:S(2)}) collective-permute-start(bf16[4,112,256]{2,1,0:T(8,128)(2,1)S(1)} %get-tuple-element.62), channel_id=1, source_target_pairs={{0,4},{4,0},{8,12},{12,8},{16,20},{20,16},{24,28},{28,24},{1,5},{5... | collective-permute-start | bytes 688136 | tf_op jit(solution)/shard_map/ppermute | solution.py:342
  82.1 6.1 %collective-permute-start.31 = (bf16[4,112,256]{2,1,0:T(8,128)(2,1)S(1)}, bf16[4,112,256]{2,1,0:T(8,128)(2,1)S(1)}, u32[]{:S(2)}, u32[]{:S(2)}) collective-permute-start(bf16[4,112,256]{2,1,0:T(8,128)(2,1)S(1)} %get-tuple-element.63), channel_id=1, source_target_pairs={{0,2},{1,3},{2,0},{3,1},{4,6},{5,7},{6,4},{7,5},{8,10},{9,11},{10,... | collective-permute-start | bytes 688136 | tf_op jit(solution)/shard_map/ppermute | solution.py:342
  84.5 8.5 %collective-permute-start.36 = (bf16[16,512]{1,0:T(8,128)(2,1)S(1)}, bf16[16,512]{1,0:T(8,128)(2,1)S(1)}, u32[]{:S(2)}, u32[]{:S(2)}) collective-permute-start(bf16[16,512]{1,0:T(8,128)(2,1)S(1)} %pad_maximum_fusion.4), channel_id=1, source_target_pairs={{0,2},{1,3},{2,0},{3,1},{4,6},{5,7},{6,4},{7,5},{8,10},{9,11},{10,... | collective-permute-start | bytes 49160 | tf_op jit(solution)/shard_map/ppermute | solution.py:342
  88.5 7.3 %collective-permute-start.32 = (bf16[112,512]{1,0:T(8,128)(2,1)S(1)}, bf16[112,512]{1,0:T(8,128)(2,1)S(1)}, u32[]{:S(2)}, u32[]{:S(2)}) collective-permute-start(bf16[112,512]{1,0:T(8,128)(2,1)S(1)} %get-tuple-element.73), channel_id=1, source_target_pairs={{0,24},{4,28},{8,16},{12,20},{16,8},{20,12},{24,0},{28,4},{1,25},{... | collective-permute-start | bytes 344072 | tf_op jit(solution)/shard_map/ppermute | solution.py:342
  90.7 8.6 %collective-permute-start.33 = (bf16[112,512]{1,0:T(8,128)(2,1)S(1)}, bf16[112,512]{1,0:T(8,128)(2,1)S(1)}, u32[]{:S(2)}, u32[]{:S(2)}) collective-permute-start(bf16[112,512]{1,0:T(8,128)(2,1)S(1)} %get-tuple-element.74), channel_id=1, source_target_pairs={{0,16},{4,20},{8,24},{12,28},{16,0},{20,4},{24,8},{28,12},{1,17},{... | collective-permute-start | bytes 344072 | tf_op jit(solution)/shard_map/ppermute | solution.py:342
  90.7 8.6 %collective-permute-start.34 = (bf16[112,512]{1,0:T(8,128)(2,1)S(1)}, bf16[112,512]{1,0:T(8,128)(2,1)S(1)}, u32[]{:S(2)}, u32[]{:S(2)}) collective-permute-start(bf16[112,512]{1,0:T(8,128)(2,1)S(1)} %get-tuple-element.75), channel_id=1, source_target_pairs={{0,8},{4,12},{8,0},{12,4},{16,24},{20,28},{24,16},{28,20},{1,9},{5... | collective-permute-start | bytes 344072 | tf_op jit(solution)/shard_map/ppermute | solution.py:342
  (8 other events, 113.7 us)

commit v9 on v8

--- a/solution.py
+++ b/solution.py
@@ -181,22 +181,18 @@
     tables[0].start()
 
     kinds = token_pieces(n_z)
-    tok_copies = [pltpu.make_async_copy(own_hbm, toks.at[0, 0], tok_sems.at[0])]
+    pltpu.make_async_copy(own_hbm, toks.at[0, 0], tok_sems.at[0, 0]).start()
     for i, piece in enumerate(pieces_in):
         blocks, runs = kinds[i % len(kinds)]
         for n, (color, dx) in enumerate(runs):
             cols = pl.ds(group_offset(rep, color, dx, i // len(kinds), width), width)
             for at, dz, count, dy in blocks:
-                tok_copies.append(
+                for k in range(count):
                     pltpu.make_async_copy(
-                        piece.at[pl.ds(at, count), pl.ds(0, tok_rows), pl.ds(n * width, width)],
-                        toks.at[pl.ds(dz, count), dy, :, cols],
-                        tok_sems.at[len(tok_copies)],
-                    )
-                )
-    for copy in tok_copies:
-        copy.start()
-
+                        piece.at[at + k, pl.ds(0, tok_rows), pl.ds(n * width, width)],
+                        toks.at[dz + k, dy, :, cols],
+                        tok_sems.at[dz + k, dy],
+                    ).start()
     for e in range(min(RING, exp_dev)):
         for copy in in_copies(e):
             copy.start()
@@ -204,10 +200,9 @@
     quarters = [slice(2 * q * width, 2 * (q + 1) * width) for q in range(4)]
     tables[0].wait()
 
-    for copy in tok_copies:
-        copy.wait()
-
     def pick(dz, carry):
+        for dy in range(2):
+            pltpu.make_async_copy(toks.at[dz, dy], toks.at[dz, dy], tok_sems.at[dz, dy]).wait()
         for dy in range(2):
             onehot = picks[2 * dz + dy]
             for cols in quarters:
@@ -324,7 +319,7 @@
             pltpu.VMEM((2, tok_rows, model_width), jnp.float32),
             pltpu.VMEM((2, tok_rows, 1), jnp.float32),
             pltpu.SemaphoreType.DMA((2,)),
-            pltpu.SemaphoreType.DMA((len(pieces) + 7,)),
+            pltpu.SemaphoreType.DMA((n_z, 2)),
             pltpu.SemaphoreType.DMA((2, RING)),
             pltpu.SemaphoreType.DMA((exp_dev,)),
         ],

time: 100 us -> 100 us (level)
  no operation moved by 1% of the time
where the time goes in v9:
time: 100 us; the launch traced here: 99.9 us
  starting transfers between devices  36.7 us (37%)
  waiting for transfers between devices  34 us (34%)
  Pallas kernels  26.5 us (26%)
  other arithmetic  1.62 us (2%)
    ppermute x37, starting transfers between devices, swap(): return lax.ppermute(value, axis, [(i, i ^ distance) for i in range(size)])  36.7 us
    ppermute x37, waiting for transfers between devices, swap(): return lax.ppermute(value, axis, [(i, i ^ distance) for i in range(size)])  34 us
    pallas_call x1, Pallas kernels, moe_partial(): pl.pallas_call(functools.partial(moe_kernel, n_pieces), out_shape=outs, i...  21.4 us
    pallas_call x1, Pallas kernels, route(): pl.pallas_call(functools.partial(route_kernel, exp_dev), out_shape=[jax.S...  2.72 us
    pallas_call x1, Pallas kernels, norm_and_base(): pl.pallas_call(norm_kernel, out_shape=[jax.ShapeDtypeStruct((tok_rows, mo...  2.46 us
  transfers between devices with their start and end apart: 37, of which 16 were waited for; matrix products, arithmetic and copies ran while one was open for 2% of the time, Pallas kernels for 3%

profile of v9, /device:TPU:0, one launch (start us, length us, event | category | flops | bytes accessed | tf_op | source)
XLA Modules:
  0.0 99.9 jit_solution(675803922960479163)
XLA Ops:
  0.0 2.5 %shard_map.82 = (bf16[128,2048]{1,0:T(8,128)(2,1)}, bf16[144,256]{1,0:T(8,128)(2,1)}, bf16[128,256]{1,0:T(8,128)(2,1)}, bf16[144,768]{1,0:T(8,128)(2,1)}, f32[1,...) custom-call(bf16[128,2048]{1,0:T(8,128)(2,1)} %tokens_ref.1, f32[1,2048]{1,0:T(1,128)} %bitcast.63, ...), custom_call_target="tpu_custom_call" | custom-call | tf_op jit(solution)/shard_map/pallas_call | solution.py:74
  2.5 5.1 %collective-permute-start.2 = (bf16[144,256]{1,0:T(8,128)(2,1)}, bf16[144,256]{1,0:T(8,128)(2,1)S(1)}, u32[]{:S(2)}, u32[]{:S(2)}) collective-permute-start(bf16[144,256]{1,0:T(8,128)(2,1)} %get-tuple-element.38), channel_id=1, source_target_pairs={{0,24},{4,28},{8,16},{12,20},{16,8},{20,12},{24,0},{28,4},{1,25},{... | collective-permute-start | bytes 221192 | tf_op jit(solution)/shard_map/ppermute | solution.py:337
  8.2 1.7 %collective-permute-start.3 = (bf16[1,144,768]{2,1,0:T(8,128)(2,1)}, bf16[1,144,768]{2,1,0:T(8,128)(2,1)S(1)}, u32[]{:S(2)}, u32[]{:S(2)}) collective-permute-start(bf16[1,144,768]{2,1,0:T(8,128)(2,1)} %bitcast.67), channel_id=1, source_target_pairs={{0,4},{4,0},{8,12},{12,8},{16,20},{20,16},{24,28},{28,24},{1,5},{5... | collective-permute-start | bytes 663560 | tf_op jit(solution)/shard_map/ppermute | solution.py:337
  10.5 3.4 %collective-permute-done.1 = bf16[144,256]{1,0:T(8,128)(2,1)S(1)} collective-permute-done((bf16[144,256]{1,0:T(8,128)(2,1)}, bf16[144,256]{1,0:T(8,128)(2,1)S(1)}, u32[]{:S(2)}, u32[]{:S(2)}) %collective-permute-start.1) | collective-permute-done | bytes 73760 | tf_op jit(solution)/shard_map/ppermute | solution.py:337
  14.0 1.0 collective-permute-done.3.refs_6_
  15.0 3.5 %collective-permute-start.7 = (bf16[128,256]{1,0:T(8,128)(2,1)}, bf16[128,256]{1,0:T(8,128)(2,1)S(1)}, u32[]{:S(2)}, u32[]{:S(2)}) collective-permute-start(bf16[128,256]{1,0:T(8,128)(2,1)} %get-tuple-element.49), channel_id=1, source_target_pairs={{0,24},{4,28},{8,16},{12,20},{16,8},{20,12},{24,0},{28,4},{1,25},{... | collective-permute-start | bytes 196616 | tf_op jit(solution)/shard_map/ppermute | solution.py:337
  18.5 0.9 collective-permute-start.5
  19.4 1.6 %collective-permute-start.4 = (bf16[3,144,256]{2,1,0:T(8,128)(2,1)S(1)}, bf16[3,144,256]{2,1,0:T(8,128)(2,1)S(1)}, u32[]{:S(2)}, u32[]{:S(2)}) collective-permute-start(bf16[3,144,256]{2,1,0:T(8,128)(2,1)S(1)} %pad_maximum_fusion.1.refs_4_), channel_id=1, source_target_pairs={{0,4},{4,0},{8,12},{12,8},{16,20},{20,16},{24,28},{28,24},{1,5},{5... | collective-permute-start | bytes 663560 | tf_op jit(solution)/shard_map/ppermute | solution.py:337
  21.0 1.5 %collective-permute-start.8 = (bf16[3,128,256]{2,1,0:T(8,128)(2,1)S(1)}, bf16[3,128,256]{2,1,0:T(8,128)(2,1)S(1)}, u32[]{:S(2)}, u32[]{:S(2)}) collective-permute-start(bf16[3,128,256]{2,1,0:T(8,128)(2,1)S(1)} %slice.121), channel_id=1, source_target_pairs={{0,2},{1,3},{2,0},{3,1},{4,6},{5,7},{6,4},{7,5},{8,10},{9,11},{10,... | collective-permute-start | bytes 589832 | tf_op jit(solution)/shard_map/ppermute | solution.py:337
  22.5 1.3 %collective-permute-done.6 = bf16[128,256]{1,0:T(8,128)(2,1)S(1)} collective-permute-done((bf16[128,256]{1,0:T(8,128)(2,1)}, bf16[128,256]{1,0:T(8,128)(2,1)S(1)}, u32[]{:S(2)}, u32[]{:S(2)}) %collective-permute-start.6) | collective-permute-done | bytes 65568 | tf_op jit(solution)/shard_map/ppermute | solution.py:337
  23.9 1.6 %collective-permute-start.10 = (bf16[3,128,256]{2,1,0:T(8,128)(2,1)S(1)}, bf16[3,128,256]{2,1,0:T(8,128)(2,1)S(1)}, u32[]{:S(2)}, u32[]{:S(2)}) collective-permute-start(bf16[3,128,256]{2,1,0:T(8,128)(2,1)S(1)} %pad_maximum_fusion.2.refs_5_), channel_id=1, source_target_pairs={{0,4},{4,0},{8,12},{12,8},{16,20},{20,16},{24,28},{28,24},{1,5},{5... | collective-permute-start | bytes 589832 | tf_op jit(solution)/shard_map/ppermute | solution.py:337
  25.6 1.6 %collective-permute-start.9 = (bf16[4,128,256]{2,1,0:T(8,128)(2,1)S(1)}, bf16[4,128,256]{2,1,0:T(8,128)(2,1)S(1)}, u32[]{:S(2)}, u32[]{:S(2)}) collective-permute-start(bf16[4,128,256]{2,1,0:T(8,128)(2,1)S(1)} %pad_maximum_fusion), channel_id=1, source_target_pairs={{0,2},{1,3},{2,0},{3,1},{4,6},{5,7},{6,4},{7,5},{8,10},{9,11},{10,... | collective-permute-start | bytes 786440 | tf_op jit(solution)/shard_map/ppermute | solution.py:337
  28.3 3.4 %collective-permute-done.10.refs_10_ = bf16[3,128,256]{2,1,0:T(8,128)(2,1)S(1)} collective-permute-done((bf16[3,128,256]{2,1,0:T(8,128)(2,1)S(1)}, bf16[3,128,256]{2,1,0:T(8,128)(2,1)S(1)}, u32[]{:S(2)}, u32[]{:S(2)}) %collective-permute-start.10) | collective-permute-done | bytes 196640 | tf_op jit(solution)/shard_map/ppermute | solution.py:337
  31.7 2.3 %collective-permute-done.9.refs_9_ = bf16[4,128,256]{2,1,0:T(8,128)(2,1)S(1)} collective-permute-done((bf16[4,128,256]{2,1,0:T(8,128)(2,1)S(1)}, bf16[4,128,256]{2,1,0:T(8,128)(2,1)S(1)}, u32[]{:S(2)}, u32[]{:S(2)}) %collective-permute-start.9) | collective-permute-done | bytes 262176 | tf_op jit(solution)/shard_map/ppermute | solution.py:337
  34.0 1.5 %collective-permute-start.12 = (bf16[3,128,256]{2,1,0:T(8,128)(2,1)S(1)}, bf16[3,128,256]{2,1,0:T(8,128)(2,1)S(1)}, u32[]{:S(2)}, u32[]{:S(2)}) collective-permute-start(bf16[3,128,256]{2,1,0:T(8,128)(2,1)S(1)} %collective-permute-done.10.refs_10_), channel_id=1, source_target_pairs={{0,2},{1,3},{2,0},{3,1},{4,6},{5,7},{6,4},{7,5},{8,10},{9,11},{10,... | collective-permute-start | bytes 589832 | tf_op jit(solution)/shard_map/ppermute | solution.py:337
  35.5 2.7 %shard_map.83 = (bf16[8,256,128]{2,1,0:T(8,128)(2,1)}, bf16[8,128,256]{2,1,0:T(8,128)(2,1)}) custom-call(bf16[8,16,128]{2,1,0:T(8,128)(2,1)} %copy-done.2), custom_call_target="tpu_custom_call" | custom-call | flops 4000000000 | bytes 2097152 | tf_op jit(solution)/shard_map/pallas_call | solution.py:132
  39.3 0.9 collective-permute-done.12.refs_12_
  40.5 1.1 %collective-permute-done.21.refs_21_ = bf16[3,128,256]{2,1,0:T(8,128)(2,1)S(1)} collective-permute-done((bf16[3,128,256]{2,1,0:T(8,128)(2,1)S(1)}, bf16[3,128,256]{2,1,0:T(8,128)(2,1)S(1)}, u32[]{:S(2)}, u32[]{:S(2)}) %collective-permute-start.21) | collective-permute-done | bytes 196640 | tf_op jit(solution)/shard_map/ppermute | solution.py:337
  41.6 21.4 %shard_map.84 = (bf16[4,4,112,256]{3,2,1,0:T(8,128)(2,1)S(1)}, bf16[4,4,112,256]{3,2,1,0:T(8,128)(2,1)S(1)}, bf16[4,2,16,1024]{3,2,1,0:T(8,128)(2,1)S(1)}, bf16[...) custom-call(bf16[8,256,128]{2,1,0:T(8,128)(2,1)} %get-tuple-element.45.re, ...), custom_call_target="tpu_custom_call" | custom-call | flops 4831838208 | bytes 46137344 | tf_op jit(solution)/shard_map/pallas_call | solution.py:305
  63.7 1.8 %collective-permute-done.23 = bf16[4,4,112,256]{3,2,1,0:T(8,128)(2,1)S(1)} collective-permute-done((bf16[4,4,112,256]{3,2,1,0:T(8,128)(2,1)S(1)}, bf16[4,4,112,256]{3,2,1,0:T(8,128)(2,1)S(1)}, u32[]{:S(2)}, u32[]{:S(2)}) %collective-permute-start.23) | collective-permute-done | bytes 917536 | tf_op jit(solution)/shard_map/ppermute | solution.py:337
  65.7 1.5 %collective-permute-start.24 = (bf16[2,4,112,256]{3,2,1,0:T(8,128)(2,1)S(1)}, bf16[2,4,112,256]{3,2,1,0:T(8,128)(2,1)S(1)}, u32[]{:S(2)}, u32[]{:S(2)}) collective-permute-start(bf16[2,4,112,256]{3,2,1,0:T(8,128)(2,1)S(1)} %get-tuple-element.58), channel_id=1, source_target_pairs={{0,2},{1,3},{2,0},{3,1},{4,6},{5,7},{6,4},{7,5},{8,10},{9,11},{10,... | collective-permute-start | bytes 1376264 | tf_op jit(solution)/shard_map/ppermute | solution.py:337
  68.0 2.1 %collective-permute-start.29 = (bf16[2,16,1024]{2,1,0:T(8,128)(2,1)S(1)}, bf16[2,16,1024]{2,1,0:T(8,128)(2,1)S(1)}, u32[]{:S(2)}, u32[]{:S(2)}) collective-permute-start(bf16[2,16,1024]{2,1,0:T(8,128)(2,1)S(1)} %get-tuple-element.76), channel_id=1, source_target_pairs={{0,24},{4,28},{8,16},{12,20},{16,8},{20,12},{24,0},{28,4},{1,25},{... | collective-permute-start | bytes 196616 | tf_op jit(solution)/shard_map/ppermute | solution.py:337
  70.2 2.3 %collective-permute-start.27 = (bf16[2,16,1024]{2,1,0:T(8,128)(2,1)S(1)}, bf16[2,16,1024]{2,1,0:T(8,128)(2,1)S(1)}, u32[]{:S(2)}, u32[]{:S(2)}) collective-permute-start(bf16[2,16,1024]{2,1,0:T(8,128)(2,1)S(1)} %get-tuple-element.78), channel_id=1, source_target_pairs={{0,8},{4,12},{8,0},{12,4},{16,24},{20,28},{24,16},{28,20},{1,9},{5... | collective-permute-start | bytes 196616 | tf_op jit(solution)/shard_map/ppermute | solution.py:337
  72.5 5.9 %collective-permute-done.24 = bf16[2,4,112,256]{3,2,1,0:T(8,128)(2,1)S(1)} collective-permute-done((bf16[2,4,112,256]{3,2,1,0:T(8,128)(2,1)S(1)}, bf16[2,4,112,256]{3,2,1,0:T(8,128)(2,1)S(1)}, u32[]{:S(2)}, u32[]{:S(2)}) %collective-permute-start.24) | collective-permute-done | bytes 458784 | tf_op jit(solution)/shard_map/ppermute | solution.py:337
  78.4 1.2 %collective-permute-done.25 = bf16[2,4,112,256]{3,2,1,0:T(8,128)(2,1)S(1)} collective-permute-done((bf16[2,4,112,256]{3,2,1,0:T(8,128)(2,1)S(1)}, bf16[2,4,112,256]{3,2,1,0:T(8,128)(2,1)S(1)}, u32[]{:S(2)}, u32[]{:S(2)}) %collective-permute-start.25) | collective-permute-done | bytes 458784 | tf_op jit(solution)/shard_map/ppermute | solution.py:337
  80.7 1.2 %collective-permute-start.30 = (bf16[4,112,256]{2,1,0:T(8,128)(2,1)S(1)}, bf16[4,112,256]{2,1,0:T(8,128)(2,1)S(1)}, u32[]{:S(2)}, u32[]{:S(2)}) collective-permute-start(bf16[4,112,256]{2,1,0:T(8,128)(2,1)S(1)} %get-tuple-element.62), channel_id=1, source_target_pairs={{0,4},{4,0},{8,12},{12,8},{16,20},{20,16},{24,28},{28,24},{1,5},{5... | collective-permute-start | bytes 688136 | tf_op jit(solution)/shard_map/ppermute | solution.py:337
  82.5 1.7 %collective-permute-done.35 = bf16[16,1024]{1,0:T(8,128)(2,1)S(1)} collective-permute-done((bf16[16,1024]{1,0:T(8,128)(2,1)S(1)}, bf16[16,1024]{1,0:T(8,128)(2,1)S(1)}, u32[]{:S(2)}, u32[]{:S(2)}) %collective-permute-start.35) | collective-permute-done | bytes 32800 | tf_op jit(solution)/shard_map/ppermute | solution.py:337
  84.8 2.6 %collective-permute-done.30 = bf16[4,112,256]{2,1,0:T(8,128)(2,1)S(1)} collective-permute-done((bf16[4,112,256]{2,1,0:T(8,128)(2,1)S(1)}, bf16[4,112,256]{2,1,0:T(8,128)(2,1)S(1)}, u32[]{:S(2)}, u32[]{:S(2)}) %collective-permute-start.30) | collective-permute-done | bytes 229408 | tf_op jit(solution)/shard_map/ppermute | solution.py:337
  88.3 2.1 %collective-permute-start.32 = (bf16[112,512]{1,0:T(8,128)(2,1)S(1)}, bf16[112,512]{1,0:T(8,128)(2,1)S(1)}, u32[]{:S(2)}, u32[]{:S(2)}) collective-permute-start(bf16[112,512]{1,0:T(8,128)(2,1)S(1)} %get-tuple-element.73), channel_id=1, source_target_pairs={{0,24},{4,28},{8,16},{12,20},{16,8},{20,12},{24,0},{28,4},{1,25},{... | collective-permute-start | bytes 344072 | tf_op jit(solution)/shard_map/ppermute | solution.py:337
  90.5 2.3 %collective-permute-start.34 = (bf16[112,512]{1,0:T(8,128)(2,1)S(1)}, bf16[112,512]{1,0:T(8,128)(2,1)S(1)}, u32[]{:S(2)}, u32[]{:S(2)}) collective-permute-start(bf16[112,512]{1,0:T(8,128)(2,1)S(1)} %get-tuple-element.75), channel_id=1, source_target_pairs={{0,8},{4,12},{8,0},{12,4},{16,24},{20,28},{24,16},{28,20},{1,9},{5... | collective-permute-start | bytes 344072 | tf_op jit(solution)/shard_map/ppermute | solution.py:337
  92.8 2.9 %collective-permute-done.32 = bf16[112,512]{1,0:T(8,128)(2,1)S(1)} collective-permute-done((bf16[112,512]{1,0:T(8,128)(2,1)S(1)}, bf16[112,512]{1,0:T(8,128)(2,1)S(1)}, u32[]{:S(2)}, u32[]{:S(2)}) %collective-permute-start.32) | collective-permute-done | bytes 114720 | tf_op jit(solution)/shard_map/ppermute | solution.py:337
  95.6 3.5 %collective-permute-done.33 = bf16[112,512]{1,0:T(8,128)(2,1)S(1)} collective-permute-done((bf16[112,512]{1,0:T(8,128)(2,1)S(1)}, bf16[112,512]{1,0:T(8,128)(2,1)S(1)}, u32[]{:S(2)}, u32[]{:S(2)}) %collective-permute-start.33) | collective-permute-done | bytes 114720 | tf_op jit(solution)/shard_map/ppermute | solution.py:337
  (78 shorter events, 9.7 us)
Async XLA Ops:
  2.5 8.1 %collective-permute-start.2 = (bf16[144,256]{1,0:T(8,128)(2,1)}, bf16[144,256]{1,0:T(8,128)(2,1)S(1)}, u32[]{:S(2)}, u32[]{:S(2)}) collective-permute-start(bf16[144,256]{1,0:T(8,128)(2,1)} %get-tuple-element.38), channel_id=1, source_target_pairs={{0,24},{4,28},{8,16},{12,20},{16,8},{20,12},{24,0},{28,4},{1,25},{... | collective-permute-start | bytes 221192 | tf_op jit(solution)/shard_map/ppermute | solution.py:337
  7.5 6.4 %collective-permute-start.1 = (bf16[144,256]{1,0:T(8,128)(2,1)}, bf16[144,256]{1,0:T(8,128)(2,1)S(1)}, u32[]{:S(2)}, u32[]{:S(2)}) collective-permute-start(bf16[144,256]{1,0:T(8,128)(2,1)} %get-tuple-element.38), channel_id=1, source_target_pairs={{0,16},{4,20},{8,24},{12,28},{16,0},{20,4},{24,8},{28,12},{1,17},{... | collective-permute-start | bytes 221192 | tf_op jit(solution)/shard_map/ppermute | solution.py:337
  7.5 6.4 %collective-permute-start = (bf16[144,256]{1,0:T(8,128)(2,1)}, bf16[144,256]{1,0:T(8,128)(2,1)S(1)}, u32[]{:S(2)}, u32[]{:S(2)}) collective-permute-start(bf16[144,256]{1,0:T(8,128)(2,1)} %get-tuple-element.38), channel_id=1, source_target_pairs={{0,8},{4,12},{8,0},{12,4},{16,24},{20,28},{24,16},{28,20},{1,9},{5... | collective-permute-start | bytes 221192 | tf_op jit(solution)/shard_map/ppermute | solution.py:337
  8.2 6.8 %collective-permute-start.3 = (bf16[1,144,768]{2,1,0:T(8,128)(2,1)}, bf16[1,144,768]{2,1,0:T(8,128)(2,1)S(1)}, u32[]{:S(2)}, u32[]{:S(2)}) collective-permute-start(bf16[1,144,768]{2,1,0:T(8,128)(2,1)} %bitcast.67), channel_id=1, source_target_pairs={{0,4},{4,0},{8,12},{12,8},{16,20},{20,16},{24,28},{28,24},{1,5},{5... | collective-permute-start | bytes 663560 | tf_op jit(solution)/shard_map/ppermute | solution.py:337
  15.0 7.5 %collective-permute-start.7 = (bf16[128,256]{1,0:T(8,128)(2,1)}, bf16[128,256]{1,0:T(8,128)(2,1)S(1)}, u32[]{:S(2)}, u32[]{:S(2)}) collective-permute-start(bf16[128,256]{1,0:T(8,128)(2,1)} %get-tuple-element.49), channel_id=1, source_target_pairs={{0,24},{4,28},{8,16},{12,20},{16,8},{20,12},{24,0},{28,4},{1,25},{... | collective-permute-start | bytes 196616 | tf_op jit(solution)/shard_map/ppermute | solution.py:337
  18.5 5.4 %collective-permute-start.6 = (bf16[128,256]{1,0:T(8,128)(2,1)}, bf16[128,256]{1,0:T(8,128)(2,1)S(1)}, u32[]{:S(2)}, u32[]{:S(2)}) collective-permute-start(bf16[128,256]{1,0:T(8,128)(2,1)} %get-tuple-element.49), channel_id=1, source_target_pairs={{0,16},{4,20},{8,24},{12,28},{16,0},{20,4},{24,8},{28,12},{1,17},{... | collective-permute-start | bytes 196616 | tf_op jit(solution)/shard_map/ppermute | solution.py:337
  18.5 5.4 %collective-permute-start.5 = (bf16[128,256]{1,0:T(8,128)(2,1)}, bf16[128,256]{1,0:T(8,128)(2,1)S(1)}, u32[]{:S(2)}, u32[]{:S(2)}) collective-permute-start(bf16[128,256]{1,0:T(8,128)(2,1)} %get-tuple-element.49), channel_id=1, source_target_pairs={{0,8},{4,12},{8,0},{12,4},{16,24},{20,28},{24,16},{28,20},{1,9},{5... | collective-permute-start | bytes 196616 | tf_op jit(solution)/shard_map/ppermute | solution.py:337
  19.4 8.2 %collective-permute-start.4 = (bf16[3,144,256]{2,1,0:T(8,128)(2,1)S(1)}, bf16[3,144,256]{2,1,0:T(8,128)(2,1)S(1)}, u32[]{:S(2)}, u32[]{:S(2)}) collective-permute-start(bf16[3,144,256]{2,1,0:T(8,128)(2,1)S(1)} %pad_maximum_fusion.1.refs_4_), channel_id=1, source_target_pairs={{0,4},{4,0},{8,12},{12,8},{16,20},{20,16},{24,28},{28,24},{1,5},{5... | collective-permute-start | bytes 663560 | tf_op jit(solution)/shard_map/ppermute | solution.py:337
  21.0 6.1 %collective-permute-start.8 = (bf16[3,128,256]{2,1,0:T(8,128)(2,1)S(1)}, bf16[3,128,256]{2,1,0:T(8,128)(2,1)S(1)}, u32[]{:S(2)}, u32[]{:S(2)}) collective-permute-start(bf16[3,128,256]{2,1,0:T(8,128)(2,1)S(1)} %slice.121), channel_id=1, source_target_pairs={{0,2},{1,3},{2,0},{3,1},{4,6},{5,7},{6,4},{7,5},{8,10},{9,11},{10,... | collective-permute-start | bytes 589832 | tf_op jit(solution)/shard_map/ppermute | solution.py:337
  23.9 3.8 %collective-permute-start.14 = (bf16[3,128,256]{2,1,0:T(8,128)(2,1)S(1)}, bf16[3,128,256]{2,1,0:T(8,128)(2,1)S(1)}, u32[]{:S(2)}, u32[]{:S(2)}) collective-permute-start(bf16[3,128,256]{2,1,0:T(8,128)(2,1)S(1)} %pad_maximum_fusion.2.refs_5_), channel_id=1, source_target_pairs={{0,1},{1,0},{2,3},{3,2},{4,5},{5,4},{6,7},{7,6},{8,9},{9,8},{10,11... | collective-permute-start | bytes 589832 | tf_op jit(solution)/shard_map/ppermute | solution.py:337
  23.9 7.8 %collective-permute-start.10 = (bf16[3,128,256]{2,1,0:T(8,128)(2,1)S(1)}, bf16[3,128,256]{2,1,0:T(8,128)(2,1)S(1)}, u32[]{:S(2)}, u32[]{:S(2)}) collective-permute-start(bf16[3,128,256]{2,1,0:T(8,128)(2,1)S(1)} %pad_maximum_fusion.2.refs_5_), channel_id=1, source_target_pairs={{0,4},{4,0},{8,12},{12,8},{16,20},{20,16},{24,28},{28,24},{1,5},{5... | collective-permute-start | bytes 589832 | tf_op jit(solution)/shard_map/ppermute | solution.py:337
  25.6 8.4 %collective-permute-start.9 = (bf16[4,128,256]{2,1,0:T(8,128)(2,1)S(1)}, bf16[4,128,256]{2,1,0:T(8,128)(2,1)S(1)}, u32[]{:S(2)}, u32[]{:S(2)}) collective-permute-start(bf16[4,128,256]{2,1,0:T(8,128)(2,1)S(1)} %pad_maximum_fusion), channel_id=1, source_target_pairs={{0,2},{1,3},{2,0},{3,1},{4,6},{5,7},{6,4},{7,5},{8,10},{9,11},{10,... | collective-permute-start | bytes 786440 | tf_op jit(solution)/shard_map/ppermute | solution.py:337
  27.1 8.4 %collective-permute-start.11 = (bf16[3,128,256]{2,1,0:T(8,128)(2,1)S(1)}, bf16[3,128,256]{2,1,0:T(8,128)(2,1)S(1)}, u32[]{:S(2)}, u32[]{:S(2)}) collective-permute-start(bf16[3,128,256]{2,1,0:T(8,128)(2,1)S(1)} %collective-permute-done.8.refs_7_), channel_id=1, source_target_pairs={{0,4},{4,0},{8,12},{12,8},{16,20},{20,16},{24,28},{28,24},{1,5},{5... | collective-permute-start | bytes 589832 | tf_op jit(solution)/shard_map/ppermute | solution.py:337
  27.6 11.1 %collective-permute-start.13 = (bf16[3,144,256]{2,1,0:T(8,128)(2,1)S(1)}, bf16[3,144,256]{2,1,0:T(8,128)(2,1)S(1)}, u32[]{:S(2)}, u32[]{:S(2)}) collective-permute-start(bf16[3,144,256]{2,1,0:T(8,128)(2,1)S(1)} %pad_maximum_fusion.1.refs_4_), channel_id=1, source_target_pairs={{0,1},{1,0},{2,3},{3,2},{4,5},{5,4},{6,7},{7,6},{8,9},{9,8},{10,11... | collective-permute-start | bytes 663560 | tf_op jit(solution)/shard_map/ppermute | solution.py:337
  27.7 10.5 %collective-permute-start.16 = (bf16[3,128,256]{2,1,0:T(8,128)(2,1)S(1)}, bf16[3,128,256]{2,1,0:T(8,128)(2,1)S(1)}, u32[]{:S(2)}, u32[]{:S(2)}) collective-permute-start(bf16[3,128,256]{2,1,0:T(8,128)(2,1)S(1)} %collective-permute-done.8.refs_7_), channel_id=1, source_target_pairs={{0,1},{1,0},{2,3},{3,2},{4,5},{5,4},{6,7},{7,6},{8,9},{9,8},{10,11... | collective-permute-start | bytes 589832 | tf_op jit(solution)/shard_map/ppermute | solution.py:337
  31.7 7.1 %collective-permute-start.17 = (bf16[3,144,256]{2,1,0:T(8,128)(2,1)S(1)}, bf16[3,144,256]{2,1,0:T(8,128)(2,1)S(1)}, u32[]{:S(2)}, u32[]{:S(2)}) collective-permute-start(bf16[3,144,256]{2,1,0:T(8,128)(2,1)S(1)} %collective-permute-done.4.refs_8_), channel_id=1, source_target_pairs={{0,1},{1,0},{2,3},{3,2},{4,5},{5,4},{6,7},{7,6},{8,9},{9,8},{10,11... | collective-permute-start | bytes 663560 | tf_op jit(solution)/shard_map/ppermute | solution.py:337
  34.0 6.1 %collective-permute-start.12 = (bf16[3,128,256]{2,1,0:T(8,128)(2,1)S(1)}, bf16[3,128,256]{2,1,0:T(8,128)(2,1)S(1)}, u32[]{:S(2)}, u32[]{:S(2)}) collective-permute-start(bf16[3,128,256]{2,1,0:T(8,128)(2,1)S(1)} %collective-permute-done.10.refs_10_), channel_id=1, source_target_pairs={{0,2},{1,3},{2,0},{3,1},{4,6},{5,7},{6,4},{7,5},{8,10},{9,11},{10,... | collective-permute-start | bytes 589832 | tf_op jit(solution)/shard_map/ppermute | solution.py:337
  35.5 5.0 %collective-permute-start.18 = (bf16[4,128,256]{2,1,0:T(8,128)(2,1)S(1)}, bf16[4,128,256]{2,1,0:T(8,128)(2,1)S(1)}, u32[]{:S(2)}, u32[]{:S(2)}) collective-permute-start(bf16[4,128,256]{2,1,0:T(8,128)(2,1)S(1)} %collective-permute-done.9.refs_9_), channel_id=1, source_target_pairs={{0,1},{1,0},{2,3},{3,2},{4,5},{5,4},{6,7},{7,6},{8,9},{9,8},{10,11... | collective-permute-start | bytes 786440 | tf_op jit(solution)/shard_map/ppermute | solution.py:337
  63.2 7.0 %collective-permute-start.22 = (bf16[4,4,112,256]{3,2,1,0:T(8,128)(2,1)S(1)}, bf16[4,4,112,256]{3,2,1,0:T(8,128)(2,1)S(1)}, u32[]{:S(2)}, u32[]{:S(2)}) collective-permute-start(bf16[4,4,112,256]{3,2,1,0:T(8,128)(2,1)S(1)} %get-tuple-element.54), channel_id=1, source_target_pairs={{0,1},{1,0},{2,3},{3,2},{4,5},{5,4},{6,7},{7,6},{8,9},{9,8},{10,11... | collective-permute-start | bytes 2752520 | tf_op jit(solution)/shard_map/ppermute | solution.py:337
  63.5 4.4 %collective-permute-start.26 = (bf16[4,2,16,1024]{3,2,1,0:T(8,128)(2,1)S(1)}, bf16[4,2,16,1024]{3,2,1,0:T(8,128)(2,1)S(1)}, u32[]{:S(2)}, u32[]{:S(2)}) collective-permute-start(bf16[4,2,16,1024]{3,2,1,0:T(8,128)(2,1)S(1)} %get-tuple-element.61), channel_id=1, source_target_pairs={{0,1},{1,0},{2,3},{3,2},{4,5},{5,4},{6,7},{7,6},{8,9},{9,8},{10,11... | collective-permute-start | bytes 786440 | tf_op jit(solution)/shard_map/ppermute | solution.py:337
  65.7 12.6 %collective-permute-start.24 = (bf16[2,4,112,256]{3,2,1,0:T(8,128)(2,1)S(1)}, bf16[2,4,112,256]{3,2,1,0:T(8,128)(2,1)S(1)}, u32[]{:S(2)}, u32[]{:S(2)}) collective-permute-start(bf16[2,4,112,256]{3,2,1,0:T(8,128)(2,1)S(1)} %get-tuple-element.58), channel_id=1, source_target_pairs={{0,2},{1,3},{2,0},{3,1},{4,6},{5,7},{6,4},{7,5},{8,10},{9,11},{10,... | collective-permute-start | bytes 1376264 | tf_op jit(solution)/shard_map/ppermute | solution.py:337
  67.3 12.3 %collective-permute-start.25 = (bf16[2,4,112,256]{3,2,1,0:T(8,128)(2,1)S(1)}, bf16[2,4,112,256]{3,2,1,0:T(8,128)(2,1)S(1)}, u32[]{:S(2)}, u32[]{:S(2)}) collective-permute-start(bf16[2,4,112,256]{3,2,1,0:T(8,128)(2,1)S(1)} %get-tuple-element.59), channel_id=1, source_target_pairs={{0,4},{4,0},{8,12},{12,8},{16,20},{20,16},{24,28},{28,24},{1,5},{5... | collective-permute-start | bytes 1376264 | tf_op jit(solution)/shard_map/ppermute | solution.py:337
  68.0 11.7 %collective-permute-start.29 = (bf16[2,16,1024]{2,1,0:T(8,128)(2,1)S(1)}, bf16[2,16,1024]{2,1,0:T(8,128)(2,1)S(1)}, u32[]{:S(2)}, u32[]{:S(2)}) collective-permute-start(bf16[2,16,1024]{2,1,0:T(8,128)(2,1)S(1)} %get-tuple-element.76), channel_id=1, source_target_pairs={{0,24},{4,28},{8,16},{12,20},{16,8},{20,12},{24,0},{28,4},{1,25},{... | collective-permute-start | bytes 196616 | tf_op jit(solution)/shard_map/ppermute | solution.py:337
  70.1 9.6 %collective-permute-start.28 = (bf16[2,16,1024]{2,1,0:T(8,128)(2,1)S(1)}, bf16[2,16,1024]{2,1,0:T(8,128)(2,1)S(1)}, u32[]{:S(2)}, u32[]{:S(2)}) collective-permute-start(bf16[2,16,1024]{2,1,0:T(8,128)(2,1)S(1)} %get-tuple-element.77), channel_id=1, source_target_pairs={{0,16},{4,20},{8,24},{12,28},{16,0},{20,4},{24,8},{28,12},{1,17},{... | collective-permute-start | bytes 196616 | tf_op jit(solution)/shard_map/ppermute | solution.py:337
  70.2 9.6 %collective-permute-start.27 = (bf16[2,16,1024]{2,1,0:T(8,128)(2,1)S(1)}, bf16[2,16,1024]{2,1,0:T(8,128)(2,1)S(1)}, u32[]{:S(2)}, u32[]{:S(2)}) collective-permute-start(bf16[2,16,1024]{2,1,0:T(8,128)(2,1)S(1)} %get-tuple-element.78), channel_id=1, source_target_pairs={{0,8},{4,12},{8,0},{12,4},{16,24},{20,28},{24,16},{28,20},{1,9},{5... | collective-permute-start | bytes 196616 | tf_op jit(solution)/shard_map/ppermute | solution.py:337
  79.8 4.4 %collective-permute-start.35 = (bf16[16,1024]{1,0:T(8,128)(2,1)S(1)}, bf16[16,1024]{1,0:T(8,128)(2,1)S(1)}, u32[]{:S(2)}, u32[]{:S(2)}) collective-permute-start(bf16[16,1024]{1,0:T(8,128)(2,1)S(1)} %slice_bitcast_fusion.4), channel_id=1, source_target_pairs={{0,4},{4,0},{8,12},{12,8},{16,20},{20,16},{24,28},{28,24},{1,5},{5... | collective-permute-start | bytes 98312 | tf_op jit(solution)/shard_map/ppermute | solution.py:337
  80.7 6.8 %collective-permute-start.30 = (bf16[4,112,256]{2,1,0:T(8,128)(2,1)S(1)}, bf16[4,112,256]{2,1,0:T(8,128)(2,1)S(1)}, u32[]{:S(2)}, u32[]{:S(2)}) collective-permute-start(bf16[4,112,256]{2,1,0:T(8,128)(2,1)S(1)} %get-tuple-element.62), channel_id=1, source_target_pairs={{0,4},{4,0},{8,12},{12,8},{16,20},{20,16},{24,28},{28,24},{1,5},{5... | collective-permute-start | bytes 688136 | tf_op jit(solution)/shard_map/ppermute | solution.py:337
  81.9 6.1 %collective-permute-start.31 = (bf16[4,112,256]{2,1,0:T(8,128)(2,1)S(1)}, bf16[4,112,256]{2,1,0:T(8,128)(2,1)S(1)}, u32[]{:S(2)}, u32[]{:S(2)}) collective-permute-start(bf16[4,112,256]{2,1,0:T(8,128)(2,1)S(1)} %get-tuple-element.63), channel_id=1, source_target_pairs={{0,2},{1,3},{2,0},{3,1},{4,6},{5,7},{6,4},{7,5},{8,10},{9,11},{10,... | collective-permute-start | bytes 688136 | tf_op jit(solution)/shard_map/ppermute | solution.py:337
  84.2 8.5 %collective-permute-start.36 = (bf16[16,512]{1,0:T(8,128)(2,1)S(1)}, bf16[16,512]{1,0:T(8,128)(2,1)S(1)}, u32[]{:S(2)}, u32[]{:S(2)}) collective-permute-start(bf16[16,512]{1,0:T(8,128)(2,1)S(1)} %pad_maximum_fusion.4), channel_id=1, source_target_pairs={{0,2},{1,3},{2,0},{3,1},{4,6},{5,7},{6,4},{7,5},{8,10},{9,11},{10,... | collective-permute-start | bytes 49160 | tf_op jit(solution)/shard_map/ppermute | solution.py:337
  88.3 7.3 %collective-permute-start.32 = (bf16[112,512]{1,0:T(8,128)(2,1)S(1)}, bf16[112,512]{1,0:T(8,128)(2,1)S(1)}, u32[]{:S(2)}, u32[]{:S(2)}) collective-permute-start(bf16[112,512]{1,0:T(8,128)(2,1)S(1)} %get-tuple-element.73), channel_id=1, source_target_pairs={{0,24},{4,28},{8,16},{12,20},{16,8},{20,12},{24,0},{28,4},{1,25},{... | collective-permute-start | bytes 344072 | tf_op jit(solution)/shard_map/ppermute | solution.py:337
  90.4 8.7 %collective-permute-start.33 = (bf16[112,512]{1,0:T(8,128)(2,1)S(1)}, bf16[112,512]{1,0:T(8,128)(2,1)S(1)}, u32[]{:S(2)}, u32[]{:S(2)}) collective-permute-start(bf16[112,512]{1,0:T(8,128)(2,1)S(1)} %get-tuple-element.74), channel_id=1, source_target_pairs={{0,16},{4,20},{8,24},{12,28},{16,0},{20,4},{24,8},{28,12},{1,17},{... | collective-permute-start | bytes 344072 | tf_op jit(solution)/shard_map/ppermute | solution.py:337
  90.5 8.7 %collective-permute-start.34 = (bf16[112,512]{1,0:T(8,128)(2,1)S(1)}, bf16[112,512]{1,0:T(8,128)(2,1)S(1)}, u32[]{:S(2)}, u32[]{:S(2)}) collective-permute-start(bf16[112,512]{1,0:T(8,128)(2,1)S(1)} %get-tuple-element.75), channel_id=1, source_target_pairs={{0,8},{4,12},{8,0},{12,4},{16,24},{20,28},{24,16},{28,20},{1,9},{5... | collective-permute-start | bytes 344072 | tf_op jit(solution)/shard_map/ppermute | solution.py:337
  (8 other events, 113.6 us)

commit v10 on v9

--- a/solution.py
+++ b/solution.py
@@ -153,8 +153,8 @@
     pieces_in = refs[4 : 4 + n_pieces]
     w_gate_hbm, w_up_hbm, w_down_hbm = refs[4 + n_pieces : 7 + n_pieces]
     out_refs = refs[7 + n_pieces : 13 + n_pieces]
-    (picks, weights, w_in, w_down, toks, rows, both, hidden, mixed, along, table_sems, tok_sems,
-     in_sems, down_sems) = refs[13 + n_pieces :]
+    (picks, weights, w_in, w_down, toks, rows, hidden, mixed, table_sems, tok_sems, in_sems,
+     down_sems) = refs[13 + n_pieces :]
     n_z, _, tok_rows, model_width = toks.shape
     n_seq = 2 * n_z
     exp_dev, hid_dev, _ = w_gate_hbm.shape
@@ -212,22 +212,21 @@
 
     lax.fori_loop(0, n_z, pick, 0)
 
-    def activate(pair):
-        for i in range(2):
-            gate_val, up_val = both[i, :hid_dev], both[i, hid_dev:]
-            act = gate_val / (1.0 + jnp.exp(-gate_val)) * up_val
-            hidden[2 * pair + i] = act.T.astype(jnp.bfloat16)
-
     def widen(pair, carry):
         experts = (2 * pair, 2 * pair + 1)
         for e in experts:
             for copy in in_copies(e):
                 copy.wait()
-        activate(jnp.maximum(pair - 1, 0))
-        for i, e in enumerate(experts):
-            both[i] = contract(
-                w_in[lax.rem(e, RING)], rows[:, e].reshape(n_seq * SLOTS, model_width), 1, 1
-            )
+        taken = [rows[:, e].reshape(n_seq * SLOTS, model_width) for e in experts]
+        both = [
+            [
+                contract(value, w_in[lax.rem(e, RING), i * hid_dev : (i + 1) * hid_dev], 1, 1)
+                for i in range(2)
+            ]
+            for e, value in zip(experts, taken)
+        ]
+        for e, (gate_val, up_val) in zip(experts, both):
+            hidden[e] = (gate_val / (1.0 + jnp.exp(-gate_val)) * up_val).astype(jnp.bfloat16)
         for e in experts:
             down_copy(e).start()
 
@@ -239,7 +238,6 @@
         return carry
 
     lax.fori_loop(0, exp_dev // 2, widen, 0)
-    activate(exp_dev // 2 - 1)
 
     def narrow(pair, carry):
         experts = (2 * pair, 2 * pair + 1)
@@ -254,7 +252,15 @@
     lax.fori_loop(0, exp_dev // 2, narrow, 0)
     tables[1].wait()
 
-    def project(dz):
+    def combine(dz, carry):
+        along = [jnp.zeros((tok_rows, 1), jnp.float32)] * 2
+        for dy in range(2):
+            j = 2 * dz + dy
+            weight = weights[j]
+            for cols in quarters:
+                got = contract(weight, rows[j, :, :, cols].reshape(slots_src, 2 * width), 1, 0)
+                mixed[dy, :, cols] = got
+                along[dy] += jnp.sum(got * unit_ref[:, cols], axis=1, keepdims=True)
         for dy in range(2):
             for dc in range(2):
                 far, near, rest = out_refs[3 * dc : 3 * dc + 3]
@@ -265,23 +271,9 @@
                     rest[dz, dy, :, n * width : (n + 1) * width] = value[split:]
                     leaves, kind = (dy, 2 + dx) if color else (dx, dy)
                     (far if leaves else near)[kind, dz] = value[:split]
-
-    def combine(dz, carry):
-        project(jnp.maximum(dz - 1, 0))
-        for dy in range(2):
-            j = 2 * dz + dy
-            total = jnp.zeros((tok_rows, 1), jnp.float32)
-            for cols in quarters:
-                got = contract(
-                    weights[j], rows[j, :, :, cols].reshape(slots_src, 2 * width), 1, 0
-                )
-                mixed[dy, :, cols] = got
-                total += jnp.sum(got * unit_ref[:, cols], axis=1, keepdims=True)
-            along[dy] = total
         return carry
 
     lax.fori_loop(0, n_z, combine, 0)
-    project(n_z - 1)
 
 
 def moe_partial(picks, weights, unit_dir, own, pieces, w_gate, w_up, w_down):
@@ -314,10 +306,8 @@
             pltpu.VMEM(w_down.shape, jnp.bfloat16),
             pltpu.VMEM((n_z, 2, tok_rows, model_width), jnp.bfloat16),
             pltpu.VMEM((n_seq, exp_dev, SLOTS, model_width), jnp.bfloat16),
-            pltpu.VMEM((2, 2 * hid_dev, n_seq * SLOTS), jnp.float32),
             pltpu.VMEM((exp_dev, n_seq * SLOTS, hid_dev), jnp.bfloat16),
             pltpu.VMEM((2, tok_rows, model_width), jnp.float32),
-            pltpu.VMEM((2, tok_rows, 1), jnp.float32),
             pltpu.SemaphoreType.DMA((2,)),
             pltpu.SemaphoreType.DMA((n_z, 2)),
             pltpu.SemaphoreType.DMA((2, RING)),

time: 100 us -> 99.5 us (level)
  no operation moved by 1% of the time
where the time goes in v10:
time: 99.5 us; the launch traced here: 99.3 us
  starting transfers between devices  36.6 us (37%)
  waiting for transfers between devices  34.1 us (34%)
  Pallas kernels  25.9 us (26%)
  other arithmetic  1.62 us (2%)
    ppermute x37, starting transfers between devices, swap(): return lax.ppermute(value, axis, [(i, i ^ distance) for i in range(size)])  36.6 us
    ppermute x37, waiting for transfers between devices, swap(): return lax.ppermute(value, axis, [(i, i ^ distance) for i in range(size)])  34.1 us
    pallas_call x1, Pallas kernels, moe_partial(): pl.pallas_call(functools.partial(moe_kernel, n_pieces), out_shape=outs, i...  20.7 us
    pallas_call x1, Pallas kernels, route(): pl.pallas_call(functools.partial(route_kernel, exp_dev), out_shape=[jax.S...  2.72 us
    pallas_call x1, Pallas kernels, norm_and_base(): pl.pallas_call(norm_kernel, out_shape=[jax.ShapeDtypeStruct((tok_rows, mo...  2.46 us
  transfers between devices with their start and end apart: 37, of which 16 were waited for; matrix products, arithmetic and copies ran while one was open for 2% of the time, Pallas kernels for 3%

profile of v10, /device:TPU:0, one launch (start us, length us, event | category | flops | bytes accessed | tf_op | source)
XLA Modules:
  0.0 99.3 jit_solution(2522201981864376815)
XLA Ops:
  0.0 2.5 %shard_map.82 = (bf16[128,2048]{1,0:T(8,128)(2,1)}, bf16[144,256]{1,0:T(8,128)(2,1)}, bf16[128,256]{1,0:T(8,128)(2,1)}, bf16[144,768]{1,0:T(8,128)(2,1)}, f32[1,...) custom-call(bf16[128,2048]{1,0:T(8,128)(2,1)} %tokens_ref.1, f32[1,2048]{1,0:T(1,128)} %bitcast.63, ...), custom_call_target="tpu_custom_call" | custom-call | tf_op jit(solution)/shard_map/pallas_call | solution.py:74
  2.5 5.1 %collective-permute-start.2 = (bf16[144,256]{1,0:T(8,128)(2,1)}, bf16[144,256]{1,0:T(8,128)(2,1)S(1)}, u32[]{:S(2)}, u32[]{:S(2)}) collective-permute-start(bf16[144,256]{1,0:T(8,128)(2,1)} %get-tuple-element.38), channel_id=1, source_target_pairs={{0,24},{4,28},{8,16},{12,20},{16,8},{20,12},{24,0},{28,4},{1,25},{... | collective-permute-start | bytes 221192 | tf_op jit(solution)/shard_map/ppermute | solution.py:327
  8.2 1.7 %collective-permute-start.3 = (bf16[1,144,768]{2,1,0:T(8,128)(2,1)}, bf16[1,144,768]{2,1,0:T(8,128)(2,1)S(1)}, u32[]{:S(2)}, u32[]{:S(2)}) collective-permute-start(bf16[1,144,768]{2,1,0:T(8,128)(2,1)} %bitcast.67), channel_id=1, source_target_pairs={{0,4},{4,0},{8,12},{12,8},{16,20},{20,16},{24,28},{28,24},{1,5},{5... | collective-permute-start | bytes 663560 | tf_op jit(solution)/shard_map/ppermute | solution.py:327
  10.5 3.4 %collective-permute-done.1 = bf16[144,256]{1,0:T(8,128)(2,1)S(1)} collective-permute-done((bf16[144,256]{1,0:T(8,128)(2,1)}, bf16[144,256]{1,0:T(8,128)(2,1)S(1)}, u32[]{:S(2)}, u32[]{:S(2)}) %collective-permute-start.1) | collective-permute-done | bytes 73760 | tf_op jit(solution)/shard_map/ppermute | solution.py:327
  14.0 1.0 %collective-permute-done.3.refs_6_ = bf16[1,144,768]{2,1,0:T(8,128)(2,1)S(1)} collective-permute-done((bf16[1,144,768]{2,1,0:T(8,128)(2,1)}, bf16[1,144,768]{2,1,0:T(8,128)(2,1)S(1)}, u32[]{:S(2)}, u32[]{:S(2)}) %collective-permute-start.3) | collective-permute-done | bytes 221216 | tf_op jit(solution)/shard_map/ppermute | solution.py:327
  15.0 3.5 %collective-permute-start.7 = (bf16[128,256]{1,0:T(8,128)(2,1)}, bf16[128,256]{1,0:T(8,128)(2,1)S(1)}, u32[]{:S(2)}, u32[]{:S(2)}) collective-permute-start(bf16[128,256]{1,0:T(8,128)(2,1)} %get-tuple-element.49), channel_id=1, source_target_pairs={{0,24},{4,28},{8,16},{12,20},{16,8},{20,12},{24,0},{28,4},{1,25},{... | collective-permute-start | bytes 196616 | tf_op jit(solution)/shard_map/ppermute | solution.py:327
  18.5 0.9 collective-permute-start.5
  19.4 1.6 %collective-permute-start.4 = (bf16[3,144,256]{2,1,0:T(8,128)(2,1)S(1)}, bf16[3,144,256]{2,1,0:T(8,128)(2,1)S(1)}, u32[]{:S(2)}, u32[]{:S(2)}) collective-permute-start(bf16[3,144,256]{2,1,0:T(8,128)(2,1)S(1)} %pad_maximum_fusion.1.refs_4_), channel_id=1, source_target_pairs={{0,4},{4,0},{8,12},{12,8},{16,20},{20,16},{24,28},{28,24},{1,5},{5... | collective-permute-start | bytes 663560 | tf_op jit(solution)/shard_map/ppermute | solution.py:327
  21.0 1.5 %collective-permute-start.8 = (bf16[3,128,256]{2,1,0:T(8,128)(2,1)S(1)}, bf16[3,128,256]{2,1,0:T(8,128)(2,1)S(1)}, u32[]{:S(2)}, u32[]{:S(2)}) collective-permute-start(bf16[3,128,256]{2,1,0:T(8,128)(2,1)S(1)} %slice.121), channel_id=1, source_target_pairs={{0,2},{1,3},{2,0},{3,1},{4,6},{5,7},{6,4},{7,5},{8,10},{9,11},{10,... | collective-permute-start | bytes 589832 | tf_op jit(solution)/shard_map/ppermute | solution.py:327
  22.5 1.3 %collective-permute-done.6 = bf16[128,256]{1,0:T(8,128)(2,1)S(1)} collective-permute-done((bf16[128,256]{1,0:T(8,128)(2,1)}, bf16[128,256]{1,0:T(8,128)(2,1)S(1)}, u32[]{:S(2)}, u32[]{:S(2)}) %collective-permute-start.6) | collective-permute-done | bytes 65568 | tf_op jit(solution)/shard_map/ppermute | solution.py:327
  23.9 1.6 %collective-permute-start.10 = (bf16[3,128,256]{2,1,0:T(8,128)(2,1)S(1)}, bf16[3,128,256]{2,1,0:T(8,128)(2,1)S(1)}, u32[]{:S(2)}, u32[]{:S(2)}) collective-permute-start(bf16[3,128,256]{2,1,0:T(8,128)(2,1)S(1)} %pad_maximum_fusion.2.refs_5_), channel_id=1, source_target_pairs={{0,4},{4,0},{8,12},{12,8},{16,20},{20,16},{24,28},{28,24},{1,5},{5... | collective-permute-start | bytes 589832 | tf_op jit(solution)/shard_map/ppermute | solution.py:327
  25.6 1.6 %collective-permute-start.9 = (bf16[4,128,256]{2,1,0:T(8,128)(2,1)S(1)}, bf16[4,128,256]{2,1,0:T(8,128)(2,1)S(1)}, u32[]{:S(2)}, u32[]{:S(2)}) collective-permute-start(bf16[4,128,256]{2,1,0:T(8,128)(2,1)S(1)} %pad_maximum_fusion), channel_id=1, source_target_pairs={{0,2},{1,3},{2,0},{3,1},{4,6},{5,7},{6,4},{7,5},{8,10},{9,11},{10,... | collective-permute-start | bytes 786440 | tf_op jit(solution)/shard_map/ppermute | solution.py:327
  28.3 3.4 %collective-permute-done.10.refs_10_ = bf16[3,128,256]{2,1,0:T(8,128)(2,1)S(1)} collective-permute-done((bf16[3,128,256]{2,1,0:T(8,128)(2,1)S(1)}, bf16[3,128,256]{2,1,0:T(8,128)(2,1)S(1)}, u32[]{:S(2)}, u32[]{:S(2)}) %collective-permute-start.10) | collective-permute-done | bytes 196640 | tf_op jit(solution)/shard_map/ppermute | solution.py:327
  31.7 2.3 %collective-permute-done.9.refs_9_ = bf16[4,128,256]{2,1,0:T(8,128)(2,1)S(1)} collective-permute-done((bf16[4,128,256]{2,1,0:T(8,128)(2,1)S(1)}, bf16[4,128,256]{2,1,0:T(8,128)(2,1)S(1)}, u32[]{:S(2)}, u32[]{:S(2)}) %collective-permute-start.9) | collective-permute-done | bytes 262176 | tf_op jit(solution)/shard_map/ppermute | solution.py:327
  34.0 1.5 %collective-permute-start.12 = (bf16[3,128,256]{2,1,0:T(8,128)(2,1)S(1)}, bf16[3,128,256]{2,1,0:T(8,128)(2,1)S(1)}, u32[]{:S(2)}, u32[]{:S(2)}) collective-permute-start(bf16[3,128,256]{2,1,0:T(8,128)(2,1)S(1)} %collective-permute-done.10.refs_10_), channel_id=1, source_target_pairs={{0,2},{1,3},{2,0},{3,1},{4,6},{5,7},{6,4},{7,5},{8,10},{9,11},{10,... | collective-permute-start | bytes 589832 | tf_op jit(solution)/shard_map/ppermute | solution.py:327
  35.5 2.7 %shard_map.83 = (bf16[8,256,128]{2,1,0:T(8,128)(2,1)}, bf16[8,128,256]{2,1,0:T(8,128)(2,1)}) custom-call(bf16[8,16,128]{2,1,0:T(8,128)(2,1)} %copy-done.2), custom_call_target="tpu_custom_call" | custom-call | flops 4000000000 | bytes 2097152 | tf_op jit(solution)/shard_map/pallas_call | solution.py:132
  39.3 0.9 collective-permute-done.12.refs_12_
  40.5 1.1 %collective-permute-done.21.refs_21_ = bf16[3,128,256]{2,1,0:T(8,128)(2,1)S(1)} collective-permute-done((bf16[3,128,256]{2,1,0:T(8,128)(2,1)S(1)}, bf16[3,128,256]{2,1,0:T(8,128)(2,1)S(1)}, u32[]{:S(2)}, u32[]{:S(2)}) %collective-permute-start.21) | collective-permute-done | bytes 196640 | tf_op jit(solution)/shard_map/ppermute | solution.py:327
  41.6 20.7 %shard_map.84 = (bf16[4,4,112,256]{3,2,1,0:T(8,128)(2,1)S(1)}, bf16[4,4,112,256]{3,2,1,0:T(8,128)(2,1)S(1)}, bf16[4,2,16,1024]{3,2,1,0:T(8,128)(2,1)S(1)}, bf16[...) custom-call(bf16[8,256,128]{2,1,0:T(8,128)(2,1)} %get-tuple-element.45.re, ...), custom_call_target="tpu_custom_call" | custom-call | flops 4831838208 | bytes 46137344 | tf_op jit(solution)/shard_map/pallas_call | solution.py:297
  63.0 1.8 %collective-permute-done.23 = bf16[4,4,112,256]{3,2,1,0:T(8,128)(2,1)S(1)} collective-permute-done((bf16[4,4,112,256]{3,2,1,0:T(8,128)(2,1)S(1)}, bf16[4,4,112,256]{3,2,1,0:T(8,128)(2,1)S(1)}, u32[]{:S(2)}, u32[]{:S(2)}) %collective-permute-start.23) | collective-permute-done | bytes 917536 | tf_op jit(solution)/shard_map/ppermute | solution.py:327
  65.0 1.6 %collective-permute-start.24 = (bf16[2,4,112,256]{3,2,1,0:T(8,128)(2,1)S(1)}, bf16[2,4,112,256]{3,2,1,0:T(8,128)(2,1)S(1)}, u32[]{:S(2)}, u32[]{:S(2)}) collective-permute-start(bf16[2,4,112,256]{3,2,1,0:T(8,128)(2,1)S(1)} %get-tuple-element.58), channel_id=1, source_target_pairs={{0,2},{1,3},{2,0},{3,1},{4,6},{5,7},{6,4},{7,5},{8,10},{9,11},{10,... | collective-permute-start | bytes 1376264 | tf_op jit(solution)/shard_map/ppermute | solution.py:327
  67.3 2.1 %collective-permute-start.29 = (bf16[2,16,1024]{2,1,0:T(8,128)(2,1)S(1)}, bf16[2,16,1024]{2,1,0:T(8,128)(2,1)S(1)}, u32[]{:S(2)}, u32[]{:S(2)}) collective-permute-start(bf16[2,16,1024]{2,1,0:T(8,128)(2,1)S(1)} %get-tuple-element.76), channel_id=1, source_target_pairs={{0,24},{4,28},{8,16},{12,20},{16,8},{20,12},{24,0},{28,4},{1,25},{... | collective-permute-start | bytes 196616 | tf_op jit(solution)/shard_map/ppermute | solution.py:327
  69.5 2.3 %collective-permute-start.27 = (bf16[2,16,1024]{2,1,0:T(8,128)(2,1)S(1)}, bf16[2,16,1024]{2,1,0:T(8,128)(2,1)S(1)}, u32[]{:S(2)}, u32[]{:S(2)}) collective-permute-start(bf16[2,16,1024]{2,1,0:T(8,128)(2,1)S(1)} %get-tuple-element.78), channel_id=1, source_target_pairs={{0,8},{4,12},{8,0},{12,4},{16,24},{20,28},{24,16},{28,20},{1,9},{5... | collective-permute-start | bytes 196616 | tf_op jit(solution)/shard_map/ppermute | solution.py:327
  71.8 5.9 %collective-permute-done.24 = bf16[2,4,112,256]{3,2,1,0:T(8,128)(2,1)S(1)} collective-permute-done((bf16[2,4,112,256]{3,2,1,0:T(8,128)(2,1)S(1)}, bf16[2,4,112,256]{3,2,1,0:T(8,128)(2,1)S(1)}, u32[]{:S(2)}, u32[]{:S(2)}) %collective-permute-start.24) | collective-permute-done | bytes 458784 | tf_op jit(solution)/shard_map/ppermute | solution.py:327
  77.7 1.2 %collective-permute-done.25 = bf16[2,4,112,256]{3,2,1,0:T(8,128)(2,1)S(1)} collective-permute-done((bf16[2,4,112,256]{3,2,1,0:T(8,128)(2,1)S(1)}, bf16[2,4,112,256]{3,2,1,0:T(8,128)(2,1)S(1)}, u32[]{:S(2)}, u32[]{:S(2)}) %collective-permute-start.25) | collective-permute-done | bytes 458784 | tf_op jit(solution)/shard_map/ppermute | solution.py:327
  80.0 1.2 %collective-permute-start.30 = (bf16[4,112,256]{2,1,0:T(8,128)(2,1)S(1)}, bf16[4,112,256]{2,1,0:T(8,128)(2,1)S(1)}, u32[]{:S(2)}, u32[]{:S(2)}) collective-permute-start(bf16[4,112,256]{2,1,0:T(8,128)(2,1)S(1)} %get-tuple-element.62), channel_id=1, source_target_pairs={{0,4},{4,0},{8,12},{12,8},{16,20},{20,16},{24,28},{28,24},{1,5},{5... | collective-permute-start | bytes 688136 | tf_op jit(solution)/shard_map/ppermute | solution.py:327
  81.8 1.7 %collective-permute-done.35 = bf16[16,1024]{1,0:T(8,128)(2,1)S(1)} collective-permute-done((bf16[16,1024]{1,0:T(8,128)(2,1)S(1)}, bf16[16,1024]{1,0:T(8,128)(2,1)S(1)}, u32[]{:S(2)}, u32[]{:S(2)}) %collective-permute-start.35) | collective-permute-done | bytes 32800 | tf_op jit(solution)/shard_map/ppermute | solution.py:327
  84.1 2.7 %collective-permute-done.30 = bf16[4,112,256]{2,1,0:T(8,128)(2,1)S(1)} collective-permute-done((bf16[4,112,256]{2,1,0:T(8,128)(2,1)S(1)}, bf16[4,112,256]{2,1,0:T(8,128)(2,1)S(1)}, u32[]{:S(2)}, u32[]{:S(2)}) %collective-permute-start.30) | collective-permute-done | bytes 229408 | tf_op jit(solution)/shard_map/ppermute | solution.py:327
  87.6 2.1 %collective-permute-start.32 = (bf16[112,512]{1,0:T(8,128)(2,1)S(1)}, bf16[112,512]{1,0:T(8,128)(2,1)S(1)}, u32[]{:S(2)}, u32[]{:S(2)}) collective-permute-start(bf16[112,512]{1,0:T(8,128)(2,1)S(1)} %get-tuple-element.73), channel_id=1, source_target_pairs={{0,24},{4,28},{8,16},{12,20},{16,8},{20,12},{24,0},{28,4},{1,25},{... | collective-permute-start | bytes 344072 | tf_op jit(solution)/shard_map/ppermute | solution.py:327
  89.8 2.3 %collective-permute-start.34 = (bf16[112,512]{1,0:T(8,128)(2,1)S(1)}, bf16[112,512]{1,0:T(8,128)(2,1)S(1)}, u32[]{:S(2)}, u32[]{:S(2)}) collective-permute-start(bf16[112,512]{1,0:T(8,128)(2,1)S(1)} %get-tuple-element.75), channel_id=1, source_target_pairs={{0,8},{4,12},{8,0},{12,4},{16,24},{20,28},{24,16},{28,20},{1,9},{5... | collective-permute-start | bytes 344072 | tf_op jit(solution)/shard_map/ppermute | solution.py:327
  92.1 2.9 %collective-permute-done.32 = bf16[112,512]{1,0:T(8,128)(2,1)S(1)} collective-permute-done((bf16[112,512]{1,0:T(8,128)(2,1)S(1)}, bf16[112,512]{1,0:T(8,128)(2,1)S(1)}, u32[]{:S(2)}, u32[]{:S(2)}) %collective-permute-start.32) | collective-permute-done | bytes 114720 | tf_op jit(solution)/shard_map/ppermute | solution.py:327
  95.0 3.5 %collective-permute-done.33 = bf16[112,512]{1,0:T(8,128)(2,1)S(1)} collective-permute-done((bf16[112,512]{1,0:T(8,128)(2,1)S(1)}, bf16[112,512]{1,0:T(8,128)(2,1)S(1)}, u32[]{:S(2)}, u32[]{:S(2)}) %collective-permute-start.33) | collective-permute-done | bytes 114720 | tf_op jit(solution)/shard_map/ppermute | solution.py:327
  (78 shorter events, 9.6 us)
Async XLA Ops:
  2.5 8.1 %collective-permute-start.2 = (bf16[144,256]{1,0:T(8,128)(2,1)}, bf16[144,256]{1,0:T(8,128)(2,1)S(1)}, u32[]{:S(2)}, u32[]{:S(2)}) collective-permute-start(bf16[144,256]{1,0:T(8,128)(2,1)} %get-tuple-element.38), channel_id=1, source_target_pairs={{0,24},{4,28},{8,16},{12,20},{16,8},{20,12},{24,0},{28,4},{1,25},{... | collective-permute-start | bytes 221192 | tf_op jit(solution)/shard_map/ppermute | solution.py:327
  7.5 6.4 %collective-permute-start.1 = (bf16[144,256]{1,0:T(8,128)(2,1)}, bf16[144,256]{1,0:T(8,128)(2,1)S(1)}, u32[]{:S(2)}, u32[]{:S(2)}) collective-permute-start(bf16[144,256]{1,0:T(8,128)(2,1)} %get-tuple-element.38), channel_id=1, source_target_pairs={{0,16},{4,20},{8,24},{12,28},{16,0},{20,4},{24,8},{28,12},{1,17},{... | collective-permute-start | bytes 221192 | tf_op jit(solution)/shard_map/ppermute | solution.py:327
  7.5 6.4 %collective-permute-start = (bf16[144,256]{1,0:T(8,128)(2,1)}, bf16[144,256]{1,0:T(8,128)(2,1)S(1)}, u32[]{:S(2)}, u32[]{:S(2)}) collective-permute-start(bf16[144,256]{1,0:T(8,128)(2,1)} %get-tuple-element.38), channel_id=1, source_target_pairs={{0,8},{4,12},{8,0},{12,4},{16,24},{20,28},{24,16},{28,20},{1,9},{5... | collective-permute-start | bytes 221192 | tf_op jit(solution)/shard_map/ppermute | solution.py:327
  8.2 6.8 %collective-permute-start.3 = (bf16[1,144,768]{2,1,0:T(8,128)(2,1)}, bf16[1,144,768]{2,1,0:T(8,128)(2,1)S(1)}, u32[]{:S(2)}, u32[]{:S(2)}) collective-permute-start(bf16[1,144,768]{2,1,0:T(8,128)(2,1)} %bitcast.67), channel_id=1, source_target_pairs={{0,4},{4,0},{8,12},{12,8},{16,20},{20,16},{24,28},{28,24},{1,5},{5... | collective-permute-start | bytes 663560 | tf_op jit(solution)/shard_map/ppermute | solution.py:327
  15.0 7.5 %collective-permute-start.7 = (bf16[128,256]{1,0:T(8,128)(2,1)}, bf16[128,256]{1,0:T(8,128)(2,1)S(1)}, u32[]{:S(2)}, u32[]{:S(2)}) collective-permute-start(bf16[128,256]{1,0:T(8,128)(2,1)} %get-tuple-element.49), channel_id=1, source_target_pairs={{0,24},{4,28},{8,16},{12,20},{16,8},{20,12},{24,0},{28,4},{1,25},{... | collective-permute-start | bytes 196616 | tf_op jit(solution)/shard_map/ppermute | solution.py:327
  18.5 5.4 %collective-permute-start.6 = (bf16[128,256]{1,0:T(8,128)(2,1)}, bf16[128,256]{1,0:T(8,128)(2,1)S(1)}, u32[]{:S(2)}, u32[]{:S(2)}) collective-permute-start(bf16[128,256]{1,0:T(8,128)(2,1)} %get-tuple-element.49), channel_id=1, source_target_pairs={{0,16},{4,20},{8,24},{12,28},{16,0},{20,4},{24,8},{28,12},{1,17},{... | collective-permute-start | bytes 196616 | tf_op jit(solution)/shard_map/ppermute | solution.py:327
  18.5 5.4 %collective-permute-start.5 = (bf16[128,256]{1,0:T(8,128)(2,1)}, bf16[128,256]{1,0:T(8,128)(2,1)S(1)}, u32[]{:S(2)}, u32[]{:S(2)}) collective-permute-start(bf16[128,256]{1,0:T(8,128)(2,1)} %get-tuple-element.49), channel_id=1, source_target_pairs={{0,8},{4,12},{8,0},{12,4},{16,24},{20,28},{24,16},{28,20},{1,9},{5... | collective-permute-start | bytes 196616 | tf_op jit(solution)/shard_map/ppermute | solution.py:327
  19.4 8.2 %collective-permute-start.4 = (bf16[3,144,256]{2,1,0:T(8,128)(2,1)S(1)}, bf16[3,144,256]{2,1,0:T(8,128)(2,1)S(1)}, u32[]{:S(2)}, u32[]{:S(2)}) collective-permute-start(bf16[3,144,256]{2,1,0:T(8,128)(2,1)S(1)} %pad_maximum_fusion.1.refs_4_), channel_id=1, source_target_pairs={{0,4},{4,0},{8,12},{12,8},{16,20},{20,16},{24,28},{28,24},{1,5},{5... | collective-permute-start | bytes 663560 | tf_op jit(solution)/shard_map/ppermute | solution.py:327
  21.0 6.1 %collective-permute-start.8 = (bf16[3,128,256]{2,1,0:T(8,128)(2,1)S(1)}, bf16[3,128,256]{2,1,0:T(8,128)(2,1)S(1)}, u32[]{:S(2)}, u32[]{:S(2)}) collective-permute-start(bf16[3,128,256]{2,1,0:T(8,128)(2,1)S(1)} %slice.121), channel_id=1, source_target_pairs={{0,2},{1,3},{2,0},{3,1},{4,6},{5,7},{6,4},{7,5},{8,10},{9,11},{10,... | collective-permute-start | bytes 589832 | tf_op jit(solution)/shard_map/ppermute | solution.py:327
  23.9 3.8 %collective-permute-start.14 = (bf16[3,128,256]{2,1,0:T(8,128)(2,1)S(1)}, bf16[3,128,256]{2,1,0:T(8,128)(2,1)S(1)}, u32[]{:S(2)}, u32[]{:S(2)}) collective-permute-start(bf16[3,128,256]{2,1,0:T(8,128)(2,1)S(1)} %pad_maximum_fusion.2.refs_5_), channel_id=1, source_target_pairs={{0,1},{1,0},{2,3},{3,2},{4,5},{5,4},{6,7},{7,6},{8,9},{9,8},{10,11... | collective-permute-start | bytes 589832 | tf_op jit(solution)/shard_map/ppermute | solution.py:327
  23.9 7.8 %collective-permute-start.10 = (bf16[3,128,256]{2,1,0:T(8,128)(2,1)S(1)}, bf16[3,128,256]{2,1,0:T(8,128)(2,1)S(1)}, u32[]{:S(2)}, u32[]{:S(2)}) collective-permute-start(bf16[3,128,256]{2,1,0:T(8,128)(2,1)S(1)} %pad_maximum_fusion.2.refs_5_), channel_id=1, source_target_pairs={{0,4},{4,0},{8,12},{12,8},{16,20},{20,16},{24,28},{28,24},{1,5},{5... | collective-permute-start | bytes 589832 | tf_op jit(solution)/shard_map/ppermute | solution.py:327
  25.6 8.4 %collective-permute-start.9 = (bf16[4,128,256]{2,1,0:T(8,128)(2,1)S(1)}, bf16[4,128,256]{2,1,0:T(8,128)(2,1)S(1)}, u32[]{:S(2)}, u32[]{:S(2)}) collective-permute-start(bf16[4,128,256]{2,1,0:T(8,128)(2,1)S(1)} %pad_maximum_fusion), channel_id=1, source_target_pairs={{0,2},{1,3},{2,0},{3,1},{4,6},{5,7},{6,4},{7,5},{8,10},{9,11},{10,... | collective-permute-start | bytes 786440 | tf_op jit(solution)/shard_map/ppermute | solution.py:327
  27.1 8.4 %collective-permute-start.11 = (bf16[3,128,256]{2,1,0:T(8,128)(2,1)S(1)}, bf16[3,128,256]{2,1,0:T(8,128)(2,1)S(1)}, u32[]{:S(2)}, u32[]{:S(2)}) collective-permute-start(bf16[3,128,256]{2,1,0:T(8,128)(2,1)S(1)} %collective-permute-done.8.refs_7_), channel_id=1, source_target_pairs={{0,4},{4,0},{8,12},{12,8},{16,20},{20,16},{24,28},{28,24},{1,5},{5... | collective-permute-start | bytes 589832 | tf_op jit(solution)/shard_map/ppermute | solution.py:327
  27.6 11.1 %collective-permute-start.13 = (bf16[3,144,256]{2,1,0:T(8,128)(2,1)S(1)}, bf16[3,144,256]{2,1,0:T(8,128)(2,1)S(1)}, u32[]{:S(2)}, u32[]{:S(2)}) collective-permute-start(bf16[3,144,256]{2,1,0:T(8,128)(2,1)S(1)} %pad_maximum_fusion.1.refs_4_), channel_id=1, source_target_pairs={{0,1},{1,0},{2,3},{3,2},{4,5},{5,4},{6,7},{7,6},{8,9},{9,8},{10,11... | collective-permute-start | bytes 663560 | tf_op jit(solution)/shard_map/ppermute | solution.py:327
  27.7 10.5 %collective-permute-start.16 = (bf16[3,128,256]{2,1,0:T(8,128)(2,1)S(1)}, bf16[3,128,256]{2,1,0:T(8,128)(2,1)S(1)}, u32[]{:S(2)}, u32[]{:S(2)}) collective-permute-start(bf16[3,128,256]{2,1,0:T(8,128)(2,1)S(1)} %collective-permute-done.8.refs_7_), channel_id=1, source_target_pairs={{0,1},{1,0},{2,3},{3,2},{4,5},{5,4},{6,7},{7,6},{8,9},{9,8},{10,11... | collective-permute-start | bytes 589832 | tf_op jit(solution)/shard_map/ppermute | solution.py:327
  31.7 7.1 %collective-permute-start.17 = (bf16[3,144,256]{2,1,0:T(8,128)(2,1)S(1)}, bf16[3,144,256]{2,1,0:T(8,128)(2,1)S(1)}, u32[]{:S(2)}, u32[]{:S(2)}) collective-permute-start(bf16[3,144,256]{2,1,0:T(8,128)(2,1)S(1)} %collective-permute-done.4.refs_8_), channel_id=1, source_target_pairs={{0,1},{1,0},{2,3},{3,2},{4,5},{5,4},{6,7},{7,6},{8,9},{9,8},{10,11... | collective-permute-start | bytes 663560 | tf_op jit(solution)/shard_map/ppermute | solution.py:327
  34.0 6.1 %collective-permute-start.12 = (bf16[3,128,256]{2,1,0:T(8,128)(2,1)S(1)}, bf16[3,128,256]{2,1,0:T(8,128)(2,1)S(1)}, u32[]{:S(2)}, u32[]{:S(2)}) collective-permute-start(bf16[3,128,256]{2,1,0:T(8,128)(2,1)S(1)} %collective-permute-done.10.refs_10_), channel_id=1, source_target_pairs={{0,2},{1,3},{2,0},{3,1},{4,6},{5,7},{6,4},{7,5},{8,10},{9,11},{10,... | collective-permute-start | bytes 589832 | tf_op jit(solution)/shard_map/ppermute | solution.py:327
  35.5 5.0 %collective-permute-start.18 = (bf16[4,128,256]{2,1,0:T(8,128)(2,1)S(1)}, bf16[4,128,256]{2,1,0:T(8,128)(2,1)S(1)}, u32[]{:S(2)}, u32[]{:S(2)}) collective-permute-start(bf16[4,128,256]{2,1,0:T(8,128)(2,1)S(1)} %collective-permute-done.9.refs_9_), channel_id=1, source_target_pairs={{0,1},{1,0},{2,3},{3,2},{4,5},{5,4},{6,7},{7,6},{8,9},{9,8},{10,11... | collective-permute-start | bytes 786440 | tf_op jit(solution)/shard_map/ppermute | solution.py:327
  62.5 7.0 %collective-permute-start.22 = (bf16[4,4,112,256]{3,2,1,0:T(8,128)(2,1)S(1)}, bf16[4,4,112,256]{3,2,1,0:T(8,128)(2,1)S(1)}, u32[]{:S(2)}, u32[]{:S(2)}) collective-permute-start(bf16[4,4,112,256]{3,2,1,0:T(8,128)(2,1)S(1)} %get-tuple-element.54), channel_id=1, source_target_pairs={{0,1},{1,0},{2,3},{3,2},{4,5},{5,4},{6,7},{7,6},{8,9},{9,8},{10,11... | collective-permute-start | bytes 2752520 | tf_op jit(solution)/shard_map/ppermute | solution.py:327
  62.9 4.4 %collective-permute-start.26 = (bf16[4,2,16,1024]{3,2,1,0:T(8,128)(2,1)S(1)}, bf16[4,2,16,1024]{3,2,1,0:T(8,128)(2,1)S(1)}, u32[]{:S(2)}, u32[]{:S(2)}) collective-permute-start(bf16[4,2,16,1024]{3,2,1,0:T(8,128)(2,1)S(1)} %get-tuple-element.61), channel_id=1, source_target_pairs={{0,1},{1,0},{2,3},{3,2},{4,5},{5,4},{6,7},{7,6},{8,9},{9,8},{10,11... | collective-permute-start | bytes 786440 | tf_op jit(solution)/shard_map/ppermute | solution.py:327
  65.0 12.6 %collective-permute-start.24 = (bf16[2,4,112,256]{3,2,1,0:T(8,128)(2,1)S(1)}, bf16[2,4,112,256]{3,2,1,0:T(8,128)(2,1)S(1)}, u32[]{:S(2)}, u32[]{:S(2)}) collective-permute-start(bf16[2,4,112,256]{3,2,1,0:T(8,128)(2,1)S(1)} %get-tuple-element.58), channel_id=1, source_target_pairs={{0,2},{1,3},{2,0},{3,1},{4,6},{5,7},{6,4},{7,5},{8,10},{9,11},{10,... | collective-permute-start | bytes 1376264 | tf_op jit(solution)/shard_map/ppermute | solution.py:327
  66.6 12.3 %collective-permute-start.25 = (bf16[2,4,112,256]{3,2,1,0:T(8,128)(2,1)S(1)}, bf16[2,4,112,256]{3,2,1,0:T(8,128)(2,1)S(1)}, u32[]{:S(2)}, u32[]{:S(2)}) collective-permute-start(bf16[2,4,112,256]{3,2,1,0:T(8,128)(2,1)S(1)} %get-tuple-element.59), channel_id=1, source_target_pairs={{0,4},{4,0},{8,12},{12,8},{16,20},{20,16},{24,28},{28,24},{1,5},{5... | collective-permute-start | bytes 1376264 | tf_op jit(solution)/shard_map/ppermute | solution.py:327
  67.3 11.7 %collective-permute-start.29 = (bf16[2,16,1024]{2,1,0:T(8,128)(2,1)S(1)}, bf16[2,16,1024]{2,1,0:T(8,128)(2,1)S(1)}, u32[]{:S(2)}, u32[]{:S(2)}) collective-permute-start(bf16[2,16,1024]{2,1,0:T(8,128)(2,1)S(1)} %get-tuple-element.76), channel_id=1, source_target_pairs={{0,24},{4,28},{8,16},{12,20},{16,8},{20,12},{24,0},{28,4},{1,25},{... | collective-permute-start | bytes 196616 | tf_op jit(solution)/shard_map/ppermute | solution.py:327
  69.5 9.6 %collective-permute-start.28 = (bf16[2,16,1024]{2,1,0:T(8,128)(2,1)S(1)}, bf16[2,16,1024]{2,1,0:T(8,128)(2,1)S(1)}, u32[]{:S(2)}, u32[]{:S(2)}) collective-permute-start(bf16[2,16,1024]{2,1,0:T(8,128)(2,1)S(1)} %get-tuple-element.77), channel_id=1, source_target_pairs={{0,16},{4,20},{8,24},{12,28},{16,0},{20,4},{24,8},{28,12},{1,17},{... | collective-permute-start | bytes 196616 | tf_op jit(solution)/shard_map/ppermute | solution.py:327
  69.5 9.6 %collective-permute-start.27 = (bf16[2,16,1024]{2,1,0:T(8,128)(2,1)S(1)}, bf16[2,16,1024]{2,1,0:T(8,128)(2,1)S(1)}, u32[]{:S(2)}, u32[]{:S(2)}) collective-permute-start(bf16[2,16,1024]{2,1,0:T(8,128)(2,1)S(1)} %get-tuple-element.78), channel_id=1, source_target_pairs={{0,8},{4,12},{8,0},{12,4},{16,24},{20,28},{24,16},{28,20},{1,9},{5... | collective-permute-start | bytes 196616 | tf_op jit(solution)/shard_map/ppermute | solution.py:327
  79.1 4.4 %collective-permute-start.35 = (bf16[16,1024]{1,0:T(8,128)(2,1)S(1)}, bf16[16,1024]{1,0:T(8,128)(2,1)S(1)}, u32[]{:S(2)}, u32[]{:S(2)}) collective-permute-start(bf16[16,1024]{1,0:T(8,128)(2,1)S(1)} %slice_bitcast_fusion.4), channel_id=1, source_target_pairs={{0,4},{4,0},{8,12},{12,8},{16,20},{20,16},{24,28},{28,24},{1,5},{5... | collective-permute-start | bytes 98312 | tf_op jit(solution)/shard_map/ppermute | solution.py:327
  80.0 6.8 %collective-permute-start.30 = (bf16[4,112,256]{2,1,0:T(8,128)(2,1)S(1)}, bf16[4,112,256]{2,1,0:T(8,128)(2,1)S(1)}, u32[]{:S(2)}, u32[]{:S(2)}) collective-permute-start(bf16[4,112,256]{2,1,0:T(8,128)(2,1)S(1)} %get-tuple-element.62), channel_id=1, source_target_pairs={{0,4},{4,0},{8,12},{12,8},{16,20},{20,16},{24,28},{28,24},{1,5},{5... | collective-permute-start | bytes 688136 | tf_op jit(solution)/shard_map/ppermute | solution.py:327
  81.2 6.1 %collective-permute-start.31 = (bf16[4,112,256]{2,1,0:T(8,128)(2,1)S(1)}, bf16[4,112,256]{2,1,0:T(8,128)(2,1)S(1)}, u32[]{:S(2)}, u32[]{:S(2)}) collective-permute-start(bf16[4,112,256]{2,1,0:T(8,128)(2,1)S(1)} %get-tuple-element.63), channel_id=1, source_target_pairs={{0,2},{1,3},{2,0},{3,1},{4,6},{5,7},{6,4},{7,5},{8,10},{9,11},{10,... | collective-permute-start | bytes 688136 | tf_op jit(solution)/shard_map/ppermute | solution.py:327
  83.5 8.5 %collective-permute-start.36 = (bf16[16,512]{1,0:T(8,128)(2,1)S(1)}, bf16[16,512]{1,0:T(8,128)(2,1)S(1)}, u32[]{:S(2)}, u32[]{:S(2)}) collective-permute-start(bf16[16,512]{1,0:T(8,128)(2,1)S(1)} %pad_maximum_fusion.4), channel_id=1, source_target_pairs={{0,2},{1,3},{2,0},{3,1},{4,6},{5,7},{6,4},{7,5},{8,10},{9,11},{10,... | collective-permute-start | bytes 49160 | tf_op jit(solution)/shard_map/ppermute | solution.py:327
  87.6 7.4 %collective-permute-start.32 = (bf16[112,512]{1,0:T(8,128)(2,1)S(1)}, bf16[112,512]{1,0:T(8,128)(2,1)S(1)}, u32[]{:S(2)}, u32[]{:S(2)}) collective-permute-start(bf16[112,512]{1,0:T(8,128)(2,1)S(1)} %get-tuple-element.73), channel_id=1, source_target_pairs={{0,24},{4,28},{8,16},{12,20},{16,8},{20,12},{24,0},{28,4},{1,25},{... | collective-permute-start | bytes 344072 | tf_op jit(solution)/shard_map/ppermute | solution.py:327
  89.7 8.8 %collective-permute-start.33 = (bf16[112,512]{1,0:T(8,128)(2,1)S(1)}, bf16[112,512]{1,0:T(8,128)(2,1)S(1)}, u32[]{:S(2)}, u32[]{:S(2)}) collective-permute-start(bf16[112,512]{1,0:T(8,128)(2,1)S(1)} %get-tuple-element.74), channel_id=1, source_target_pairs={{0,16},{4,20},{8,24},{12,28},{16,0},{20,4},{24,8},{28,12},{1,17},{... | collective-permute-start | bytes 344072 | tf_op jit(solution)/shard_map/ppermute | solution.py:327
  89.8 8.7 %collective-permute-start.34 = (bf16[112,512]{1,0:T(8,128)(2,1)S(1)}, bf16[112,512]{1,0:T(8,128)(2,1)S(1)}, u32[]{:S(2)}, u32[]{:S(2)}) collective-permute-start(bf16[112,512]{1,0:T(8,128)(2,1)S(1)} %get-tuple-element.75), channel_id=1, source_target_pairs={{0,8},{4,12},{8,0},{12,4},{16,24},{20,28},{24,16},{28,20},{1,9},{5... | collective-permute-start | bytes 344072 | tf_op jit(solution)/shard_map/ppermute | solution.py:327
  (8 other events, 112.9 us)

commit v11 on v10

--- a/solution.py
+++ b/solution.py
@@ -9,7 +9,7 @@
 
 CAP = 12
 SLOTS = 16
-RING = 6
+RING = 10
 
 
 def contract(lhs, rhs, lhs_dim, rhs_dim):
@@ -174,6 +174,10 @@
     def down_copy(e):
         return pltpu.make_async_copy(w_down_hbm.at[e], w_down.at[e], down_sems.at[e])
 
+    def start_down(e, carry):
+        down_copy(e).start()
+        return carry
+
     tables = [
         pltpu.make_async_copy(picks_hbm, picks, table_sems.at[0]),
         pltpu.make_async_copy(weights_hbm, weights, table_sems.at[1]),
@@ -228,12 +232,15 @@
         for e, (gate_val, up_val) in zip(experts, both):
             hidden[e] = (gate_val / (1.0 + jnp.exp(-gate_val)) * up_val).astype(jnp.bfloat16)
         for e in experts:
-            down_copy(e).start()
 
             @pl.when(e + RING < exp_dev)
             def _():
                 for copy in in_copies(e + RING):
                     copy.start()
+
+        @pl.when(pair == max((exp_dev - RING) // 2 - 1, 0))
+        def _():
+            lax.fori_loop(0, exp_dev, start_down, 0)
 
         return carry
 
@@ -313,7 +320,7 @@
             pltpu.SemaphoreType.DMA((2, RING)),
             pltpu.SemaphoreType.DMA((exp_dev,)),
         ],
-        compiler_params=pltpu.CompilerParams(vmem_limit_bytes=42 * 1024 * 1024),
+        compiler_params=pltpu.CompilerParams(vmem_limit_bytes=48 * 1024 * 1024),
         cost_estimate=pl.CostEstimate(
             flops=6 * n_seq * SLOTS * exp_dev * hid_dev * model_width,
             bytes_accessed=6 * exp_dev * hid_dev * model_width + 4 * n_seq * own.size,

time: 99.5 us -> 101 us (1.015)
  Pallas kernels: 25.9 us -> 27 us
    pallas_call x1, Pallas kernels: 20.7 us -> 21.8 us  [moe_partial(): pl.pallas_call(functools.partial(moe_kernel, n_pieces), out_shape=outs, i...]
where the time goes in v11:
time: 101 us
  starting transfers between devices  36.7 us (36%)
  waiting for transfers between devices  34.3 us (34%)
  Pallas kernels  27 us (27%)
  other arithmetic  1.61 us (2%)
    ppermute x37, starting transfers between devices, swap(): return lax.ppermute(value, axis, [(i, i ^ distance) for i in range(size)])  36.7 us
    ppermute x37, waiting for transfers between devices, swap(): return lax.ppermute(value, axis, [(i, i ^ distance) for i in range(size)])  34.3 us
    pallas_call x1, Pallas kernels, moe_partial(): pl.pallas_call(functools.partial(moe_kernel, n_pieces), out_shape=outs, i...  21.8 us
    pallas_call x1, Pallas kernels, route(): pl.pallas_call(functools.partial(route_kernel, exp_dev), out_shape=[jax.S...  2.72 us
    pallas_call x1, Pallas kernels, norm_and_base(): pl.pallas_call(norm_kernel, out_shape=[jax.ShapeDtypeStruct((tok_rows, mo...  2.46 us
  transfers between devices with their start and end apart: 37, of which 16 were waited for; matrix products, arithmetic and copies ran while one was open for 2% of the time, Pallas kernels for 3%

profile of v11, /device:TPU:0, one launch (start us, length us, event | category | flops | bytes accessed | tf_op | source)
XLA Modules:
  0.0 100.6 jit_solution(4789280995722723939)
XLA Ops:
  0.0 2.5 %shard_map.82 = (bf16[128,2048]{1,0:T(8,128)(2,1)}, bf16[144,256]{1,0:T(8,128)(2,1)}, bf16[128,256]{1,0:T(8,128)(2,1)}, bf16[144,768]{1,0:T(8,128)(2,1)}, f32[1,...) custom-call(bf16[128,2048]{1,0:T(8,128)(2,1)} %tokens_ref.1, f32[1,2048]{1,0:T(1,128)} %bitcast.63, ...), custom_call_target="tpu_custom_call" | custom-call | tf_op jit(solution)/shard_map/pallas_call | solution.py:74
  2.5 5.1 %collective-permute-start.2 = (bf16[144,256]{1,0:T(8,128)(2,1)}, bf16[144,256]{1,0:T(8,128)(2,1)S(1)}, u32[]{:S(2)}, u32[]{:S(2)}) collective-permute-start(bf16[144,256]{1,0:T(8,128)(2,1)} %get-tuple-element.38), channel_id=1, source_target_pairs={{0,24},{4,28},{8,16},{12,20},{16,8},{20,12},{24,0},{28,4},{1,25},{... | collective-permute-start | bytes 221192 | tf_op jit(solution)/shard_map/ppermute | solution.py:334
  8.2 1.7 %collective-permute-start.3 = (bf16[1,144,768]{2,1,0:T(8,128)(2,1)}, bf16[1,144,768]{2,1,0:T(8,128)(2,1)S(1)}, u32[]{:S(2)}, u32[]{:S(2)}) collective-permute-start(bf16[1,144,768]{2,1,0:T(8,128)(2,1)} %bitcast.67), channel_id=1, source_target_pairs={{0,4},{4,0},{8,12},{12,8},{16,20},{20,16},{24,28},{28,24},{1,5},{5... | collective-permute-start | bytes 663560 | tf_op jit(solution)/shard_map/ppermute | solution.py:334
  10.5 3.4 %collective-permute-done.1 = bf16[144,256]{1,0:T(8,128)(2,1)S(1)} collective-permute-done((bf16[144,256]{1,0:T(8,128)(2,1)}, bf16[144,256]{1,0:T(8,128)(2,1)S(1)}, u32[]{:S(2)}, u32[]{:S(2)}) %collective-permute-start.1) | collective-permute-done | bytes 73760 | tf_op jit(solution)/shard_map/ppermute | solution.py:334
  14.0 1.0 collective-permute-done.3.refs_6_
  15.0 3.5 %collective-permute-start.7 = (bf16[128,256]{1,0:T(8,128)(2,1)}, bf16[128,256]{1,0:T(8,128)(2,1)S(1)}, u32[]{:S(2)}, u32[]{:S(2)}) collective-permute-start(bf16[128,256]{1,0:T(8,128)(2,1)} %get-tuple-element.49), channel_id=1, source_target_pairs={{0,24},{4,28},{8,16},{12,20},{16,8},{20,12},{24,0},{28,4},{1,25},{... | collective-permute-start | bytes 196616 | tf_op jit(solution)/shard_map/ppermute | solution.py:334
  18.5 0.9 collective-permute-start.5
  19.4 1.6 %collective-permute-start.4 = (bf16[3,144,256]{2,1,0:T(8,128)(2,1)S(1)}, bf16[3,144,256]{2,1,0:T(8,128)(2,1)S(1)}, u32[]{:S(2)}, u32[]{:S(2)}) collective-permute-start(bf16[3,144,256]{2,1,0:T(8,128)(2,1)S(1)} %pad_maximum_fusion.1.refs_4_), channel_id=1, source_target_pairs={{0,4},{4,0},{8,12},{12,8},{16,20},{20,16},{24,28},{28,24},{1,5},{5... | collective-permute-start | bytes 663560 | tf_op jit(solution)/shard_map/ppermute | solution.py:334
  21.0 1.5 %collective-permute-start.8 = (bf16[3,128,256]{2,1,0:T(8,128)(2,1)S(1)}, bf16[3,128,256]{2,1,0:T(8,128)(2,1)S(1)}, u32[]{:S(2)}, u32[]{:S(2)}) collective-permute-start(bf16[3,128,256]{2,1,0:T(8,128)(2,1)S(1)} %slice.121), channel_id=1, source_target_pairs={{0,2},{1,3},{2,0},{3,1},{4,6},{5,7},{6,4},{7,5},{8,10},{9,11},{10,... | collective-permute-start | bytes 589832 | tf_op jit(solution)/shard_map/ppermute | solution.py:334
  22.5 1.3 %collective-permute-done.6 = bf16[128,256]{1,0:T(8,128)(2,1)S(1)} collective-permute-done((bf16[128,256]{1,0:T(8,128)(2,1)}, bf16[128,256]{1,0:T(8,128)(2,1)S(1)}, u32[]{:S(2)}, u32[]{:S(2)}) %collective-permute-start.6) | collective-permute-done | bytes 65568 | tf_op jit(solution)/shard_map/ppermute | solution.py:334
  23.9 1.6 %collective-permute-start.10 = (bf16[3,128,256]{2,1,0:T(8,128)(2,1)S(1)}, bf16[3,128,256]{2,1,0:T(8,128)(2,1)S(1)}, u32[]{:S(2)}, u32[]{:S(2)}) collective-permute-start(bf16[3,128,256]{2,1,0:T(8,128)(2,1)S(1)} %pad_maximum_fusion.2.refs_5_), channel_id=1, source_target_pairs={{0,4},{4,0},{8,12},{12,8},{16,20},{20,16},{24,28},{28,24},{1,5},{5... | collective-permute-start | bytes 589832 | tf_op jit(solution)/shard_map/ppermute | solution.py:334
  25.6 1.6 %collective-permute-start.9 = (bf16[4,128,256]{2,1,0:T(8,128)(2,1)S(1)}, bf16[4,128,256]{2,1,0:T(8,128)(2,1)S(1)}, u32[]{:S(2)}, u32[]{:S(2)}) collective-permute-start(bf16[4,128,256]{2,1,0:T(8,128)(2,1)S(1)} %pad_maximum_fusion), channel_id=1, source_target_pairs={{0,2},{1,3},{2,0},{3,1},{4,6},{5,7},{6,4},{7,5},{8,10},{9,11},{10,... | collective-permute-start | bytes 786440 | tf_op jit(solution)/shard_map/ppermute | solution.py:334
  28.3 3.4 %collective-permute-done.10.refs_10_ = bf16[3,128,256]{2,1,0:T(8,128)(2,1)S(1)} collective-permute-done((bf16[3,128,256]{2,1,0:T(8,128)(2,1)S(1)}, bf16[3,128,256]{2,1,0:T(8,128)(2,1)S(1)}, u32[]{:S(2)}, u32[]{:S(2)}) %collective-permute-start.10) | collective-permute-done | bytes 196640 | tf_op jit(solution)/shard_map/ppermute | solution.py:334
  31.7 2.3 %collective-permute-done.9.refs_9_ = bf16[4,128,256]{2,1,0:T(8,128)(2,1)S(1)} collective-permute-done((bf16[4,128,256]{2,1,0:T(8,128)(2,1)S(1)}, bf16[4,128,256]{2,1,0:T(8,128)(2,1)S(1)}, u32[]{:S(2)}, u32[]{:S(2)}) %collective-permute-start.9) | collective-permute-done | bytes 262176 | tf_op jit(solution)/shard_map/ppermute | solution.py:334
  34.0 1.5 %collective-permute-start.12 = (bf16[3,128,256]{2,1,0:T(8,128)(2,1)S(1)}, bf16[3,128,256]{2,1,0:T(8,128)(2,1)S(1)}, u32[]{:S(2)}, u32[]{:S(2)}) collective-permute-start(bf16[3,128,256]{2,1,0:T(8,128)(2,1)S(1)} %collective-permute-done.10.refs_10_), channel_id=1, source_target_pairs={{0,2},{1,3},{2,0},{3,1},{4,6},{5,7},{6,4},{7,5},{8,10},{9,11},{10,... | collective-permute-start | bytes 589832 | tf_op jit(solution)/shard_map/ppermute | solution.py:334
  35.5 2.7 %shard_map.83 = (bf16[8,256,128]{2,1,0:T(8,128)(2,1)}, bf16[8,128,256]{2,1,0:T(8,128)(2,1)}) custom-call(bf16[8,16,128]{2,1,0:T(8,128)(2,1)} %copy-done.2), custom_call_target="tpu_custom_call" | custom-call | flops 4000000000 | bytes 2097152 | tf_op jit(solution)/shard_map/pallas_call | solution.py:132
  39.3 0.9 collective-permute-done.12.refs_12_
  40.5 1.1 %collective-permute-done.21.refs_21_ = bf16[3,128,256]{2,1,0:T(8,128)(2,1)S(1)} collective-permute-done((bf16[3,128,256]{2,1,0:T(8,128)(2,1)S(1)}, bf16[3,128,256]{2,1,0:T(8,128)(2,1)S(1)}, u32[]{:S(2)}, u32[]{:S(2)}) %collective-permute-start.21) | collective-permute-done | bytes 196640 | tf_op jit(solution)/shard_map/ppermute | solution.py:334
  41.6 21.8 %shard_map.84 = (bf16[4,4,112,256]{3,2,1,0:T(8,128)(2,1)S(1)}, bf16[4,4,112,256]{3,2,1,0:T(8,128)(2,1)S(1)}, bf16[4,2,16,1024]{3,2,1,0:T(8,128)(2,1)S(1)}, bf16[...) custom-call(bf16[8,256,128]{2,1,0:T(8,128)(2,1)} %get-tuple-element.45.refs_0_, ...), custom_call_target="tpu_custom_call" | custom-call | flops 4831838208 | bytes 46137344 | tf_op jit(solution)/shard_map/pallas_call | solution.py:304
  64.2 2.0 %collective-permute-done.23 = bf16[4,4,112,256]{3,2,1,0:T(8,128)(2,1)S(1)} collective-permute-done((bf16[4,4,112,256]{3,2,1,0:T(8,128)(2,1)}, bf16[4,4,112,256]{3,2,1,0:T(8,128)(2,1)S(1)}, u32[]{:S(2)}, u32[]{:S(2)}) %collective-permute-start.23) | collective-permute-done | bytes 917536 | tf_op jit(solution)/shard_map/ppermute | solution.py:334
  66.4 1.6 %collective-permute-start.24 = (bf16[2,4,112,256]{3,2,1,0:T(8,128)(2,1)S(1)}, bf16[2,4,112,256]{3,2,1,0:T(8,128)(2,1)S(1)}, u32[]{:S(2)}, u32[]{:S(2)}) collective-permute-start(bf16[2,4,112,256]{3,2,1,0:T(8,128)(2,1)S(1)} %get-tuple-element.58), channel_id=1, source_target_pairs={{0,2},{1,3},{2,0},{3,1},{4,6},{5,7},{6,4},{7,5},{8,10},{9,11},{10,... | collective-permute-start | bytes 1376264 | tf_op jit(solution)/shard_map/ppermute | solution.py:334
  68.7 2.1 %collective-permute-start.29 = (bf16[2,16,1024]{2,1,0:T(8,128)(2,1)S(1)}, bf16[2,16,1024]{2,1,0:T(8,128)(2,1)S(1)}, u32[]{:S(2)}, u32[]{:S(2)}) collective-permute-start(bf16[2,16,1024]{2,1,0:T(8,128)(2,1)S(1)} %get-tuple-element.76), channel_id=1, source_target_pairs={{0,24},{4,28},{8,16},{12,20},{16,8},{20,12},{24,0},{28,4},{1,25},{... | collective-permute-start | bytes 196616 | tf_op jit(solution)/shard_map/ppermute | solution.py:334
  70.9 2.3 %collective-permute-start.27 = (bf16[2,16,1024]{2,1,0:T(8,128)(2,1)S(1)}, bf16[2,16,1024]{2,1,0:T(8,128)(2,1)S(1)}, u32[]{:S(2)}, u32[]{:S(2)}) collective-permute-start(bf16[2,16,1024]{2,1,0:T(8,128)(2,1)S(1)} %get-tuple-element.78), channel_id=1, source_target_pairs={{0,8},{4,12},{8,0},{12,4},{16,24},{20,28},{24,16},{28,20},{1,9},{5... | collective-permute-start | bytes 196616 | tf_op jit(solution)/shard_map/ppermute | solution.py:334
  73.2 5.9 %collective-permute-done.24 = bf16[2,4,112,256]{3,2,1,0:T(8,128)(2,1)S(1)} collective-permute-done((bf16[2,4,112,256]{3,2,1,0:T(8,128)(2,1)S(1)}, bf16[2,4,112,256]{3,2,1,0:T(8,128)(2,1)S(1)}, u32[]{:S(2)}, u32[]{:S(2)}) %collective-permute-start.24) | collective-permute-done | bytes 458784 | tf_op jit(solution)/shard_map/ppermute | solution.py:334
  79.1 1.2 %collective-permute-done.25 = bf16[2,4,112,256]{3,2,1,0:T(8,128)(2,1)S(1)} collective-permute-done((bf16[2,4,112,256]{3,2,1,0:T(8,128)(2,1)S(1)}, bf16[2,4,112,256]{3,2,1,0:T(8,128)(2,1)S(1)}, u32[]{:S(2)}, u32[]{:S(2)}) %collective-permute-start.25) | collective-permute-done | bytes 458784 | tf_op jit(solution)/shard_map/ppermute | solution.py:334
  81.4 1.2 %collective-permute-start.30 = (bf16[4,112,256]{2,1,0:T(8,128)(2,1)S(1)}, bf16[4,112,256]{2,1,0:T(8,128)(2,1)S(1)}, u32[]{:S(2)}, u32[]{:S(2)}) collective-permute-start(bf16[4,112,256]{2,1,0:T(8,128)(2,1)S(1)} %get-tuple-element.62), channel_id=1, source_target_pairs={{0,4},{4,0},{8,12},{12,8},{16,20},{20,16},{24,28},{28,24},{1,5},{5... | collective-permute-start | bytes 688136 | tf_op jit(solution)/shard_map/ppermute | solution.py:334
  83.2 1.7 %collective-permute-done.35 = bf16[16,1024]{1,0:T(8,128)(2,1)S(1)} collective-permute-done((bf16[16,1024]{1,0:T(8,128)(2,1)S(1)}, bf16[16,1024]{1,0:T(8,128)(2,1)S(1)}, u32[]{:S(2)}, u32[]{:S(2)}) %collective-permute-start.35) | collective-permute-done | bytes 32800 | tf_op jit(solution)/shard_map/ppermute | solution.py:334
  85.5 2.6 %collective-permute-done.30 = bf16[4,112,256]{2,1,0:T(8,128)(2,1)S(1)} collective-permute-done((bf16[4,112,256]{2,1,0:T(8,128)(2,1)S(1)}, bf16[4,112,256]{2,1,0:T(8,128)(2,1)S(1)}, u32[]{:S(2)}, u32[]{:S(2)}) %collective-permute-start.30) | collective-permute-done | bytes 229408 | tf_op jit(solution)/shard_map/ppermute | solution.py:334
  89.0 2.1 %collective-permute-start.32 = (bf16[112,512]{1,0:T(8,128)(2,1)S(1)}, bf16[112,512]{1,0:T(8,128)(2,1)S(1)}, u32[]{:S(2)}, u32[]{:S(2)}) collective-permute-start(bf16[112,512]{1,0:T(8,128)(2,1)S(1)} %get-tuple-element.73), channel_id=1, source_target_pairs={{0,24},{4,28},{8,16},{12,20},{16,8},{20,12},{24,0},{28,4},{1,25},{... | collective-permute-start | bytes 344072 | tf_op jit(solution)/shard_map/ppermute | solution.py:334
  91.2 2.3 %collective-permute-start.34 = (bf16[112,512]{1,0:T(8,128)(2,1)S(1)}, bf16[112,512]{1,0:T(8,128)(2,1)S(1)}, u32[]{:S(2)}, u32[]{:S(2)}) collective-permute-start(bf16[112,512]{1,0:T(8,128)(2,1)S(1)} %get-tuple-element.75), channel_id=1, source_target_pairs={{0,8},{4,12},{8,0},{12,4},{16,24},{20,28},{24,16},{28,20},{1,9},{5... | collective-permute-start | bytes 344072 | tf_op jit(solution)/shard_map/ppermute | solution.py:334
  93.5 2.8 %collective-permute-done.32 = bf16[112,512]{1,0:T(8,128)(2,1)S(1)} collective-permute-done((bf16[112,512]{1,0:T(8,128)(2,1)S(1)}, bf16[112,512]{1,0:T(8,128)(2,1)S(1)}, u32[]{:S(2)}, u32[]{:S(2)}) %collective-permute-start.32) | collective-permute-done | bytes 114720 | tf_op jit(solution)/shard_map/ppermute | solution.py:334
  96.3 3.5 %collective-permute-done.33 = bf16[112,512]{1,0:T(8,128)(2,1)S(1)} collective-permute-done((bf16[112,512]{1,0:T(8,128)(2,1)S(1)}, bf16[112,512]{1,0:T(8,128)(2,1)S(1)}, u32[]{:S(2)}, u32[]{:S(2)}) %collective-permute-start.33) | collective-permute-done | bytes 114720 | tf_op jit(solution)/shard_map/ppermute | solution.py:334
  (78 shorter events, 9.6 us)
Async XLA Ops:
  2.5 8.1 %collective-permute-start.2 = (bf16[144,256]{1,0:T(8,128)(2,1)}, bf16[144,256]{1,0:T(8,128)(2,1)S(1)}, u32[]{:S(2)}, u32[]{:S(2)}) collective-permute-start(bf16[144,256]{1,0:T(8,128)(2,1)} %get-tuple-element.38), channel_id=1, source_target_pairs={{0,24},{4,28},{8,16},{12,20},{16,8},{20,12},{24,0},{28,4},{1,25},{... | collective-permute-start | bytes 221192 | tf_op jit(solution)/shard_map/ppermute | solution.py:334
  7.5 6.4 %collective-permute-start.1 = (bf16[144,256]{1,0:T(8,128)(2,1)}, bf16[144,256]{1,0:T(8,128)(2,1)S(1)}, u32[]{:S(2)}, u32[]{:S(2)}) collective-permute-start(bf16[144,256]{1,0:T(8,128)(2,1)} %get-tuple-element.38), channel_id=1, source_target_pairs={{0,16},{4,20},{8,24},{12,28},{16,0},{20,4},{24,8},{28,12},{1,17},{... | collective-permute-start | bytes 221192 | tf_op jit(solution)/shard_map/ppermute | solution.py:334
  7.5 6.4 %collective-permute-start = (bf16[144,256]{1,0:T(8,128)(2,1)}, bf16[144,256]{1,0:T(8,128)(2,1)S(1)}, u32[]{:S(2)}, u32[]{:S(2)}) collective-permute-start(bf16[144,256]{1,0:T(8,128)(2,1)} %get-tuple-element.38), channel_id=1, source_target_pairs={{0,8},{4,12},{8,0},{12,4},{16,24},{20,28},{24,16},{28,20},{1,9},{5... | collective-permute-start | bytes 221192 | tf_op jit(solution)/shard_map/ppermute | solution.py:334
  8.2 6.8 %collective-permute-start.3 = (bf16[1,144,768]{2,1,0:T(8,128)(2,1)}, bf16[1,144,768]{2,1,0:T(8,128)(2,1)S(1)}, u32[]{:S(2)}, u32[]{:S(2)}) collective-permute-start(bf16[1,144,768]{2,1,0:T(8,128)(2,1)} %bitcast.67), channel_id=1, source_target_pairs={{0,4},{4,0},{8,12},{12,8},{16,20},{20,16},{24,28},{28,24},{1,5},{5... | collective-permute-start | bytes 663560 | tf_op jit(solution)/shard_map/ppermute | solution.py:334
  15.0 7.5 %collective-permute-start.7 = (bf16[128,256]{1,0:T(8,128)(2,1)}, bf16[128,256]{1,0:T(8,128)(2,1)S(1)}, u32[]{:S(2)}, u32[]{:S(2)}) collective-permute-start(bf16[128,256]{1,0:T(8,128)(2,1)} %get-tuple-element.49), channel_id=1, source_target_pairs={{0,24},{4,28},{8,16},{12,20},{16,8},{20,12},{24,0},{28,4},{1,25},{... | collective-permute-start | bytes 196616 | tf_op jit(solution)/shard_map/ppermute | solution.py:334
  18.5 5.4 %collective-permute-start.6 = (bf16[128,256]{1,0:T(8,128)(2,1)}, bf16[128,256]{1,0:T(8,128)(2,1)S(1)}, u32[]{:S(2)}, u32[]{:S(2)}) collective-permute-start(bf16[128,256]{1,0:T(8,128)(2,1)} %get-tuple-element.49), channel_id=1, source_target_pairs={{0,16},{4,20},{8,24},{12,28},{16,0},{20,4},{24,8},{28,12},{1,17},{... | collective-permute-start | bytes 196616 | tf_op jit(solution)/shard_map/ppermute | solution.py:334
  18.5 5.4 %collective-permute-start.5 = (bf16[128,256]{1,0:T(8,128)(2,1)}, bf16[128,256]{1,0:T(8,128)(2,1)S(1)}, u32[]{:S(2)}, u32[]{:S(2)}) collective-permute-start(bf16[128,256]{1,0:T(8,128)(2,1)} %get-tuple-element.49), channel_id=1, source_target_pairs={{0,8},{4,12},{8,0},{12,4},{16,24},{20,28},{24,16},{28,20},{1,9},{5... | collective-permute-start | bytes 196616 | tf_op jit(solution)/shard_map/ppermute | solution.py:334
  19.4 8.2 %collective-permute-start.4 = (bf16[3,144,256]{2,1,0:T(8,128)(2,1)S(1)}, bf16[3,144,256]{2,1,0:T(8,128)(2,1)S(1)}, u32[]{:S(2)}, u32[]{:S(2)}) collective-permute-start(bf16[3,144,256]{2,1,0:T(8,128)(2,1)S(1)} %pad_maximum_fusion.1.refs_4_), channel_id=1, source_target_pairs={{0,4},{4,0},{8,12},{12,8},{16,20},{20,16},{24,28},{28,24},{1,5},{5... | collective-permute-start | bytes 663560 | tf_op jit(solution)/shard_map/ppermute | solution.py:334
  21.0 6.1 %collective-permute-start.8 = (bf16[3,128,256]{2,1,0:T(8,128)(2,1)S(1)}, bf16[3,128,256]{2,1,0:T(8,128)(2,1)S(1)}, u32[]{:S(2)}, u32[]{:S(2)}) collective-permute-start(bf16[3,128,256]{2,1,0:T(8,128)(2,1)S(1)} %slice.121), channel_id=1, source_target_pairs={{0,2},{1,3},{2,0},{3,1},{4,6},{5,7},{6,4},{7,5},{8,10},{9,11},{10,... | collective-permute-start | bytes 589832 | tf_op jit(solution)/shard_map/ppermute | solution.py:334
  23.9 3.8 %collective-permute-start.14 = (bf16[3,128,256]{2,1,0:T(8,128)(2,1)S(1)}, bf16[3,128,256]{2,1,0:T(8,128)(2,1)S(1)}, u32[]{:S(2)}, u32[]{:S(2)}) collective-permute-start(bf16[3,128,256]{2,1,0:T(8,128)(2,1)S(1)} %pad_maximum_fusion.2.refs_5_), channel_id=1, source_target_pairs={{0,1},{1,0},{2,3},{3,2},{4,5},{5,4},{6,7},{7,6},{8,9},{9,8},{10,11... | collective-permute-start | bytes 589832 | tf_op jit(solution)/shard_map/ppermute | solution.py:334
  23.9 7.8 %collective-permute-start.10 = (bf16[3,128,256]{2,1,0:T(8,128)(2,1)S(1)}, bf16[3,128,256]{2,1,0:T(8,128)(2,1)S(1)}, u32[]{:S(2)}, u32[]{:S(2)}) collective-permute-start(bf16[3,128,256]{2,1,0:T(8,128)(2,1)S(1)} %pad_maximum_fusion.2.refs_5_), channel_id=1, source_target_pairs={{0,4},{4,0},{8,12},{12,8},{16,20},{20,16},{24,28},{28,24},{1,5},{5... | collective-permute-start | bytes 589832 | tf_op jit(solution)/shard_map/ppermute | solution.py:334
  25.6 8.4 %collective-permute-start.9 = (bf16[4,128,256]{2,1,0:T(8,128)(2,1)S(1)}, bf16[4,128,256]{2,1,0:T(8,128)(2,1)S(1)}, u32[]{:S(2)}, u32[]{:S(2)}) collective-permute-start(bf16[4,128,256]{2,1,0:T(8,128)(2,1)S(1)} %pad_maximum_fusion), channel_id=1, source_target_pairs={{0,2},{1,3},{2,0},{3,1},{4,6},{5,7},{6,4},{7,5},{8,10},{9,11},{10,... | collective-permute-start | bytes 786440 | tf_op jit(solution)/shard_map/ppermute | solution.py:334
  27.1 8.4 %collective-permute-start.11 = (bf16[3,128,256]{2,1,0:T(8,128)(2,1)S(1)}, bf16[3,128,256]{2,1,0:T(8,128)(2,1)S(1)}, u32[]{:S(2)}, u32[]{:S(2)}) collective-permute-start(bf16[3,128,256]{2,1,0:T(8,128)(2,1)S(1)} %collective-permute-done.8.refs_7_), channel_id=1, source_target_pairs={{0,4},{4,0},{8,12},{12,8},{16,20},{20,16},{24,28},{28,24},{1,5},{5... | collective-permute-start | bytes 589832 | tf_op jit(solution)/shard_map/ppermute | solution.py:334
  27.6 11.1 %collective-permute-start.13 = (bf16[3,144,256]{2,1,0:T(8,128)(2,1)S(1)}, bf16[3,144,256]{2,1,0:T(8,128)(2,1)S(1)}, u32[]{:S(2)}, u32[]{:S(2)}) collective-permute-start(bf16[3,144,256]{2,1,0:T(8,128)(2,1)S(1)} %pad_maximum_fusion.1.refs_4_), channel_id=1, source_target_pairs={{0,1},{1,0},{2,3},{3,2},{4,5},{5,4},{6,7},{7,6},{8,9},{9,8},{10,11... | collective-permute-start | bytes 663560 | tf_op jit(solution)/shard_map/ppermute | solution.py:334
  27.7 10.5 %collective-permute-start.16 = (bf16[3,128,256]{2,1,0:T(8,128)(2,1)S(1)}, bf16[3,128,256]{2,1,0:T(8,128)(2,1)S(1)}, u32[]{:S(2)}, u32[]{:S(2)}) collective-permute-start(bf16[3,128,256]{2,1,0:T(8,128)(2,1)S(1)} %collective-permute-done.8.refs_7_), channel_id=1, source_target_pairs={{0,1},{1,0},{2,3},{3,2},{4,5},{5,4},{6,7},{7,6},{8,9},{9,8},{10,11... | collective-permute-start | bytes 589832 | tf_op jit(solution)/shard_map/ppermute | solution.py:334
  31.7 7.1 %collective-permute-start.17 = (bf16[3,144,256]{2,1,0:T(8,128)(2,1)S(1)}, bf16[3,144,256]{2,1,0:T(8,128)(2,1)S(1)}, u32[]{:S(2)}, u32[]{:S(2)}) collective-permute-start(bf16[3,144,256]{2,1,0:T(8,128)(2,1)S(1)} %collective-permute-done.4.refs_8_), channel_id=1, source_target_pairs={{0,1},{1,0},{2,3},{3,2},{4,5},{5,4},{6,7},{7,6},{8,9},{9,8},{10,11... | collective-permute-start | bytes 663560 | tf_op jit(solution)/shard_map/ppermute | solution.py:334
  34.0 6.1 %collective-permute-start.12 = (bf16[3,128,256]{2,1,0:T(8,128)(2,1)S(1)}, bf16[3,128,256]{2,1,0:T(8,128)(2,1)S(1)}, u32[]{:S(2)}, u32[]{:S(2)}) collective-permute-start(bf16[3,128,256]{2,1,0:T(8,128)(2,1)S(1)} %collective-permute-done.10.refs_10_), channel_id=1, source_target_pairs={{0,2},{1,3},{2,0},{3,1},{4,6},{5,7},{6,4},{7,5},{8,10},{9,11},{10,... | collective-permute-start | bytes 589832 | tf_op jit(solution)/shard_map/ppermute | solution.py:334
  35.5 5.0 %collective-permute-start.18 = (bf16[4,128,256]{2,1,0:T(8,128)(2,1)S(1)}, bf16[4,128,256]{2,1,0:T(8,128)(2,1)S(1)}, u32[]{:S(2)}, u32[]{:S(2)}) collective-permute-start(bf16[4,128,256]{2,1,0:T(8,128)(2,1)S(1)} %collective-permute-done.9.refs_9_), channel_id=1, source_target_pairs={{0,1},{1,0},{2,3},{3,2},{4,5},{5,4},{6,7},{7,6},{8,9},{9,8},{10,11... | collective-permute-start | bytes 786440 | tf_op jit(solution)/shard_map/ppermute | solution.py:334
  63.7 7.2 %collective-permute-start.22 = (bf16[4,4,112,256]{3,2,1,0:T(8,128)(2,1)}, bf16[4,4,112,256]{3,2,1,0:T(8,128)(2,1)S(1)}, u32[]{:S(2)}, u32[]{:S(2)}) collective-permute-start(bf16[4,4,112,256]{3,2,1,0:T(8,128)(2,1)} %get-tuple-element.54), channel_id=1, source_target_pairs={{0,1},{1,0},{2,3},{3,2},{4,5},{5,4},{6,7},{7,6},{8,9},{9,8},{10,11... | collective-permute-start | bytes 2752520 | tf_op jit(solution)/shard_map/ppermute | solution.py:334
  64.0 4.6 %collective-permute-start.26 = (bf16[4,2,16,1024]{3,2,1,0:T(8,128)(2,1)S(1)}, bf16[4,2,16,1024]{3,2,1,0:T(8,128)(2,1)S(1)}, u32[]{:S(2)}, u32[]{:S(2)}) collective-permute-start(bf16[4,2,16,1024]{3,2,1,0:T(8,128)(2,1)S(1)} %get-tuple-element.61), channel_id=1, source_target_pairs={{0,1},{1,0},{2,3},{3,2},{4,5},{5,4},{6,7},{7,6},{8,9},{9,8},{10,11... | collective-permute-start | bytes 786440 | tf_op jit(solution)/shard_map/ppermute | solution.py:334
  66.4 12.6 %collective-permute-start.24 = (bf16[2,4,112,256]{3,2,1,0:T(8,128)(2,1)S(1)}, bf16[2,4,112,256]{3,2,1,0:T(8,128)(2,1)S(1)}, u32[]{:S(2)}, u32[]{:S(2)}) collective-permute-start(bf16[2,4,112,256]{3,2,1,0:T(8,128)(2,1)S(1)} %get-tuple-element.58), channel_id=1, source_target_pairs={{0,2},{1,3},{2,0},{3,1},{4,6},{5,7},{6,4},{7,5},{8,10},{9,11},{10,... | collective-permute-start | bytes 1376264 | tf_op jit(solution)/shard_map/ppermute | solution.py:334
  68.0 12.3 %collective-permute-start.25 = (bf16[2,4,112,256]{3,2,1,0:T(8,128)(2,1)S(1)}, bf16[2,4,112,256]{3,2,1,0:T(8,128)(2,1)S(1)}, u32[]{:S(2)}, u32[]{:S(2)}) collective-permute-start(bf16[2,4,112,256]{3,2,1,0:T(8,128)(2,1)S(1)} %get-tuple-element.59), channel_id=1, source_target_pairs={{0,4},{4,0},{8,12},{12,8},{16,20},{20,16},{24,28},{28,24},{1,5},{5... | collective-permute-start | bytes 1376264 | tf_op jit(solution)/shard_map/ppermute | solution.py:334
  68.7 11.7 %collective-permute-start.29 = (bf16[2,16,1024]{2,1,0:T(8,128)(2,1)S(1)}, bf16[2,16,1024]{2,1,0:T(8,128)(2,1)S(1)}, u32[]{:S(2)}, u32[]{:S(2)}) collective-permute-start(bf16[2,16,1024]{2,1,0:T(8,128)(2,1)S(1)} %get-tuple-element.76), channel_id=1, source_target_pairs={{0,24},{4,28},{8,16},{12,20},{16,8},{20,12},{24,0},{28,4},{1,25},{... | collective-permute-start | bytes 196616 | tf_op jit(solution)/shard_map/ppermute | solution.py:334
  70.8 9.6 %collective-permute-start.28 = (bf16[2,16,1024]{2,1,0:T(8,128)(2,1)S(1)}, bf16[2,16,1024]{2,1,0:T(8,128)(2,1)S(1)}, u32[]{:S(2)}, u32[]{:S(2)}) collective-permute-start(bf16[2,16,1024]{2,1,0:T(8,128)(2,1)S(1)} %get-tuple-element.77), channel_id=1, source_target_pairs={{0,16},{4,20},{8,24},{12,28},{16,0},{20,4},{24,8},{28,12},{1,17},{... | collective-permute-start | bytes 196616 | tf_op jit(solution)/shard_map/ppermute | solution.py:334
  70.9 9.6 %collective-permute-start.27 = (bf16[2,16,1024]{2,1,0:T(8,128)(2,1)S(1)}, bf16[2,16,1024]{2,1,0:T(8,128)(2,1)S(1)}, u32[]{:S(2)}, u32[]{:S(2)}) collective-permute-start(bf16[2,16,1024]{2,1,0:T(8,128)(2,1)S(1)} %get-tuple-element.78), channel_id=1, source_target_pairs={{0,8},{4,12},{8,0},{12,4},{16,24},{20,28},{24,16},{28,20},{1,9},{5... | collective-permute-start | bytes 196616 | tf_op jit(solution)/shard_map/ppermute | solution.py:334
  80.5 4.4 %collective-permute-start.35 = (bf16[16,1024]{1,0:T(8,128)(2,1)S(1)}, bf16[16,1024]{1,0:T(8,128)(2,1)S(1)}, u32[]{:S(2)}, u32[]{:S(2)}) collective-permute-start(bf16[16,1024]{1,0:T(8,128)(2,1)S(1)} %slice_bitcast_fusion.4), channel_id=1, source_target_pairs={{0,4},{4,0},{8,12},{12,8},{16,20},{20,16},{24,28},{28,24},{1,5},{5... | collective-permute-start | bytes 98312 | tf_op jit(solution)/shard_map/ppermute | solution.py:334
  81.4 6.8 %collective-permute-start.30 = (bf16[4,112,256]{2,1,0:T(8,128)(2,1)S(1)}, bf16[4,112,256]{2,1,0:T(8,128)(2,1)S(1)}, u32[]{:S(2)}, u32[]{:S(2)}) collective-permute-start(bf16[4,112,256]{2,1,0:T(8,128)(2,1)S(1)} %get-tuple-element.62), channel_id=1, source_target_pairs={{0,4},{4,0},{8,12},{12,8},{16,20},{20,16},{24,28},{28,24},{1,5},{5... | collective-permute-start | bytes 688136 | tf_op jit(solution)/shard_map/ppermute | solution.py:334
  82.6 6.1 %collective-permute-start.31 = (bf16[4,112,256]{2,1,0:T(8,128)(2,1)S(1)}, bf16[4,112,256]{2,1,0:T(8,128)(2,1)S(1)}, u32[]{:S(2)}, u32[]{:S(2)}) collective-permute-start(bf16[4,112,256]{2,1,0:T(8,128)(2,1)S(1)} %get-tuple-element.63), channel_id=1, source_target_pairs={{0,2},{1,3},{2,0},{3,1},{4,6},{5,7},{6,4},{7,5},{8,10},{9,11},{10,... | collective-permute-start | bytes 688136 | tf_op jit(solution)/shard_map/ppermute | solution.py:334
  84.9 8.5 %collective-permute-start.36 = (bf16[16,512]{1,0:T(8,128)(2,1)S(1)}, bf16[16,512]{1,0:T(8,128)(2,1)S(1)}, u32[]{:S(2)}, u32[]{:S(2)}) collective-permute-start(bf16[16,512]{1,0:T(8,128)(2,1)S(1)} %pad_maximum_fusion.4), channel_id=1, source_target_pairs={{0,2},{1,3},{2,0},{3,1},{4,6},{5,7},{6,4},{7,5},{8,10},{9,11},{10,... | collective-permute-start | bytes 49160 | tf_op jit(solution)/shard_map/ppermute | solution.py:334
  89.0 7.3 %collective-permute-start.32 = (bf16[112,512]{1,0:T(8,128)(2,1)S(1)}, bf16[112,512]{1,0:T(8,128)(2,1)S(1)}, u32[]{:S(2)}, u32[]{:S(2)}) collective-permute-start(bf16[112,512]{1,0:T(8,128)(2,1)S(1)} %get-tuple-element.73), channel_id=1, source_target_pairs={{0,24},{4,28},{8,16},{12,20},{16,8},{20,12},{24,0},{28,4},{1,25},{... | collective-permute-start | bytes 344072 | tf_op jit(solution)/shard_map/ppermute | solution.py:334
  91.1 8.7 %collective-permute-start.33 = (bf16[112,512]{1,0:T(8,128)(2,1)S(1)}, bf16[112,512]{1,0:T(8,128)(2,1)S(1)}, u32[]{:S(2)}, u32[]{:S(2)}) collective-permute-start(bf16[112,512]{1,0:T(8,128)(2,1)S(1)} %get-tuple-element.74), channel_id=1, source_target_pairs={{0,16},{4,20},{8,24},{12,28},{16,0},{20,4},{24,8},{28,12},{1,17},{... | collective-permute-start | bytes 344072 | tf_op jit(solution)/shard_map/ppermute | solution.py:334
  91.2 8.7 %collective-permute-start.34 = (bf16[112,512]{1,0:T(8,128)(2,1)S(1)}, bf16[112,512]{1,0:T(8,128)(2,1)S(1)}, u32[]{:S(2)}, u32[]{:S(2)}) collective-permute-start(bf16[112,512]{1,0:T(8,128)(2,1)S(1)} %get-tuple-element.75), channel_id=1, source_target_pairs={{0,8},{4,12},{8,0},{12,4},{16,24},{20,28},{24,16},{28,20},{1,9},{5... | collective-permute-start | bytes 344072 | tf_op jit(solution)/shard_map/ppermute | solution.py:334
  (8 other events, 114.4 us)

commit v12 on v10

--- a/solution.py
+++ b/solution.py
@@ -9,7 +9,7 @@
 
 CAP = 12
 SLOTS = 16
-RING = 6
+RING = 8
 
 
 def contract(lhs, rhs, lhs_dim, rhs_dim):
@@ -196,6 +196,8 @@
     for e in range(min(RING, exp_dev)):
         for copy in in_copies(e):
             copy.start()
+    for e in range(exp_dev // 2):
+        down_copy(e).start()
     tables[1].start()
     quarters = [slice(2 * q * width, 2 * (q + 1) * width) for q in range(4)]
     tables[0].wait()
@@ -227,8 +229,8 @@
         ]
         for e, (gate_val, up_val) in zip(experts, both):
             hidden[e] = (gate_val / (1.0 + jnp.exp(-gate_val)) * up_val).astype(jnp.bfloat16)
+        down_copy(exp_dev // 2 + pair).start()
         for e in experts:
-            down_copy(e).start()
 
             @pl.when(e + RING < exp_dev)
             def _():
@@ -313,7 +315,7 @@
             pltpu.SemaphoreType.DMA((2, RING)),
             pltpu.SemaphoreType.DMA((exp_dev,)),
         ],
-        compiler_params=pltpu.CompilerParams(vmem_limit_bytes=42 * 1024 * 1024),
+        compiler_params=pltpu.CompilerParams(vmem_limit_bytes=45 * 1024 * 1024),
         cost_estimate=pl.CostEstimate(
             flops=6 * n_seq * SLOTS * exp_dev * hid_dev * model_width,
             bytes_accessed=6 * exp_dev * hid_dev * model_width + 4 * n_seq * own.size,

time: 99.5 us -> 99.1 us (level)
  no operation moved by 1% of the time
where the time goes in v12:
time: 99.1 us; the launch traced here: 98.9 us
  starting transfers between devices  36.6 us (37%)
  waiting for transfers between devices  34.1 us (34%)
  Pallas kernels  25.5 us (26%)
  other arithmetic  1.62 us (2%)
    ppermute x37, starting transfers between devices, swap(): return lax.ppermute(value, axis, [(i, i ^ distance) for i in range(size)])  36.6 us
    ppermute x37, waiting for transfers between devices, swap(): return lax.ppermute(value, axis, [(i, i ^ distance) for i in range(size)])  34.1 us
    pallas_call x1, Pallas kernels, moe_partial(): pl.pallas_call(functools.partial(moe_kernel, n_pieces), out_shape=outs, i...  20.3 us
    pallas_call x1, Pallas kernels, route(): pl.pallas_call(functools.partial(route_kernel, exp_dev), out_shape=[jax.S...  2.72 us
    pallas_call x1, Pallas kernels, norm_and_base(): pl.pallas_call(norm_kernel, out_shape=[jax.ShapeDtypeStruct((tok_rows, mo...  2.46 us
  transfers between devices with their start and end apart: 37, of which 16 were waited for; matrix products, arithmetic and copies ran while one was open for 2% of the time, Pallas kernels for 3%

profile of v12, /device:TPU:0, one launch (start us, length us, event | category | flops | bytes accessed | tf_op | source)
XLA Modules:
  0.0 98.9 jit_solution(15185201201998038952)
XLA Ops:
  0.0 2.5 %shard_map.82 = (bf16[128,2048]{1,0:T(8,128)(2,1)}, bf16[144,256]{1,0:T(8,128)(2,1)}, bf16[128,256]{1,0:T(8,128)(2,1)}, bf16[144,768]{1,0:T(8,128)(2,1)}, f32[1,...) custom-call(bf16[128,2048]{1,0:T(8,128)(2,1)} %tokens_ref.1, f32[1,2048]{1,0:T(1,128)} %bitcast.63, ...), custom_call_target="tpu_custom_call" | custom-call | tf_op jit(solution)/shard_map/pallas_call | solution.py:74
  2.5 5.1 %collective-permute-start.2 = (bf16[144,256]{1,0:T(8,128)(2,1)}, bf16[144,256]{1,0:T(8,128)(2,1)S(1)}, u32[]{:S(2)}, u32[]{:S(2)}) collective-permute-start(bf16[144,256]{1,0:T(8,128)(2,1)} %get-tuple-element.38), channel_id=1, source_target_pairs={{0,24},{4,28},{8,16},{12,20},{16,8},{20,12},{24,0},{28,4},{1,25},{... | collective-permute-start | bytes 221192 | tf_op jit(solution)/shard_map/ppermute | solution.py:329
  8.2 1.7 %collective-permute-start.3 = (bf16[1,144,768]{2,1,0:T(8,128)(2,1)}, bf16[1,144,768]{2,1,0:T(8,128)(2,1)S(1)}, u32[]{:S(2)}, u32[]{:S(2)}) collective-permute-start(bf16[1,144,768]{2,1,0:T(8,128)(2,1)} %bitcast.67), channel_id=1, source_target_pairs={{0,4},{4,0},{8,12},{12,8},{16,20},{20,16},{24,28},{28,24},{1,5},{5... | collective-permute-start | bytes 663560 | tf_op jit(solution)/shard_map/ppermute | solution.py:329
  10.5 3.4 %collective-permute-done.1 = bf16[144,256]{1,0:T(8,128)(2,1)S(1)} collective-permute-done((bf16[144,256]{1,0:T(8,128)(2,1)}, bf16[144,256]{1,0:T(8,128)(2,1)S(1)}, u32[]{:S(2)}, u32[]{:S(2)}) %collective-permute-start.1) | collective-permute-done | bytes 73760 | tf_op jit(solution)/shard_map/ppermute | solution.py:329
  14.0 1.0 %collective-permute-done.3.refs_6_ = bf16[1,144,768]{2,1,0:T(8,128)(2,1)S(1)} collective-permute-done((bf16[1,144,768]{2,1,0:T(8,128)(2,1)}, bf16[1,144,768]{2,1,0:T(8,128)(2,1)S(1)}, u32[]{:S(2)}, u32[]{:S(2)}) %collective-permute-start.3) | collective-permute-done | bytes 221216 | tf_op jit(solution)/shard_map/ppermute | solution.py:329
  15.0 3.5 %collective-permute-start.7 = (bf16[128,256]{1,0:T(8,128)(2,1)}, bf16[128,256]{1,0:T(8,128)(2,1)S(1)}, u32[]{:S(2)}, u32[]{:S(2)}) collective-permute-start(bf16[128,256]{1,0:T(8,128)(2,1)} %get-tuple-element.49), channel_id=1, source_target_pairs={{0,24},{4,28},{8,16},{12,20},{16,8},{20,12},{24,0},{28,4},{1,25},{... | collective-permute-start | bytes 196616 | tf_op jit(solution)/shard_map/ppermute | solution.py:329
  18.5 0.9 collective-permute-start.5
  19.4 1.6 %collective-permute-start.4 = (bf16[3,144,256]{2,1,0:T(8,128)(2,1)S(1)}, bf16[3,144,256]{2,1,0:T(8,128)(2,1)S(1)}, u32[]{:S(2)}, u32[]{:S(2)}) collective-permute-start(bf16[3,144,256]{2,1,0:T(8,128)(2,1)S(1)} %pad_maximum_fusion.1.refs_4_), channel_id=1, source_target_pairs={{0,4},{4,0},{8,12},{12,8},{16,20},{20,16},{24,28},{28,24},{1,5},{5... | collective-permute-start | bytes 663560 | tf_op jit(solution)/shard_map/ppermute | solution.py:329
  21.0 1.5 %collective-permute-start.8 = (bf16[3,128,256]{2,1,0:T(8,128)(2,1)S(1)}, bf16[3,128,256]{2,1,0:T(8,128)(2,1)S(1)}, u32[]{:S(2)}, u32[]{:S(2)}) collective-permute-start(bf16[3,128,256]{2,1,0:T(8,128)(2,1)S(1)} %slice.121), channel_id=1, source_target_pairs={{0,2},{1,3},{2,0},{3,1},{4,6},{5,7},{6,4},{7,5},{8,10},{9,11},{10,... | collective-permute-start | bytes 589832 | tf_op jit(solution)/shard_map/ppermute | solution.py:329
  22.5 1.3 %collective-permute-done.6 = bf16[128,256]{1,0:T(8,128)(2,1)S(1)} collective-permute-done((bf16[128,256]{1,0:T(8,128)(2,1)}, bf16[128,256]{1,0:T(8,128)(2,1)S(1)}, u32[]{:S(2)}, u32[]{:S(2)}) %collective-permute-start.6) | collective-permute-done | bytes 65568 | tf_op jit(solution)/shard_map/ppermute | solution.py:329
  23.9 1.6 %collective-permute-start.10 = (bf16[3,128,256]{2,1,0:T(8,128)(2,1)S(1)}, bf16[3,128,256]{2,1,0:T(8,128)(2,1)S(1)}, u32[]{:S(2)}, u32[]{:S(2)}) collective-permute-start(bf16[3,128,256]{2,1,0:T(8,128)(2,1)S(1)} %pad_maximum_fusion.2.refs_5_), channel_id=1, source_target_pairs={{0,4},{4,0},{8,12},{12,8},{16,20},{20,16},{24,28},{28,24},{1,5},{5... | collective-permute-start | bytes 589832 | tf_op jit(solution)/shard_map/ppermute | solution.py:329
  25.6 1.6 %collective-permute-start.9 = (bf16[4,128,256]{2,1,0:T(8,128)(2,1)S(1)}, bf16[4,128,256]{2,1,0:T(8,128)(2,1)S(1)}, u32[]{:S(2)}, u32[]{:S(2)}) collective-permute-start(bf16[4,128,256]{2,1,0:T(8,128)(2,1)S(1)} %pad_maximum_fusion), channel_id=1, source_target_pairs={{0,2},{1,3},{2,0},{3,1},{4,6},{5,7},{6,4},{7,5},{8,10},{9,11},{10,... | collective-permute-start | bytes 786440 | tf_op jit(solution)/shard_map/ppermute | solution.py:329
  28.3 3.4 %collective-permute-done.10.refs_10_ = bf16[3,128,256]{2,1,0:T(8,128)(2,1)S(1)} collective-permute-done((bf16[3,128,256]{2,1,0:T(8,128)(2,1)S(1)}, bf16[3,128,256]{2,1,0:T(8,128)(2,1)S(1)}, u32[]{:S(2)}, u32[]{:S(2)}) %collective-permute-start.10) | collective-permute-done | bytes 196640 | tf_op jit(solution)/shard_map/ppermute | solution.py:329
  31.7 2.3 %collective-permute-done.9.refs_9_ = bf16[4,128,256]{2,1,0:T(8,128)(2,1)S(1)} collective-permute-done((bf16[4,128,256]{2,1,0:T(8,128)(2,1)S(1)}, bf16[4,128,256]{2,1,0:T(8,128)(2,1)S(1)}, u32[]{:S(2)}, u32[]{:S(2)}) %collective-permute-start.9) | collective-permute-done | bytes 262176 | tf_op jit(solution)/shard_map/ppermute | solution.py:329
  34.0 1.5 %collective-permute-start.12 = (bf16[3,128,256]{2,1,0:T(8,128)(2,1)S(1)}, bf16[3,128,256]{2,1,0:T(8,128)(2,1)S(1)}, u32[]{:S(2)}, u32[]{:S(2)}) collective-permute-start(bf16[3,128,256]{2,1,0:T(8,128)(2,1)S(1)} %collective-permute-done.10.refs_10_), channel_id=1, source_target_pairs={{0,2},{1,3},{2,0},{3,1},{4,6},{5,7},{6,4},{7,5},{8,10},{9,11},{10,... | collective-permute-start | bytes 589832 | tf_op jit(solution)/shard_map/ppermute | solution.py:329
  35.5 2.7 %shard_map.83 = (bf16[8,256,128]{2,1,0:T(8,128)(2,1)}, bf16[8,128,256]{2,1,0:T(8,128)(2,1)}) custom-call(bf16[8,16,128]{2,1,0:T(8,128)(2,1)} %copy-done.2), custom_call_target="tpu_custom_call" | custom-call | flops 4000000000 | bytes 2097152 | tf_op jit(solution)/shard_map/pallas_call | solution.py:132
  39.3 0.9 collective-permute-done.12.refs_12_
  40.5 1.1 %collective-permute-done.21.refs_21_ = bf16[3,128,256]{2,1,0:T(8,128)(2,1)S(1)} collective-permute-done((bf16[3,128,256]{2,1,0:T(8,128)(2,1)S(1)}, bf16[3,128,256]{2,1,0:T(8,128)(2,1)S(1)}, u32[]{:S(2)}, u32[]{:S(2)}) %collective-permute-start.21) | collective-permute-done | bytes 196640 | tf_op jit(solution)/shard_map/ppermute | solution.py:329
  41.6 20.3 %shard_map.84 = (bf16[4,4,112,256]{3,2,1,0:T(8,128)(2,1)S(1)}, bf16[4,4,112,256]{3,2,1,0:T(8,128)(2,1)S(1)}, bf16[4,2,16,1024]{3,2,1,0:T(8,128)(2,1)S(1)}, bf16[...) custom-call(bf16[8,256,128]{2,1,0:T(8,128)(2,1)} %get-tuple-element.45.re, ...), custom_call_target="tpu_custom_call" | custom-call | flops 4831838208 | bytes 46137344 | tf_op jit(solution)/shard_map/pallas_call | solution.py:299
  62.6 1.8 %collective-permute-done.23 = bf16[4,4,112,256]{3,2,1,0:T(8,128)(2,1)S(1)} collective-permute-done((bf16[4,4,112,256]{3,2,1,0:T(8,128)(2,1)S(1)}, bf16[4,4,112,256]{3,2,1,0:T(8,128)(2,1)S(1)}, u32[]{:S(2)}, u32[]{:S(2)}) %collective-permute-start.23) | collective-permute-done | bytes 917536 | tf_op jit(solution)/shard_map/ppermute | solution.py:329
  64.7 1.6 %collective-permute-start.24 = (bf16[2,4,112,256]{3,2,1,0:T(8,128)(2,1)S(1)}, bf16[2,4,112,256]{3,2,1,0:T(8,128)(2,1)S(1)}, u32[]{:S(2)}, u32[]{:S(2)}) collective-permute-start(bf16[2,4,112,256]{3,2,1,0:T(8,128)(2,1)S(1)} %get-tuple-element.58), channel_id=1, source_target_pairs={{0,2},{1,3},{2,0},{3,1},{4,6},{5,7},{6,4},{7,5},{8,10},{9,11},{10,... | collective-permute-start | bytes 1376264 | tf_op jit(solution)/shard_map/ppermute | solution.py:329
  67.0 2.1 %collective-permute-start.29 = (bf16[2,16,1024]{2,1,0:T(8,128)(2,1)S(1)}, bf16[2,16,1024]{2,1,0:T(8,128)(2,1)S(1)}, u32[]{:S(2)}, u32[]{:S(2)}) collective-permute-start(bf16[2,16,1024]{2,1,0:T(8,128)(2,1)S(1)} %get-tuple-element.76), channel_id=1, source_target_pairs={{0,24},{4,28},{8,16},{12,20},{16,8},{20,12},{24,0},{28,4},{1,25},{... | collective-permute-start | bytes 196616 | tf_op jit(solution)/shard_map/ppermute | solution.py:329
  69.1 2.3 %collective-permute-start.27 = (bf16[2,16,1024]{2,1,0:T(8,128)(2,1)S(1)}, bf16[2,16,1024]{2,1,0:T(8,128)(2,1)S(1)}, u32[]{:S(2)}, u32[]{:S(2)}) collective-permute-start(bf16[2,16,1024]{2,1,0:T(8,128)(2,1)S(1)} %get-tuple-element.78), channel_id=1, source_target_pairs={{0,8},{4,12},{8,0},{12,4},{16,24},{20,28},{24,16},{28,20},{1,9},{5... | collective-permute-start | bytes 196616 | tf_op jit(solution)/shard_map/ppermute | solution.py:329
  71.4 5.9 %collective-permute-done.24 = bf16[2,4,112,256]{3,2,1,0:T(8,128)(2,1)S(1)} collective-permute-done((bf16[2,4,112,256]{3,2,1,0:T(8,128)(2,1)S(1)}, bf16[2,4,112,256]{3,2,1,0:T(8,128)(2,1)S(1)}, u32[]{:S(2)}, u32[]{:S(2)}) %collective-permute-start.24) | collective-permute-done | bytes 458784 | tf_op jit(solution)/shard_map/ppermute | solution.py:329
  77.3 1.2 %collective-permute-done.25 = bf16[2,4,112,256]{3,2,1,0:T(8,128)(2,1)S(1)} collective-permute-done((bf16[2,4,112,256]{3,2,1,0:T(8,128)(2,1)S(1)}, bf16[2,4,112,256]{3,2,1,0:T(8,128)(2,1)S(1)}, u32[]{:S(2)}, u32[]{:S(2)}) %collective-permute-start.25) | collective-permute-done | bytes 458784 | tf_op jit(solution)/shard_map/ppermute | solution.py:329
  79.7 1.2 %collective-permute-start.30 = (bf16[4,112,256]{2,1,0:T(8,128)(2,1)S(1)}, bf16[4,112,256]{2,1,0:T(8,128)(2,1)S(1)}, u32[]{:S(2)}, u32[]{:S(2)}) collective-permute-start(bf16[4,112,256]{2,1,0:T(8,128)(2,1)S(1)} %get-tuple-element.62), channel_id=1, source_target_pairs={{0,4},{4,0},{8,12},{12,8},{16,20},{20,16},{24,28},{28,24},{1,5},{5... | collective-permute-start | bytes 688136 | tf_op jit(solution)/shard_map/ppermute | solution.py:329
  81.4 1.7 %collective-permute-done.35 = bf16[16,1024]{1,0:T(8,128)(2,1)S(1)} collective-permute-done((bf16[16,1024]{1,0:T(8,128)(2,1)S(1)}, bf16[16,1024]{1,0:T(8,128)(2,1)S(1)}, u32[]{:S(2)}, u32[]{:S(2)}) %collective-permute-start.35) | collective-permute-done | bytes 32800 | tf_op jit(solution)/shard_map/ppermute | solution.py:329
  83.8 2.7 %collective-permute-done.30 = bf16[4,112,256]{2,1,0:T(8,128)(2,1)S(1)} collective-permute-done((bf16[4,112,256]{2,1,0:T(8,128)(2,1)S(1)}, bf16[4,112,256]{2,1,0:T(8,128)(2,1)S(1)}, u32[]{:S(2)}, u32[]{:S(2)}) %collective-permute-start.30) | collective-permute-done | bytes 229408 | tf_op jit(solution)/shard_map/ppermute | solution.py:329
  87.3 2.1 %collective-permute-start.32 = (bf16[112,512]{1,0:T(8,128)(2,1)S(1)}, bf16[112,512]{1,0:T(8,128)(2,1)S(1)}, u32[]{:S(2)}, u32[]{:S(2)}) collective-permute-start(bf16[112,512]{1,0:T(8,128)(2,1)S(1)} %get-tuple-element.73), channel_id=1, source_target_pairs={{0,24},{4,28},{8,16},{12,20},{16,8},{20,12},{24,0},{28,4},{1,25},{... | collective-permute-start | bytes 344072 | tf_op jit(solution)/shard_map/ppermute | solution.py:329
  89.4 2.3 %collective-permute-start.34 = (bf16[112,512]{1,0:T(8,128)(2,1)S(1)}, bf16[112,512]{1,0:T(8,128)(2,1)S(1)}, u32[]{:S(2)}, u32[]{:S(2)}) collective-permute-start(bf16[112,512]{1,0:T(8,128)(2,1)S(1)} %get-tuple-element.75), channel_id=1, source_target_pairs={{0,8},{4,12},{8,0},{12,4},{16,24},{20,28},{24,16},{28,20},{1,9},{5... | collective-permute-start | bytes 344072 | tf_op jit(solution)/shard_map/ppermute | solution.py:329
  91.7 2.9 %collective-permute-done.32 = bf16[112,512]{1,0:T(8,128)(2,1)S(1)} collective-permute-done((bf16[112,512]{1,0:T(8,128)(2,1)S(1)}, bf16[112,512]{1,0:T(8,128)(2,1)S(1)}, u32[]{:S(2)}, u32[]{:S(2)}) %collective-permute-start.32) | collective-permute-done | bytes 114720 | tf_op jit(solution)/shard_map/ppermute | solution.py:329
  94.6 3.5 %collective-permute-done.33 = bf16[112,512]{1,0:T(8,128)(2,1)S(1)} collective-permute-done((bf16[112,512]{1,0:T(8,128)(2,1)S(1)}, bf16[112,512]{1,0:T(8,128)(2,1)S(1)}, u32[]{:S(2)}, u32[]{:S(2)}) %collective-permute-start.33) | collective-permute-done | bytes 114720 | tf_op jit(solution)/shard_map/ppermute | solution.py:329
  (78 shorter events, 9.6 us)
Async XLA Ops:
  2.5 8.1 %collective-permute-start.2 = (bf16[144,256]{1,0:T(8,128)(2,1)}, bf16[144,256]{1,0:T(8,128)(2,1)S(1)}, u32[]{:S(2)}, u32[]{:S(2)}) collective-permute-start(bf16[144,256]{1,0:T(8,128)(2,1)} %get-tuple-element.38), channel_id=1, source_target_pairs={{0,24},{4,28},{8,16},{12,20},{16,8},{20,12},{24,0},{28,4},{1,25},{... | collective-permute-start | bytes 221192 | tf_op jit(solution)/shard_map/ppermute | solution.py:329
  7.5 6.4 %collective-permute-start.1 = (bf16[144,256]{1,0:T(8,128)(2,1)}, bf16[144,256]{1,0:T(8,128)(2,1)S(1)}, u32[]{:S(2)}, u32[]{:S(2)}) collective-permute-start(bf16[144,256]{1,0:T(8,128)(2,1)} %get-tuple-element.38), channel_id=1, source_target_pairs={{0,16},{4,20},{8,24},{12,28},{16,0},{20,4},{24,8},{28,12},{1,17},{... | collective-permute-start | bytes 221192 | tf_op jit(solution)/shard_map/ppermute | solution.py:329
  7.5 6.4 %collective-permute-start = (bf16[144,256]{1,0:T(8,128)(2,1)}, bf16[144,256]{1,0:T(8,128)(2,1)S(1)}, u32[]{:S(2)}, u32[]{:S(2)}) collective-permute-start(bf16[144,256]{1,0:T(8,128)(2,1)} %get-tuple-element.38), channel_id=1, source_target_pairs={{0,8},{4,12},{8,0},{12,4},{16,24},{20,28},{24,16},{28,20},{1,9},{5... | collective-permute-start | bytes 221192 | tf_op jit(solution)/shard_map/ppermute | solution.py:329
  8.2 6.8 %collective-permute-start.3 = (bf16[1,144,768]{2,1,0:T(8,128)(2,1)}, bf16[1,144,768]{2,1,0:T(8,128)(2,1)S(1)}, u32[]{:S(2)}, u32[]{:S(2)}) collective-permute-start(bf16[1,144,768]{2,1,0:T(8,128)(2,1)} %bitcast.67), channel_id=1, source_target_pairs={{0,4},{4,0},{8,12},{12,8},{16,20},{20,16},{24,28},{28,24},{1,5},{5... | collective-permute-start | bytes 663560 | tf_op jit(solution)/shard_map/ppermute | solution.py:329
  15.0 7.5 %collective-permute-start.7 = (bf16[128,256]{1,0:T(8,128)(2,1)}, bf16[128,256]{1,0:T(8,128)(2,1)S(1)}, u32[]{:S(2)}, u32[]{:S(2)}) collective-permute-start(bf16[128,256]{1,0:T(8,128)(2,1)} %get-tuple-element.49), channel_id=1, source_target_pairs={{0,24},{4,28},{8,16},{12,20},{16,8},{20,12},{24,0},{28,4},{1,25},{... | collective-permute-start | bytes 196616 | tf_op jit(solution)/shard_map/ppermute | solution.py:329
  18.5 5.4 %collective-permute-start.6 = (bf16[128,256]{1,0:T(8,128)(2,1)}, bf16[128,256]{1,0:T(8,128)(2,1)S(1)}, u32[]{:S(2)}, u32[]{:S(2)}) collective-permute-start(bf16[128,256]{1,0:T(8,128)(2,1)} %get-tuple-element.49), channel_id=1, source_target_pairs={{0,16},{4,20},{8,24},{12,28},{16,0},{20,4},{24,8},{28,12},{1,17},{... | collective-permute-start | bytes 196616 | tf_op jit(solution)/shard_map/ppermute | solution.py:329
  18.5 5.4 %collective-permute-start.5 = (bf16[128,256]{1,0:T(8,128)(2,1)}, bf16[128,256]{1,0:T(8,128)(2,1)S(1)}, u32[]{:S(2)}, u32[]{:S(2)}) collective-permute-start(bf16[128,256]{1,0:T(8,128)(2,1)} %get-tuple-element.49), channel_id=1, source_target_pairs={{0,8},{4,12},{8,0},{12,4},{16,24},{20,28},{24,16},{28,20},{1,9},{5... | collective-permute-start | bytes 196616 | tf_op jit(solution)/shard_map/ppermute | solution.py:329
  19.4 8.2 %collective-permute-start.4 = (bf16[3,144,256]{2,1,0:T(8,128)(2,1)S(1)}, bf16[3,144,256]{2,1,0:T(8,128)(2,1)S(1)}, u32[]{:S(2)}, u32[]{:S(2)}) collective-permute-start(bf16[3,144,256]{2,1,0:T(8,128)(2,1)S(1)} %pad_maximum_fusion.1.refs_4_), channel_id=1, source_target_pairs={{0,4},{4,0},{8,12},{12,8},{16,20},{20,16},{24,28},{28,24},{1,5},{5... | collective-permute-start | bytes 663560 | tf_op jit(solution)/shard_map/ppermute | solution.py:329
  21.0 6.1 %collective-permute-start.8 = (bf16[3,128,256]{2,1,0:T(8,128)(2,1)S(1)}, bf16[3,128,256]{2,1,0:T(8,128)(2,1)S(1)}, u32[]{:S(2)}, u32[]{:S(2)}) collective-permute-start(bf16[3,128,256]{2,1,0:T(8,128)(2,1)S(1)} %slice.121), channel_id=1, source_target_pairs={{0,2},{1,3},{2,0},{3,1},{4,6},{5,7},{6,4},{7,5},{8,10},{9,11},{10,... | collective-permute-start | bytes 589832 | tf_op jit(solution)/shard_map/ppermute | solution.py:329
  23.9 3.8 %collective-permute-start.14 = (bf16[3,128,256]{2,1,0:T(8,128)(2,1)S(1)}, bf16[3,128,256]{2,1,0:T(8,128)(2,1)S(1)}, u32[]{:S(2)}, u32[]{:S(2)}) collective-permute-start(bf16[3,128,256]{2,1,0:T(8,128)(2,1)S(1)} %pad_maximum_fusion.2.refs_5_), channel_id=1, source_target_pairs={{0,1},{1,0},{2,3},{3,2},{4,5},{5,4},{6,7},{7,6},{8,9},{9,8},{10,11... | collective-permute-start | bytes 589832 | tf_op jit(solution)/shard_map/ppermute | solution.py:329
  23.9 7.8 %collective-permute-start.10 = (bf16[3,128,256]{2,1,0:T(8,128)(2,1)S(1)}, bf16[3,128,256]{2,1,0:T(8,128)(2,1)S(1)}, u32[]{:S(2)}, u32[]{:S(2)}) collective-permute-start(bf16[3,128,256]{2,1,0:T(8,128)(2,1)S(1)} %pad_maximum_fusion.2.refs_5_), channel_id=1, source_target_pairs={{0,4},{4,0},{8,12},{12,8},{16,20},{20,16},{24,28},{28,24},{1,5},{5... | collective-permute-start | bytes 589832 | tf_op jit(solution)/shard_map/ppermute | solution.py:329
  25.6 8.4 %collective-permute-start.9 = (bf16[4,128,256]{2,1,0:T(8,128)(2,1)S(1)}, bf16[4,128,256]{2,1,0:T(8,128)(2,1)S(1)}, u32[]{:S(2)}, u32[]{:S(2)}) collective-permute-start(bf16[4,128,256]{2,1,0:T(8,128)(2,1)S(1)} %pad_maximum_fusion), channel_id=1, source_target_pairs={{0,2},{1,3},{2,0},{3,1},{4,6},{5,7},{6,4},{7,5},{8,10},{9,11},{10,... | collective-permute-start | bytes 786440 | tf_op jit(solution)/shard_map/ppermute | solution.py:329
  27.1 8.4 %collective-permute-start.11 = (bf16[3,128,256]{2,1,0:T(8,128)(2,1)S(1)}, bf16[3,128,256]{2,1,0:T(8,128)(2,1)S(1)}, u32[]{:S(2)}, u32[]{:S(2)}) collective-permute-start(bf16[3,128,256]{2,1,0:T(8,128)(2,1)S(1)} %collective-permute-done.8.refs_7_), channel_id=1, source_target_pairs={{0,4},{4,0},{8,12},{12,8},{16,20},{20,16},{24,28},{28,24},{1,5},{5... | collective-permute-start | bytes 589832 | tf_op jit(solution)/shard_map/ppermute | solution.py:329
  27.6 11.1 %collective-permute-start.13 = (bf16[3,144,256]{2,1,0:T(8,128)(2,1)S(1)}, bf16[3,144,256]{2,1,0:T(8,128)(2,1)S(1)}, u32[]{:S(2)}, u32[]{:S(2)}) collective-permute-start(bf16[3,144,256]{2,1,0:T(8,128)(2,1)S(1)} %pad_maximum_fusion.1.refs_4_), channel_id=1, source_target_pairs={{0,1},{1,0},{2,3},{3,2},{4,5},{5,4},{6,7},{7,6},{8,9},{9,8},{10,11... | collective-permute-start | bytes 663560 | tf_op jit(solution)/shard_map/ppermute | solution.py:329
  27.7 10.5 %collective-permute-start.16 = (bf16[3,128,256]{2,1,0:T(8,128)(2,1)S(1)}, bf16[3,128,256]{2,1,0:T(8,128)(2,1)S(1)}, u32[]{:S(2)}, u32[]{:S(2)}) collective-permute-start(bf16[3,128,256]{2,1,0:T(8,128)(2,1)S(1)} %collective-permute-done.8.refs_7_), channel_id=1, source_target_pairs={{0,1},{1,0},{2,3},{3,2},{4,5},{5,4},{6,7},{7,6},{8,9},{9,8},{10,11... | collective-permute-start | bytes 589832 | tf_op jit(solution)/shard_map/ppermute | solution.py:329
  31.7 7.1 %collective-permute-start.17 = (bf16[3,144,256]{2,1,0:T(8,128)(2,1)S(1)}, bf16[3,144,256]{2,1,0:T(8,128)(2,1)S(1)}, u32[]{:S(2)}, u32[]{:S(2)}) collective-permute-start(bf16[3,144,256]{2,1,0:T(8,128)(2,1)S(1)} %collective-permute-done.4.refs_8_), channel_id=1, source_target_pairs={{0,1},{1,0},{2,3},{3,2},{4,5},{5,4},{6,7},{7,6},{8,9},{9,8},{10,11... | collective-permute-start | bytes 663560 | tf_op jit(solution)/shard_map/ppermute | solution.py:329
  34.0 6.1 %collective-permute-start.12 = (bf16[3,128,256]{2,1,0:T(8,128)(2,1)S(1)}, bf16[3,128,256]{2,1,0:T(8,128)(2,1)S(1)}, u32[]{:S(2)}, u32[]{:S(2)}) collective-permute-start(bf16[3,128,256]{2,1,0:T(8,128)(2,1)S(1)} %collective-permute-done.10.refs_10_), channel_id=1, source_target_pairs={{0,2},{1,3},{2,0},{3,1},{4,6},{5,7},{6,4},{7,5},{8,10},{9,11},{10,... | collective-permute-start | bytes 589832 | tf_op jit(solution)/shard_map/ppermute | solution.py:329
  35.5 5.0 %collective-permute-start.18 = (bf16[4,128,256]{2,1,0:T(8,128)(2,1)S(1)}, bf16[4,128,256]{2,1,0:T(8,128)(2,1)S(1)}, u32[]{:S(2)}, u32[]{:S(2)}) collective-permute-start(bf16[4,128,256]{2,1,0:T(8,128)(2,1)S(1)} %collective-permute-done.9.refs_9_), channel_id=1, source_target_pairs={{0,1},{1,0},{2,3},{3,2},{4,5},{5,4},{6,7},{7,6},{8,9},{9,8},{10,11... | collective-permute-start | bytes 786440 | tf_op jit(solution)/shard_map/ppermute | solution.py:329
  62.1 7.0 %collective-permute-start.22 = (bf16[4,4,112,256]{3,2,1,0:T(8,128)(2,1)S(1)}, bf16[4,4,112,256]{3,2,1,0:T(8,128)(2,1)S(1)}, u32[]{:S(2)}, u32[]{:S(2)}) collective-permute-start(bf16[4,4,112,256]{3,2,1,0:T(8,128)(2,1)S(1)} %get-tuple-element.54), channel_id=1, source_target_pairs={{0,1},{1,0},{2,3},{3,2},{4,5},{5,4},{6,7},{7,6},{8,9},{9,8},{10,11... | collective-permute-start | bytes 2752520 | tf_op jit(solution)/shard_map/ppermute | solution.py:329
  62.5 4.4 %collective-permute-start.26 = (bf16[4,2,16,1024]{3,2,1,0:T(8,128)(2,1)S(1)}, bf16[4,2,16,1024]{3,2,1,0:T(8,128)(2,1)S(1)}, u32[]{:S(2)}, u32[]{:S(2)}) collective-permute-start(bf16[4,2,16,1024]{3,2,1,0:T(8,128)(2,1)S(1)} %get-tuple-element.61), channel_id=1, source_target_pairs={{0,1},{1,0},{2,3},{3,2},{4,5},{5,4},{6,7},{7,6},{8,9},{9,8},{10,11... | collective-permute-start | bytes 786440 | tf_op jit(solution)/shard_map/ppermute | solution.py:329
  64.7 12.6 %collective-permute-start.24 = (bf16[2,4,112,256]{3,2,1,0:T(8,128)(2,1)S(1)}, bf16[2,4,112,256]{3,2,1,0:T(8,128)(2,1)S(1)}, u32[]{:S(2)}, u32[]{:S(2)}) collective-permute-start(bf16[2,4,112,256]{3,2,1,0:T(8,128)(2,1)S(1)} %get-tuple-element.58), channel_id=1, source_target_pairs={{0,2},{1,3},{2,0},{3,1},{4,6},{5,7},{6,4},{7,5},{8,10},{9,11},{10,... | collective-permute-start | bytes 1376264 | tf_op jit(solution)/shard_map/ppermute | solution.py:329
  66.2 12.3 %collective-permute-start.25 = (bf16[2,4,112,256]{3,2,1,0:T(8,128)(2,1)S(1)}, bf16[2,4,112,256]{3,2,1,0:T(8,128)(2,1)S(1)}, u32[]{:S(2)}, u32[]{:S(2)}) collective-permute-start(bf16[2,4,112,256]{3,2,1,0:T(8,128)(2,1)S(1)} %get-tuple-element.59), channel_id=1, source_target_pairs={{0,4},{4,0},{8,12},{12,8},{16,20},{20,16},{24,28},{28,24},{1,5},{5... | collective-permute-start | bytes 1376264 | tf_op jit(solution)/shard_map/ppermute | solution.py:329
  67.0 11.7 %collective-permute-start.29 = (bf16[2,16,1024]{2,1,0:T(8,128)(2,1)S(1)}, bf16[2,16,1024]{2,1,0:T(8,128)(2,1)S(1)}, u32[]{:S(2)}, u32[]{:S(2)}) collective-permute-start(bf16[2,16,1024]{2,1,0:T(8,128)(2,1)S(1)} %get-tuple-element.76), channel_id=1, source_target_pairs={{0,24},{4,28},{8,16},{12,20},{16,8},{20,12},{24,0},{28,4},{1,25},{... | collective-permute-start | bytes 196616 | tf_op jit(solution)/shard_map/ppermute | solution.py:329
  69.1 9.6 %collective-permute-start.28 = (bf16[2,16,1024]{2,1,0:T(8,128)(2,1)S(1)}, bf16[2,16,1024]{2,1,0:T(8,128)(2,1)S(1)}, u32[]{:S(2)}, u32[]{:S(2)}) collective-permute-start(bf16[2,16,1024]{2,1,0:T(8,128)(2,1)S(1)} %get-tuple-element.77), channel_id=1, source_target_pairs={{0,16},{4,20},{8,24},{12,28},{16,0},{20,4},{24,8},{28,12},{1,17},{... | collective-permute-start | bytes 196616 | tf_op jit(solution)/shard_map/ppermute | solution.py:329
  69.1 9.6 %collective-permute-start.27 = (bf16[2,16,1024]{2,1,0:T(8,128)(2,1)S(1)}, bf16[2,16,1024]{2,1,0:T(8,128)(2,1)S(1)}, u32[]{:S(2)}, u32[]{:S(2)}) collective-permute-start(bf16[2,16,1024]{2,1,0:T(8,128)(2,1)S(1)} %get-tuple-element.78), channel_id=1, source_target_pairs={{0,8},{4,12},{8,0},{12,4},{16,24},{20,28},{24,16},{28,20},{1,9},{5... | collective-permute-start | bytes 196616 | tf_op jit(solution)/shard_map/ppermute | solution.py:329
  78.8 4.4 %collective-permute-start.35 = (bf16[16,1024]{1,0:T(8,128)(2,1)S(1)}, bf16[16,1024]{1,0:T(8,128)(2,1)S(1)}, u32[]{:S(2)}, u32[]{:S(2)}) collective-permute-start(bf16[16,1024]{1,0:T(8,128)(2,1)S(1)} %slice_bitcast_fusion.4), channel_id=1, source_target_pairs={{0,4},{4,0},{8,12},{12,8},{16,20},{20,16},{24,28},{28,24},{1,5},{5... | collective-permute-start | bytes 98312 | tf_op jit(solution)/shard_map/ppermute | solution.py:329
  79.7 6.8 %collective-permute-start.30 = (bf16[4,112,256]{2,1,0:T(8,128)(2,1)S(1)}, bf16[4,112,256]{2,1,0:T(8,128)(2,1)S(1)}, u32[]{:S(2)}, u32[]{:S(2)}) collective-permute-start(bf16[4,112,256]{2,1,0:T(8,128)(2,1)S(1)} %get-tuple-element.62), channel_id=1, source_target_pairs={{0,4},{4,0},{8,12},{12,8},{16,20},{20,16},{24,28},{28,24},{1,5},{5... | collective-permute-start | bytes 688136 | tf_op jit(solution)/shard_map/ppermute | solution.py:329
  80.9 6.1 %collective-permute-start.31 = (bf16[4,112,256]{2,1,0:T(8,128)(2,1)S(1)}, bf16[4,112,256]{2,1,0:T(8,128)(2,1)S(1)}, u32[]{:S(2)}, u32[]{:S(2)}) collective-permute-start(bf16[4,112,256]{2,1,0:T(8,128)(2,1)S(1)} %get-tuple-element.63), channel_id=1, source_target_pairs={{0,2},{1,3},{2,0},{3,1},{4,6},{5,7},{6,4},{7,5},{8,10},{9,11},{10,... | collective-permute-start | bytes 688136 | tf_op jit(solution)/shard_map/ppermute | solution.py:329
  83.2 8.5 %collective-permute-start.36 = (bf16[16,512]{1,0:T(8,128)(2,1)S(1)}, bf16[16,512]{1,0:T(8,128)(2,1)S(1)}, u32[]{:S(2)}, u32[]{:S(2)}) collective-permute-start(bf16[16,512]{1,0:T(8,128)(2,1)S(1)} %pad_maximum_fusion.4), channel_id=1, source_target_pairs={{0,2},{1,3},{2,0},{3,1},{4,6},{5,7},{6,4},{7,5},{8,10},{9,11},{10,... | collective-permute-start | bytes 49160 | tf_op jit(solution)/shard_map/ppermute | solution.py:329
  87.3 7.3 %collective-permute-start.32 = (bf16[112,512]{1,0:T(8,128)(2,1)S(1)}, bf16[112,512]{1,0:T(8,128)(2,1)S(1)}, u32[]{:S(2)}, u32[]{:S(2)}) collective-permute-start(bf16[112,512]{1,0:T(8,128)(2,1)S(1)} %get-tuple-element.73), channel_id=1, source_target_pairs={{0,24},{4,28},{8,16},{12,20},{16,8},{20,12},{24,0},{28,4},{1,25},{... | collective-permute-start | bytes 344072 | tf_op jit(solution)/shard_map/ppermute | solution.py:329
  89.4 8.7 %collective-permute-start.33 = (bf16[112,512]{1,0:T(8,128)(2,1)S(1)}, bf16[112,512]{1,0:T(8,128)(2,1)S(1)}, u32[]{:S(2)}, u32[]{:S(2)}) collective-permute-start(bf16[112,512]{1,0:T(8,128)(2,1)S(1)} %get-tuple-element.74), channel_id=1, source_target_pairs={{0,16},{4,20},{8,24},{12,28},{16,0},{20,4},{24,8},{28,12},{1,17},{... | collective-permute-start | bytes 344072 | tf_op jit(solution)/shard_map/ppermute | solution.py:329
  89.4 8.7 %collective-permute-start.34 = (bf16[112,512]{1,0:T(8,128)(2,1)S(1)}, bf16[112,512]{1,0:T(8,128)(2,1)S(1)}, u32[]{:S(2)}, u32[]{:S(2)}) collective-permute-start(bf16[112,512]{1,0:T(8,128)(2,1)S(1)} %get-tuple-element.75), channel_id=1, source_target_pairs={{0,8},{4,12},{8,0},{12,4},{16,24},{20,28},{24,16},{28,20},{1,9},{5... | collective-permute-start | bytes 344072 | tf_op jit(solution)/shard_map/ppermute | solution.py:329
  (8 other events, 112.5 us)

commit v13 on v12

--- a/solution.py
+++ b/solution.py
@@ -152,9 +152,9 @@
     picks_hbm, weights_hbm, unit_ref, own_hbm = refs[:4]
     pieces_in = refs[4 : 4 + n_pieces]
     w_gate_hbm, w_up_hbm, w_down_hbm = refs[4 + n_pieces : 7 + n_pieces]
-    out_refs = refs[7 + n_pieces : 13 + n_pieces]
+    out_refs = refs[7 + n_pieces : 15 + n_pieces]
     (picks, weights, w_in, w_down, toks, rows, hidden, mixed, table_sems, tok_sems, in_sems,
-     down_sems) = refs[13 + n_pieces :]
+     down_sems) = refs[15 + n_pieces :]
     n_z, _, tok_rows, model_width = toks.shape
     n_seq = 2 * n_z
     exp_dev, hid_dev, _ = w_gate_hbm.shape
@@ -265,14 +265,18 @@
                 along[dy] += jnp.sum(got * unit_ref[:, cols], axis=1, keepdims=True)
         for dy in range(2):
             for dc in range(2):
-                far, near, rest = out_refs[3 * dc : 3 * dc + 3]
+                far_x, far_y, near, rest = out_refs[4 * dc : 4 * dc + 4]
                 for n, (color, dx) in enumerate(((0, 1), (0, 0), (1, 0), (1, 1))):
                     cols = pl.ds(group_offset(rep, color, dx, dc, width), width)
                     value = mixed[dy, :, cols] - along[dy] * unit_ref[:, cols]
                     value = value.astype(jnp.bfloat16)
                     rest[dz, dy, :, n * width : (n + 1) * width] = value[split:]
-                    leaves, kind = (dy, 2 + dx) if color else (dx, dy)
-                    (far if leaves else near)[kind, dz] = value[:split]
+                    if color and dy:
+                        far_y[dx, dz] = value[:split]
+                    elif not color and dx:
+                        far_x[dy, dz] = value[:split]
+                    else:
+                        near[2 + dx if color else dy, dz] = value[:split]
         return carry
 
     lax.fori_loop(0, n_z, combine, 0)
@@ -291,10 +295,12 @@
         pltpu.with_memory_space_constraint(value, pltpu.HBM) for value in (picks, weights, own)
     ]
     n_z, split = n_seq // 2, most_rows(tok_rows)
-    most = (4, n_z, split, width)
+    far, near = (2, n_z, split, width), (4, n_z, split, width)
     rest = (n_z, 2, tok_rows - split, 4 * width)
     outs = [
-        jax.ShapeDtypeStruct(shape, jnp.bfloat16) for _ in range(2) for shape in (most, most, rest)
+        jax.ShapeDtypeStruct(shape, jnp.bfloat16)
+        for _ in range(2)
+        for shape in (far, far, near, rest)
     ]
     return pl.pallas_call(
         functools.partial(moe_kernel, n_pieces),
@@ -364,17 +370,17 @@
     pieces = [second, first, from_y, *last, *early, *[swap(piece, "rep", 1) for piece in last]]
 
     sums = moe_partial(picks, weights, unit_dir, normed, pieces, w_gate, w_up, w_down)
-    return (base + summed_up(sums[:3], sums[3:], width)).astype(jnp.bfloat16)
+    return (base + summed_up(sums[:4], sums[4:], width)).astype(jnp.bfloat16)
 
 
 def summed_up(kept, sent, width):
     n_z = kept[0].shape[1]
     others = range(1, n_z)
-    far, near, rest = zip(kept, [swap(piece, "rep", 1) for piece in sent])
-
-    to_x, to_y, rest_kept = lax.optimization_barrier(
-        (added(*[term[:2] for term in far]), added(*[term[2:] for term in far]), rest[0])
-    )
+    far_x, far_y, near, rest = zip(kept, [swap(piece, "rep", 1) for piece in sent])
+
+    to_x = added(*far_x)
+    to_y, rest_kept, arrived = lax.optimization_barrier((added(*far_y), rest[0], near[1]))
+    near = (near[0], arrived)
     by_x, by_y = swap(to_x, "rep", 2), swap(to_y, "seq", 1)
     rest = added(rest_kept, rest[1])
     by_z = [swap(rest[d], "seq", 2 * d) for d in others]

time: 99.1 us -> 99.7 us (level)
  starting transfers between devices: 36.6 us -> 39 us
  waiting for transfers between devices: 34.1 us -> 32.3 us
    ppermute x37 -> x38, starting transfers between devices: 36.6 us -> 39 us  [swap(): return lax.ppermute(value, axis, [(i, i ^ distance) for i in range(size)])]
    ppermute x37 -> x38, waiting for transfers between devices: 34.1 us -> 32.3 us  [swap(): return lax.ppermute(value, axis, [(i, i ^ distance) for i in range(size)])]
  transfers between devices with their start and end apart: 37 -> 38, of which waited for: 16 -> 17; matrix products, arithmetic and copies ran while one was open for 2% -> 2% of each run, Pallas kernels for 3% -> 3%
where the time goes in v13:
time: 99.7 us; the launch traced here: 99.5 us
  starting transfers between devices  39 us (39%)
  waiting for transfers between devices  32.3 us (32%)
  Pallas kernels  25.5 us (26%)
  other arithmetic  1.62 us (2%)
    ppermute x38, starting transfers between devices, swap(): return lax.ppermute(value, axis, [(i, i ^ distance) for i in range(size)])  39 us
    ppermute x38, waiting for transfers between devices, swap(): return lax.ppermute(value, axis, [(i, i ^ distance) for i in range(size)])  32.3 us
    pallas_call x1, Pallas kernels, moe_partial(): pl.pallas_call(functools.partial(moe_kernel, n_pieces), out_shape=outs, i...  20.3 us
    pallas_call x1, Pallas kernels, route(): pl.pallas_call(functools.partial(route_kernel, exp_dev), out_shape=[jax.S...  2.72 us
    pallas_call x1, Pallas kernels, norm_and_base(): pl.pallas_call(norm_kernel, out_shape=[jax.ShapeDtypeStruct((tok_rows, mo...  2.46 us
  transfers between devices with their start and end apart: 38, of which 17 were waited for; matrix products, arithmetic and copies ran while one was open for 2% of the time, Pallas kernels for 3%

profile of v13, /device:TPU:0, one launch (start us, length us, event | category | flops | bytes accessed | tf_op | source)
XLA Modules:
  0.0 99.5 jit_solution(3681078392662991352)
XLA Ops:
  0.0 2.5 %shard_map.82 = (bf16[128,2048]{1,0:T(8,128)(2,1)}, bf16[144,256]{1,0:T(8,128)(2,1)}, bf16[128,256]{1,0:T(8,128)(2,1)}, bf16[144,768]{1,0:T(8,128)(2,1)}, f32[1,...) custom-call(bf16[128,2048]{1,0:T(8,128)(2,1)} %tokens_ref.1, f32[1,2048]{1,0:T(1,128)} %bitcast.63, ...), custom_call_target="tpu_custom_call" | custom-call | tf_op jit(solution)/shard_map/pallas_call | solution.py:74
  2.5 5.1 %collective-permute-start.2 = (bf16[144,256]{1,0:T(8,128)(2,1)}, bf16[144,256]{1,0:T(8,128)(2,1)S(1)}, u32[]{:S(2)}, u32[]{:S(2)}) collective-permute-start(bf16[144,256]{1,0:T(8,128)(2,1)} %get-tuple-element.40), channel_id=1, source_target_pairs={{0,24},{4,28},{8,16},{12,20},{16,8},{20,12},{24,0},{28,4},{1,25},{... | collective-permute-start | bytes 221192 | tf_op jit(solution)/shard_map/ppermute | solution.py:335
  8.2 1.7 %collective-permute-start.3 = (bf16[1,144,768]{2,1,0:T(8,128)(2,1)}, bf16[1,144,768]{2,1,0:T(8,128)(2,1)S(1)}, u32[]{:S(2)}, u32[]{:S(2)}) collective-permute-start(bf16[1,144,768]{2,1,0:T(8,128)(2,1)} %bitcast.67), channel_id=1, source_target_pairs={{0,4},{4,0},{8,12},{12,8},{16,20},{20,16},{24,28},{28,24},{1,5},{5... | collective-permute-start | bytes 663560 | tf_op jit(solution)/shard_map/ppermute | solution.py:335
  10.5 3.4 %collective-permute-done.1 = bf16[144,256]{1,0:T(8,128)(2,1)S(1)} collective-permute-done((bf16[144,256]{1,0:T(8,128)(2,1)}, bf16[144,256]{1,0:T(8,128)(2,1)S(1)}, u32[]{:S(2)}, u32[]{:S(2)}) %collective-permute-start.1) | collective-permute-done | bytes 73760 | tf_op jit(solution)/shard_map/ppermute | solution.py:335
  14.0 1.0 %collective-permute-done.3.refs_6_ = bf16[1,144,768]{2,1,0:T(8,128)(2,1)S(1)} collective-permute-done((bf16[1,144,768]{2,1,0:T(8,128)(2,1)}, bf16[1,144,768]{2,1,0:T(8,128)(2,1)S(1)}, u32[]{:S(2)}, u32[]{:S(2)}) %collective-permute-start.3) | collective-permute-done | bytes 221216 | tf_op jit(solution)/shard_map/ppermute | solution.py:335
  15.0 3.5 %collective-permute-start.7 = (bf16[128,256]{1,0:T(8,128)(2,1)}, bf16[128,256]{1,0:T(8,128)(2,1)S(1)}, u32[]{:S(2)}, u32[]{:S(2)}) collective-permute-start(bf16[128,256]{1,0:T(8,128)(2,1)} %get-tuple-element.51), channel_id=1, source_target_pairs={{0,24},{4,28},{8,16},{12,20},{16,8},{20,12},{24,0},{28,4},{1,25},{... | collective-permute-start | bytes 196616 | tf_op jit(solution)/shard_map/ppermute | solution.py:335
  18.5 0.9 collective-permute-start.5
  19.4 1.6 %collective-permute-start.4 = (bf16[3,144,256]{2,1,0:T(8,128)(2,1)S(1)}, bf16[3,144,256]{2,1,0:T(8,128)(2,1)S(1)}, u32[]{:S(2)}, u32[]{:S(2)}) collective-permute-start(bf16[3,144,256]{2,1,0:T(8,128)(2,1)S(1)} %pad_maximum_fusion.1.refs_4_), channel_id=1, source_target_pairs={{0,4},{4,0},{8,12},{12,8},{16,20},{20,16},{24,28},{28,24},{1,5},{5... | collective-permute-start | bytes 663560 | tf_op jit(solution)/shard_map/ppermute | solution.py:335
  21.0 1.5 %collective-permute-start.8 = (bf16[3,128,256]{2,1,0:T(8,128)(2,1)S(1)}, bf16[3,128,256]{2,1,0:T(8,128)(2,1)S(1)}, u32[]{:S(2)}, u32[]{:S(2)}) collective-permute-start(bf16[3,128,256]{2,1,0:T(8,128)(2,1)S(1)} %slice.109), channel_id=1, source_target_pairs={{0,2},{1,3},{2,0},{3,1},{4,6},{5,7},{6,4},{7,5},{8,10},{9,11},{10,... | collective-permute-start | bytes 589832 | tf_op jit(solution)/shard_map/ppermute | solution.py:335
  22.5 1.3 %collective-permute-done.6 = bf16[128,256]{1,0:T(8,128)(2,1)S(1)} collective-permute-done((bf16[128,256]{1,0:T(8,128)(2,1)}, bf16[128,256]{1,0:T(8,128)(2,1)S(1)}, u32[]{:S(2)}, u32[]{:S(2)}) %collective-permute-start.6) | collective-permute-done | bytes 65568 | tf_op jit(solution)/shard_map/ppermute | solution.py:335
  23.9 1.6 %collective-permute-start.10 = (bf16[3,128,256]{2,1,0:T(8,128)(2,1)S(1)}, bf16[3,128,256]{2,1,0:T(8,128)(2,1)S(1)}, u32[]{:S(2)}, u32[]{:S(2)}) collective-permute-start(bf16[3,128,256]{2,1,0:T(8,128)(2,1)S(1)} %pad_maximum_fusion.2.refs_5_), channel_id=1, source_target_pairs={{0,4},{4,0},{8,12},{12,8},{16,20},{20,16},{24,28},{28,24},{1,5},{5... | collective-permute-start | bytes 589832 | tf_op jit(solution)/shard_map/ppermute | solution.py:335
  25.6 1.6 %collective-permute-start.9 = (bf16[4,128,256]{2,1,0:T(8,128)(2,1)S(1)}, bf16[4,128,256]{2,1,0:T(8,128)(2,1)S(1)}, u32[]{:S(2)}, u32[]{:S(2)}) collective-permute-start(bf16[4,128,256]{2,1,0:T(8,128)(2,1)S(1)} %pad_maximum_fusion), channel_id=1, source_target_pairs={{0,2},{1,3},{2,0},{3,1},{4,6},{5,7},{6,4},{7,5},{8,10},{9,11},{10,... | collective-permute-start | bytes 786440 | tf_op jit(solution)/shard_map/ppermute | solution.py:335
  28.3 3.4 %collective-permute-done.10.refs_10_ = bf16[3,128,256]{2,1,0:T(8,128)(2,1)S(1)} collective-permute-done((bf16[3,128,256]{2,1,0:T(8,128)(2,1)S(1)}, bf16[3,128,256]{2,1,0:T(8,128)(2,1)S(1)}, u32[]{:S(2)}, u32[]{:S(2)}) %collective-permute-start.10) | collective-permute-done | bytes 196640 | tf_op jit(solution)/shard_map/ppermute | solution.py:335
  31.7 2.3 %collective-permute-done.9.refs_9_ = bf16[4,128,256]{2,1,0:T(8,128)(2,1)S(1)} collective-permute-done((bf16[4,128,256]{2,1,0:T(8,128)(2,1)S(1)}, bf16[4,128,256]{2,1,0:T(8,128)(2,1)S(1)}, u32[]{:S(2)}, u32[]{:S(2)}) %collective-permute-start.9) | collective-permute-done | bytes 262176 | tf_op jit(solution)/shard_map/ppermute | solution.py:335
  34.0 1.5 %collective-permute-start.12 = (bf16[3,128,256]{2,1,0:T(8,128)(2,1)S(1)}, bf16[3,128,256]{2,1,0:T(8,128)(2,1)S(1)}, u32[]{:S(2)}, u32[]{:S(2)}) collective-permute-start(bf16[3,128,256]{2,1,0:T(8,128)(2,1)S(1)} %collective-permute-done.10.refs_10_), channel_id=1, source_target_pairs={{0,2},{1,3},{2,0},{3,1},{4,6},{5,7},{6,4},{7,5},{8,10},{9,11},{10,... | collective-permute-start | bytes 589832 | tf_op jit(solution)/shard_map/ppermute | solution.py:335
  35.5 2.7 %shard_map.83 = (bf16[8,256,128]{2,1,0:T(8,128)(2,1)}, bf16[8,128,256]{2,1,0:T(8,128)(2,1)}) custom-call(bf16[8,16,128]{2,1,0:T(8,128)(2,1)} %copy-done.2), custom_call_target="tpu_custom_call" | custom-call | flops 4000000000 | bytes 2097152 | tf_op jit(solution)/shard_map/pallas_call | solution.py:132
  39.3 0.9 collective-permute-done.12.refs_12_
  40.5 1.1 %collective-permute-done.21.refs_21_ = bf16[3,128,256]{2,1,0:T(8,128)(2,1)S(1)} collective-permute-done((bf16[3,128,256]{2,1,0:T(8,128)(2,1)S(1)}, bf16[3,128,256]{2,1,0:T(8,128)(2,1)S(1)}, u32[]{:S(2)}, u32[]{:S(2)}) %collective-permute-start.21) | collective-permute-done | bytes 196640 | tf_op jit(solution)/shard_map/ppermute | solution.py:335
  41.6 20.3 %shard_map.84 = (bf16[2,4,112,256]{3,2,1,0:T(8,128)(2,1)S(1)}, bf16[2,4,112,256]{3,2,1,0:T(8,128)(2,1)S(1)}, bf16[4,4,112,256]{3,2,1,0:T(8,128)(2,1)S(1)}, bf16[...) custom-call(bf16[8,256,128]{2,1,0:T(8,128)(2,1)} %get-tuple-element., ...), custom_call_target="tpu_custom_call" | custom-call | flops 4831838208 | bytes 46137344 | tf_op jit(solution)/shard_map/pallas_call | solution.py:305
  63.9 1.6 %collective-permute-start.25 = (bf16[2,4,112,256]{3,2,1,0:T(8,128)(2,1)S(1)}, bf16[2,4,112,256]{3,2,1,0:T(8,128)(2,1)S(1)}, u32[]{:S(2)}, u32[]{:S(2)}) collective-permute-start(bf16[2,4,112,256]{3,2,1,0:T(8,128)(2,1)S(1)} %add_convert_fusion), channel_id=1, source_target_pairs={{0,2},{1,3},{2,0},{3,1},{4,6},{5,7},{6,4},{7,5},{8,10},{9,11},{10,... | collective-permute-start | bytes 1376264 | tf_op jit(solution)/shard_map/ppermute | solution.py:335
  66.7 2.1 %collective-permute-start.30 = (bf16[2,16,1024]{2,1,0:T(8,128)(2,1)S(1)}, bf16[2,16,1024]{2,1,0:T(8,128)(2,1)S(1)}, u32[]{:S(2)}, u32[]{:S(2)}) collective-permute-start(bf16[2,16,1024]{2,1,0:T(8,128)(2,1)S(1)} %get-tuple-element.78), channel_id=1, source_target_pairs={{0,24},{4,28},{8,16},{12,20},{16,8},{20,12},{24,0},{28,4},{1,25},{... | collective-permute-start | bytes 196616 | tf_op jit(solution)/shard_map/ppermute | solution.py:335
  68.9 2.3 %collective-permute-start.28 = (bf16[2,16,1024]{2,1,0:T(8,128)(2,1)S(1)}, bf16[2,16,1024]{2,1,0:T(8,128)(2,1)S(1)}, u32[]{:S(2)}, u32[]{:S(2)}) collective-permute-start(bf16[2,16,1024]{2,1,0:T(8,128)(2,1)S(1)} %get-tuple-element.80), channel_id=1, source_target_pairs={{0,8},{4,12},{8,0},{12,4},{16,24},{20,28},{24,16},{28,20},{1,9},{5... | collective-permute-start | bytes 196616 | tf_op jit(solution)/shard_map/ppermute | solution.py:335
  71.1 5.4 %collective-permute-done.25 = bf16[2,4,112,256]{3,2,1,0:T(8,128)(2,1)S(1)} collective-permute-done((bf16[2,4,112,256]{3,2,1,0:T(8,128)(2,1)S(1)}, bf16[2,4,112,256]{3,2,1,0:T(8,128)(2,1)S(1)}, u32[]{:S(2)}, u32[]{:S(2)}) %collective-permute-start.25) | collective-permute-done | bytes 458784 | tf_op jit(solution)/shard_map/ppermute | solution.py:335
  76.5 2.0 %collective-permute-done.26 = bf16[2,4,112,256]{3,2,1,0:T(8,128)(2,1)S(1)} collective-permute-done((bf16[2,4,112,256]{3,2,1,0:T(8,128)(2,1)S(1)}, bf16[2,4,112,256]{3,2,1,0:T(8,128)(2,1)S(1)}, u32[]{:S(2)}, u32[]{:S(2)}) %collective-permute-start.26) | collective-permute-done | bytes 458784 | tf_op jit(solution)/shard_map/ppermute | solution.py:335
  79.6 1.2 %collective-permute-start.31 = (bf16[4,112,256]{2,1,0:T(8,128)(2,1)S(1)}, bf16[4,112,256]{2,1,0:T(8,128)(2,1)S(1)}, u32[]{:S(2)}, u32[]{:S(2)}) collective-permute-start(bf16[4,112,256]{2,1,0:T(8,128)(2,1)S(1)} %get-tuple-element.66), channel_id=1, source_target_pairs={{0,4},{4,0},{8,12},{12,8},{16,20},{20,16},{24,28},{28,24},{1,5},{5... | collective-permute-start | bytes 688136 | tf_op jit(solution)/shard_map/ppermute | solution.py:335
  80.9 1.5 %collective-permute-start.32 = (bf16[4,112,256]{2,1,0:T(8,128)(2,1)S(1)}, bf16[4,112,256]{2,1,0:T(8,128)(2,1)S(1)}, u32[]{:S(2)}, u32[]{:S(2)}) collective-permute-start(bf16[4,112,256]{2,1,0:T(8,128)(2,1)S(1)} %get-tuple-element.67), channel_id=1, source_target_pairs={{0,2},{1,3},{2,0},{3,1},{4,6},{5,7},{6,4},{7,5},{8,10},{9,11},{10,... | collective-permute-start | bytes 688136 | tf_op jit(solution)/shard_map/ppermute | solution.py:335
  83.1 1.6 %collective-permute-start.37 = (bf16[16,512]{1,0:T(8,128)(2,1)S(1)}, bf16[16,512]{1,0:T(8,128)(2,1)S(1)}, u32[]{:S(2)}, u32[]{:S(2)}) collective-permute-start(bf16[16,512]{1,0:T(8,128)(2,1)S(1)} %pad_maximum_fusion.4), channel_id=1, source_target_pairs={{0,2},{1,3},{2,0},{3,1},{4,6},{5,7},{6,4},{7,5},{8,10},{9,11},{10,... | collective-permute-start | bytes 49160 | tf_op jit(solution)/shard_map/ppermute | solution.py:335
  84.7 2.0 %collective-permute-done.31 = bf16[4,112,256]{2,1,0:T(8,128)(2,1)S(1)} collective-permute-done((bf16[4,112,256]{2,1,0:T(8,128)(2,1)S(1)}, bf16[4,112,256]{2,1,0:T(8,128)(2,1)S(1)}, u32[]{:S(2)}, u32[]{:S(2)}) %collective-permute-start.31) | collective-permute-done | bytes 229408 | tf_op jit(solution)/shard_map/ppermute | solution.py:335
  87.6 2.1 %collective-permute-start.33 = (bf16[112,512]{1,0:T(8,128)(2,1)S(1)}, bf16[112,512]{1,0:T(8,128)(2,1)S(1)}, u32[]{:S(2)}, u32[]{:S(2)}) collective-permute-start(bf16[112,512]{1,0:T(8,128)(2,1)S(1)} %get-tuple-element.75), channel_id=1, source_target_pairs={{0,24},{4,28},{8,16},{12,20},{16,8},{20,12},{24,0},{28,4},{1,25},{... | collective-permute-start | bytes 344072 | tf_op jit(solution)/shard_map/ppermute | solution.py:335
  89.7 2.3 %collective-permute-start.35 = (bf16[112,512]{1,0:T(8,128)(2,1)S(1)}, bf16[112,512]{1,0:T(8,128)(2,1)S(1)}, u32[]{:S(2)}, u32[]{:S(2)}) collective-permute-start(bf16[112,512]{1,0:T(8,128)(2,1)S(1)} %get-tuple-element.77), channel_id=1, source_target_pairs={{0,8},{4,12},{8,0},{12,4},{16,24},{20,28},{24,16},{28,20},{1,9},{5... | collective-permute-start | bytes 344072 | tf_op jit(solution)/shard_map/ppermute | solution.py:335
  92.0 3.0 %collective-permute-done.33 = bf16[112,512]{1,0:T(8,128)(2,1)S(1)} collective-permute-done((bf16[112,512]{1,0:T(8,128)(2,1)S(1)}, bf16[112,512]{1,0:T(8,128)(2,1)S(1)}, u32[]{:S(2)}, u32[]{:S(2)}) %collective-permute-start.33) | collective-permute-done | bytes 114720 | tf_op jit(solution)/shard_map/ppermute | solution.py:335
  95.1 3.6 %collective-permute-done.34 = bf16[112,512]{1,0:T(8,128)(2,1)S(1)} collective-permute-done((bf16[112,512]{1,0:T(8,128)(2,1)S(1)}, bf16[112,512]{1,0:T(8,128)(2,1)S(1)}, u32[]{:S(2)}, u32[]{:S(2)}) %collective-permute-start.34) | collective-permute-done | bytes 114720 | tf_op jit(solution)/shard_map/ppermute | solution.py:335
  (81 shorter events, 10.7 us)
Async XLA Ops:
  2.5 8.1 %collective-permute-start.2 = (bf16[144,256]{1,0:T(8,128)(2,1)}, bf16[144,256]{1,0:T(8,128)(2,1)S(1)}, u32[]{:S(2)}, u32[]{:S(2)}) collective-permute-start(bf16[144,256]{1,0:T(8,128)(2,1)} %get-tuple-element.40), channel_id=1, source_target_pairs={{0,24},{4,28},{8,16},{12,20},{16,8},{20,12},{24,0},{28,4},{1,25},{... | collective-permute-start | bytes 221192 | tf_op jit(solution)/shard_map/ppermute | solution.py:335
  7.5 6.4 %collective-permute-start.1 = (bf16[144,256]{1,0:T(8,128)(2,1)}, bf16[144,256]{1,0:T(8,128)(2,1)S(1)}, u32[]{:S(2)}, u32[]{:S(2)}) collective-permute-start(bf16[144,256]{1,0:T(8,128)(2,1)} %get-tuple-element.40), channel_id=1, source_target_pairs={{0,16},{4,20},{8,24},{12,28},{16,0},{20,4},{24,8},{28,12},{1,17},{... | collective-permute-start | bytes 221192 | tf_op jit(solution)/shard_map/ppermute | solution.py:335
  7.5 6.4 %collective-permute-start = (bf16[144,256]{1,0:T(8,128)(2,1)}, bf16[144,256]{1,0:T(8,128)(2,1)S(1)}, u32[]{:S(2)}, u32[]{:S(2)}) collective-permute-start(bf16[144,256]{1,0:T(8,128)(2,1)} %get-tuple-element.40), channel_id=1, source_target_pairs={{0,8},{4,12},{8,0},{12,4},{16,24},{20,28},{24,16},{28,20},{1,9},{5... | collective-permute-start | bytes 221192 | tf_op jit(solution)/shard_map/ppermute | solution.py:335
  8.2 6.8 %collective-permute-start.3 = (bf16[1,144,768]{2,1,0:T(8,128)(2,1)}, bf16[1,144,768]{2,1,0:T(8,128)(2,1)S(1)}, u32[]{:S(2)}, u32[]{:S(2)}) collective-permute-start(bf16[1,144,768]{2,1,0:T(8,128)(2,1)} %bitcast.67), channel_id=1, source_target_pairs={{0,4},{4,0},{8,12},{12,8},{16,20},{20,16},{24,28},{28,24},{1,5},{5... | collective-permute-start | bytes 663560 | tf_op jit(solution)/shard_map/ppermute | solution.py:335
  15.0 7.5 %collective-permute-start.7 = (bf16[128,256]{1,0:T(8,128)(2,1)}, bf16[128,256]{1,0:T(8,128)(2,1)S(1)}, u32[]{:S(2)}, u32[]{:S(2)}) collective-permute-start(bf16[128,256]{1,0:T(8,128)(2,1)} %get-tuple-element.51), channel_id=1, source_target_pairs={{0,24},{4,28},{8,16},{12,20},{16,8},{20,12},{24,0},{28,4},{1,25},{... | collective-permute-start | bytes 196616 | tf_op jit(solution)/shard_map/ppermute | solution.py:335
  18.5 5.4 %collective-permute-start.6 = (bf16[128,256]{1,0:T(8,128)(2,1)}, bf16[128,256]{1,0:T(8,128)(2,1)S(1)}, u32[]{:S(2)}, u32[]{:S(2)}) collective-permute-start(bf16[128,256]{1,0:T(8,128)(2,1)} %get-tuple-element.51), channel_id=1, source_target_pairs={{0,16},{4,20},{8,24},{12,28},{16,0},{20,4},{24,8},{28,12},{1,17},{... | collective-permute-start | bytes 196616 | tf_op jit(solution)/shard_map/ppermute | solution.py:335
  18.5 5.4 %collective-permute-start.5 = (bf16[128,256]{1,0:T(8,128)(2,1)}, bf16[128,256]{1,0:T(8,128)(2,1)S(1)}, u32[]{:S(2)}, u32[]{:S(2)}) collective-permute-start(bf16[128,256]{1,0:T(8,128)(2,1)} %get-tuple-element.51), channel_id=1, source_target_pairs={{0,8},{4,12},{8,0},{12,4},{16,24},{20,28},{24,16},{28,20},{1,9},{5... | collective-permute-start | bytes 196616 | tf_op jit(solution)/shard_map/ppermute | solution.py:335
  19.4 8.2 %collective-permute-start.4 = (bf16[3,144,256]{2,1,0:T(8,128)(2,1)S(1)}, bf16[3,144,256]{2,1,0:T(8,128)(2,1)S(1)}, u32[]{:S(2)}, u32[]{:S(2)}) collective-permute-start(bf16[3,144,256]{2,1,0:T(8,128)(2,1)S(1)} %pad_maximum_fusion.1.refs_4_), channel_id=1, source_target_pairs={{0,4},{4,0},{8,12},{12,8},{16,20},{20,16},{24,28},{28,24},{1,5},{5... | collective-permute-start | bytes 663560 | tf_op jit(solution)/shard_map/ppermute | solution.py:335
  21.0 6.1 %collective-permute-start.8 = (bf16[3,128,256]{2,1,0:T(8,128)(2,1)S(1)}, bf16[3,128,256]{2,1,0:T(8,128)(2,1)S(1)}, u32[]{:S(2)}, u32[]{:S(2)}) collective-permute-start(bf16[3,128,256]{2,1,0:T(8,128)(2,1)S(1)} %slice.109), channel_id=1, source_target_pairs={{0,2},{1,3},{2,0},{3,1},{4,6},{5,7},{6,4},{7,5},{8,10},{9,11},{10,... | collective-permute-start | bytes 589832 | tf_op jit(solution)/shard_map/ppermute | solution.py:335
  23.9 3.8 %collective-permute-start.14 = (bf16[3,128,256]{2,1,0:T(8,128)(2,1)S(1)}, bf16[3,128,256]{2,1,0:T(8,128)(2,1)S(1)}, u32[]{:S(2)}, u32[]{:S(2)}) collective-permute-start(bf16[3,128,256]{2,1,0:T(8,128)(2,1)S(1)} %pad_maximum_fusion.2.refs_5_), channel_id=1, source_target_pairs={{0,1},{1,0},{2,3},{3,2},{4,5},{5,4},{6,7},{7,6},{8,9},{9,8},{10,11... | collective-permute-start | bytes 589832 | tf_op jit(solution)/shard_map/ppermute | solution.py:335
  23.9 7.8 %collective-permute-start.10 = (bf16[3,128,256]{2,1,0:T(8,128)(2,1)S(1)}, bf16[3,128,256]{2,1,0:T(8,128)(2,1)S(1)}, u32[]{:S(2)}, u32[]{:S(2)}) collective-permute-start(bf16[3,128,256]{2,1,0:T(8,128)(2,1)S(1)} %pad_maximum_fusion.2.refs_5_), channel_id=1, source_target_pairs={{0,4},{4,0},{8,12},{12,8},{16,20},{20,16},{24,28},{28,24},{1,5},{5... | collective-permute-start | bytes 589832 | tf_op jit(solution)/shard_map/ppermute | solution.py:335
  25.6 8.4 %collective-permute-start.9 = (bf16[4,128,256]{2,1,0:T(8,128)(2,1)S(1)}, bf16[4,128,256]{2,1,0:T(8,128)(2,1)S(1)}, u32[]{:S(2)}, u32[]{:S(2)}) collective-permute-start(bf16[4,128,256]{2,1,0:T(8,128)(2,1)S(1)} %pad_maximum_fusion), channel_id=1, source_target_pairs={{0,2},{1,3},{2,0},{3,1},{4,6},{5,7},{6,4},{7,5},{8,10},{9,11},{10,... | collective-permute-start | bytes 786440 | tf_op jit(solution)/shard_map/ppermute | solution.py:335
  27.1 8.4 %collective-permute-start.11 = (bf16[3,128,256]{2,1,0:T(8,128)(2,1)S(1)}, bf16[3,128,256]{2,1,0:T(8,128)(2,1)S(1)}, u32[]{:S(2)}, u32[]{:S(2)}) collective-permute-start(bf16[3,128,256]{2,1,0:T(8,128)(2,1)S(1)} %collective-permute-done.8.refs_7_), channel_id=1, source_target_pairs={{0,4},{4,0},{8,12},{12,8},{16,20},{20,16},{24,28},{28,24},{1,5},{5... | collective-permute-start | bytes 589832 | tf_op jit(solution)/shard_map/ppermute | solution.py:335
  27.6 11.1 %collective-permute-start.13 = (bf16[3,144,256]{2,1,0:T(8,128)(2,1)S(1)}, bf16[3,144,256]{2,1,0:T(8,128)(2,1)S(1)}, u32[]{:S(2)}, u32[]{:S(2)}) collective-permute-start(bf16[3,144,256]{2,1,0:T(8,128)(2,1)S(1)} %pad_maximum_fusion.1.refs_4_), channel_id=1, source_target_pairs={{0,1},{1,0},{2,3},{3,2},{4,5},{5,4},{6,7},{7,6},{8,9},{9,8},{10,11... | collective-permute-start | bytes 663560 | tf_op jit(solution)/shard_map/ppermute | solution.py:335
  27.7 10.5 %collective-permute-start.16 = (bf16[3,128,256]{2,1,0:T(8,128)(2,1)S(1)}, bf16[3,128,256]{2,1,0:T(8,128)(2,1)S(1)}, u32[]{:S(2)}, u32[]{:S(2)}) collective-permute-start(bf16[3,128,256]{2,1,0:T(8,128)(2,1)S(1)} %collective-permute-done.8.refs_7_), channel_id=1, source_target_pairs={{0,1},{1,0},{2,3},{3,2},{4,5},{5,4},{6,7},{7,6},{8,9},{9,8},{10,11... | collective-permute-start | bytes 589832 | tf_op jit(solution)/shard_map/ppermute | solution.py:335
  31.7 7.1 %collective-permute-start.17 = (bf16[3,144,256]{2,1,0:T(8,128)(2,1)S(1)}, bf16[3,144,256]{2,1,0:T(8,128)(2,1)S(1)}, u32[]{:S(2)}, u32[]{:S(2)}) collective-permute-start(bf16[3,144,256]{2,1,0:T(8,128)(2,1)S(1)} %collective-permute-done.4.refs_8_), channel_id=1, source_target_pairs={{0,1},{1,0},{2,3},{3,2},{4,5},{5,4},{6,7},{7,6},{8,9},{9,8},{10,11... | collective-permute-start | bytes 663560 | tf_op jit(solution)/shard_map/ppermute | solution.py:335
  34.0 6.1 %collective-permute-start.12 = (bf16[3,128,256]{2,1,0:T(8,128)(2,1)S(1)}, bf16[3,128,256]{2,1,0:T(8,128)(2,1)S(1)}, u32[]{:S(2)}, u32[]{:S(2)}) collective-permute-start(bf16[3,128,256]{2,1,0:T(8,128)(2,1)S(1)} %collective-permute-done.10.refs_10_), channel_id=1, source_target_pairs={{0,2},{1,3},{2,0},{3,1},{4,6},{5,7},{6,4},{7,5},{8,10},{9,11},{10,... | collective-permute-start | bytes 589832 | tf_op jit(solution)/shard_map/ppermute | solution.py:335
  35.5 5.0 %collective-permute-start.18 = (bf16[4,128,256]{2,1,0:T(8,128)(2,1)S(1)}, bf16[4,128,256]{2,1,0:T(8,128)(2,1)S(1)}, u32[]{:S(2)}, u32[]{:S(2)}) collective-permute-start(bf16[4,128,256]{2,1,0:T(8,128)(2,1)S(1)} %collective-permute-done.9.refs_9_), channel_id=1, source_target_pairs={{0,1},{1,0},{2,3},{3,2},{4,5},{5,4},{6,7},{7,6},{8,9},{9,8},{10,11... | collective-permute-start | bytes 786440 | tf_op jit(solution)/shard_map/ppermute | solution.py:335
  62.1 3.8 %collective-permute-start.23 = (bf16[4,4,112,256]{3,2,1,0:T(8,128)(2,1)S(1)}, bf16[4,4,112,256]{3,2,1,0:T(8,128)(2,1)S(1)}, u32[]{:S(2)}, u32[]{:S(2)}) collective-permute-start(bf16[4,4,112,256]{3,2,1,0:T(8,128)(2,1)S(1)} %get-tuple-element.59), channel_id=1, source_target_pairs={{0,1},{1,0},{2,3},{3,2},{4,5},{5,4},{6,7},{7,6},{8,9},{9,8},{10,11... | collective-permute-start | bytes 2752520 | tf_op jit(solution)/shard_map/ppermute | solution.py:335
  62.6 4.0 %collective-permute-start.27 = (bf16[4,2,16,1024]{3,2,1,0:T(8,128)(2,1)S(1)}, bf16[4,2,16,1024]{3,2,1,0:T(8,128)(2,1)S(1)}, u32[]{:S(2)}, u32[]{:S(2)}) collective-permute-start(bf16[4,2,16,1024]{3,2,1,0:T(8,128)(2,1)S(1)} %get-tuple-element.65), channel_id=1, source_target_pairs={{0,1},{1,0},{2,3},{3,2},{4,5},{5,4},{6,7},{7,6},{8,9},{9,8},{10,11... | collective-permute-start | bytes 786440 | tf_op jit(solution)/shard_map/ppermute | solution.py:335
  63.9 12.6 %collective-permute-start.25 = (bf16[2,4,112,256]{3,2,1,0:T(8,128)(2,1)S(1)}, bf16[2,4,112,256]{3,2,1,0:T(8,128)(2,1)S(1)}, u32[]{:S(2)}, u32[]{:S(2)}) collective-permute-start(bf16[2,4,112,256]{3,2,1,0:T(8,128)(2,1)S(1)} %add_convert_fusion), channel_id=1, source_target_pairs={{0,2},{1,3},{2,0},{3,1},{4,6},{5,7},{6,4},{7,5},{8,10},{9,11},{10,... | collective-permute-start | bytes 1376264 | tf_op jit(solution)/shard_map/ppermute | solution.py:335
  65.9 12.6 %collective-permute-start.26 = (bf16[2,4,112,256]{3,2,1,0:T(8,128)(2,1)S(1)}, bf16[2,4,112,256]{3,2,1,0:T(8,128)(2,1)S(1)}, u32[]{:S(2)}, u32[]{:S(2)}) collective-permute-start(bf16[2,4,112,256]{3,2,1,0:T(8,128)(2,1)S(1)} %add_convert_fusion.1), channel_id=1, source_target_pairs={{0,4},{4,0},{8,12},{12,8},{16,20},{20,16},{24,28},{28,24},{1,5},{5... | collective-permute-start | bytes 1376264 | tf_op jit(solution)/shard_map/ppermute | solution.py:335
  66.7 12.0 %collective-permute-start.30 = (bf16[2,16,1024]{2,1,0:T(8,128)(2,1)S(1)}, bf16[2,16,1024]{2,1,0:T(8,128)(2,1)S(1)}, u32[]{:S(2)}, u32[]{:S(2)}) collective-permute-start(bf16[2,16,1024]{2,1,0:T(8,128)(2,1)S(1)} %get-tuple-element.78), channel_id=1, source_target_pairs={{0,24},{4,28},{8,16},{12,20},{16,8},{20,12},{24,0},{28,4},{1,25},{... | collective-permute-start | bytes 196616 | tf_op jit(solution)/shard_map/ppermute | solution.py:335
  68.8 9.9 %collective-permute-start.29 = (bf16[2,16,1024]{2,1,0:T(8,128)(2,1)S(1)}, bf16[2,16,1024]{2,1,0:T(8,128)(2,1)S(1)}, u32[]{:S(2)}, u32[]{:S(2)}) collective-permute-start(bf16[2,16,1024]{2,1,0:T(8,128)(2,1)S(1)} %get-tuple-element.79), channel_id=1, source_target_pairs={{0,16},{4,20},{8,24},{12,28},{16,0},{20,4},{24,8},{28,12},{1,17},{... | collective-permute-start | bytes 196616 | tf_op jit(solution)/shard_map/ppermute | solution.py:335
  68.9 9.8 %collective-permute-start.28 = (bf16[2,16,1024]{2,1,0:T(8,128)(2,1)S(1)}, bf16[2,16,1024]{2,1,0:T(8,128)(2,1)S(1)}, u32[]{:S(2)}, u32[]{:S(2)}) collective-permute-start(bf16[2,16,1024]{2,1,0:T(8,128)(2,1)S(1)} %get-tuple-element.80), channel_id=1, source_target_pairs={{0,8},{4,12},{8,0},{12,4},{16,24},{20,28},{24,16},{28,20},{1,9},{5... | collective-permute-start | bytes 196616 | tf_op jit(solution)/shard_map/ppermute | solution.py:335
  78.8 4.3 %collective-permute-start.36 = (bf16[16,1024]{1,0:T(8,128)(2,1)S(1)}, bf16[16,1024]{1,0:T(8,128)(2,1)S(1)}, u32[]{:S(2)}, u32[]{:S(2)}) collective-permute-start(bf16[16,1024]{1,0:T(8,128)(2,1)S(1)} %slice_bitcast_fusion.4), channel_id=1, source_target_pairs={{0,4},{4,0},{8,12},{12,8},{16,20},{20,16},{24,28},{28,24},{1,5},{5... | collective-permute-start | bytes 98312 | tf_op jit(solution)/shard_map/ppermute | solution.py:335
  79.6 7.1 %collective-permute-start.31 = (bf16[4,112,256]{2,1,0:T(8,128)(2,1)S(1)}, bf16[4,112,256]{2,1,0:T(8,128)(2,1)S(1)}, u32[]{:S(2)}, u32[]{:S(2)}) collective-permute-start(bf16[4,112,256]{2,1,0:T(8,128)(2,1)S(1)} %get-tuple-element.66), channel_id=1, source_target_pairs={{0,4},{4,0},{8,12},{12,8},{16,20},{20,16},{24,28},{28,24},{1,5},{5... | collective-permute-start | bytes 688136 | tf_op jit(solution)/shard_map/ppermute | solution.py:335
  80.9 6.4 %collective-permute-start.32 = (bf16[4,112,256]{2,1,0:T(8,128)(2,1)S(1)}, bf16[4,112,256]{2,1,0:T(8,128)(2,1)S(1)}, u32[]{:S(2)}, u32[]{:S(2)}) collective-permute-start(bf16[4,112,256]{2,1,0:T(8,128)(2,1)S(1)} %get-tuple-element.67), channel_id=1, source_target_pairs={{0,2},{1,3},{2,0},{3,1},{4,6},{5,7},{6,4},{7,5},{8,10},{9,11},{10,... | collective-permute-start | bytes 688136 | tf_op jit(solution)/shard_map/ppermute | solution.py:335
  83.1 8.9 %collective-permute-start.37 = (bf16[16,512]{1,0:T(8,128)(2,1)S(1)}, bf16[16,512]{1,0:T(8,128)(2,1)S(1)}, u32[]{:S(2)}, u32[]{:S(2)}) collective-permute-start(bf16[16,512]{1,0:T(8,128)(2,1)S(1)} %pad_maximum_fusion.4), channel_id=1, source_target_pairs={{0,2},{1,3},{2,0},{3,1},{4,6},{5,7},{6,4},{7,5},{8,10},{9,11},{10,... | collective-permute-start | bytes 49160 | tf_op jit(solution)/shard_map/ppermute | solution.py:335
  87.6 7.5 %collective-permute-start.33 = (bf16[112,512]{1,0:T(8,128)(2,1)S(1)}, bf16[112,512]{1,0:T(8,128)(2,1)S(1)}, u32[]{:S(2)}, u32[]{:S(2)}) collective-permute-start(bf16[112,512]{1,0:T(8,128)(2,1)S(1)} %get-tuple-element.75), channel_id=1, source_target_pairs={{0,24},{4,28},{8,16},{12,20},{16,8},{20,12},{24,0},{28,4},{1,25},{... | collective-permute-start | bytes 344072 | tf_op jit(solution)/shard_map/ppermute | solution.py:335
  89.7 9.0 %collective-permute-start.34 = (bf16[112,512]{1,0:T(8,128)(2,1)S(1)}, bf16[112,512]{1,0:T(8,128)(2,1)S(1)}, u32[]{:S(2)}, u32[]{:S(2)}) collective-permute-start(bf16[112,512]{1,0:T(8,128)(2,1)S(1)} %get-tuple-element.76), channel_id=1, source_target_pairs={{0,16},{4,20},{8,24},{12,28},{16,0},{20,4},{24,8},{28,12},{1,17},{... | collective-permute-start | bytes 344072 | tf_op jit(solution)/shard_map/ppermute | solution.py:335
  89.7 9.0 %collective-permute-start.35 = (bf16[112,512]{1,0:T(8,128)(2,1)S(1)}, bf16[112,512]{1,0:T(8,128)(2,1)S(1)}, u32[]{:S(2)}, u32[]{:S(2)}) collective-permute-start(bf16[112,512]{1,0:T(8,128)(2,1)S(1)} %get-tuple-element.77), channel_id=1, source_target_pairs={{0,8},{4,12},{8,0},{12,4},{16,24},{20,28},{24,16},{28,20},{1,9},{5... | collective-permute-start | bytes 344072 | tf_op jit(solution)/shard_map/ppermute | solution.py:335
  (9 other events, 115.7 us)

commit v14 on v12

--- a/solution.py
+++ b/solution.py
@@ -145,7 +145,7 @@
 
 
 def most_rows(tok_rows):
-    return tok_rows // 128 * 112
+    return tok_rows // 4 * 3
 
 
 def moe_kernel(n_pieces, *refs):
@@ -378,20 +378,23 @@
     by_x, by_y = swap(to_x, "rep", 2), swap(to_y, "seq", 1)
     rest = added(rest_kept, rest[1])
     by_z = [swap(rest[d], "seq", 2 * d) for d in others]
-    to_y, to_x, *by_z = lax.optimization_barrier(
+    to_y, to_x, *by_z[1:] = lax.optimization_barrier(
         (
             added(*[term[1] for term in near], by_x[1]),
             added(*[term[3] for term in near], by_y[1]),
-            *by_z,
+            *by_z[1:],
         )
     )
-    first_far, second_far = swap(to_y, "seq", 1), swap(to_x, "rep", 2)
+    first_far, second_far, rest = lax.optimization_barrier(
+        (swap(to_y, "seq", 1), swap(to_x, "rep", 2), rest[0])
+    )
     first = added(*[term[0] for term in near], by_x[0], first_far)
     second = added(*[term[2] for term in near], by_y[0], second_far)
     blocks = jnp.concatenate([first, second], axis=2)
     most = [swap(blocks[d], "seq", 2 * d) for d in reversed(others)] + [blocks[0]]
-    rest = added(rest[0], *by_z)
+    rest = added(rest, *by_z)
     rest = added(rest[0], swap(rest[1], "seq", 1))
+    most[0], rest = lax.optimization_barrier((most[0], rest))
     far = jnp.concatenate([rest[:, :width], rest[:, 3 * width :]], axis=1)
     rest = [rest[:, width : 3 * width], swap(far, "rep", 2)]
     return jnp.concatenate(

time: 99.1 us -> 101 us (1.019)
  waiting for transfers between devices: 34.1 us -> 38.5 us
  starting transfers between devices: 36.6 us -> 34.5 us
    ppermute x37, waiting for transfers between devices: 34.1 us -> 38.5 us  [swap(): return lax.ppermute(value, axis, [(i, i ^ distance) for i in range(size)])]
    ppermute x37, starting transfers between devices: 36.6 us -> 34.5 us  [swap(): return lax.ppermute(value, axis, [(i, i ^ distance) for i in range(size)])]
where the time goes in v14:
time: 101 us
  waiting for transfers between devices  38.5 us (38%)
  starting transfers between devices  34.5 us (34%)
  Pallas kernels  25.5 us (25%)
  other arithmetic  1.79 us (2%)
    ppermute x37, waiting for transfers between devices, swap(): return lax.ppermute(value, axis, [(i, i ^ distance) for i in range(size)])  38.5 us
    ppermute x37, starting transfers between devices, swap(): return lax.ppermute(value, axis, [(i, i ^ distance) for i in range(size)])  34.5 us
    pallas_call x1, Pallas kernels, moe_partial(): pl.pallas_call(functools.partial(moe_kernel, n_pieces), out_shape=outs, i...  20.3 us
    pallas_call x1, Pallas kernels, route(): pl.pallas_call(functools.partial(route_kernel, exp_dev), out_shape=[jax.S...  2.72 us
    pallas_call x1, Pallas kernels, norm_and_base(): pl.pallas_call(norm_kernel, out_shape=[jax.ShapeDtypeStruct((tok_rows, mo...  2.46 us
  transfers between devices with their start and end apart: 37, of which 16 were waited for; matrix products, arithmetic and copies ran while one was open for 2% of the time, Pallas kernels for 3%

profile of v14, /device:TPU:0, one launch (start us, length us, event | category | flops | bytes accessed | tf_op | source)
XLA Modules:
  0.0 101.2 jit_solution(4642438952755744428)
XLA Ops:
  0.0 2.5 %shard_map.82 = (bf16[128,2048]{1,0:T(8,128)(2,1)}, bf16[144,256]{1,0:T(8,128)(2,1)}, bf16[128,256]{1,0:T(8,128)(2,1)}, bf16[144,768]{1,0:T(8,128)(2,1)}, f32[1,...) custom-call(bf16[128,2048]{1,0:T(8,128)(2,1)} %tokens_ref.1, f32[1,2048]{1,0:T(1,128)} %bitcast.60, ...), custom_call_target="tpu_custom_call" | custom-call | tf_op jit(solution)/shard_map/pallas_call | solution.py:74
  2.5 5.1 %collective-permute-start.2 = (bf16[144,256]{1,0:T(8,128)(2,1)}, bf16[144,256]{1,0:T(8,128)(2,1)S(1)}, u32[]{:S(2)}, u32[]{:S(2)}) collective-permute-start(bf16[144,256]{1,0:T(8,128)(2,1)} %get-tuple-element.42), channel_id=1, source_target_pairs={{0,24},{4,28},{8,16},{12,20},{16,8},{20,12},{24,0},{28,4},{1,25},{... | collective-permute-start | bytes 221192 | tf_op jit(solution)/shard_map/ppermute | solution.py:329
  8.2 1.7 %collective-permute-start.3 = (bf16[1,144,768]{2,1,0:T(8,128)(2,1)}, bf16[1,144,768]{2,1,0:T(8,128)(2,1)S(1)}, u32[]{:S(2)}, u32[]{:S(2)}) collective-permute-start(bf16[1,144,768]{2,1,0:T(8,128)(2,1)} %bitcast.64), channel_id=1, source_target_pairs={{0,4},{4,0},{8,12},{12,8},{16,20},{20,16},{24,28},{28,24},{1,5},{5... | collective-permute-start | bytes 663560 | tf_op jit(solution)/shard_map/ppermute | solution.py:329
  10.5 3.4 %collective-permute-done.1 = bf16[144,256]{1,0:T(8,128)(2,1)S(1)} collective-permute-done((bf16[144,256]{1,0:T(8,128)(2,1)}, bf16[144,256]{1,0:T(8,128)(2,1)S(1)}, u32[]{:S(2)}, u32[]{:S(2)}) %collective-permute-start.1) | collective-permute-done | bytes 73760 | tf_op jit(solution)/shard_map/ppermute | solution.py:329
  14.0 1.0 collective-permute-done.3.refs_6_
  15.0 3.5 %collective-permute-start.7 = (bf16[128,256]{1,0:T(8,128)(2,1)}, bf16[128,256]{1,0:T(8,128)(2,1)S(1)}, u32[]{:S(2)}, u32[]{:S(2)}) collective-permute-start(bf16[128,256]{1,0:T(8,128)(2,1)} %get-tuple-element.53), channel_id=1, source_target_pairs={{0,24},{4,28},{8,16},{12,20},{16,8},{20,12},{24,0},{28,4},{1,25},{... | collective-permute-start | bytes 196616 | tf_op jit(solution)/shard_map/ppermute | solution.py:329
  18.5 0.9 collective-permute-start.5
  19.4 1.6 %collective-permute-start.4 = (bf16[3,144,256]{2,1,0:T(8,128)(2,1)S(1)}, bf16[3,144,256]{2,1,0:T(8,128)(2,1)S(1)}, u32[]{:S(2)}, u32[]{:S(2)}) collective-permute-start(bf16[3,144,256]{2,1,0:T(8,128)(2,1)S(1)} %pad_maximum_fusion.1.refs_4_), channel_id=1, source_target_pairs={{0,4},{4,0},{8,12},{12,8},{16,20},{20,16},{24,28},{28,24},{1,5},{5... | collective-permute-start | bytes 663560 | tf_op jit(solution)/shard_map/ppermute | solution.py:329
  21.0 1.5 %collective-permute-start.8 = (bf16[3,128,256]{2,1,0:T(8,128)(2,1)S(1)}, bf16[3,128,256]{2,1,0:T(8,128)(2,1)S(1)}, u32[]{:S(2)}, u32[]{:S(2)}) collective-permute-start(bf16[3,128,256]{2,1,0:T(8,128)(2,1)S(1)} %slice.121), channel_id=1, source_target_pairs={{0,2},{1,3},{2,0},{3,1},{4,6},{5,7},{6,4},{7,5},{8,10},{9,11},{10,... | collective-permute-start | bytes 589832 | tf_op jit(solution)/shard_map/ppermute | solution.py:329
  22.5 1.3 %collective-permute-done.6 = bf16[128,256]{1,0:T(8,128)(2,1)S(1)} collective-permute-done((bf16[128,256]{1,0:T(8,128)(2,1)}, bf16[128,256]{1,0:T(8,128)(2,1)S(1)}, u32[]{:S(2)}, u32[]{:S(2)}) %collective-permute-start.6) | collective-permute-done | bytes 65568 | tf_op jit(solution)/shard_map/ppermute | solution.py:329
  23.9 1.6 %collective-permute-start.10 = (bf16[3,128,256]{2,1,0:T(8,128)(2,1)S(1)}, bf16[3,128,256]{2,1,0:T(8,128)(2,1)S(1)}, u32[]{:S(2)}, u32[]{:S(2)}) collective-permute-start(bf16[3,128,256]{2,1,0:T(8,128)(2,1)S(1)} %pad_maximum_fusion.2.refs_5_), channel_id=1, source_target_pairs={{0,4},{4,0},{8,12},{12,8},{16,20},{20,16},{24,28},{28,24},{1,5},{5... | collective-permute-start | bytes 589832 | tf_op jit(solution)/shard_map/ppermute | solution.py:329
  25.6 1.6 %collective-permute-start.9 = (bf16[4,128,256]{2,1,0:T(8,128)(2,1)S(1)}, bf16[4,128,256]{2,1,0:T(8,128)(2,1)S(1)}, u32[]{:S(2)}, u32[]{:S(2)}) collective-permute-start(bf16[4,128,256]{2,1,0:T(8,128)(2,1)S(1)} %pad_maximum_fusion), channel_id=1, source_target_pairs={{0,2},{1,3},{2,0},{3,1},{4,6},{5,7},{6,4},{7,5},{8,10},{9,11},{10,... | collective-permute-start | bytes 786440 | tf_op jit(solution)/shard_map/ppermute | solution.py:329
  28.3 3.4 %collective-permute-done.10.refs_10_ = bf16[3,128,256]{2,1,0:T(8,128)(2,1)S(1)} collective-permute-done((bf16[3,128,256]{2,1,0:T(8,128)(2,1)S(1)}, bf16[3,128,256]{2,1,0:T(8,128)(2,1)S(1)}, u32[]{:S(2)}, u32[]{:S(2)}) %collective-permute-start.10) | collective-permute-done | bytes 196640 | tf_op jit(solution)/shard_map/ppermute | solution.py:329
  31.7 2.3 %collective-permute-done.9.refs_9_ = bf16[4,128,256]{2,1,0:T(8,128)(2,1)S(1)} collective-permute-done((bf16[4,128,256]{2,1,0:T(8,128)(2,1)S(1)}, bf16[4,128,256]{2,1,0:T(8,128)(2,1)S(1)}, u32[]{:S(2)}, u32[]{:S(2)}) %collective-permute-start.9) | collective-permute-done | bytes 262176 | tf_op jit(solution)/shard_map/ppermute | solution.py:329
  34.0 1.5 %collective-permute-start.12 = (bf16[3,128,256]{2,1,0:T(8,128)(2,1)S(1)}, bf16[3,128,256]{2,1,0:T(8,128)(2,1)S(1)}, u32[]{:S(2)}, u32[]{:S(2)}) collective-permute-start(bf16[3,128,256]{2,1,0:T(8,128)(2,1)S(1)} %collective-permute-done.10.refs_10_), channel_id=1, source_target_pairs={{0,2},{1,3},{2,0},{3,1},{4,6},{5,7},{6,4},{7,5},{8,10},{9,11},{10,... | collective-permute-start | bytes 589832 | tf_op jit(solution)/shard_map/ppermute | solution.py:329
  35.5 2.7 %shard_map.83 = (bf16[8,256,128]{2,1,0:T(8,128)(2,1)}, bf16[8,128,256]{2,1,0:T(8,128)(2,1)}) custom-call(bf16[8,16,128]{2,1,0:T(8,128)(2,1)} %copy-done.2), custom_call_target="tpu_custom_call" | custom-call | flops 4000000000 | bytes 2097152 | tf_op jit(solution)/shard_map/pallas_call | solution.py:132
  40.5 1.1 %collective-permute-done.21.refs_21_ = bf16[3,128,256]{2,1,0:T(8,128)(2,1)S(1)} collective-permute-done((bf16[3,128,256]{2,1,0:T(8,128)(2,1)S(1)}, bf16[3,128,256]{2,1,0:T(8,128)(2,1)S(1)}, u32[]{:S(2)}, u32[]{:S(2)}) %collective-permute-start.21) | collective-permute-done | bytes 196640 | tf_op jit(solution)/shard_map/ppermute | solution.py:329
  41.6 20.3 %shard_map.84 = (bf16[4,4,96,256]{3,2,1,0:T(8,128)(2,1)S(1)}, bf16[4,4,96,256]{3,2,1,0:T(8,128)(2,1)S(1)}, bf16[4,2,32,1024]{3,2,1,0:T(8,128)(2,1)S(1)}, bf16[4,...) custom-call(bf16[8,256,128]{2,1,0:T(8,128)(2,1)} %get-tuple-element.49.refs_0, ...), custom_call_target="tpu_custom_call" | custom-call | flops 4831838208 | bytes 46137344 | tf_op jit(solution)/shard_map/pallas_call | solution.py:299
  62.6 1.6 %collective-permute-done.23 = bf16[4,4,96,256]{3,2,1,0:T(8,128)(2,1)S(1)} collective-permute-done((bf16[4,4,96,256]{3,2,1,0:T(8,128)(2,1)S(1)}, bf16[4,4,96,256]{3,2,1,0:T(8,128)(2,1)S(1)}, u32[]{:S(2)}, u32[]{:S(2)}) %collective-permute-start.23) | collective-permute-done | bytes 786464 | tf_op jit(solution)/shard_map/ppermute | solution.py:329
  64.5 1.6 %collective-permute-start.24 = (bf16[2,4,96,256]{3,2,1,0:T(8,128)(2,1)S(1)}, bf16[2,4,96,256]{3,2,1,0:T(8,128)(2,1)S(1)}, u32[]{:S(2)}, u32[]{:S(2)}) collective-permute-start(bf16[2,4,96,256]{3,2,1,0:T(8,128)(2,1)S(1)} %get-tuple-element.62), channel_id=1, source_target_pairs={{0,2},{1,3},{2,0},{3,1},{4,6},{5,7},{6,4},{7,5},{8,10},{9,11},{10,... | collective-permute-start | bytes 1179656 | tf_op jit(solution)/shard_map/ppermute | solution.py:329
  67.0 2.1 %collective-permute-start.28 = (bf16[2,32,1024]{2,1,0:T(8,128)(2,1)S(1)}, bf16[2,32,1024]{2,1,0:T(8,128)(2,1)S(1)}, u32[]{:S(2)}, u32[]{:S(2)}) collective-permute-start(bf16[2,32,1024]{2,1,0:T(8,128)(2,1)S(1)} %get-tuple-element.83), channel_id=1, source_target_pairs={{0,24},{4,28},{8,16},{12,20},{16,8},{20,12},{24,0},{28,4},{1,25},{... | collective-permute-start | bytes 393224 | tf_op jit(solution)/shard_map/ppermute | solution.py:329
  69.1 6.6 %collective-permute-done.24 = bf16[2,4,96,256]{3,2,1,0:T(8,128)(2,1)S(1)} collective-permute-done((bf16[2,4,96,256]{3,2,1,0:T(8,128)(2,1)S(1)}, bf16[2,4,96,256]{3,2,1,0:T(8,128)(2,1)S(1)}, u32[]{:S(2)}, u32[]{:S(2)}) %collective-permute-start.24) | collective-permute-done | bytes 393248 | tf_op jit(solution)/shard_map/ppermute | solution.py:329
  75.7 1.2 %collective-permute-done.25 = bf16[2,4,96,256]{3,2,1,0:T(8,128)(2,1)S(1)} collective-permute-done((bf16[2,4,96,256]{3,2,1,0:T(8,128)(2,1)S(1)}, bf16[2,4,96,256]{3,2,1,0:T(8,128)(2,1)S(1)}, u32[]{:S(2)}, u32[]{:S(2)}) %collective-permute-start.25) | collective-permute-done | bytes 393248 | tf_op jit(solution)/shard_map/ppermute | solution.py:329
  77.1 3.8 %collective-permute-done.27 = bf16[2,32,1024]{2,1,0:T(8,128)(2,1)S(1)} collective-permute-done((bf16[2,32,1024]{2,1,0:T(8,128)(2,1)S(1)}, bf16[2,32,1024]{2,1,0:T(8,128)(2,1)S(1)}, u32[]{:S(2)}, u32[]{:S(2)}) %collective-permute-start.27) | collective-permute-done | bytes 131104 | tf_op jit(solution)/shard_map/ppermute | solution.py:329
  80.9 1.2 %collective-permute-start.29 = (bf16[4,96,256]{2,1,0:T(8,128)(2,1)S(1)}, bf16[4,96,256]{2,1,0:T(8,128)(2,1)S(1)}, u32[]{:S(2)}, u32[]{:S(2)}) collective-permute-start(bf16[4,96,256]{2,1,0:T(8,128)(2,1)S(1)} %get-tuple-element.66), channel_id=1, source_target_pairs={{0,4},{4,0},{8,12},{12,8},{16,20},{20,16},{24,28},{28,24},{1,5},{5... | collective-permute-start | bytes 589832 | tf_op jit(solution)/shard_map/ppermute | solution.py:329
  82.6 4.3 %collective-permute-done.29 = bf16[4,96,256]{2,1,0:T(8,128)(2,1)S(1)} collective-permute-done((bf16[4,96,256]{2,1,0:T(8,128)(2,1)S(1)}, bf16[4,96,256]{2,1,0:T(8,128)(2,1)S(1)}, u32[]{:S(2)}, u32[]{:S(2)}) %collective-permute-start.29) | collective-permute-done | bytes 196640 | tf_op jit(solution)/shard_map/ppermute | solution.py:329
  87.9 0.9 collective-permute-start.33
  89.0 1.0 %collective-permute-start.34 = (bf16[96,512]{1,0:T(8,128)(2,1)S(1)}, bf16[96,512]{1,0:T(8,128)(2,1)S(1)}, u32[]{:S(2)}, u32[]{:S(2)}) collective-permute-start(bf16[96,512]{1,0:T(8,128)(2,1)S(1)} %get-tuple-element.85), channel_id=1, source_target_pairs={{0,16},{4,20},{8,24},{12,28},{16,0},{20,4},{24,8},{28,12},{1,17},{... | collective-permute-start | bytes 294920 | tf_op jit(solution)/shard_map/ppermute | solution.py:329
  90.1 1.7 %collective-permute-start.31 = (bf16[96,512]{1,0:T(8,128)(2,1)S(1)}, bf16[96,512]{1,0:T(8,128)(2,1)S(1)}, u32[]{:S(2)}, u32[]{:S(2)}) collective-permute-start(bf16[96,512]{1,0:T(8,128)(2,1)S(1)} %get-tuple-element.86), channel_id=1, source_target_pairs={{0,24},{4,28},{8,16},{12,20},{16,8},{20,12},{24,0},{28,4},{1,25},{... | collective-permute-start | bytes 294920 | tf_op jit(solution)/shard_map/ppermute | solution.py:329
  92.6 3.9 %collective-permute-done.31 = bf16[96,512]{1,0:T(8,128)(2,1)S(1)} collective-permute-done((bf16[96,512]{1,0:T(8,128)(2,1)S(1)}, bf16[96,512]{1,0:T(8,128)(2,1)S(1)}, u32[]{:S(2)}, u32[]{:S(2)}) %collective-permute-start.31) | collective-permute-done | bytes 98336 | tf_op jit(solution)/shard_map/ppermute | solution.py:329
  96.6 1.6 %collective-permute-start.36 = (bf16[32,512]{1,0:T(8,128)(2,1)S(1)}, bf16[32,512]{1,0:T(8,128)(2,1)S(1)}, u32[]{:S(2)}, u32[]{:S(2)}) collective-permute-start(bf16[32,512]{1,0:T(8,128)(2,1)S(1)} %pad_maximum_fusion.4), channel_id=1, source_target_pairs={{0,2},{1,3},{2,0},{3,1},{4,6},{5,7},{6,4},{7,5},{8,10},{9,11},{10,... | collective-permute-start | bytes 98312 | tf_op jit(solution)/shard_map/ppermute | solution.py:329
  98.2 2.4 %collective-permute-done.36 = bf16[32,512]{1,0:T(8,128)(2,1)S(1)} collective-permute-done((bf16[32,512]{1,0:T(8,128)(2,1)S(1)}, bf16[32,512]{1,0:T(8,128)(2,1)S(1)}, u32[]{:S(2)}, u32[]{:S(2)}) %collective-permute-start.36) | collective-permute-done | bytes 32800 | tf_op jit(solution)/shard_map/ppermute | solution.py:329
  (78 shorter events, 10.3 us)
Async XLA Ops:
  2.5 8.1 %collective-permute-start.2 = (bf16[144,256]{1,0:T(8,128)(2,1)}, bf16[144,256]{1,0:T(8,128)(2,1)S(1)}, u32[]{:S(2)}, u32[]{:S(2)}) collective-permute-start(bf16[144,256]{1,0:T(8,128)(2,1)} %get-tuple-element.42), channel_id=1, source_target_pairs={{0,24},{4,28},{8,16},{12,20},{16,8},{20,12},{24,0},{28,4},{1,25},{... | collective-permute-start | bytes 221192 | tf_op jit(solution)/shard_map/ppermute | solution.py:329
  7.5 6.4 %collective-permute-start.1 = (bf16[144,256]{1,0:T(8,128)(2,1)}, bf16[144,256]{1,0:T(8,128)(2,1)S(1)}, u32[]{:S(2)}, u32[]{:S(2)}) collective-permute-start(bf16[144,256]{1,0:T(8,128)(2,1)} %get-tuple-element.42), channel_id=1, source_target_pairs={{0,16},{4,20},{8,24},{12,28},{16,0},{20,4},{24,8},{28,12},{1,17},{... | collective-permute-start | bytes 221192 | tf_op jit(solution)/shard_map/ppermute | solution.py:329
  7.5 6.4 %collective-permute-start = (bf16[144,256]{1,0:T(8,128)(2,1)}, bf16[144,256]{1,0:T(8,128)(2,1)S(1)}, u32[]{:S(2)}, u32[]{:S(2)}) collective-permute-start(bf16[144,256]{1,0:T(8,128)(2,1)} %get-tuple-element.42), channel_id=1, source_target_pairs={{0,8},{4,12},{8,0},{12,4},{16,24},{20,28},{24,16},{28,20},{1,9},{5... | collective-permute-start | bytes 221192 | tf_op jit(solution)/shard_map/ppermute | solution.py:329
  8.2 6.8 %collective-permute-start.3 = (bf16[1,144,768]{2,1,0:T(8,128)(2,1)}, bf16[1,144,768]{2,1,0:T(8,128)(2,1)S(1)}, u32[]{:S(2)}, u32[]{:S(2)}) collective-permute-start(bf16[1,144,768]{2,1,0:T(8,128)(2,1)} %bitcast.64), channel_id=1, source_target_pairs={{0,4},{4,0},{8,12},{12,8},{16,20},{20,16},{24,28},{28,24},{1,5},{5... | collective-permute-start | bytes 663560 | tf_op jit(solution)/shard_map/ppermute | solution.py:329
  15.0 7.5 %collective-permute-start.7 = (bf16[128,256]{1,0:T(8,128)(2,1)}, bf16[128,256]{1,0:T(8,128)(2,1)S(1)}, u32[]{:S(2)}, u32[]{:S(2)}) collective-permute-start(bf16[128,256]{1,0:T(8,128)(2,1)} %get-tuple-element.53), channel_id=1, source_target_pairs={{0,24},{4,28},{8,16},{12,20},{16,8},{20,12},{24,0},{28,4},{1,25},{... | collective-permute-start | bytes 196616 | tf_op jit(solution)/shard_map/ppermute | solution.py:329
  18.5 5.4 %collective-permute-start.6 = (bf16[128,256]{1,0:T(8,128)(2,1)}, bf16[128,256]{1,0:T(8,128)(2,1)S(1)}, u32[]{:S(2)}, u32[]{:S(2)}) collective-permute-start(bf16[128,256]{1,0:T(8,128)(2,1)} %get-tuple-element.53), channel_id=1, source_target_pairs={{0,16},{4,20},{8,24},{12,28},{16,0},{20,4},{24,8},{28,12},{1,17},{... | collective-permute-start | bytes 196616 | tf_op jit(solution)/shard_map/ppermute | solution.py:329
  18.5 5.4 %collective-permute-start.5 = (bf16[128,256]{1,0:T(8,128)(2,1)}, bf16[128,256]{1,0:T(8,128)(2,1)S(1)}, u32[]{:S(2)}, u32[]{:S(2)}) collective-permute-start(bf16[128,256]{1,0:T(8,128)(2,1)} %get-tuple-element.53), channel_id=1, source_target_pairs={{0,8},{4,12},{8,0},{12,4},{16,24},{20,28},{24,16},{28,20},{1,9},{5... | collective-permute-start | bytes 196616 | tf_op jit(solution)/shard_map/ppermute | solution.py:329
  19.4 8.2 %collective-permute-start.4 = (bf16[3,144,256]{2,1,0:T(8,128)(2,1)S(1)}, bf16[3,144,256]{2,1,0:T(8,128)(2,1)S(1)}, u32[]{:S(2)}, u32[]{:S(2)}) collective-permute-start(bf16[3,144,256]{2,1,0:T(8,128)(2,1)S(1)} %pad_maximum_fusion.1.refs_4_), channel_id=1, source_target_pairs={{0,4},{4,0},{8,12},{12,8},{16,20},{20,16},{24,28},{28,24},{1,5},{5... | collective-permute-start | bytes 663560 | tf_op jit(solution)/shard_map/ppermute | solution.py:329
  21.0 6.1 %collective-permute-start.8 = (bf16[3,128,256]{2,1,0:T(8,128)(2,1)S(1)}, bf16[3,128,256]{2,1,0:T(8,128)(2,1)S(1)}, u32[]{:S(2)}, u32[]{:S(2)}) collective-permute-start(bf16[3,128,256]{2,1,0:T(8,128)(2,1)S(1)} %slice.121), channel_id=1, source_target_pairs={{0,2},{1,3},{2,0},{3,1},{4,6},{5,7},{6,4},{7,5},{8,10},{9,11},{10,... | collective-permute-start | bytes 589832 | tf_op jit(solution)/shard_map/ppermute | solution.py:329
  23.9 3.8 %collective-permute-start.14 = (bf16[3,128,256]{2,1,0:T(8,128)(2,1)S(1)}, bf16[3,128,256]{2,1,0:T(8,128)(2,1)S(1)}, u32[]{:S(2)}, u32[]{:S(2)}) collective-permute-start(bf16[3,128,256]{2,1,0:T(8,128)(2,1)S(1)} %pad_maximum_fusion.2.refs_5_), channel_id=1, source_target_pairs={{0,1},{1,0},{2,3},{3,2},{4,5},{5,4},{6,7},{7,6},{8,9},{9,8},{10,11... | collective-permute-start | bytes 589832 | tf_op jit(solution)/shard_map/ppermute | solution.py:329
  23.9 7.8 %collective-permute-start.10 = (bf16[3,128,256]{2,1,0:T(8,128)(2,1)S(1)}, bf16[3,128,256]{2,1,0:T(8,128)(2,1)S(1)}, u32[]{:S(2)}, u32[]{:S(2)}) collective-permute-start(bf16[3,128,256]{2,1,0:T(8,128)(2,1)S(1)} %pad_maximum_fusion.2.refs_5_), channel_id=1, source_target_pairs={{0,4},{4,0},{8,12},{12,8},{16,20},{20,16},{24,28},{28,24},{1,5},{5... | collective-permute-start | bytes 589832 | tf_op jit(solution)/shard_map/ppermute | solution.py:329
  25.6 8.4 %collective-permute-start.9 = (bf16[4,128,256]{2,1,0:T(8,128)(2,1)S(1)}, bf16[4,128,256]{2,1,0:T(8,128)(2,1)S(1)}, u32[]{:S(2)}, u32[]{:S(2)}) collective-permute-start(bf16[4,128,256]{2,1,0:T(8,128)(2,1)S(1)} %pad_maximum_fusion), channel_id=1, source_target_pairs={{0,2},{1,3},{2,0},{3,1},{4,6},{5,7},{6,4},{7,5},{8,10},{9,11},{10,... | collective-permute-start | bytes 786440 | tf_op jit(solution)/shard_map/ppermute | solution.py:329
  27.1 8.4 %collective-permute-start.11 = (bf16[3,128,256]{2,1,0:T(8,128)(2,1)S(1)}, bf16[3,128,256]{2,1,0:T(8,128)(2,1)S(1)}, u32[]{:S(2)}, u32[]{:S(2)}) collective-permute-start(bf16[3,128,256]{2,1,0:T(8,128)(2,1)S(1)} %collective-permute-done.8.refs_7_), channel_id=1, source_target_pairs={{0,4},{4,0},{8,12},{12,8},{16,20},{20,16},{24,28},{28,24},{1,5},{5... | collective-permute-start | bytes 589832 | tf_op jit(solution)/shard_map/ppermute | solution.py:329
  27.6 11.1 %collective-permute-start.13 = (bf16[3,144,256]{2,1,0:T(8,128)(2,1)S(1)}, bf16[3,144,256]{2,1,0:T(8,128)(2,1)S(1)}, u32[]{:S(2)}, u32[]{:S(2)}) collective-permute-start(bf16[3,144,256]{2,1,0:T(8,128)(2,1)S(1)} %pad_maximum_fusion.1.refs_4_), channel_id=1, source_target_pairs={{0,1},{1,0},{2,3},{3,2},{4,5},{5,4},{6,7},{7,6},{8,9},{9,8},{10,11... | collective-permute-start | bytes 663560 | tf_op jit(solution)/shard_map/ppermute | solution.py:329
  27.7 10.5 %collective-permute-start.16 = (bf16[3,128,256]{2,1,0:T(8,128)(2,1)S(1)}, bf16[3,128,256]{2,1,0:T(8,128)(2,1)S(1)}, u32[]{:S(2)}, u32[]{:S(2)}) collective-permute-start(bf16[3,128,256]{2,1,0:T(8,128)(2,1)S(1)} %collective-permute-done.8.refs_7_), channel_id=1, source_target_pairs={{0,1},{1,0},{2,3},{3,2},{4,5},{5,4},{6,7},{7,6},{8,9},{9,8},{10,11... | collective-permute-start | bytes 589832 | tf_op jit(solution)/shard_map/ppermute | solution.py:329
  31.7 7.1 %collective-permute-start.17 = (bf16[3,144,256]{2,1,0:T(8,128)(2,1)S(1)}, bf16[3,144,256]{2,1,0:T(8,128)(2,1)S(1)}, u32[]{:S(2)}, u32[]{:S(2)}) collective-permute-start(bf16[3,144,256]{2,1,0:T(8,128)(2,1)S(1)} %collective-permute-done.4.refs_8_), channel_id=1, source_target_pairs={{0,1},{1,0},{2,3},{3,2},{4,5},{5,4},{6,7},{7,6},{8,9},{9,8},{10,11... | collective-permute-start | bytes 663560 | tf_op jit(solution)/shard_map/ppermute | solution.py:329
  34.0 6.1 %collective-permute-start.12 = (bf16[3,128,256]{2,1,0:T(8,128)(2,1)S(1)}, bf16[3,128,256]{2,1,0:T(8,128)(2,1)S(1)}, u32[]{:S(2)}, u32[]{:S(2)}) collective-permute-start(bf16[3,128,256]{2,1,0:T(8,128)(2,1)S(1)} %collective-permute-done.10.refs_10_), channel_id=1, source_target_pairs={{0,2},{1,3},{2,0},{3,1},{4,6},{5,7},{6,4},{7,5},{8,10},{9,11},{10,... | collective-permute-start | bytes 589832 | tf_op jit(solution)/shard_map/ppermute | solution.py:329
  35.5 5.0 %collective-permute-start.18 = (bf16[4,128,256]{2,1,0:T(8,128)(2,1)S(1)}, bf16[4,128,256]{2,1,0:T(8,128)(2,1)S(1)}, u32[]{:S(2)}, u32[]{:S(2)}) collective-permute-start(bf16[4,128,256]{2,1,0:T(8,128)(2,1)S(1)} %collective-permute-done.9.refs_9_), channel_id=1, source_target_pairs={{0,1},{1,0},{2,3},{3,2},{4,5},{5,4},{6,7},{7,6},{8,9},{9,8},{10,11... | collective-permute-start | bytes 786440 | tf_op jit(solution)/shard_map/ppermute | solution.py:329
  62.1 4.6 %collective-permute-start.26 = (bf16[4,2,32,1024]{3,2,1,0:T(8,128)(2,1)S(1)}, bf16[4,2,32,1024]{3,2,1,0:T(8,128)(2,1)S(1)}, u32[]{:S(2)}, u32[]{:S(2)}) collective-permute-start(bf16[4,2,32,1024]{3,2,1,0:T(8,128)(2,1)S(1)} %get-tuple-element.65), channel_id=1, source_target_pairs={{0,1},{1,0},{2,3},{3,2},{4,5},{5,4},{6,7},{7,6},{8,9},{9,8},{10,11... | collective-permute-start | bytes 1572872 | tf_op jit(solution)/shard_map/ppermute | solution.py:329
  62.5 6.6 %collective-permute-start.22 = (bf16[4,4,96,256]{3,2,1,0:T(8,128)(2,1)S(1)}, bf16[4,4,96,256]{3,2,1,0:T(8,128)(2,1)S(1)}, u32[]{:S(2)}, u32[]{:S(2)}) collective-permute-start(bf16[4,4,96,256]{3,2,1,0:T(8,128)(2,1)S(1)} %get-tuple-element.58), channel_id=1, source_target_pairs={{0,1},{1,0},{2,3},{3,2},{4,5},{5,4},{6,7},{7,6},{8,9},{9,8},{10,11... | collective-permute-start | bytes 2359304 | tf_op jit(solution)/shard_map/ppermute | solution.py:329
  64.5 11.2 %collective-permute-start.24 = (bf16[2,4,96,256]{3,2,1,0:T(8,128)(2,1)S(1)}, bf16[2,4,96,256]{3,2,1,0:T(8,128)(2,1)S(1)}, u32[]{:S(2)}, u32[]{:S(2)}) collective-permute-start(bf16[2,4,96,256]{3,2,1,0:T(8,128)(2,1)S(1)} %get-tuple-element.62), channel_id=1, source_target_pairs={{0,2},{1,3},{2,0},{3,1},{4,6},{5,7},{6,4},{7,5},{8,10},{9,11},{10,... | collective-permute-start | bytes 1179656 | tf_op jit(solution)/shard_map/ppermute | solution.py:329
  66.1 10.9 %collective-permute-start.25 = (bf16[2,4,96,256]{3,2,1,0:T(8,128)(2,1)S(1)}, bf16[2,4,96,256]{3,2,1,0:T(8,128)(2,1)S(1)}, u32[]{:S(2)}, u32[]{:S(2)}) collective-permute-start(bf16[2,4,96,256]{3,2,1,0:T(8,128)(2,1)S(1)} %get-tuple-element.63), channel_id=1, source_target_pairs={{0,4},{4,0},{8,12},{12,8},{16,20},{20,16},{24,28},{28,24},{1,5},{5... | collective-permute-start | bytes 1179656 | tf_op jit(solution)/shard_map/ppermute | solution.py:329
  67.0 10.2 %collective-permute-start.28 = (bf16[2,32,1024]{2,1,0:T(8,128)(2,1)S(1)}, bf16[2,32,1024]{2,1,0:T(8,128)(2,1)S(1)}, u32[]{:S(2)}, u32[]{:S(2)}) collective-permute-start(bf16[2,32,1024]{2,1,0:T(8,128)(2,1)S(1)} %get-tuple-element.83), channel_id=1, source_target_pairs={{0,24},{4,28},{8,16},{12,20},{16,8},{20,12},{24,0},{28,4},{1,25},{... | collective-permute-start | bytes 393224 | tf_op jit(solution)/shard_map/ppermute | solution.py:329
  69.1 11.8 %collective-permute-start.27 = (bf16[2,32,1024]{2,1,0:T(8,128)(2,1)S(1)}, bf16[2,32,1024]{2,1,0:T(8,128)(2,1)S(1)}, u32[]{:S(2)}, u32[]{:S(2)}) collective-permute-start(bf16[2,32,1024]{2,1,0:T(8,128)(2,1)S(1)} %get-tuple-element.84), channel_id=1, source_target_pairs={{0,16},{4,20},{8,24},{12,28},{16,0},{20,4},{24,8},{28,12},{1,17},{... | collective-permute-start | bytes 393224 | tf_op jit(solution)/shard_map/ppermute | solution.py:329
  80.9 6.0 %collective-permute-start.29 = (bf16[4,96,256]{2,1,0:T(8,128)(2,1)S(1)}, bf16[4,96,256]{2,1,0:T(8,128)(2,1)S(1)}, u32[]{:S(2)}, u32[]{:S(2)}) collective-permute-start(bf16[4,96,256]{2,1,0:T(8,128)(2,1)S(1)} %get-tuple-element.66), channel_id=1, source_target_pairs={{0,4},{4,0},{8,12},{12,8},{16,20},{20,16},{24,28},{28,24},{1,5},{5... | collective-permute-start | bytes 589832 | tf_op jit(solution)/shard_map/ppermute | solution.py:329
  82.1 5.7 %collective-permute-start.30 = (bf16[4,96,256]{2,1,0:T(8,128)(2,1)S(1)}, bf16[4,96,256]{2,1,0:T(8,128)(2,1)S(1)}, u32[]{:S(2)}, u32[]{:S(2)}) collective-permute-start(bf16[4,96,256]{2,1,0:T(8,128)(2,1)S(1)} %get-tuple-element.67), channel_id=1, source_target_pairs={{0,2},{1,3},{2,0},{3,1},{4,6},{5,7},{6,4},{7,5},{8,10},{9,11},{10,... | collective-permute-start | bytes 589832 | tf_op jit(solution)/shard_map/ppermute | solution.py:329
  82.6 5.1 %collective-permute-start.32 = (bf16[2,32,1024]{2,1,0:T(8,128)(2,1)S(1)}, bf16[2,32,1024]{2,1,0:T(8,128)(2,1)S(1)}, u32[]{:S(2)}, u32[]{:S(2)}) collective-permute-start(bf16[2,32,1024]{2,1,0:T(8,128)(2,1)S(1)} %get-tuple-element.81), channel_id=1, source_target_pairs={{0,8},{4,12},{8,0},{12,4},{16,24},{20,28},{24,16},{28,20},{1,9},{5... | collective-permute-start | bytes 393224 | tf_op jit(solution)/shard_map/ppermute | solution.py:329
  87.9 4.7 %collective-permute-start.33 = (bf16[32,1024]{1,0:T(8,128)(2,1)S(1)}, bf16[32,1024]{1,0:T(8,128)(2,1)S(1)}, u32[]{:S(2)}, u32[]{:S(2)}) collective-permute-start(bf16[32,1024]{1,0:T(8,128)(2,1)S(1)} %slice_bitcast_fusion.4), channel_id=1, source_target_pairs={{0,4},{4,0},{8,12},{12,8},{16,20},{20,16},{24,28},{28,24},{1,5},{5... | collective-permute-start | bytes 196616 | tf_op jit(solution)/shard_map/ppermute | solution.py:329
  89.0 9.1 %collective-permute-start.34 = (bf16[96,512]{1,0:T(8,128)(2,1)S(1)}, bf16[96,512]{1,0:T(8,128)(2,1)S(1)}, u32[]{:S(2)}, u32[]{:S(2)}) collective-permute-start(bf16[96,512]{1,0:T(8,128)(2,1)S(1)} %get-tuple-element.85), channel_id=1, source_target_pairs={{0,16},{4,20},{8,24},{12,28},{16,0},{20,4},{24,8},{28,12},{1,17},{... | collective-permute-start | bytes 294920 | tf_op jit(solution)/shard_map/ppermute | solution.py:329
  90.1 6.5 %collective-permute-start.31 = (bf16[96,512]{1,0:T(8,128)(2,1)S(1)}, bf16[96,512]{1,0:T(8,128)(2,1)S(1)}, u32[]{:S(2)}, u32[]{:S(2)}) collective-permute-start(bf16[96,512]{1,0:T(8,128)(2,1)S(1)} %get-tuple-element.86), channel_id=1, source_target_pairs={{0,24},{4,28},{8,16},{12,20},{16,8},{20,12},{24,0},{28,4},{1,25},{... | collective-permute-start | bytes 294920 | tf_op jit(solution)/shard_map/ppermute | solution.py:329
  91.8 6.3 %collective-permute-start.35 = (bf16[96,512]{1,0:T(8,128)(2,1)S(1)}, bf16[96,512]{1,0:T(8,128)(2,1)S(1)}, u32[]{:S(2)}, u32[]{:S(2)}) collective-permute-start(bf16[96,512]{1,0:T(8,128)(2,1)S(1)} %get-tuple-element.87), channel_id=1, source_target_pairs={{0,8},{4,12},{8,0},{12,4},{16,24},{20,28},{24,16},{28,20},{1,9},{5... | collective-permute-start | bytes 294920 | tf_op jit(solution)/shard_map/ppermute | solution.py:329
  96.6 4.0 %collective-permute-start.36 = (bf16[32,512]{1,0:T(8,128)(2,1)S(1)}, bf16[32,512]{1,0:T(8,128)(2,1)S(1)}, u32[]{:S(2)}, u32[]{:S(2)}) collective-permute-start(bf16[32,512]{1,0:T(8,128)(2,1)S(1)} %pad_maximum_fusion.4), channel_id=1, source_target_pairs={{0,2},{1,3},{2,0},{3,1},{4,6},{5,7},{6,4},{7,5},{8,10},{9,11},{10,... | collective-permute-start | bytes 98312 | tf_op jit(solution)/shard_map/ppermute | solution.py:329
  (8 other events, 114.7 us)

commit v15 on v12

--- a/solution.py
+++ b/solution.py
@@ -361,7 +361,9 @@
     early = [swap(piece, "rep", 1) for piece in (to_core, first, to_core_y)]
     x_three = swap(y_two, "rep", 2)
     last = [x_two, y_one, x_one, y_two, y_three, x_three]
-    pieces = [second, first, from_y, *last, *early, *[swap(piece, "rep", 1) for piece in last]]
+    to_core = list(last)
+    to_core[1:4] = lax.optimization_barrier((y_one, x_one, y_two))
+    pieces = [second, first, from_y, *last, *early, *[swap(piece, "rep", 1) for piece in to_core]]
 
     sums = moe_partial(picks, weights, unit_dir, normed, pieces, w_gate, w_up, w_down)
     return (base + summed_up(sums[:3], sums[3:], width)).astype(jnp.bfloat16)

time: 99.1 us -> 98.8 us (level)
  transfers between devices with their start and end apart: 37 -> 37, of which waited for: 16 -> 15; matrix products, arithmetic and copies ran while one was open for 2% -> 2% of each run, Pallas kernels for 3% -> 3%
where the time goes in v15:
time: 98.8 us; the launch traced here: 98.6 us
  starting transfers between devices  36.5 us (37%)
  waiting for transfers between devices  33.4 us (34%)
  Pallas kernels  25.5 us (26%)
  other arithmetic  1.66 us (2%)
  local copies, waits for them, and re-layouts  1.4 us (1%)
    ppermute x37, starting transfers between devices, swap(): return lax.ppermute(value, axis, [(i, i ^ distance) for i in range(size)])  36.5 us
    ppermute x37, waiting for transfers between devices, swap(): return lax.ppermute(value, axis, [(i, i ^ distance) for i in range(size)])  33.4 us
    pallas_call x1, Pallas kernels, moe_partial(): pl.pallas_call(functools.partial(moe_kernel, n_pieces), out_shape=outs, i...  20.3 us
    pallas_call x1, Pallas kernels, route(): pl.pallas_call(functools.partial(route_kernel, exp_dev), out_shape=[jax.S...  2.72 us
    pallas_call x1, Pallas kernels, norm_and_base(): pl.pallas_call(norm_kernel, out_shape=[jax.ShapeDtypeStruct((tok_rows, mo...  2.46 us
  transfers between devices with their start and end apart: 37, of which 15 were waited for; matrix products, arithmetic and copies ran while one was open for 2% of the time, Pallas kernels for 3%

profile of v15, /device:TPU:0, one launch (start us, length us, event | category | flops | bytes accessed | tf_op | source)
XLA Modules:
  0.0 98.6 jit_solution(646102058243671602)
XLA Ops:
  0.0 2.5 %shard_map.82 = (bf16[128,2048]{1,0:T(8,128)(2,1)}, bf16[144,256]{1,0:T(8,128)(2,1)}, bf16[128,256]{1,0:T(8,128)(2,1)}, bf16[144,768]{1,0:T(8,128)(2,1)}, f32[1,...) custom-call(bf16[128,2048]{1,0:T(8,128)(2,1)} %tokens_ref.1, f32[1,2048]{1,0:T(1,128)} %bitcast.63, ...), custom_call_target="tpu_custom_call" | custom-call | tf_op jit(solution)/shard_map/pallas_call | solution.py:74
  2.5 5.1 %collective-permute-start.2 = (bf16[144,256]{1,0:T(8,128)(2,1)}, bf16[144,256]{1,0:T(8,128)(2,1)S(1)}, u32[]{:S(2)}, u32[]{:S(2)}) collective-permute-start(bf16[144,256]{1,0:T(8,128)(2,1)} %get-tuple-element.41), channel_id=1, source_target_pairs={{0,24},{4,28},{8,16},{12,20},{16,8},{20,12},{24,0},{28,4},{1,25},{... | collective-permute-start | bytes 221192 | tf_op jit(solution)/shard_map/ppermute | solution.py:329
  8.2 1.7 %collective-permute-start.3 = (bf16[1,144,768]{2,1,0:T(8,128)(2,1)}, bf16[1,144,768]{2,1,0:T(8,128)(2,1)S(1)}, u32[]{:S(2)}, u32[]{:S(2)}) collective-permute-start(bf16[1,144,768]{2,1,0:T(8,128)(2,1)} %bitcast.67), channel_id=1, source_target_pairs={{0,4},{4,0},{8,12},{12,8},{16,20},{20,16},{24,28},{28,24},{1,5},{5... | collective-permute-start | bytes 663560 | tf_op jit(solution)/shard_map/ppermute | solution.py:329
  10.5 3.4 %collective-permute-done.1 = bf16[144,256]{1,0:T(8,128)(2,1)S(1)} collective-permute-done((bf16[144,256]{1,0:T(8,128)(2,1)}, bf16[144,256]{1,0:T(8,128)(2,1)S(1)}, u32[]{:S(2)}, u32[]{:S(2)}) %collective-permute-start.1) | collective-permute-done | bytes 73760 | tf_op jit(solution)/shard_map/ppermute | solution.py:329
  14.0 1.0 %collective-permute-done.3.refs_6_ = bf16[1,144,768]{2,1,0:T(8,128)(2,1)S(1)} collective-permute-done((bf16[1,144,768]{2,1,0:T(8,128)(2,1)}, bf16[1,144,768]{2,1,0:T(8,128)(2,1)S(1)}, u32[]{:S(2)}, u32[]{:S(2)}) %collective-permute-start.3) | collective-permute-done | bytes 221216 | tf_op jit(solution)/shard_map/ppermute | solution.py:329
  15.0 3.5 %collective-permute-start.7 = (bf16[128,256]{1,0:T(8,128)(2,1)}, bf16[128,256]{1,0:T(8,128)(2,1)S(1)}, u32[]{:S(2)}, u32[]{:S(2)}) collective-permute-start(bf16[128,256]{1,0:T(8,128)(2,1)} %get-tuple-element.52), channel_id=1, source_target_pairs={{0,24},{4,28},{8,16},{12,20},{16,8},{20,12},{24,0},{28,4},{1,25},{... | collective-permute-start | bytes 196616 | tf_op jit(solution)/shard_map/ppermute | solution.py:329
  18.5 0.9 collective-permute-start.5
  19.4 1.6 %collective-permute-start.4 = (bf16[3,144,256]{2,1,0:T(8,128)(2,1)S(1)}, bf16[3,144,256]{2,1,0:T(8,128)(2,1)S(1)}, u32[]{:S(2)}, u32[]{:S(2)}) collective-permute-start(bf16[3,144,256]{2,1,0:T(8,128)(2,1)S(1)} %pad_maximum_fusion.1.refs_4_), channel_id=1, source_target_pairs={{0,4},{4,0},{8,12},{12,8},{16,20},{20,16},{24,28},{28,24},{1,5},{5... | collective-permute-start | bytes 663560 | tf_op jit(solution)/shard_map/ppermute | solution.py:329
  21.0 1.5 %collective-permute-start.8 = (bf16[3,128,256]{2,1,0:T(8,128)(2,1)S(1)}, bf16[3,128,256]{2,1,0:T(8,128)(2,1)S(1)}, u32[]{:S(2)}, u32[]{:S(2)}) collective-permute-start(bf16[3,128,256]{2,1,0:T(8,128)(2,1)S(1)} %slice.121), channel_id=1, source_target_pairs={{0,2},{1,3},{2,0},{3,1},{4,6},{5,7},{6,4},{7,5},{8,10},{9,11},{10,... | collective-permute-start | bytes 589832 | tf_op jit(solution)/shard_map/ppermute | solution.py:329
  22.5 1.3 %collective-permute-done.6 = bf16[128,256]{1,0:T(8,128)(2,1)S(1)} collective-permute-done((bf16[128,256]{1,0:T(8,128)(2,1)}, bf16[128,256]{1,0:T(8,128)(2,1)S(1)}, u32[]{:S(2)}, u32[]{:S(2)}) %collective-permute-start.6) | collective-permute-done | bytes 65568 | tf_op jit(solution)/shard_map/ppermute | solution.py:329
  23.9 1.6 %collective-permute-start.10 = (bf16[3,128,256]{2,1,0:T(8,128)(2,1)S(1)}, bf16[3,128,256]{2,1,0:T(8,128)(2,1)S(1)}, u32[]{:S(2)}, u32[]{:S(2)}) collective-permute-start(bf16[3,128,256]{2,1,0:T(8,128)(2,1)S(1)} %pad_maximum_fusion.2.refs_5_), channel_id=1, source_target_pairs={{0,4},{4,0},{8,12},{12,8},{16,20},{20,16},{24,28},{28,24},{1,5},{5... | collective-permute-start | bytes 589832 | tf_op jit(solution)/shard_map/ppermute | solution.py:329
  25.6 1.6 %collective-permute-start.9 = (bf16[4,128,256]{2,1,0:T(8,128)(2,1)S(1)}, bf16[4,128,256]{2,1,0:T(8,128)(2,1)S(1)}, u32[]{:S(2)}, u32[]{:S(2)}) collective-permute-start(bf16[4,128,256]{2,1,0:T(8,128)(2,1)S(1)} %pad_maximum_fusion), channel_id=1, source_target_pairs={{0,2},{1,3},{2,0},{3,1},{4,6},{5,7},{6,4},{7,5},{8,10},{9,11},{10,... | collective-permute-start | bytes 786440 | tf_op jit(solution)/shard_map/ppermute | solution.py:329
  28.3 2.7 %shard_map.83 = (bf16[8,256,128]{2,1,0:T(8,128)(2,1)}, bf16[8,128,256]{2,1,0:T(8,128)(2,1)}) custom-call(bf16[8,16,128]{2,1,0:T(8,128)(2,1)} %copy-done.2), custom_call_target="tpu_custom_call" | custom-call | flops 4000000000 | bytes 2097152 | tf_op jit(solution)/shard_map/pallas_call | solution.py:132
  31.7 2.3 %collective-permute-done.9.refs_9_ = bf16[4,128,256]{2,1,0:T(8,128)(2,1)S(1)} collective-permute-done((bf16[4,128,256]{2,1,0:T(8,128)(2,1)S(1)}, bf16[4,128,256]{2,1,0:T(8,128)(2,1)S(1)}, u32[]{:S(2)}, u32[]{:S(2)}) %collective-permute-start.9) | collective-permute-done | bytes 262176 | tf_op jit(solution)/shard_map/ppermute | solution.py:329
  34.0 1.5 %collective-permute-start.12 = (bf16[3,128,256]{2,1,0:T(8,128)(2,1)S(1)}, bf16[3,128,256]{2,1,0:T(8,128)(2,1)S(1)}, u32[]{:S(2)}, u32[]{:S(2)}) collective-permute-start(bf16[3,128,256]{2,1,0:T(8,128)(2,1)S(1)} %collective-permute-done.10.refs_10_), channel_id=1, source_target_pairs={{0,2},{1,3},{2,0},{3,1},{4,6},{5,7},{6,4},{7,5},{8,10},{9,11},{10,... | collective-permute-start | bytes 589832 | tf_op jit(solution)/shard_map/ppermute | solution.py:329
  36.5 3.6 %collective-permute-done.12.refs_12_ = bf16[3,128,256]{2,1,0:T(8,128)(2,1)S(1)} collective-permute-done((bf16[3,128,256]{2,1,0:T(8,128)(2,1)S(1)}, bf16[3,128,256]{2,1,0:T(8,128)(2,1)S(1)}, u32[]{:S(2)}, u32[]{:S(2)}) %collective-permute-start.12) | collective-permute-done | bytes 196640 | tf_op jit(solution)/shard_map/ppermute | solution.py:329
  40.2 1.4 %collective-permute-done.21.refs_21_ = bf16[3,128,256]{2,1,0:T(8,128)(2,1)S(1)} collective-permute-done((bf16[3,128,256]{2,1,0:T(8,128)(2,1)S(1)}, bf16[3,128,256]{2,1,0:T(8,128)(2,1)S(1)}, u32[]{:S(2)}, u32[]{:S(2)}) %collective-permute-start.21) | collective-permute-done | bytes 196640 | tf_op jit(solution)/shard_map/ppermute | solution.py:329
  41.6 20.3 %shard_map.84 = (bf16[4,4,112,256]{3,2,1,0:T(8,128)(2,1)S(1)}, bf16[4,4,112,256]{3,2,1,0:T(8,128)(2,1)S(1)}, bf16[4,2,16,1024]{3,2,1,0:T(8,128)(2,1)S(1)}, bf16[...) custom-call(bf16[8,256,128]{2,1,0:T(8,128)(2,1)} %get-tuple-element.48.re, ...), custom_call_target="tpu_custom_call" | custom-call | flops 4831838208 | bytes 46137344 | tf_op jit(solution)/shard_map/pallas_call | solution.py:299
  62.6 1.8 %collective-permute-done.23 = bf16[4,4,112,256]{3,2,1,0:T(8,128)(2,1)S(1)} collective-permute-done((bf16[4,4,112,256]{3,2,1,0:T(8,128)(2,1)S(1)}, bf16[4,4,112,256]{3,2,1,0:T(8,128)(2,1)S(1)}, u32[]{:S(2)}, u32[]{:S(2)}) %collective-permute-start.23) | collective-permute-done | bytes 917536 | tf_op jit(solution)/shard_map/ppermute | solution.py:329
  64.7 1.6 %collective-permute-start.24 = (bf16[2,4,112,256]{3,2,1,0:T(8,128)(2,1)S(1)}, bf16[2,4,112,256]{3,2,1,0:T(8,128)(2,1)S(1)}, u32[]{:S(2)}, u32[]{:S(2)}) collective-permute-start(bf16[2,4,112,256]{3,2,1,0:T(8,128)(2,1)S(1)} %get-tuple-element.64), channel_id=1, source_target_pairs={{0,2},{1,3},{2,0},{3,1},{4,6},{5,7},{6,4},{7,5},{8,10},{9,11},{10,... | collective-permute-start | bytes 1376264 | tf_op jit(solution)/shard_map/ppermute | solution.py:329
  66.9 2.8 %collective-permute-start.29 = (bf16[2,16,1024]{2,1,0:T(8,128)(2,1)S(1)}, bf16[2,16,1024]{2,1,0:T(8,128)(2,1)S(1)}, u32[]{:S(2)}, u32[]{:S(2)}) collective-permute-start(bf16[2,16,1024]{2,1,0:T(8,128)(2,1)S(1)} %get-tuple-element.82), channel_id=1, source_target_pairs={{0,24},{4,28},{8,16},{12,20},{16,8},{20,12},{24,0},{28,4},{1,25},{... | collective-permute-start | bytes 196616 | tf_op jit(solution)/shard_map/ppermute | solution.py:329
  69.7 1.6 %collective-permute-start.27 = (bf16[2,16,1024]{2,1,0:T(8,128)(2,1)S(1)}, bf16[2,16,1024]{2,1,0:T(8,128)(2,1)S(1)}, u32[]{:S(2)}, u32[]{:S(2)}) collective-permute-start(bf16[2,16,1024]{2,1,0:T(8,128)(2,1)S(1)} %get-tuple-element.84), channel_id=1, source_target_pairs={{0,8},{4,12},{8,0},{12,4},{16,24},{20,28},{24,16},{28,20},{1,9},{5... | collective-permute-start | bytes 196616 | tf_op jit(solution)/shard_map/ppermute | solution.py:329
  71.3 6.0 %collective-permute-done.24 = bf16[2,4,112,256]{3,2,1,0:T(8,128)(2,1)S(1)} collective-permute-done((bf16[2,4,112,256]{3,2,1,0:T(8,128)(2,1)S(1)}, bf16[2,4,112,256]{3,2,1,0:T(8,128)(2,1)S(1)}, u32[]{:S(2)}, u32[]{:S(2)}) %collective-permute-start.24) | collective-permute-done | bytes 458784 | tf_op jit(solution)/shard_map/ppermute | solution.py:329
  77.3 1.2 %collective-permute-done.25 = bf16[2,4,112,256]{3,2,1,0:T(8,128)(2,1)S(1)} collective-permute-done((bf16[2,4,112,256]{3,2,1,0:T(8,128)(2,1)S(1)}, bf16[2,4,112,256]{3,2,1,0:T(8,128)(2,1)S(1)}, u32[]{:S(2)}, u32[]{:S(2)}) %collective-permute-start.25) | collective-permute-done | bytes 458784 | tf_op jit(solution)/shard_map/ppermute | solution.py:329
  79.4 1.5 %collective-permute-start.30 = (bf16[4,112,256]{2,1,0:T(8,128)(2,1)S(1)}, bf16[4,112,256]{2,1,0:T(8,128)(2,1)S(1)}, u32[]{:S(2)}, u32[]{:S(2)}) collective-permute-start(bf16[4,112,256]{2,1,0:T(8,128)(2,1)S(1)} %get-tuple-element.68), channel_id=1, source_target_pairs={{0,4},{4,0},{8,12},{12,8},{16,20},{20,16},{24,28},{28,24},{1,5},{5... | collective-permute-start | bytes 688136 | tf_op jit(solution)/shard_map/ppermute | solution.py:329
  81.4 1.8 %collective-permute-done.35 = bf16[16,1024]{1,0:T(8,128)(2,1)S(1)} collective-permute-done((bf16[16,1024]{1,0:T(8,128)(2,1)S(1)}, bf16[16,1024]{1,0:T(8,128)(2,1)S(1)}, u32[]{:S(2)}, u32[]{:S(2)}) %collective-permute-start.35) | collective-permute-done | bytes 32800 | tf_op jit(solution)/shard_map/ppermute | solution.py:329
  83.8 2.2 %collective-permute-done.30 = bf16[4,112,256]{2,1,0:T(8,128)(2,1)S(1)} collective-permute-done((bf16[4,112,256]{2,1,0:T(8,128)(2,1)S(1)}, bf16[4,112,256]{2,1,0:T(8,128)(2,1)S(1)}, u32[]{:S(2)}, u32[]{:S(2)}) %collective-permute-start.30) | collective-permute-done | bytes 229408 | tf_op jit(solution)/shard_map/ppermute | solution.py:329
  86.1 0.9 collective-permute-done.31
  87.3 2.1 %collective-permute-start.32 = (bf16[112,512]{1,0:T(8,128)(2,1)S(1)}, bf16[112,512]{1,0:T(8,128)(2,1)S(1)}, u32[]{:S(2)}, u32[]{:S(2)}) collective-permute-start(bf16[112,512]{1,0:T(8,128)(2,1)S(1)} %get-tuple-element.79), channel_id=1, source_target_pairs={{0,24},{4,28},{8,16},{12,20},{16,8},{20,12},{24,0},{28,4},{1,25},{... | collective-permute-start | bytes 344072 | tf_op jit(solution)/shard_map/ppermute | solution.py:329
  89.5 2.3 %collective-permute-start.34 = (bf16[112,512]{1,0:T(8,128)(2,1)S(1)}, bf16[112,512]{1,0:T(8,128)(2,1)S(1)}, u32[]{:S(2)}, u32[]{:S(2)}) collective-permute-start(bf16[112,512]{1,0:T(8,128)(2,1)S(1)} %get-tuple-element.81), channel_id=1, source_target_pairs={{0,8},{4,12},{8,0},{12,4},{16,24},{20,28},{24,16},{28,20},{1,9},{5... | collective-permute-start | bytes 344072 | tf_op jit(solution)/shard_map/ppermute | solution.py:329
  91.8 2.5 %collective-permute-done.32 = bf16[112,512]{1,0:T(8,128)(2,1)S(1)} collective-permute-done((bf16[112,512]{1,0:T(8,128)(2,1)S(1)}, bf16[112,512]{1,0:T(8,128)(2,1)S(1)}, u32[]{:S(2)}, u32[]{:S(2)}) %collective-permute-start.32) | collective-permute-done | bytes 114720 | tf_op jit(solution)/shard_map/ppermute | solution.py:329
  94.3 3.5 %collective-permute-done.33 = bf16[112,512]{1,0:T(8,128)(2,1)S(1)} collective-permute-done((bf16[112,512]{1,0:T(8,128)(2,1)S(1)}, bf16[112,512]{1,0:T(8,128)(2,1)S(1)}, u32[]{:S(2)}, u32[]{:S(2)}) %collective-permute-start.33) | collective-permute-done | bytes 114720 | tf_op jit(solution)/shard_map/ppermute | solution.py:329
  (78 shorter events, 9.0 us)
Async XLA Ops:
  2.5 8.1 %collective-permute-start.2 = (bf16[144,256]{1,0:T(8,128)(2,1)}, bf16[144,256]{1,0:T(8,128)(2,1)S(1)}, u32[]{:S(2)}, u32[]{:S(2)}) collective-permute-start(bf16[144,256]{1,0:T(8,128)(2,1)} %get-tuple-element.41), channel_id=1, source_target_pairs={{0,24},{4,28},{8,16},{12,20},{16,8},{20,12},{24,0},{28,4},{1,25},{... | collective-permute-start | bytes 221192 | tf_op jit(solution)/shard_map/ppermute | solution.py:329
  7.5 6.4 %collective-permute-start.1 = (bf16[144,256]{1,0:T(8,128)(2,1)}, bf16[144,256]{1,0:T(8,128)(2,1)S(1)}, u32[]{:S(2)}, u32[]{:S(2)}) collective-permute-start(bf16[144,256]{1,0:T(8,128)(2,1)} %get-tuple-element.41), channel_id=1, source_target_pairs={{0,16},{4,20},{8,24},{12,28},{16,0},{20,4},{24,8},{28,12},{1,17},{... | collective-permute-start | bytes 221192 | tf_op jit(solution)/shard_map/ppermute | solution.py:329
  7.5 6.4 %collective-permute-start = (bf16[144,256]{1,0:T(8,128)(2,1)}, bf16[144,256]{1,0:T(8,128)(2,1)S(1)}, u32[]{:S(2)}, u32[]{:S(2)}) collective-permute-start(bf16[144,256]{1,0:T(8,128)(2,1)} %get-tuple-element.41), channel_id=1, source_target_pairs={{0,8},{4,12},{8,0},{12,4},{16,24},{20,28},{24,16},{28,20},{1,9},{5... | collective-permute-start | bytes 221192 | tf_op jit(solution)/shard_map/ppermute | solution.py:329
  8.2 6.8 %collective-permute-start.3 = (bf16[1,144,768]{2,1,0:T(8,128)(2,1)}, bf16[1,144,768]{2,1,0:T(8,128)(2,1)S(1)}, u32[]{:S(2)}, u32[]{:S(2)}) collective-permute-start(bf16[1,144,768]{2,1,0:T(8,128)(2,1)} %bitcast.67), channel_id=1, source_target_pairs={{0,4},{4,0},{8,12},{12,8},{16,20},{20,16},{24,28},{28,24},{1,5},{5... | collective-permute-start | bytes 663560 | tf_op jit(solution)/shard_map/ppermute | solution.py:329
  15.0 7.5 %collective-permute-start.7 = (bf16[128,256]{1,0:T(8,128)(2,1)}, bf16[128,256]{1,0:T(8,128)(2,1)S(1)}, u32[]{:S(2)}, u32[]{:S(2)}) collective-permute-start(bf16[128,256]{1,0:T(8,128)(2,1)} %get-tuple-element.52), channel_id=1, source_target_pairs={{0,24},{4,28},{8,16},{12,20},{16,8},{20,12},{24,0},{28,4},{1,25},{... | collective-permute-start | bytes 196616 | tf_op jit(solution)/shard_map/ppermute | solution.py:329
  18.5 5.4 %collective-permute-start.6 = (bf16[128,256]{1,0:T(8,128)(2,1)}, bf16[128,256]{1,0:T(8,128)(2,1)S(1)}, u32[]{:S(2)}, u32[]{:S(2)}) collective-permute-start(bf16[128,256]{1,0:T(8,128)(2,1)} %get-tuple-element.52), channel_id=1, source_target_pairs={{0,16},{4,20},{8,24},{12,28},{16,0},{20,4},{24,8},{28,12},{1,17},{... | collective-permute-start | bytes 196616 | tf_op jit(solution)/shard_map/ppermute | solution.py:329
  18.5 5.4 %collective-permute-start.5 = (bf16[128,256]{1,0:T(8,128)(2,1)}, bf16[128,256]{1,0:T(8,128)(2,1)S(1)}, u32[]{:S(2)}, u32[]{:S(2)}) collective-permute-start(bf16[128,256]{1,0:T(8,128)(2,1)} %get-tuple-element.52), channel_id=1, source_target_pairs={{0,8},{4,12},{8,0},{12,4},{16,24},{20,28},{24,16},{28,20},{1,9},{5... | collective-permute-start | bytes 196616 | tf_op jit(solution)/shard_map/ppermute | solution.py:329
  19.4 8.2 %collective-permute-start.4 = (bf16[3,144,256]{2,1,0:T(8,128)(2,1)S(1)}, bf16[3,144,256]{2,1,0:T(8,128)(2,1)S(1)}, u32[]{:S(2)}, u32[]{:S(2)}) collective-permute-start(bf16[3,144,256]{2,1,0:T(8,128)(2,1)S(1)} %pad_maximum_fusion.1.refs_4_), channel_id=1, source_target_pairs={{0,4},{4,0},{8,12},{12,8},{16,20},{20,16},{24,28},{28,24},{1,5},{5... | collective-permute-start | bytes 663560 | tf_op jit(solution)/shard_map/ppermute | solution.py:329
  21.0 6.1 %collective-permute-start.8 = (bf16[3,128,256]{2,1,0:T(8,128)(2,1)S(1)}, bf16[3,128,256]{2,1,0:T(8,128)(2,1)S(1)}, u32[]{:S(2)}, u32[]{:S(2)}) collective-permute-start(bf16[3,128,256]{2,1,0:T(8,128)(2,1)S(1)} %slice.121), channel_id=1, source_target_pairs={{0,2},{1,3},{2,0},{3,1},{4,6},{5,7},{6,4},{7,5},{8,10},{9,11},{10,... | collective-permute-start | bytes 589832 | tf_op jit(solution)/shard_map/ppermute | solution.py:329
  23.9 7.2 %collective-permute-start.14 = (bf16[3,128,256]{2,1,0:T(8,128)(2,1)S(1)}, bf16[3,128,256]{2,1,0:T(8,128)(2,1)S(1)}, u32[]{:S(2)}, u32[]{:S(2)}) collective-permute-start(bf16[3,128,256]{2,1,0:T(8,128)(2,1)S(1)} %pad_maximum_fusion.2.refs_5_), channel_id=1, source_target_pairs={{0,1},{1,0},{2,3},{3,2},{4,5},{5,4},{6,7},{7,6},{8,9},{9,8},{10,11... | collective-permute-start | bytes 589832 | tf_op jit(solution)/shard_map/ppermute | solution.py:329
  23.9 7.8 %collective-permute-start.10 = (bf16[3,128,256]{2,1,0:T(8,128)(2,1)S(1)}, bf16[3,128,256]{2,1,0:T(8,128)(2,1)S(1)}, u32[]{:S(2)}, u32[]{:S(2)}) collective-permute-start(bf16[3,128,256]{2,1,0:T(8,128)(2,1)S(1)} %pad_maximum_fusion.2.refs_5_), channel_id=1, source_target_pairs={{0,4},{4,0},{8,12},{12,8},{16,20},{20,16},{24,28},{28,24},{1,5},{5... | collective-permute-start | bytes 589832 | tf_op jit(solution)/shard_map/ppermute | solution.py:329
  25.6 8.4 %collective-permute-start.9 = (bf16[4,128,256]{2,1,0:T(8,128)(2,1)S(1)}, bf16[4,128,256]{2,1,0:T(8,128)(2,1)S(1)}, u32[]{:S(2)}, u32[]{:S(2)}) collective-permute-start(bf16[4,128,256]{2,1,0:T(8,128)(2,1)S(1)} %pad_maximum_fusion), channel_id=1, source_target_pairs={{0,2},{1,3},{2,0},{3,1},{4,6},{5,7},{6,4},{7,5},{8,10},{9,11},{10,... | collective-permute-start | bytes 786440 | tf_op jit(solution)/shard_map/ppermute | solution.py:329
  27.1 8.4 %collective-permute-start.11 = (bf16[3,128,256]{2,1,0:T(8,128)(2,1)S(1)}, bf16[3,128,256]{2,1,0:T(8,128)(2,1)S(1)}, u32[]{:S(2)}, u32[]{:S(2)}) collective-permute-start(bf16[3,128,256]{2,1,0:T(8,128)(2,1)S(1)} %collective-permute-done.8.refs_7_), channel_id=1, source_target_pairs={{0,4},{4,0},{8,12},{12,8},{16,20},{20,16},{24,28},{28,24},{1,5},{5... | collective-permute-start | bytes 589832 | tf_op jit(solution)/shard_map/ppermute | solution.py:329
  27.6 8.4 %collective-permute-start.13 = (bf16[3,144,256]{2,1,0:T(8,128)(2,1)S(1)}, bf16[3,144,256]{2,1,0:T(8,128)(2,1)S(1)}, u32[]{:S(2)}, u32[]{:S(2)}) collective-permute-start(bf16[3,144,256]{2,1,0:T(8,128)(2,1)S(1)} %pad_maximum_fusion.1.refs_4_), channel_id=1, source_target_pairs={{0,1},{1,0},{2,3},{3,2},{4,5},{5,4},{6,7},{7,6},{8,9},{9,8},{10,11... | collective-permute-start | bytes 663560 | tf_op jit(solution)/shard_map/ppermute | solution.py:329
  31.0 4.5 %collective-permute-start.16 = (bf16[3,128,256]{2,1,0:T(8,128)(2,1)S(1)}, bf16[3,128,256]{2,1,0:T(8,128)(2,1)S(1)}, u32[]{:S(2)}, u32[]{:S(2)}) collective-permute-start(bf16[3,128,256]{2,1,0:T(8,128)(2,1)S(1)} %collective-permute-done.8.refs_7_), channel_id=1, source_target_pairs={{0,1},{1,0},{2,3},{3,2},{4,5},{5,4},{6,7},{7,6},{8,9},{9,8},{10,11... | collective-permute-start | bytes 589832 | tf_op jit(solution)/shard_map/ppermute | solution.py:329
  31.7 4.4 %collective-permute-start.15 = (bf16[1,144,768]{2,1,0:T(8,128)(2,1)S(1)}, bf16[1,144,768]{2,1,0:T(8,128)(2,1)S(1)}, u32[]{:S(2)}, u32[]{:S(2)}) collective-permute-start(bf16[1,144,768]{2,1,0:T(8,128)(2,1)S(1)} %collective-permute-done.3.refs_6_), channel_id=1, source_target_pairs={{0,1},{1,0},{2,3},{3,2},{4,5},{5,4},{6,7},{7,6},{8,9},{9,8},{10,11... | collective-permute-start | bytes 663560 | tf_op jit(solution)/shard_map/ppermute | solution.py:329
  34.0 6.1 %collective-permute-start.12 = (bf16[3,128,256]{2,1,0:T(8,128)(2,1)S(1)}, bf16[3,128,256]{2,1,0:T(8,128)(2,1)S(1)}, u32[]{:S(2)}, u32[]{:S(2)}) collective-permute-start(bf16[3,128,256]{2,1,0:T(8,128)(2,1)S(1)} %collective-permute-done.10.refs_10_), channel_id=1, source_target_pairs={{0,2},{1,3},{2,0},{3,1},{4,6},{5,7},{6,4},{7,5},{8,10},{9,11},{10,... | collective-permute-start | bytes 589832 | tf_op jit(solution)/shard_map/ppermute | solution.py:329
  35.5 4.7 %collective-permute-start.18 = (bf16[4,128,256]{2,1,0:T(8,128)(2,1)S(1)}, bf16[4,128,256]{2,1,0:T(8,128)(2,1)S(1)}, u32[]{:S(2)}, u32[]{:S(2)}) collective-permute-start(bf16[4,128,256]{2,1,0:T(8,128)(2,1)S(1)} %collective-permute-done.9.refs_9_), channel_id=1, source_target_pairs={{0,1},{1,0},{2,3},{3,2},{4,5},{5,4},{6,7},{7,6},{8,9},{9,8},{10,11... | collective-permute-start | bytes 786440 | tf_op jit(solution)/shard_map/ppermute | solution.py:329
  35.5 4.6 %collective-permute-start.17 = (bf16[3,144,256]{2,1,0:T(8,128)(2,1)S(1)}, bf16[3,144,256]{2,1,0:T(8,128)(2,1)S(1)}, u32[]{:S(2)}, u32[]{:S(2)}) collective-permute-start(bf16[3,144,256]{2,1,0:T(8,128)(2,1)S(1)} %collective-permute-done.4.refs_8_), channel_id=1, source_target_pairs={{0,1},{1,0},{2,3},{3,2},{4,5},{5,4},{6,7},{7,6},{8,9},{9,8},{10,11... | collective-permute-start | bytes 663560 | tf_op jit(solution)/shard_map/ppermute | solution.py:329
  62.1 7.6 %collective-permute-start.22 = (bf16[4,4,112,256]{3,2,1,0:T(8,128)(2,1)S(1)}, bf16[4,4,112,256]{3,2,1,0:T(8,128)(2,1)S(1)}, u32[]{:S(2)}, u32[]{:S(2)}) collective-permute-start(bf16[4,4,112,256]{3,2,1,0:T(8,128)(2,1)S(1)} %get-tuple-element.60), channel_id=1, source_target_pairs={{0,1},{1,0},{2,3},{3,2},{4,5},{5,4},{6,7},{7,6},{8,9},{9,8},{10,11... | collective-permute-start | bytes 2752520 | tf_op jit(solution)/shard_map/ppermute | solution.py:329
  64.7 12.6 %collective-permute-start.24 = (bf16[2,4,112,256]{3,2,1,0:T(8,128)(2,1)S(1)}, bf16[2,4,112,256]{3,2,1,0:T(8,128)(2,1)S(1)}, u32[]{:S(2)}, u32[]{:S(2)}) collective-permute-start(bf16[2,4,112,256]{3,2,1,0:T(8,128)(2,1)S(1)} %get-tuple-element.64), channel_id=1, source_target_pairs={{0,2},{1,3},{2,0},{3,1},{4,6},{5,7},{6,4},{7,5},{8,10},{9,11},{10,... | collective-permute-start | bytes 1376264 | tf_op jit(solution)/shard_map/ppermute | solution.py:329
  66.3 12.3 %collective-permute-start.25 = (bf16[2,4,112,256]{3,2,1,0:T(8,128)(2,1)S(1)}, bf16[2,4,112,256]{3,2,1,0:T(8,128)(2,1)S(1)}, u32[]{:S(2)}, u32[]{:S(2)}) collective-permute-start(bf16[2,4,112,256]{3,2,1,0:T(8,128)(2,1)S(1)} %get-tuple-element.65), channel_id=1, source_target_pairs={{0,4},{4,0},{8,12},{12,8},{16,20},{20,16},{24,28},{28,24},{1,5},{5... | collective-permute-start | bytes 1376264 | tf_op jit(solution)/shard_map/ppermute | solution.py:329
  66.9 11.9 %collective-permute-start.29 = (bf16[2,16,1024]{2,1,0:T(8,128)(2,1)S(1)}, bf16[2,16,1024]{2,1,0:T(8,128)(2,1)S(1)}, u32[]{:S(2)}, u32[]{:S(2)}) collective-permute-start(bf16[2,16,1024]{2,1,0:T(8,128)(2,1)S(1)} %get-tuple-element.82), channel_id=1, source_target_pairs={{0,24},{4,28},{8,16},{12,20},{16,8},{20,12},{24,0},{28,4},{1,25},{... | collective-permute-start | bytes 196616 | tf_op jit(solution)/shard_map/ppermute | solution.py:329
  69.7 9.1 %collective-permute-start.28 = (bf16[2,16,1024]{2,1,0:T(8,128)(2,1)S(1)}, bf16[2,16,1024]{2,1,0:T(8,128)(2,1)S(1)}, u32[]{:S(2)}, u32[]{:S(2)}) collective-permute-start(bf16[2,16,1024]{2,1,0:T(8,128)(2,1)S(1)} %get-tuple-element.83), channel_id=1, source_target_pairs={{0,16},{4,20},{8,24},{12,28},{16,0},{20,4},{24,8},{28,12},{1,17},{... | collective-permute-start | bytes 196616 | tf_op jit(solution)/shard_map/ppermute | solution.py:329
  69.7 9.1 %collective-permute-start.27 = (bf16[2,16,1024]{2,1,0:T(8,128)(2,1)S(1)}, bf16[2,16,1024]{2,1,0:T(8,128)(2,1)S(1)}, u32[]{:S(2)}, u32[]{:S(2)}) collective-permute-start(bf16[2,16,1024]{2,1,0:T(8,128)(2,1)S(1)} %get-tuple-element.84), channel_id=1, source_target_pairs={{0,8},{4,12},{8,0},{12,4},{16,24},{20,28},{24,16},{28,20},{1,9},{5... | collective-permute-start | bytes 196616 | tf_op jit(solution)/shard_map/ppermute | solution.py:329
  78.8 4.4 %collective-permute-start.35 = (bf16[16,1024]{1,0:T(8,128)(2,1)S(1)}, bf16[16,1024]{1,0:T(8,128)(2,1)S(1)}, u32[]{:S(2)}, u32[]{:S(2)}) collective-permute-start(bf16[16,1024]{1,0:T(8,128)(2,1)S(1)} %slice_bitcast_fusion.4), channel_id=1, source_target_pairs={{0,4},{4,0},{8,12},{12,8},{16,20},{20,16},{24,28},{28,24},{1,5},{5... | collective-permute-start | bytes 98312 | tf_op jit(solution)/shard_map/ppermute | solution.py:329
  79.4 6.7 %collective-permute-start.30 = (bf16[4,112,256]{2,1,0:T(8,128)(2,1)S(1)}, bf16[4,112,256]{2,1,0:T(8,128)(2,1)S(1)}, u32[]{:S(2)}, u32[]{:S(2)}) collective-permute-start(bf16[4,112,256]{2,1,0:T(8,128)(2,1)S(1)} %get-tuple-element.68), channel_id=1, source_target_pairs={{0,4},{4,0},{8,12},{12,8},{16,20},{20,16},{24,28},{28,24},{1,5},{5... | collective-permute-start | bytes 688136 | tf_op jit(solution)/shard_map/ppermute | solution.py:329
  80.9 6.1 %collective-permute-start.31 = (bf16[4,112,256]{2,1,0:T(8,128)(2,1)S(1)}, bf16[4,112,256]{2,1,0:T(8,128)(2,1)S(1)}, u32[]{:S(2)}, u32[]{:S(2)}) collective-permute-start(bf16[4,112,256]{2,1,0:T(8,128)(2,1)S(1)} %get-tuple-element.69), channel_id=1, source_target_pairs={{0,2},{1,3},{2,0},{3,1},{4,6},{5,7},{6,4},{7,5},{8,10},{9,11},{10,... | collective-permute-start | bytes 688136 | tf_op jit(solution)/shard_map/ppermute | solution.py:329
  83.2 8.5 %collective-permute-start.36 = (bf16[16,512]{1,0:T(8,128)(2,1)S(1)}, bf16[16,512]{1,0:T(8,128)(2,1)S(1)}, u32[]{:S(2)}, u32[]{:S(2)}) collective-permute-start(bf16[16,512]{1,0:T(8,128)(2,1)S(1)} %pad_maximum_fusion.4), channel_id=1, source_target_pairs={{0,2},{1,3},{2,0},{3,1},{4,6},{5,7},{6,4},{7,5},{8,10},{9,11},{10,... | collective-permute-start | bytes 49160 | tf_op jit(solution)/shard_map/ppermute | solution.py:329
  87.3 7.0 %collective-permute-start.32 = (bf16[112,512]{1,0:T(8,128)(2,1)S(1)}, bf16[112,512]{1,0:T(8,128)(2,1)S(1)}, u32[]{:S(2)}, u32[]{:S(2)}) collective-permute-start(bf16[112,512]{1,0:T(8,128)(2,1)S(1)} %get-tuple-element.79), channel_id=1, source_target_pairs={{0,24},{4,28},{8,16},{12,20},{16,8},{20,12},{24,0},{28,4},{1,25},{... | collective-permute-start | bytes 344072 | tf_op jit(solution)/shard_map/ppermute | solution.py:329
  89.4 8.4 %collective-permute-start.33 = (bf16[112,512]{1,0:T(8,128)(2,1)S(1)}, bf16[112,512]{1,0:T(8,128)(2,1)S(1)}, u32[]{:S(2)}, u32[]{:S(2)}) collective-permute-start(bf16[112,512]{1,0:T(8,128)(2,1)S(1)} %get-tuple-element.80), channel_id=1, source_target_pairs={{0,16},{4,20},{8,24},{12,28},{16,0},{20,4},{24,8},{28,12},{1,17},{... | collective-permute-start | bytes 344072 | tf_op jit(solution)/shard_map/ppermute | solution.py:329
  89.5 8.4 %collective-permute-start.34 = (bf16[112,512]{1,0:T(8,128)(2,1)S(1)}, bf16[112,512]{1,0:T(8,128)(2,1)S(1)}, u32[]{:S(2)}, u32[]{:S(2)}) collective-permute-start(bf16[112,512]{1,0:T(8,128)(2,1)S(1)} %get-tuple-element.81), channel_id=1, source_target_pairs={{0,8},{4,12},{8,0},{12,4},{16,24},{20,28},{24,16},{28,20},{1,9},{5... | collective-permute-start | bytes 344072 | tf_op jit(solution)/shard_map/ppermute | solution.py:329
  (8 other events, 112.5 us)

commit v16 on v15

--- a/solution.py
+++ b/solution.py
@@ -196,7 +196,7 @@
     for e in range(min(RING, exp_dev)):
         for copy in in_copies(e):
             copy.start()
-    for e in range(exp_dev // 2):
+    for e in range(exp_dev):
         down_copy(e).start()
     tables[1].start()
     quarters = [slice(2 * q * width, 2 * (q + 1) * width) for q in range(4)]
@@ -229,7 +229,6 @@
         ]
         for e, (gate_val, up_val) in zip(experts, both):
             hidden[e] = (gate_val / (1.0 + jnp.exp(-gate_val)) * up_val).astype(jnp.bfloat16)
-        down_copy(exp_dev // 2 + pair).start()
         for e in experts:
 
             @pl.when(e + RING < exp_dev)

time: 98.8 us -> 100 us (1.012)
  Pallas kernels: 25.5 us -> 26.6 us
    pallas_call x1, Pallas kernels: 20.3 us -> 21.4 us  [moe_partial(): pl.pallas_call(functools.partial(moe_kernel, n_pieces), out_shape=outs, i...]
where the time goes in v16:
time: 100 us; the launch traced here: 99.7 us
  starting transfers between devices  36.5 us (36%)
  waiting for transfers between devices  33.4 us (33%)
  Pallas kernels  26.6 us (27%)
  other arithmetic  1.66 us (2%)
  local copies, waits for them, and re-layouts  1.4 us (1%)
    ppermute x37, starting transfers between devices, swap(): return lax.ppermute(value, axis, [(i, i ^ distance) for i in range(size)])  36.5 us
    ppermute x37, waiting for transfers between devices, swap(): return lax.ppermute(value, axis, [(i, i ^ distance) for i in range(size)])  33.4 us
    pallas_call x1, Pallas kernels, moe_partial(): pl.pallas_call(functools.partial(moe_kernel, n_pieces), out_shape=outs, i...  21.4 us
    pallas_call x1, Pallas kernels, route(): pl.pallas_call(functools.partial(route_kernel, exp_dev), out_shape=[jax.S...  2.72 us
    pallas_call x1, Pallas kernels, norm_and_base(): pl.pallas_call(norm_kernel, out_shape=[jax.ShapeDtypeStruct((tok_rows, mo...  2.46 us
  transfers between devices with their start and end apart: 37, of which 15 were waited for; matrix products, arithmetic and copies ran while one was open for 2% of the time, Pallas kernels for 3%

profile of v16, /device:TPU:0, one launch (start us, length us, event | category | flops | bytes accessed | tf_op | source)
XLA Modules:
  0.0 99.7 jit_solution(10726879355019570412)
XLA Ops:
  0.0 2.5 %shard_map.82 = (bf16[128,2048]{1,0:T(8,128)(2,1)}, bf16[144,256]{1,0:T(8,128)(2,1)}, bf16[128,256]{1,0:T(8,128)(2,1)}, bf16[144,768]{1,0:T(8,128)(2,1)}, f32[1,...) custom-call(bf16[128,2048]{1,0:T(8,128)(2,1)} %tokens_ref.1, f32[1,2048]{1,0:T(1,128)} %bitcast.63, ...), custom_call_target="tpu_custom_call" | custom-call | tf_op jit(solution)/shard_map/pallas_call | solution.py:74
  2.5 5.1 %collective-permute-start.2 = (bf16[144,256]{1,0:T(8,128)(2,1)}, bf16[144,256]{1,0:T(8,128)(2,1)S(1)}, u32[]{:S(2)}, u32[]{:S(2)}) collective-permute-start(bf16[144,256]{1,0:T(8,128)(2,1)} %get-tuple-element.41), channel_id=1, source_target_pairs={{0,24},{4,28},{8,16},{12,20},{16,8},{20,12},{24,0},{28,4},{1,25},{... | collective-permute-start | bytes 221192 | tf_op jit(solution)/shard_map/ppermute | solution.py:328
  8.2 1.7 %collective-permute-start.3 = (bf16[1,144,768]{2,1,0:T(8,128)(2,1)}, bf16[1,144,768]{2,1,0:T(8,128)(2,1)S(1)}, u32[]{:S(2)}, u32[]{:S(2)}) collective-permute-start(bf16[1,144,768]{2,1,0:T(8,128)(2,1)} %bitcast.67), channel_id=1, source_target_pairs={{0,4},{4,0},{8,12},{12,8},{16,20},{20,16},{24,28},{28,24},{1,5},{5... | collective-permute-start | bytes 663560 | tf_op jit(solution)/shard_map/ppermute | solution.py:328
  10.5 3.4 %collective-permute-done.1 = bf16[144,256]{1,0:T(8,128)(2,1)S(1)} collective-permute-done((bf16[144,256]{1,0:T(8,128)(2,1)}, bf16[144,256]{1,0:T(8,128)(2,1)S(1)}, u32[]{:S(2)}, u32[]{:S(2)}) %collective-permute-start.1) | collective-permute-done | bytes 73760 | tf_op jit(solution)/shard_map/ppermute | solution.py:328
  14.0 1.0 %collective-permute-done.3.refs_6_ = bf16[1,144,768]{2,1,0:T(8,128)(2,1)S(1)} collective-permute-done((bf16[1,144,768]{2,1,0:T(8,128)(2,1)}, bf16[1,144,768]{2,1,0:T(8,128)(2,1)S(1)}, u32[]{:S(2)}, u32[]{:S(2)}) %collective-permute-start.3) | collective-permute-done | bytes 221216 | tf_op jit(solution)/shard_map/ppermute | solution.py:328
  15.0 3.5 %collective-permute-start.7 = (bf16[128,256]{1,0:T(8,128)(2,1)}, bf16[128,256]{1,0:T(8,128)(2,1)S(1)}, u32[]{:S(2)}, u32[]{:S(2)}) collective-permute-start(bf16[128,256]{1,0:T(8,128)(2,1)} %get-tuple-element.52), channel_id=1, source_target_pairs={{0,24},{4,28},{8,16},{12,20},{16,8},{20,12},{24,0},{28,4},{1,25},{... | collective-permute-start | bytes 196616 | tf_op jit(solution)/shard_map/ppermute | solution.py:328
  18.5 0.9 collective-permute-start.5
  19.4 1.6 %collective-permute-start.4 = (bf16[3,144,256]{2,1,0:T(8,128)(2,1)S(1)}, bf16[3,144,256]{2,1,0:T(8,128)(2,1)S(1)}, u32[]{:S(2)}, u32[]{:S(2)}) collective-permute-start(bf16[3,144,256]{2,1,0:T(8,128)(2,1)S(1)} %pad_maximum_fusion.1.refs_4_), channel_id=1, source_target_pairs={{0,4},{4,0},{8,12},{12,8},{16,20},{20,16},{24,28},{28,24},{1,5},{5... | collective-permute-start | bytes 663560 | tf_op jit(solution)/shard_map/ppermute | solution.py:328
  21.0 1.5 %collective-permute-start.8 = (bf16[3,128,256]{2,1,0:T(8,128)(2,1)S(1)}, bf16[3,128,256]{2,1,0:T(8,128)(2,1)S(1)}, u32[]{:S(2)}, u32[]{:S(2)}) collective-permute-start(bf16[3,128,256]{2,1,0:T(8,128)(2,1)S(1)} %slice.121), channel_id=1, source_target_pairs={{0,2},{1,3},{2,0},{3,1},{4,6},{5,7},{6,4},{7,5},{8,10},{9,11},{10,... | collective-permute-start | bytes 589832 | tf_op jit(solution)/shard_map/ppermute | solution.py:328
  22.5 1.3 %collective-permute-done.6 = bf16[128,256]{1,0:T(8,128)(2,1)S(1)} collective-permute-done((bf16[128,256]{1,0:T(8,128)(2,1)}, bf16[128,256]{1,0:T(8,128)(2,1)S(1)}, u32[]{:S(2)}, u32[]{:S(2)}) %collective-permute-start.6) | collective-permute-done | bytes 65568 | tf_op jit(solution)/shard_map/ppermute | solution.py:328
  23.9 1.6 %collective-permute-start.10 = (bf16[3,128,256]{2,1,0:T(8,128)(2,1)S(1)}, bf16[3,128,256]{2,1,0:T(8,128)(2,1)S(1)}, u32[]{:S(2)}, u32[]{:S(2)}) collective-permute-start(bf16[3,128,256]{2,1,0:T(8,128)(2,1)S(1)} %pad_maximum_fusion.2.refs_5_), channel_id=1, source_target_pairs={{0,4},{4,0},{8,12},{12,8},{16,20},{20,16},{24,28},{28,24},{1,5},{5... | collective-permute-start | bytes 589832 | tf_op jit(solution)/shard_map/ppermute | solution.py:328
  25.6 1.6 %collective-permute-start.9 = (bf16[4,128,256]{2,1,0:T(8,128)(2,1)S(1)}, bf16[4,128,256]{2,1,0:T(8,128)(2,1)S(1)}, u32[]{:S(2)}, u32[]{:S(2)}) collective-permute-start(bf16[4,128,256]{2,1,0:T(8,128)(2,1)S(1)} %pad_maximum_fusion), channel_id=1, source_target_pairs={{0,2},{1,3},{2,0},{3,1},{4,6},{5,7},{6,4},{7,5},{8,10},{9,11},{10,... | collective-permute-start | bytes 786440 | tf_op jit(solution)/shard_map/ppermute | solution.py:328
  28.3 2.7 %shard_map.83 = (bf16[8,256,128]{2,1,0:T(8,128)(2,1)}, bf16[8,128,256]{2,1,0:T(8,128)(2,1)}) custom-call(bf16[8,16,128]{2,1,0:T(8,128)(2,1)} %copy-done.2), custom_call_target="tpu_custom_call" | custom-call | flops 4000000000 | bytes 2097152 | tf_op jit(solution)/shard_map/pallas_call | solution.py:132
  31.7 2.3 %collective-permute-done.9.refs_9_ = bf16[4,128,256]{2,1,0:T(8,128)(2,1)S(1)} collective-permute-done((bf16[4,128,256]{2,1,0:T(8,128)(2,1)S(1)}, bf16[4,128,256]{2,1,0:T(8,128)(2,1)S(1)}, u32[]{:S(2)}, u32[]{:S(2)}) %collective-permute-start.9) | collective-permute-done | bytes 262176 | tf_op jit(solution)/shard_map/ppermute | solution.py:328
  34.0 1.5 %collective-permute-start.12 = (bf16[3,128,256]{2,1,0:T(8,128)(2,1)S(1)}, bf16[3,128,256]{2,1,0:T(8,128)(2,1)S(1)}, u32[]{:S(2)}, u32[]{:S(2)}) collective-permute-start(bf16[3,128,256]{2,1,0:T(8,128)(2,1)S(1)} %collective-permute-done.10.refs_10_), channel_id=1, source_target_pairs={{0,2},{1,3},{2,0},{3,1},{4,6},{5,7},{6,4},{7,5},{8,10},{9,11},{10,... | collective-permute-start | bytes 589832 | tf_op jit(solution)/shard_map/ppermute | solution.py:328
  36.5 3.6 %collective-permute-done.12.refs_12_ = bf16[3,128,256]{2,1,0:T(8,128)(2,1)S(1)} collective-permute-done((bf16[3,128,256]{2,1,0:T(8,128)(2,1)S(1)}, bf16[3,128,256]{2,1,0:T(8,128)(2,1)S(1)}, u32[]{:S(2)}, u32[]{:S(2)}) %collective-permute-start.12) | collective-permute-done | bytes 196640 | tf_op jit(solution)/shard_map/ppermute | solution.py:328
  40.2 1.4 %collective-permute-done.21.refs_21_ = bf16[3,128,256]{2,1,0:T(8,128)(2,1)S(1)} collective-permute-done((bf16[3,128,256]{2,1,0:T(8,128)(2,1)S(1)}, bf16[3,128,256]{2,1,0:T(8,128)(2,1)S(1)}, u32[]{:S(2)}, u32[]{:S(2)}) %collective-permute-start.21) | collective-permute-done | bytes 196640 | tf_op jit(solution)/shard_map/ppermute | solution.py:328
  41.6 21.4 %shard_map.84 = (bf16[4,4,112,256]{3,2,1,0:T(8,128)(2,1)S(1)}, bf16[4,4,112,256]{3,2,1,0:T(8,128)(2,1)S(1)}, bf16[4,2,16,1024]{3,2,1,0:T(8,128)(2,1)S(1)}, bf16[...) custom-call(bf16[8,256,128]{2,1,0:T(8,128)(2,1)} %get-tuple-element.48.re, ...), custom_call_target="tpu_custom_call" | custom-call | flops 4831838208 | bytes 46137344 | tf_op jit(solution)/shard_map/pallas_call | solution.py:298
  63.7 1.8 %collective-permute-done.23 = bf16[4,4,112,256]{3,2,1,0:T(8,128)(2,1)S(1)} collective-permute-done((bf16[4,4,112,256]{3,2,1,0:T(8,128)(2,1)S(1)}, bf16[4,4,112,256]{3,2,1,0:T(8,128)(2,1)S(1)}, u32[]{:S(2)}, u32[]{:S(2)}) %collective-permute-start.23) | collective-permute-done | bytes 917536 | tf_op jit(solution)/shard_map/ppermute | solution.py:328
  65.8 1.6 %collective-permute-start.24 = (bf16[2,4,112,256]{3,2,1,0:T(8,128)(2,1)S(1)}, bf16[2,4,112,256]{3,2,1,0:T(8,128)(2,1)S(1)}, u32[]{:S(2)}, u32[]{:S(2)}) collective-permute-start(bf16[2,4,112,256]{3,2,1,0:T(8,128)(2,1)S(1)} %get-tuple-element.64), channel_id=1, source_target_pairs={{0,2},{1,3},{2,0},{3,1},{4,6},{5,7},{6,4},{7,5},{8,10},{9,11},{10,... | collective-permute-start | bytes 1376264 | tf_op jit(solution)/shard_map/ppermute | solution.py:328
  68.0 2.8 %collective-permute-start.29 = (bf16[2,16,1024]{2,1,0:T(8,128)(2,1)S(1)}, bf16[2,16,1024]{2,1,0:T(8,128)(2,1)S(1)}, u32[]{:S(2)}, u32[]{:S(2)}) collective-permute-start(bf16[2,16,1024]{2,1,0:T(8,128)(2,1)S(1)} %get-tuple-element.82), channel_id=1, source_target_pairs={{0,24},{4,28},{8,16},{12,20},{16,8},{20,12},{24,0},{28,4},{1,25},{... | collective-permute-start | bytes 196616 | tf_op jit(solution)/shard_map/ppermute | solution.py:328
  70.8 1.7 %collective-permute-start.27 = (bf16[2,16,1024]{2,1,0:T(8,128)(2,1)S(1)}, bf16[2,16,1024]{2,1,0:T(8,128)(2,1)S(1)}, u32[]{:S(2)}, u32[]{:S(2)}) collective-permute-start(bf16[2,16,1024]{2,1,0:T(8,128)(2,1)S(1)} %get-tuple-element.84), channel_id=1, source_target_pairs={{0,8},{4,12},{8,0},{12,4},{16,24},{20,28},{24,16},{28,20},{1,9},{5... | collective-permute-start | bytes 196616 | tf_op jit(solution)/shard_map/ppermute | solution.py:328
  72.5 6.0 %collective-permute-done.24 = bf16[2,4,112,256]{3,2,1,0:T(8,128)(2,1)S(1)} collective-permute-done((bf16[2,4,112,256]{3,2,1,0:T(8,128)(2,1)S(1)}, bf16[2,4,112,256]{3,2,1,0:T(8,128)(2,1)S(1)}, u32[]{:S(2)}, u32[]{:S(2)}) %collective-permute-start.24) | collective-permute-done | bytes 458784 | tf_op jit(solution)/shard_map/ppermute | solution.py:328
  78.5 1.2 %collective-permute-done.25 = bf16[2,4,112,256]{3,2,1,0:T(8,128)(2,1)S(1)} collective-permute-done((bf16[2,4,112,256]{3,2,1,0:T(8,128)(2,1)S(1)}, bf16[2,4,112,256]{3,2,1,0:T(8,128)(2,1)S(1)}, u32[]{:S(2)}, u32[]{:S(2)}) %collective-permute-start.25) | collective-permute-done | bytes 458784 | tf_op jit(solution)/shard_map/ppermute | solution.py:328
  80.5 1.5 %collective-permute-start.30 = (bf16[4,112,256]{2,1,0:T(8,128)(2,1)S(1)}, bf16[4,112,256]{2,1,0:T(8,128)(2,1)S(1)}, u32[]{:S(2)}, u32[]{:S(2)}) collective-permute-start(bf16[4,112,256]{2,1,0:T(8,128)(2,1)S(1)} %get-tuple-element.68), channel_id=1, source_target_pairs={{0,4},{4,0},{8,12},{12,8},{16,20},{20,16},{24,28},{28,24},{1,5},{5... | collective-permute-start | bytes 688136 | tf_op jit(solution)/shard_map/ppermute | solution.py:328
  82.6 1.8 %collective-permute-done.35 = bf16[16,1024]{1,0:T(8,128)(2,1)S(1)} collective-permute-done((bf16[16,1024]{1,0:T(8,128)(2,1)S(1)}, bf16[16,1024]{1,0:T(8,128)(2,1)S(1)}, u32[]{:S(2)}, u32[]{:S(2)}) %collective-permute-start.35) | collective-permute-done | bytes 32800 | tf_op jit(solution)/shard_map/ppermute | solution.py:328
  85.0 2.2 %collective-permute-done.30 = bf16[4,112,256]{2,1,0:T(8,128)(2,1)S(1)} collective-permute-done((bf16[4,112,256]{2,1,0:T(8,128)(2,1)S(1)}, bf16[4,112,256]{2,1,0:T(8,128)(2,1)S(1)}, u32[]{:S(2)}, u32[]{:S(2)}) %collective-permute-start.30) | collective-permute-done | bytes 229408 | tf_op jit(solution)/shard_map/ppermute | solution.py:328
  87.2 0.9 collective-permute-done.31
  88.4 2.1 %collective-permute-start.32 = (bf16[112,512]{1,0:T(8,128)(2,1)S(1)}, bf16[112,512]{1,0:T(8,128)(2,1)S(1)}, u32[]{:S(2)}, u32[]{:S(2)}) collective-permute-start(bf16[112,512]{1,0:T(8,128)(2,1)S(1)} %get-tuple-element.79), channel_id=1, source_target_pairs={{0,24},{4,28},{8,16},{12,20},{16,8},{20,12},{24,0},{28,4},{1,25},{... | collective-permute-start | bytes 344072 | tf_op jit(solution)/shard_map/ppermute | solution.py:328
  90.6 2.3 %collective-permute-start.34 = (bf16[112,512]{1,0:T(8,128)(2,1)S(1)}, bf16[112,512]{1,0:T(8,128)(2,1)S(1)}, u32[]{:S(2)}, u32[]{:S(2)}) collective-permute-start(bf16[112,512]{1,0:T(8,128)(2,1)S(1)} %get-tuple-element.81), channel_id=1, source_target_pairs={{0,8},{4,12},{8,0},{12,4},{16,24},{20,28},{24,16},{28,20},{1,9},{5... | collective-permute-start | bytes 344072 | tf_op jit(solution)/shard_map/ppermute | solution.py:328
  92.9 2.6 %collective-permute-done.32 = bf16[112,512]{1,0:T(8,128)(2,1)S(1)} collective-permute-done((bf16[112,512]{1,0:T(8,128)(2,1)S(1)}, bf16[112,512]{1,0:T(8,128)(2,1)S(1)}, u32[]{:S(2)}, u32[]{:S(2)}) %collective-permute-start.32) | collective-permute-done | bytes 114720 | tf_op jit(solution)/shard_map/ppermute | solution.py:328
  95.5 3.5 %collective-permute-done.33 = bf16[112,512]{1,0:T(8,128)(2,1)S(1)} collective-permute-done((bf16[112,512]{1,0:T(8,128)(2,1)S(1)}, bf16[112,512]{1,0:T(8,128)(2,1)S(1)}, u32[]{:S(2)}, u32[]{:S(2)}) %collective-permute-start.33) | collective-permute-done | bytes 114720 | tf_op jit(solution)/shard_map/ppermute | solution.py:328
  (78 shorter events, 9.0 us)
Async XLA Ops:
  2.5 8.1 %collective-permute-start.2 = (bf16[144,256]{1,0:T(8,128)(2,1)}, bf16[144,256]{1,0:T(8,128)(2,1)S(1)}, u32[]{:S(2)}, u32[]{:S(2)}) collective-permute-start(bf16[144,256]{1,0:T(8,128)(2,1)} %get-tuple-element.41), channel_id=1, source_target_pairs={{0,24},{4,28},{8,16},{12,20},{16,8},{20,12},{24,0},{28,4},{1,25},{... | collective-permute-start | bytes 221192 | tf_op jit(solution)/shard_map/ppermute | solution.py:328
  7.5 6.4 %collective-permute-start.1 = (bf16[144,256]{1,0:T(8,128)(2,1)}, bf16[144,256]{1,0:T(8,128)(2,1)S(1)}, u32[]{:S(2)}, u32[]{:S(2)}) collective-permute-start(bf16[144,256]{1,0:T(8,128)(2,1)} %get-tuple-element.41), channel_id=1, source_target_pairs={{0,16},{4,20},{8,24},{12,28},{16,0},{20,4},{24,8},{28,12},{1,17},{... | collective-permute-start | bytes 221192 | tf_op jit(solution)/shard_map/ppermute | solution.py:328
  7.5 6.4 %collective-permute-start = (bf16[144,256]{1,0:T(8,128)(2,1)}, bf16[144,256]{1,0:T(8,128)(2,1)S(1)}, u32[]{:S(2)}, u32[]{:S(2)}) collective-permute-start(bf16[144,256]{1,0:T(8,128)(2,1)} %get-tuple-element.41), channel_id=1, source_target_pairs={{0,8},{4,12},{8,0},{12,4},{16,24},{20,28},{24,16},{28,20},{1,9},{5... | collective-permute-start | bytes 221192 | tf_op jit(solution)/shard_map/ppermute | solution.py:328
  8.2 6.8 %collective-permute-start.3 = (bf16[1,144,768]{2,1,0:T(8,128)(2,1)}, bf16[1,144,768]{2,1,0:T(8,128)(2,1)S(1)}, u32[]{:S(2)}, u32[]{:S(2)}) collective-permute-start(bf16[1,144,768]{2,1,0:T(8,128)(2,1)} %bitcast.67), channel_id=1, source_target_pairs={{0,4},{4,0},{8,12},{12,8},{16,20},{20,16},{24,28},{28,24},{1,5},{5... | collective-permute-start | bytes 663560 | tf_op jit(solution)/shard_map/ppermute | solution.py:328
  15.0 7.5 %collective-permute-start.7 = (bf16[128,256]{1,0:T(8,128)(2,1)}, bf16[128,256]{1,0:T(8,128)(2,1)S(1)}, u32[]{:S(2)}, u32[]{:S(2)}) collective-permute-start(bf16[128,256]{1,0:T(8,128)(2,1)} %get-tuple-element.52), channel_id=1, source_target_pairs={{0,24},{4,28},{8,16},{12,20},{16,8},{20,12},{24,0},{28,4},{1,25},{... | collective-permute-start | bytes 196616 | tf_op jit(solution)/shard_map/ppermute | solution.py:328
  18.5 5.4 %collective-permute-start.6 = (bf16[128,256]{1,0:T(8,128)(2,1)}, bf16[128,256]{1,0:T(8,128)(2,1)S(1)}, u32[]{:S(2)}, u32[]{:S(2)}) collective-permute-start(bf16[128,256]{1,0:T(8,128)(2,1)} %get-tuple-element.52), channel_id=1, source_target_pairs={{0,16},{4,20},{8,24},{12,28},{16,0},{20,4},{24,8},{28,12},{1,17},{... | collective-permute-start | bytes 196616 | tf_op jit(solution)/shard_map/ppermute | solution.py:328
  18.5 5.4 %collective-permute-start.5 = (bf16[128,256]{1,0:T(8,128)(2,1)}, bf16[128,256]{1,0:T(8,128)(2,1)S(1)}, u32[]{:S(2)}, u32[]{:S(2)}) collective-permute-start(bf16[128,256]{1,0:T(8,128)(2,1)} %get-tuple-element.52), channel_id=1, source_target_pairs={{0,8},{4,12},{8,0},{12,4},{16,24},{20,28},{24,16},{28,20},{1,9},{5... | collective-permute-start | bytes 196616 | tf_op jit(solution)/shard_map/ppermute | solution.py:328
  19.4 8.2 %collective-permute-start.4 = (bf16[3,144,256]{2,1,0:T(8,128)(2,1)S(1)}, bf16[3,144,256]{2,1,0:T(8,128)(2,1)S(1)}, u32[]{:S(2)}, u32[]{:S(2)}) collective-permute-start(bf16[3,144,256]{2,1,0:T(8,128)(2,1)S(1)} %pad_maximum_fusion.1.refs_4_), channel_id=1, source_target_pairs={{0,4},{4,0},{8,12},{12,8},{16,20},{20,16},{24,28},{28,24},{1,5},{5... | collective-permute-start | bytes 663560 | tf_op jit(solution)/shard_map/ppermute | solution.py:328
  21.0 6.1 %collective-permute-start.8 = (bf16[3,128,256]{2,1,0:T(8,128)(2,1)S(1)}, bf16[3,128,256]{2,1,0:T(8,128)(2,1)S(1)}, u32[]{:S(2)}, u32[]{:S(2)}) collective-permute-start(bf16[3,128,256]{2,1,0:T(8,128)(2,1)S(1)} %slice.121), channel_id=1, source_target_pairs={{0,2},{1,3},{2,0},{3,1},{4,6},{5,7},{6,4},{7,5},{8,10},{9,11},{10,... | collective-permute-start | bytes 589832 | tf_op jit(solution)/shard_map/ppermute | solution.py:328
  23.9 7.2 %collective-permute-start.14 = (bf16[3,128,256]{2,1,0:T(8,128)(2,1)S(1)}, bf16[3,128,256]{2,1,0:T(8,128)(2,1)S(1)}, u32[]{:S(2)}, u32[]{:S(2)}) collective-permute-start(bf16[3,128,256]{2,1,0:T(8,128)(2,1)S(1)} %pad_maximum_fusion.2.refs_5_), channel_id=1, source_target_pairs={{0,1},{1,0},{2,3},{3,2},{4,5},{5,4},{6,7},{7,6},{8,9},{9,8},{10,11... | collective-permute-start | bytes 589832 | tf_op jit(solution)/shard_map/ppermute | solution.py:328
  23.9 7.8 %collective-permute-start.10 = (bf16[3,128,256]{2,1,0:T(8,128)(2,1)S(1)}, bf16[3,128,256]{2,1,0:T(8,128)(2,1)S(1)}, u32[]{:S(2)}, u32[]{:S(2)}) collective-permute-start(bf16[3,128,256]{2,1,0:T(8,128)(2,1)S(1)} %pad_maximum_fusion.2.refs_5_), channel_id=1, source_target_pairs={{0,4},{4,0},{8,12},{12,8},{16,20},{20,16},{24,28},{28,24},{1,5},{5... | collective-permute-start | bytes 589832 | tf_op jit(solution)/shard_map/ppermute | solution.py:328
  25.6 8.4 %collective-permute-start.9 = (bf16[4,128,256]{2,1,0:T(8,128)(2,1)S(1)}, bf16[4,128,256]{2,1,0:T(8,128)(2,1)S(1)}, u32[]{:S(2)}, u32[]{:S(2)}) collective-permute-start(bf16[4,128,256]{2,1,0:T(8,128)(2,1)S(1)} %pad_maximum_fusion), channel_id=1, source_target_pairs={{0,2},{1,3},{2,0},{3,1},{4,6},{5,7},{6,4},{7,5},{8,10},{9,11},{10,... | collective-permute-start | bytes 786440 | tf_op jit(solution)/shard_map/ppermute | solution.py:328
  27.1 8.4 %collective-permute-start.11 = (bf16[3,128,256]{2,1,0:T(8,128)(2,1)S(1)}, bf16[3,128,256]{2,1,0:T(8,128)(2,1)S(1)}, u32[]{:S(2)}, u32[]{:S(2)}) collective-permute-start(bf16[3,128,256]{2,1,0:T(8,128)(2,1)S(1)} %collective-permute-done.8.refs_7_), channel_id=1, source_target_pairs={{0,4},{4,0},{8,12},{12,8},{16,20},{20,16},{24,28},{28,24},{1,5},{5... | collective-permute-start | bytes 589832 | tf_op jit(solution)/shard_map/ppermute | solution.py:328
  27.6 8.4 %collective-permute-start.13 = (bf16[3,144,256]{2,1,0:T(8,128)(2,1)S(1)}, bf16[3,144,256]{2,1,0:T(8,128)(2,1)S(1)}, u32[]{:S(2)}, u32[]{:S(2)}) collective-permute-start(bf16[3,144,256]{2,1,0:T(8,128)(2,1)S(1)} %pad_maximum_fusion.1.refs_4_), channel_id=1, source_target_pairs={{0,1},{1,0},{2,3},{3,2},{4,5},{5,4},{6,7},{7,6},{8,9},{9,8},{10,11... | collective-permute-start | bytes 663560 | tf_op jit(solution)/shard_map/ppermute | solution.py:328
  31.0 4.5 %collective-permute-start.16 = (bf16[3,128,256]{2,1,0:T(8,128)(2,1)S(1)}, bf16[3,128,256]{2,1,0:T(8,128)(2,1)S(1)}, u32[]{:S(2)}, u32[]{:S(2)}) collective-permute-start(bf16[3,128,256]{2,1,0:T(8,128)(2,1)S(1)} %collective-permute-done.8.refs_7_), channel_id=1, source_target_pairs={{0,1},{1,0},{2,3},{3,2},{4,5},{5,4},{6,7},{7,6},{8,9},{9,8},{10,11... | collective-permute-start | bytes 589832 | tf_op jit(solution)/shard_map/ppermute | solution.py:328
  31.7 4.4 %collective-permute-start.15 = (bf16[1,144,768]{2,1,0:T(8,128)(2,1)S(1)}, bf16[1,144,768]{2,1,0:T(8,128)(2,1)S(1)}, u32[]{:S(2)}, u32[]{:S(2)}) collective-permute-start(bf16[1,144,768]{2,1,0:T(8,128)(2,1)S(1)} %collective-permute-done.3.refs_6_), channel_id=1, source_target_pairs={{0,1},{1,0},{2,3},{3,2},{4,5},{5,4},{6,7},{7,6},{8,9},{9,8},{10,11... | collective-permute-start | bytes 663560 | tf_op jit(solution)/shard_map/ppermute | solution.py:328
  34.0 6.1 %collective-permute-start.12 = (bf16[3,128,256]{2,1,0:T(8,128)(2,1)S(1)}, bf16[3,128,256]{2,1,0:T(8,128)(2,1)S(1)}, u32[]{:S(2)}, u32[]{:S(2)}) collective-permute-start(bf16[3,128,256]{2,1,0:T(8,128)(2,1)S(1)} %collective-permute-done.10.refs_10_), channel_id=1, source_target_pairs={{0,2},{1,3},{2,0},{3,1},{4,6},{5,7},{6,4},{7,5},{8,10},{9,11},{10,... | collective-permute-start | bytes 589832 | tf_op jit(solution)/shard_map/ppermute | solution.py:328
  35.5 4.7 %collective-permute-start.18 = (bf16[4,128,256]{2,1,0:T(8,128)(2,1)S(1)}, bf16[4,128,256]{2,1,0:T(8,128)(2,1)S(1)}, u32[]{:S(2)}, u32[]{:S(2)}) collective-permute-start(bf16[4,128,256]{2,1,0:T(8,128)(2,1)S(1)} %collective-permute-done.9.refs_9_), channel_id=1, source_target_pairs={{0,1},{1,0},{2,3},{3,2},{4,5},{5,4},{6,7},{7,6},{8,9},{9,8},{10,11... | collective-permute-start | bytes 786440 | tf_op jit(solution)/shard_map/ppermute | solution.py:328
  35.5 4.6 %collective-permute-start.17 = (bf16[3,144,256]{2,1,0:T(8,128)(2,1)S(1)}, bf16[3,144,256]{2,1,0:T(8,128)(2,1)S(1)}, u32[]{:S(2)}, u32[]{:S(2)}) collective-permute-start(bf16[3,144,256]{2,1,0:T(8,128)(2,1)S(1)} %collective-permute-done.4.refs_8_), channel_id=1, source_target_pairs={{0,1},{1,0},{2,3},{3,2},{4,5},{5,4},{6,7},{7,6},{8,9},{9,8},{10,11... | collective-permute-start | bytes 663560 | tf_op jit(solution)/shard_map/ppermute | solution.py:328
  63.2 7.6 %collective-permute-start.22 = (bf16[4,4,112,256]{3,2,1,0:T(8,128)(2,1)S(1)}, bf16[4,4,112,256]{3,2,1,0:T(8,128)(2,1)S(1)}, u32[]{:S(2)}, u32[]{:S(2)}) collective-permute-start(bf16[4,4,112,256]{3,2,1,0:T(8,128)(2,1)S(1)} %get-tuple-element.60), channel_id=1, source_target_pairs={{0,1},{1,0},{2,3},{3,2},{4,5},{5,4},{6,7},{7,6},{8,9},{9,8},{10,11... | collective-permute-start | bytes 2752520 | tf_op jit(solution)/shard_map/ppermute | solution.py:328
  65.8 12.6 %collective-permute-start.24 = (bf16[2,4,112,256]{3,2,1,0:T(8,128)(2,1)S(1)}, bf16[2,4,112,256]{3,2,1,0:T(8,128)(2,1)S(1)}, u32[]{:S(2)}, u32[]{:S(2)}) collective-permute-start(bf16[2,4,112,256]{3,2,1,0:T(8,128)(2,1)S(1)} %get-tuple-element.64), channel_id=1, source_target_pairs={{0,2},{1,3},{2,0},{3,1},{4,6},{5,7},{6,4},{7,5},{8,10},{9,11},{10,... | collective-permute-start | bytes 1376264 | tf_op jit(solution)/shard_map/ppermute | solution.py:328
  67.4 12.3 %collective-permute-start.25 = (bf16[2,4,112,256]{3,2,1,0:T(8,128)(2,1)S(1)}, bf16[2,4,112,256]{3,2,1,0:T(8,128)(2,1)S(1)}, u32[]{:S(2)}, u32[]{:S(2)}) collective-permute-start(bf16[2,4,112,256]{3,2,1,0:T(8,128)(2,1)S(1)} %get-tuple-element.65), channel_id=1, source_target_pairs={{0,4},{4,0},{8,12},{12,8},{16,20},{20,16},{24,28},{28,24},{1,5},{5... | collective-permute-start | bytes 1376264 | tf_op jit(solution)/shard_map/ppermute | solution.py:328
  68.0 11.9 %collective-permute-start.29 = (bf16[2,16,1024]{2,1,0:T(8,128)(2,1)S(1)}, bf16[2,16,1024]{2,1,0:T(8,128)(2,1)S(1)}, u32[]{:S(2)}, u32[]{:S(2)}) collective-permute-start(bf16[2,16,1024]{2,1,0:T(8,128)(2,1)S(1)} %get-tuple-element.82), channel_id=1, source_target_pairs={{0,24},{4,28},{8,16},{12,20},{16,8},{20,12},{24,0},{28,4},{1,25},{... | collective-permute-start | bytes 196616 | tf_op jit(solution)/shard_map/ppermute | solution.py:328
  70.8 9.1 %collective-permute-start.28 = (bf16[2,16,1024]{2,1,0:T(8,128)(2,1)S(1)}, bf16[2,16,1024]{2,1,0:T(8,128)(2,1)S(1)}, u32[]{:S(2)}, u32[]{:S(2)}) collective-permute-start(bf16[2,16,1024]{2,1,0:T(8,128)(2,1)S(1)} %get-tuple-element.83), channel_id=1, source_target_pairs={{0,16},{4,20},{8,24},{12,28},{16,0},{20,4},{24,8},{28,12},{1,17},{... | collective-permute-start | bytes 196616 | tf_op jit(solution)/shard_map/ppermute | solution.py:328
  70.8 9.1 %collective-permute-start.27 = (bf16[2,16,1024]{2,1,0:T(8,128)(2,1)S(1)}, bf16[2,16,1024]{2,1,0:T(8,128)(2,1)S(1)}, u32[]{:S(2)}, u32[]{:S(2)}) collective-permute-start(bf16[2,16,1024]{2,1,0:T(8,128)(2,1)S(1)} %get-tuple-element.84), channel_id=1, source_target_pairs={{0,8},{4,12},{8,0},{12,4},{16,24},{20,28},{24,16},{28,20},{1,9},{5... | collective-permute-start | bytes 196616 | tf_op jit(solution)/shard_map/ppermute | solution.py:328
  79.9 4.4 %collective-permute-start.35 = (bf16[16,1024]{1,0:T(8,128)(2,1)S(1)}, bf16[16,1024]{1,0:T(8,128)(2,1)S(1)}, u32[]{:S(2)}, u32[]{:S(2)}) collective-permute-start(bf16[16,1024]{1,0:T(8,128)(2,1)S(1)} %slice_bitcast_fusion.4), channel_id=1, source_target_pairs={{0,4},{4,0},{8,12},{12,8},{16,20},{20,16},{24,28},{28,24},{1,5},{5... | collective-permute-start | bytes 98312 | tf_op jit(solution)/shard_map/ppermute | solution.py:328
  80.5 6.7 %collective-permute-start.30 = (bf16[4,112,256]{2,1,0:T(8,128)(2,1)S(1)}, bf16[4,112,256]{2,1,0:T(8,128)(2,1)S(1)}, u32[]{:S(2)}, u32[]{:S(2)}) collective-permute-start(bf16[4,112,256]{2,1,0:T(8,128)(2,1)S(1)} %get-tuple-element.68), channel_id=1, source_target_pairs={{0,4},{4,0},{8,12},{12,8},{16,20},{20,16},{24,28},{28,24},{1,5},{5... | collective-permute-start | bytes 688136 | tf_op jit(solution)/shard_map/ppermute | solution.py:328
  82.0 6.1 %collective-permute-start.31 = (bf16[4,112,256]{2,1,0:T(8,128)(2,1)S(1)}, bf16[4,112,256]{2,1,0:T(8,128)(2,1)S(1)}, u32[]{:S(2)}, u32[]{:S(2)}) collective-permute-start(bf16[4,112,256]{2,1,0:T(8,128)(2,1)S(1)} %get-tuple-element.69), channel_id=1, source_target_pairs={{0,2},{1,3},{2,0},{3,1},{4,6},{5,7},{6,4},{7,5},{8,10},{9,11},{10,... | collective-permute-start | bytes 688136 | tf_op jit(solution)/shard_map/ppermute | solution.py:328
  84.4 8.5 %collective-permute-start.36 = (bf16[16,512]{1,0:T(8,128)(2,1)S(1)}, bf16[16,512]{1,0:T(8,128)(2,1)S(1)}, u32[]{:S(2)}, u32[]{:S(2)}) collective-permute-start(bf16[16,512]{1,0:T(8,128)(2,1)S(1)} %pad_maximum_fusion.4), channel_id=1, source_target_pairs={{0,2},{1,3},{2,0},{3,1},{4,6},{5,7},{6,4},{7,5},{8,10},{9,11},{10,... | collective-permute-start | bytes 49160 | tf_op jit(solution)/shard_map/ppermute | solution.py:328
  88.4 7.1 %collective-permute-start.32 = (bf16[112,512]{1,0:T(8,128)(2,1)S(1)}, bf16[112,512]{1,0:T(8,128)(2,1)S(1)}, u32[]{:S(2)}, u32[]{:S(2)}) collective-permute-start(bf16[112,512]{1,0:T(8,128)(2,1)S(1)} %get-tuple-element.79), channel_id=1, source_target_pairs={{0,24},{4,28},{8,16},{12,20},{16,8},{20,12},{24,0},{28,4},{1,25},{... | collective-permute-start | bytes 344072 | tf_op jit(solution)/shard_map/ppermute | solution.py:328
  90.5 8.4 %collective-permute-start.33 = (bf16[112,512]{1,0:T(8,128)(2,1)S(1)}, bf16[112,512]{1,0:T(8,128)(2,1)S(1)}, u32[]{:S(2)}, u32[]{:S(2)}) collective-permute-start(bf16[112,512]{1,0:T(8,128)(2,1)S(1)} %get-tuple-element.80), channel_id=1, source_target_pairs={{0,16},{4,20},{8,24},{12,28},{16,0},{20,4},{24,8},{28,12},{1,17},{... | collective-permute-start | bytes 344072 | tf_op jit(solution)/shard_map/ppermute | solution.py:328
  90.6 8.4 %collective-permute-start.34 = (bf16[112,512]{1,0:T(8,128)(2,1)S(1)}, bf16[112,512]{1,0:T(8,128)(2,1)S(1)}, u32[]{:S(2)}, u32[]{:S(2)}) collective-permute-start(bf16[112,512]{1,0:T(8,128)(2,1)S(1)} %get-tuple-element.81), channel_id=1, source_target_pairs={{0,8},{4,12},{8,0},{12,4},{16,24},{20,28},{24,16},{28,20},{1,9},{5... | collective-permute-start | bytes 344072 | tf_op jit(solution)/shard_map/ppermute | solution.py:328
  (8 other events, 113.7 us)
